TPU v7x, 32 devices: a whole 2x2x4 slice. The times are simulated.
32 devices in a mesh: dp: 8 (over y, x, core), space: 4 (over z).
Axes of the slice: x: 2, y: 2, z: 4, core: 2. Of those that a mesh axis runs over, the one named last changes fastest.
Arguments:
- features: bfloat16 [8, 24, 32, 1024], P('dp', 'space'), may hold values from -6 to 6
- labels: int32 [8, 24, 32], P('dp', 'space'), may hold values from 0 to 2
- pixel_weight: int32 [8, 24, 32], P('dp', 'space'), may hold values from 1 to 4
- conv_weight: bfloat16 [1024, 9, 128], replicated, may hold values from -0.0625 to 0.0625
- conv_bias: float32 [128], replicated, may hold values from -3 to 3
- class_weight: bfloat16 [128, 3], replicated, may hold values from -1.5 to 1.5
Outputs:
- features_grad: float32 [8, 24, 32, 1024], P('dp', 'space')
- weight_grad: float32 [9216, 128], P(('dp', 'space'))
All inputs are finite; a program needn't handle non-finite values.
Results may differ from a plain program's by a relative error of at most 0.011.
Values may be sent and summed in bfloat16 or wider, within the bound.
No kernel may reach another device: no remote copies, remote signals or barrier semaphores. Data moves between devices by JAX's collectives and lax.ppermute only.
A program may use at most 64 MiB of HBM per device.

v0:
```python
import jax
import jax.numpy as jnp
from jax import lax
from jax.sharding import PartitionSpec as P

DILATION_SIZE = 6


def padded(array, sides, width):
    for axis, dim in sides:
        count, length = (lax.axis_size(axis), array.shape[dim])
        up = [(i, (i + 1) % count) for i in range(count - 1)]
        down = [(j, i) for i, j in up]
        last = lax.slice_in_dim(array, length - width, length, axis=dim)
        leading = lax.slice_in_dim(array, 0, width, axis=dim)
        before = lax.ppermute(last, axis, up)
        after = lax.ppermute(leading, axis, down)
        array = jnp.concatenate([before, array, after], axis=dim)
    return array


def on_device(features, labels, pixel_weight, conv_weight, conv_bias, class_weight):
    input_image = features[0]
    band_row_span, band_column_span, input_width = input_image.shape
    tap_count = conv_weight.shape[1]
    output_width = conv_weight.shape[2]
    pixel_count = band_row_span * band_column_span
    flat_weight = conv_weight.reshape(input_width, tap_count * output_width)
    flat_image = input_image.reshape(pixel_count, input_width)
    extended_rows = padded(input_image, (("space", 0),), DILATION_SIZE)
    widened_input = jnp.pad(extended_rows, ((0, 0), (DILATION_SIZE, DILATION_SIZE), (0, 0)))
    stacked = jnp.stack(
        [
            widened_input[
                tap_row * DILATION_SIZE : tap_row * DILATION_SIZE + band_row_span,
                column_tap * DILATION_SIZE : column_tap * DILATION_SIZE + band_column_span,
            ]
            for tap_row in range(3)
            for column_tap in range(3)
        ],
        axis=2,
    )
    conv_out = lax.dot_general(
        stacked.reshape(pixel_count, tap_count, input_width),
        conv_weight,
        (((1, 2), (1, 0)), ((), ())),
        preferred_element_type=jnp.float32,
    )
    preact = conv_out + conv_bias
    sigmoid_z = jax.nn.sigmoid(preact)
    hidden = (preact * sigmoid_z).astype(jnp.bfloat16)
    logits = jnp.dot(hidden, class_weight, preferred_element_type=jnp.float32)
    exponent = jnp.exp(logits)
    chances = exponent / jnp.sum(exponent, axis=1, keepdims=True)
    classes = lax.broadcasted_iota(jnp.int32, (1, class_weight.shape[1]), 1)
    onehot = (labels.reshape(pixel_count, 1) == classes).astype(jnp.float32)
    grad_logits = pixel_weight.reshape(pixel_count, 1).astype(jnp.float32) * (chances - onehot)
    hidden_grad = jnp.dot(
        grad_logits, class_weight.astype(jnp.float32).T, precision=lax.Precision.HIGHEST
    )
    preact_gradient = (hidden_grad * sigmoid_z * (1.0 + preact * (1.0 - sigmoid_z))).astype(
        jnp.bfloat16
    )
    extended_gradient = padded(
        preact_gradient.reshape(band_row_span, band_column_span, output_width),
        (("space", 0),),
        DILATION_SIZE,
    )
    widened_gradient = jnp.pad(extended_gradient, ((0, 0), (DILATION_SIZE, DILATION_SIZE), (0, 0)))
    grad_cols = jnp.concatenate(
        [
            widened_gradient[
                (2 - tap_row) * DILATION_SIZE : (2 - tap_row) * DILATION_SIZE + band_row_span,
                (2 - column_tap) * DILATION_SIZE : (2 - column_tap) * DILATION_SIZE
                + band_column_span,
            ].reshape(pixel_count, output_width)
            for tap_row in range(3)
            for column_tap in range(3)
        ],
        axis=1,
    )
    feature_grad = lax.dot_general(
        grad_cols, flat_weight, (((1,), (1,)), ((), ())), preferred_element_type=jnp.float32
    )
    feature_grad = feature_grad.reshape(1, band_row_span, band_column_span, input_width)
    replicas = lax.axis_size("dp")
    band_count = lax.axis_size("space")
    contribution = lax.dot_general(
        flat_image, grad_cols, (((0,), (0,)), ((), ())), preferred_element_type=jnp.float32
    )
    block_rows = input_width * tap_count // (replicas * band_count)
    contribution = contribution.reshape(replicas, band_count, block_rows, output_width).transpose(
        1, 0, 2, 3
    )
    contribution = contribution.reshape(input_width * tap_count, output_width)
    within = lax.psum_scatter(
        contribution.astype(jnp.bfloat16), "space", scatter_dimension=0, tiled=True
    ).astype(jnp.float32)
    summed = lax.psum_scatter(within, "dp", scatter_dimension=0, tiled=True)
    weight_grad = summed / replicas
    return (feature_grad, weight_grad)


def solution(mesh):
    placed = (
        P("dp", "space", None, None),
        P("dp", "space", None),
        P("dp", "space", None),
        P(),
        P(),
        P(),
    )
    return jax.shard_map(
        on_device,
        mesh=mesh,
        in_specs=placed,
        out_specs=(P("dp", "space", None, None), P(("dp", "space"), None)),
        check_vma=False,
    )
```

profile of v0, /device:TPU:0, one launch (start us, length us, event | category | flops | bytes accessed | tf_op | source)
XLA Modules:
  0.0 145.1 jit_solution(15367932020451679683)
XLA Ops:
  7.2 0.0 copy-start
  7.2 0.0 reduce-scatter.3.cloned.1.call-start
  7.2 5.0 %collective-permute-start = (bf16[6,32,1024]{2,1,0:T(8,128)(2,1)}, bf16[6,32,1024]{2,1,0:T(8,128)(2,1)S(1)}, u32[]{:S(2)}, u32[]{:S(2)}) collective-permute-start(bf16[6,32,1024]{2,1,0:T(8,128)(2,1)} %bitcast.62), channel_id=1, source_target_pairs={{0,1},{1,2},{2,3},{4,5},{5,6},{6,7},{8,9},{9,10},{10,11},{12,13},{... | collective-permute-start | bytes 1179656 | tf_op jit(solution)/shard_map/ppermute | solution.py:16
  12.2 1.3 collective-permute-start.1
  13.5 0.7 convert_reduce_fusion
  14.2 0.1 convert_element_type.44
  14.3 0.7 reduce.1
  15.0 0.1 eq.15
  15.0 5.8 %collective-permute-done = bf16[6,32,1024]{2,1,0:T(8,128)(2,1)S(1)} collective-permute-done((bf16[6,32,1024]{2,1,0:T(8,128)(2,1)}, bf16[6,32,1024]{2,1,0:T(8,128)(2,1)S(1)}, u32[]{:S(2)}, u32[]{:S(2)}) %collective-permute-start) | collective-permute-done | bytes 393248 | tf_op jit(solution)/shard_map/ppermute | solution.py:16
  20.8 4.0 %collective-permute-done.1 = bf16[6,32,1024]{2,1,0:T(8,128)(2,1)S(1)} collective-permute-done((bf16[6,32,1024]{2,1,0:T(8,128)(2,1)}, bf16[6,32,1024]{2,1,0:T(8,128)(2,1)S(1)}, u32[]{:S(2)}, u32[]{:S(2)}) %collective-permute-start.1) | collective-permute-done | bytes 393248 | tf_op jit(solution)/shard_map/ppermute | solution.py:17
  24.9 1.6 %fusion.6 = bf16[18,44,1024]{2,1,0:T(8,128)(2,1)S(1)} fusion(bf16[6,32,1024]{2,1,0:T(8,128)(2,1)S(1)} %collective-permute-done.1, bf16[6,32,1024]{2,1,0:T(8,128)(2,1)} %bitcast.64, bf16[6,32,1024]{2,1,0:T(8,128)(2,1)S(1)} %collective-permute-done), kind=kLoop, calls=%fused_computation.9 | loop fusion | flops 9732096 | bytes 2801664 | tf_op jit(solution)/shard_map/concatenate | solution.py:18
  26.5 0.0 copy-start.3
  26.5 0.6 fusion.22
  27.1 0.0 copy-start.1
  27.3 0.2 copy-done.3
  27.7 1.2 copy-done.1
  28.8 1.1 fusion.8
  30.0 0.2 fusion.24
  30.2 0.3 fusion.9
  30.5 3.5 %collective-permute-start.2 = (bf16[6,32,128]{2,1,0:T(8,128)(2,1)S(1)}, bf16[6,32,128]{2,1,0:T(8,128)(2,1)S(1)}, u32[]{:S(2)}, u32[]{:S(2)}) collective-permute-start(bf16[6,32,128]{2,1,0:T(8,128)(2,1)S(1)} %bitcast.76), channel_id=1, source_target_pairs={{0,1},{1,2},{2,3},{4,5},{5,6},{6,7},{8,9},{9,10},{10,11},{12,13},{... | collective-permute-start | bytes 147464 | tf_op jit(solution)/shard_map/ppermute | solution.py:16
  33.9 1.3 collective-permute-start.3
  35.2 0.4 collective-permute-done.2
  35.7 4.3 %collective-permute-done.3 = bf16[6,32,128]{2,1,0:T(8,128)(2,1)S(1)} collective-permute-done((bf16[6,32,128]{2,1,0:T(8,128)(2,1)S(1)}, bf16[6,32,128]{2,1,0:T(8,128)(2,1)S(1)}, u32[]{:S(2)}, u32[]{:S(2)}) %collective-permute-start.3) | collective-permute-done | bytes 49184 | tf_op jit(solution)/shard_map/ppermute | solution.py:17
  39.9 0.1 fusion.16
  40.0 0.1 fusion.23
  40.3 0.8 fusion.1
  41.1 2.5 %copy.13 = bf16[1024,1152]{1,0:T(8,128)(2,1)} copy(bf16[1024,1152]{0,1:T(8,128)(2,1)S(1)} %fusion.1) | data formatting | bytes 4718592 | tf_op jit(solution)/shard_map/convert_element_type | solution.py:97
  43.6 4.5 %convert_element_type.50 = bf16[8,4,288,128]{3,2,1,0:T(8,128)(2,1)S(1)} reshape(bf16[1024,1152]{1,0:T(8,128)(2,1)} %copy.13) | data formatting | bytes 4718592 | tf_op jit(solution)/shard_map/convert_element_type | solution.py:97
  48.1 1.6 %copy.14 = bf16[4,8,288,128]{3,2,1,0:T(8,128)(2,1)} copy(bf16[4,8,288,128]{3,2,0,1:T(8,128)(2,1)S(1)} %bitcast.61) | data formatting | bytes 4718592 | tf_op jit(solution)/shard_map/convert_element_type | solution.py:97
  49.7 0.0 reduce-scatter.3.cloned.1.call-update
  49.7 0.0 reduce-scatter.5.cloned.1.call-start
  49.8 1.6 %copy-done.2 = bf16[1024,9,128]{2,0,1:T(8,128)(2,1)S(1)} copy-done((bf16[1024,9,128]{2,0,1:T(8,128)(2,1)S(1)}, bf16[1024,9,128]{2,0,1:T(8,128)(2,1)}, u32[]{:S(2)}) %copy-start.2) | copy-done | bytes 2359320
  51.3 2.5 %copy.11 = bf16[1024,9,128]{0,2,1:T(8,128)(2,1)} copy(bf16[1024,9,128]{2,0,1:T(8,128)(2,1)S(1)} %copy-done.2) | data formatting | bytes 4718592 | tf_op args[3]
  53.8 0.6 constant_dynamic-update-slice_fusion.17
  54.5 42.7 %reduce-scatter.3.cloned.1.call-done = bf16[2304,128]{1,0:T(8,128)(2,1)} async-done(((bf16[9216,128]{1,0:T(8,128)(2,1)}), bf16[2304,128]{1,0:T(8,128)(2,1)}) %reduce-scatter.3.cloned.1.call-update) | async-done | bytes 589840 | tf_op jit(solution)/shard_map/reduce_scatter | solution.py:96
  97.1 2.2 %convert_element_type.53 = f32[2304,128]{1,0:T(8,128)} convert(bf16[2304,128]{1,0:T(8,128)(2,1)} %reduce-scatter.3.cloned.1.call-done) | non-fusion elementwise | flops 294912 | bytes 1769472 | tf_op jit(solution)/shard_map/convert_element_type | solution.py:98
  99.3 0.0 reduce-scatter.5.cloned.1.call-update
  99.3 0.7 constant_dynamic-update-slice_fusion.16
  100.0 0.6 constant_dynamic-update-slice_fusion.15
  100.6 0.6 constant_dynamic-update-slice_fusion.14
  101.2 0.6 constant_dynamic-update-slice_fusion.13
  101.9 0.6 constant_dynamic-update-slice_fusion.12
  102.5 0.7 constant_dynamic-update-slice_fusion.11
  103.1 0.6 constant_dynamic-update-slice_fusion.10
  103.8 0.6 constant_dynamic-update-slice_fusion.9
  104.4 2.7 %convolution_bitcast_fusion = f32[1,6,32,1024]{3,2,1,0:T(8,128)} fusion(bf16[1024,1152,1]{0,1,2:T(8,128)(2,1)S(1)} %bitcast.67, bf16[1,6,32,1152]{3,2,1,0:T(8,128)(2,1)} %constant_dynamic-update-slice_fusion.9), kind=kOutput, calls=%fused_computation.10 | convolution fusion | flops 452984832 | bytes 3588096 | tf_op jit(solution)/shard_map/dot_general | solution.py:82
  107.1 29.6 %reduce-scatter.5.cloned.1.call-done = f32[288,128]{1,0:T(8,128)} async-done(((f32[2304,128]{1,0:T(8,128)}), f32[288,128]{1,0:T(8,128)}) %reduce-scatter.5.cloned.1.call-update) | async-done | bytes 147472 | tf_op jit(solution)/shard_map/reduce_scatter | solution.py:99
  136.7 1.6 %broadcast_multiply_fusion = f32[288,128]{1,0:T(8,128)} fusion(f32[288,128]{1,0:T(8,128)} %reduce-scatter.5.cloned.1.call-done), kind=kLoop, calls=%fused_computation.28 | loop fusion | flops 36864 | bytes 294912 | tf_op jit(solution)/shard_map/div | solution.py:100
  (24 shorter events, 0.4 us)
Async XLA Ops:
  7.2 22.8 %copy-start = (bf16[128,3]{0,1:T(4,128)(2,1)S(1)}, bf16[128,3]{0,1:T(4,128)(2,1)}, u32[]{:S(2)}) copy-start(bf16[128,3]{0,1:T(4,128)(2,1)} %param.11) | copy-start | bytes 2308
  7.2 89.9 %reduce-scatter.3.cloned.1.call-start = ((), (), s32[]{:S(2)}) async-start(), calls=%async_computation.2 | async-start | bytes 2949120 | tf_op jit(solution)/shard_map/reduce_scatter | solution.py:96
  7.2 13.6 %collective-permute-start = (bf16[6,32,1024]{2,1,0:T(8,128)(2,1)}, bf16[6,32,1024]{2,1,0:T(8,128)(2,1)S(1)}, u32[]{:S(2)}, u32[]{:S(2)}) collective-permute-start(bf16[6,32,1024]{2,1,0:T(8,128)(2,1)} %bitcast.62), channel_id=1, source_target_pairs={{0,1},{1,2},{2,3},{4,5},{5,6},{6,7},{8,9},{9,10},{10,11},{12,13},{... | collective-permute-start | bytes 1179656 | tf_op jit(solution)/shard_map/ppermute | solution.py:16
  12.2 12.7 %collective-permute-start.1 = (bf16[6,32,1024]{2,1,0:T(8,128)(2,1)}, bf16[6,32,1024]{2,1,0:T(8,128)(2,1)S(1)}, u32[]{:S(2)}, u32[]{:S(2)}) collective-permute-start(bf16[6,32,1024]{2,1,0:T(8,128)(2,1)} %bitcast.63), channel_id=1, source_target_pairs={{1,0},{2,1},{3,2},{5,4},{6,5},{7,6},{9,8},{10,9},{11,10},{13,12},{... | collective-permute-start | bytes 1179656 | tf_op jit(solution)/shard_map/ppermute | solution.py:17
  26.5 1.0 copy-start.3
  27.1 1.7 %copy-start.1 = (bf16[1024,9,128]{2,0,1:T(8,128)(2,1)S(1)}, bf16[1024,9,128]{2,0,1:T(8,128)(2,1)}, u32[]{:S(2)}) copy-start(bf16[1024,9,128]{2,0,1:T(8,128)(2,1)} %param.9) | copy-start | bytes 7077892
  27.2 1.7 %copy-start.5 = (f32[128]{0:T(128)S(1)}, f32[128]{0:T(128)}, u32[]{:S(2)}) copy-start(f32[128]{0:T(128)} %param.10) | copy-start | bytes 1540
  30.5 5.2 %collective-permute-start.2 = (bf16[6,32,128]{2,1,0:T(8,128)(2,1)S(1)}, bf16[6,32,128]{2,1,0:T(8,128)(2,1)S(1)}, u32[]{:S(2)}, u32[]{:S(2)}) collective-permute-start(bf16[6,32,128]{2,1,0:T(8,128)(2,1)S(1)} %bitcast.76), channel_id=1, source_target_pairs={{0,1},{1,2},{2,3},{4,5},{5,6},{6,7},{8,9},{9,10},{10,11},{12,13},{... | collective-permute-start | bytes 147464 | tf_op jit(solution)/shard_map/ppermute | solution.py:16
  33.9 6.0 %collective-permute-start.3 = (bf16[6,32,128]{2,1,0:T(8,128)(2,1)S(1)}, bf16[6,32,128]{2,1,0:T(8,128)(2,1)S(1)}, u32[]{:S(2)}, u32[]{:S(2)}) collective-permute-start(bf16[6,32,128]{2,1,0:T(8,128)(2,1)S(1)} %bitcast.77), channel_id=1, source_target_pairs={{1,0},{2,1},{3,2},{5,4},{6,5},{7,6},{9,8},{10,9},{11,10},{13,12},{... | collective-permute-start | bytes 147464 | tf_op jit(solution)/shard_map/ppermute | solution.py:17
  49.7 1.7 %copy-start.2 = (bf16[1024,9,128]{2,0,1:T(8,128)(2,1)S(1)}, bf16[1024,9,128]{2,0,1:T(8,128)(2,1)}, u32[]{:S(2)}) copy-start(bf16[1024,9,128]{2,0,1:T(8,128)(2,1)} %param.9) | copy-start | bytes 7077892
  49.7 87.0 %reduce-scatter.5.cloned.1.call-start = ((), (), s32[]{:S(2)}) async-start(), calls=%async_computation.3 | async-start | bytes 1327104 | tf_op jit(solution)/shard_map/reduce_scatter | solution.py:99
  53.8 50.6 %copy-start.4 = (bf16[1024,9,128]{0,2,1:T(8,128)(2,1)S(1)}, bf16[1024,9,128]{0,2,1:T(8,128)(2,1)}, u32[]{:S(2)}) copy-start(bf16[1024,9,128]{0,2,1:T(8,128)(2,1)} %copy.11) | copy-start | bytes 7077892
Sparse Core Ops, SparseCore 0:
  49.8 47.2 reduce-scatter.2
  100.3 36.3 reduce-scatter.4
where the time goes:
time: 146 us; the launch traced here: 145 us
  waiting for transfers between devices  86.8 us (59%)
  local copies, waits for them, and re-layouts  21 us (14%)
  between operations  14.3 us (10%)
  starting transfers between devices  11.1 us (8%)
  other arithmetic  6.84 us (5%)
  matrix products  5.07 us (3%)
    reduce_scatter x1, waiting for transfers between devices, on_device(): lax.psum_scatter(contribution.astype(jnp.bfloat16), 'space', scatter_dime...  42.7 us
    reduce_scatter x1, waiting for transfers between devices, on_device(): summed = lax.psum_scatter(within, 'dp', scatter_dimension=0, tiled=True)  29.6 us
    unnamed x37, local copies, waits for them, and re-layouts  10.9 us
    convert_element_type x3, local copies, waits for them, and re-layouts, on_device(): contribution.astype(jnp.bfloat16)  8.58 us
    ppermute x2, starting transfers between devices, padded(): before = lax.ppermute(last, axis, up)  8.42 us
    ppermute x2, waiting for transfers between devices, padded(): after = lax.ppermute(leading, axis, down)  8.29 us
    ppermute x2, waiting for transfers between devices, padded(): before = lax.ppermute(last, axis, up)  6.22 us
  transfers between devices with their start and end apart: 6, of which 6 were waited for; matrix products, arithmetic and copies ran while one was open for 9% of the time, Pallas kernels for 0%

commit v1 on v0

v1 whole, which is shorter than its diff:
```python
import jax
import jax.numpy as jnp
from jax import lax
from jax.sharding import PartitionSpec as P

DILATION_SIZE = 6


def channel_plan(channels, taps, replicas, bands):
    rows = channels * taps // (replicas * bands)
    starts = [[(d * bands + s) * rows // taps for d in range(replicas)] for s in range(bands)]
    offsets = [[(d * bands + s) * rows % taps for d in range(replicas)] for s in range(bands)]
    cover = max(-(-(off + rows) // taps) for line in offsets for off in line)
    picks = [[min(c + k, channels - 1) for c in line for k in range(cover)] for line in starts]
    return rows, cover, picks, offsets


def column_shift(array, by):
    width = array.shape[1]
    if by == 0:
        return array
    if by > 0:
        return jnp.pad(array[:, by:], ((0, 0), (0, by), (0, 0)))
    return jnp.pad(array[:, : width + by], ((0, 0), (-by, 0), (0, 0)))


def on_device(features, labels, pixel_weight, conv_weight, conv_bias, class_weight):
    image = features[0]
    band_rows, columns, channels = image.shape
    taps, width = conv_weight.shape[1:]
    pixels = band_rows * columns
    replicas = lax.axis_size("dp")
    bands = lax.axis_size("space")
    band = lax.axis_index("space")
    reach = DILATION_SIZE

    block_rows, cover, picks, offsets = channel_plan(channels, taps, replicas, bands)
    flat = image.reshape(pixels, channels)
    if block_rows % taps == 0:
        split = flat.reshape(pixels, replicas, bands, cover).transpose(2, 0, 1, 3)
        split = split.reshape(bands, pixels, replicas * cover)
    else:
        order = jnp.array([c for line in picks for c in line], jnp.int32)
        split = jnp.take(flat, order, axis=1).reshape(pixels, bands, replicas * cover).transpose(1, 0, 2)
    whole = lax.all_to_all(split, "space", 0, 0)

    product = lax.dot_general(
        flat, conv_weight, (((1,), (0,)), ((), ())), preferred_element_type=jnp.float32
    ).reshape(band_rows, columns, taps, width)
    parts = [
        sum(column_shift(product[:, :, 3 * a + b], (b - 1) * reach) for b in range(3)) for a in range(3)
    ]
    spread = sum(
        jnp.pad(parts[a], (((2 - a) * reach, a * reach), (0, 0), (0, 0))) for a in range(3)
    )
    before = spread[:reach].astype(jnp.bfloat16)
    after = spread[reach + band_rows :].astype(jnp.bfloat16)
    index = jnp.arange(bands)[:, None, None, None]
    blocks = jnp.where(index == band - 1, before, jnp.where(index == band + 1, after, jnp.bfloat16(0)))
    came = lax.all_to_all(blocks, "space", 0, 0)
    from_above = jnp.sum(jnp.where(index == band - 1, came, 0), axis=0, dtype=jnp.float32)
    from_below = jnp.sum(jnp.where(index == band + 1, came, 0), axis=0, dtype=jnp.float32)
    middle = spread[reach : reach + band_rows]
    middle = middle + jnp.pad(from_above, ((0, band_rows - reach), (0, 0), (0, 0)))
    middle = middle + jnp.pad(from_below, ((band_rows - reach, 0), (0, 0), (0, 0)))
    preact = middle.reshape(pixels, width) + conv_bias

    sigmoid_z = jax.nn.sigmoid(preact)
    hidden = (preact * sigmoid_z).astype(jnp.bfloat16)
    logits = jnp.dot(hidden, class_weight, preferred_element_type=jnp.float32)
    exponent = jnp.exp(logits)
    chances = exponent / jnp.sum(exponent, axis=1, keepdims=True)
    classes = lax.broadcasted_iota(jnp.int32, (1, class_weight.shape[1]), 1)
    onehot = (labels.reshape(pixels, 1) == classes).astype(jnp.float32)
    grad_logits = pixel_weight.reshape(pixels, 1).astype(jnp.float32) * (chances - onehot)
    hidden_grad = jnp.dot(
        grad_logits, class_weight.astype(jnp.float32).T, precision=lax.Precision.HIGHEST
    )
    gradient = (hidden_grad * sigmoid_z * (1.0 + preact * (1.0 - sigmoid_z))).astype(jnp.bfloat16)

    gathered = lax.all_to_all(
        jnp.broadcast_to(gradient[None], (bands, pixels, width)), "space", 0, 0
    ).reshape(bands * band_rows, columns, width)
    wide = jnp.pad(gathered, ((reach, reach), (reach, reach), (0, 0)))
    tap_views = [
        wide[(2 - a) * reach : (2 - a) * reach + bands * band_rows, (2 - b) * reach : (2 - b) * reach + columns]
        for a in range(3)
        for b in range(3)
    ]
    shifted = jnp.concatenate(
        [view.reshape(bands * pixels, width) for view in tap_views], axis=1
    )
    kernel_grad = lax.dot_general(
        whole.reshape(bands * pixels, replicas * cover),
        shifted,
        (((0,), (0,)), ((), ())),
        preferred_element_type=jnp.float32,
    )
    blocks = kernel_grad.astype(jnp.bfloat16).reshape(replicas, cover, taps * width)
    came = lax.all_to_all(blocks, "dp", 0, 0)
    weight_grad = jnp.sum(came.astype(jnp.float32), axis=0) / replicas
    weight_grad = weight_grad.reshape(cover * taps, width)
    if block_rows % taps:
        me = lax.axis_index("dp")
        weight_grad = lax.dynamic_slice_in_dim(weight_grad, jnp.array(offsets)[band, me], block_rows)

    local = lax.dynamic_slice_in_dim(shifted, band * pixels, pixels)
    feature_grad = lax.dot_general(
        local.reshape(pixels, taps, width),
        conv_weight,
        (((1, 2), (1, 2)), ((), ())),
        preferred_element_type=jnp.float32,
    )
    return feature_grad.reshape(1, band_rows, columns, channels), weight_grad


def solution(mesh):
    placed = (
        P("dp", "space", None, None),
        P("dp", "space", None),
        P("dp", "space", None),
        P(),
        P(),
        P(),
    )
    return jax.shard_map(
        on_device,
        mesh=mesh,
        in_specs=placed,
        out_specs=(P("dp", "space", None, None), P(("dp", "space"), None)),
        check_vma=False,
    )
```

time: 146 us -> 63.5 us (0.43)
  waiting for transfers between devices: 86.8 us -> 15.8 us
  between operations: 14.3 us -> 0.86 us
  starting transfers between devices: 11.1 us -> 18.4 us
  other arithmetic: 6.84 us -> 1.24 us
  matrix products: 5.07 us -> 8.16 us
  local copies, waits for them, and re-layouts: 21 us -> 18.3 us
    reduce_scatter x2 -> x0, waiting for transfers between devices: 72.3 us -> none  [the longest x1 42.7 us: on_device(): lax.psum_scatter(contribution.astype(jnp.bfloat16), 'space', scatter_dime...]
    all_to_all x0 -> x4, starting transfers between devices: none -> 18.4 us  [the longest x1 6.32 us: on_device(): came = lax.all_to_all(blocks, 'space', 0, 0)]
    all_to_all x0 -> x4, waiting for transfers between devices: none -> 15.8 us  [the longest x1 7.31 us: on_device(): came = lax.all_to_all(blocks, 'space', 0, 0)]
    ppermute x4 -> x0, waiting for transfers between devices: 14.5 us -> none  [the longest x2 8.29 us: padded(): after = lax.ppermute(leading, axis, down)]
    ppermute x4 -> x0, starting transfers between devices: 11 us -> none  [the longest x2 8.42 us: padded(): before = lax.ppermute(last, axis, up)]
    convert_element_type x4 -> x1, local copies, waits for them, and re-layouts: 8.66 us -> 0.08 us  [on_device(): pixel_weight.reshape(pixels, 1).astype(jnp.float32) * (chances - onehot)]
    another operation x1 -> x2, local copies, waits for them, and re-layouts: 0.03 us -> 3.52 us  [the longest x1 2.39 us: on_device(): split = flat.reshape(pixels, replicas, bands, cover).transpose(2, 0, 1, 3)]
    unnamed x37 -> x20, local copies, waits for them, and re-layouts: 10.9 us -> 7.42 us
  transfers between devices with their start and end apart: 6 -> 4, of which waited for: 6 -> 3; matrix products, arithmetic and copies ran while one was open for 9% -> 29% of each run, Pallas kernels for 0% -> 0%
where the time goes in v1:
time: 63.5 us; the launch traced here: 62.8 us
  starting transfers between devices  18.4 us (29%)
  local copies, waits for them, and re-layouts  18.3 us (29%)
  waiting for transfers between devices  15.8 us (25%)
  matrix products  8.16 us (13%)
  other arithmetic  1.24 us (2%)
  between operations  0.86 us (1%)
    unnamed x20, local copies, waits for them, and re-layouts  7.42 us
    all_to_all x1, waiting for transfers between devices, on_device(): came = lax.all_to_all(blocks, 'space', 0, 0)  7.31 us
    all_to_all x1, starting transfers between devices, on_device(): came = lax.all_to_all(blocks, 'space', 0, 0)  6.32 us
    all_to_all x1, waiting for transfers between devices, on_device(): came = lax.all_to_all(blocks, 'dp', 0, 0)  5.3 us
    all_to_all x1, starting transfers between devices, on_device(): whole = lax.all_to_all(split, 'space', 0, 0)  5.01 us
    all_to_all x1, starting transfers between devices, on_device(): came = lax.all_to_all(blocks, 'dp', 0, 0)  3.73 us
    all_to_all x1, starting transfers between devices, on_device(): lax.all_to_all(jnp.broadcast_to(gradient[None], (bands, pixels, width)),...  3.36 us
    all_to_all x1, waiting for transfers between devices, on_device(): whole = lax.all_to_all(split, 'space', 0, 0)  3.16 us
  transfers between devices with their start and end apart: 4, of which 3 were waited for; matrix products, arithmetic and copies ran while one was open for 29% of the time, Pallas kernels for 0%

profile of v1, /device:TPU:0, one launch (start us, length us, event | category | flops | bytes accessed | tf_op | source)
XLA Modules:
  0.0 62.8 jit_solution(16875448182122553780)
XLA Ops:
  0.6 0.0 copy-start
  0.6 1.7 %copy-done = bf16[1024,9,128]{2,0,1:T(8,128)(2,1)S(1)} copy-done((bf16[1024,9,128]{2,0,1:T(8,128)(2,1)S(1)}, bf16[1024,9,128]{2,0,1:T(8,128)(2,1)}, u32[]{:S(2)}) %copy-start) | copy-done | bytes 2359320
  2.3 1.7 %fusion.2 = f32[6,32,9,128]{3,1,2,0:T(8,128)S(1)} fusion(bf16[1024,9,128]{2,0,1:T(8,128)(2,1)S(1)} %copy-done, bf16[1,6,32,1024]{3,2,1,0:T(8,128)(2,1)} %param.6), kind=kOutput, calls=%fused_computation.3 | convolution fusion | flops 452984832 | bytes 3637248 | tf_op jit(solution)/shard_map/dot_general | solution.py:47
  4.0 0.0 copy-start.2
  4.0 0.0 copy-start.3
  4.1 0.0 copy-start.4
  4.1 0.0 copy-start.5
  4.1 0.1 fusion.17
  4.3 0.0 copy-start.1
  4.3 0.8 %select_select_fusion = bf16[4,6,32,128]{3,2,1,0:T(8,128)(2,1)} fusion(pred[4]{0:T(512)(128)(4,1)S(1)} %get-tuple-element.27, pred[4]{0:T(512)(128)(4,1)S(1)} %get-tuple-element.28, bf16[6,32,128]{2,1,0:T(8,128)(2,1)S(1)} %get-tuple-element.24, bf16[6,32,128]{2,1,0:T(8,128)(2,1)S(1)} %get-tuple-element.23), kind=kLoop, calls=%fused_computation.24 | loop fusion | flops 196608 | bytes 294920 | tf_op jit(solution)/shard_map/jit(_where)/select_n | solution.py:59
  5.1 6.3 %all-to-all-start = ((bf16[4,6,32,128]{3,2,1,0:T(8,128)(2,1)}), bf16[4,6,32,128]{3,2,1,0:T(8,128)(2,1)S(1)}, u32[]{:S(2)}, u32[]{:S(2)}) async-start(bf16[4,6,32,128]{3,2,1,0:T(8,128)(2,1)} %select_select_fusion), calls=%async_computation | async-start | bytes 393216 | tf_op jit(solution)/shard_map/all_to_all | solution.py:60
  11.4 0.0 copy-done.2
  11.4 0.1 convert_element_type.58
  11.5 0.0 copy-done.3
  11.5 0.1 eq.45
  11.6 7.3 %all-to-all-done = bf16[4,6,32,128]{3,2,1,0:T(8,128)(2,1)S(1)} async-done(((bf16[4,6,32,128]{3,2,1,0:T(8,128)(2,1)}), bf16[4,6,32,128]{3,2,1,0:T(8,128)(2,1)S(1)}, u32[]{:S(2)}, u32[]{:S(2)}) %all-to-all-start) | async-done | bytes 196640 | tf_op jit(solution)/shard_map/all_to_all | solution.py:60
  18.9 0.2 convert_reduce_fusion.2
  19.1 0.0 copy-done.4
  19.2 0.0 copy-done.5
  19.2 0.2 fusion.25
  19.4 0.3 fusion.8
  19.7 0.7 %broadcast_in_dim.54 = bf16[4,192,128]{2,1,0:T(8,128)(2,1)} broadcast(bf16[192,128]{1,0:T(8,128)(2,1)S(1)} %fusion.8), dimensions={1,2} | broadcast | bytes 245760 | tf_op jit(solution)/shard_map/broadcast_in_dim | solution.py:82
  20.4 3.4 %all-to-all-start.1 = ((bf16[4,192,128]{2,1,0:T(8,128)(2,1)}), bf16[4,192,128]{2,1,0:T(8,128)(2,1)S(1)}, u32[]{:S(2)}, u32[]{:S(2)}) async-start(bf16[4,192,128]{2,1,0:T(8,128)(2,1)} %broadcast_in_dim.54), calls=%async_computation.1 | async-start | bytes 393216 | tf_op jit(solution)/shard_map/all_to_all | solution.py:81
  23.7 0.0 copy-done.1
  23.8 2.4 %reshape_reshape_squeeze.3 = bf16[192,8,4,32]{3,2,1,0:T(4,128)(2,1)} reshape(bf16[1,6,32,1024]{3,2,1,0:T(8,128)(2,1)S(1)} %copy-done.1) | data formatting | bytes 786432 | tf_op jit(solution)/shard_map/reshape;reshape;squeeze | solution.py:40
  26.1 2.8 %copy.57 = bf16[4,192,8,32]{1,3,2,0:T(8,128)(2,1)S(1)} copy(bf16[4,192,8,32]{3,0,2,1:T(4,128)(2,1)} %bitcast.90) | data formatting | bytes 786432 | tf_op jit(solution)/shard_map/transpose | solution.py:40
  29.0 1.0 %copy.58 = bf16[4,192,256]{2,1,0:T(8,128)(2,1)} copy(bf16[4,192,256]{1,2,0:T(8,128)(2,1)S(1)} %bitcast.91) | data formatting | bytes 786432 | tf_op jit(solution)/shard_map/reshape | solution.py:41
  29.9 0.0 all-to-all-done.1
  30.0 5.0 %all-to-all-start.2 = ((bf16[4,192,256]{2,1,0:T(8,128)(2,1)}), bf16[4,192,256]{2,1,0:T(8,128)(2,1)S(1)}, u32[]{:S(2)}, u32[]{:S(2)}) async-start(bf16[4,192,256]{2,1,0:T(8,128)(2,1)} %copy.58), calls=%async_computation.2 | async-start | bytes 786432 | tf_op jit(solution)/shard_map/all_to_all | solution.py:45
  35.0 0.3 pad_slice_fusion
  35.2 0.7 %constant_dynamic-update-slice_fusion.8 = bf16[768,1152]{1,0:T(8,128)(2,1)} fusion(bf16[768,128]{1,0:T(8,128)(2,1)S(1)} %bitcast.101), kind=kLoop, calls=%fused_computation.54 | loop fusion | bytes 393216
  36.0 0.7 %constant_dynamic-update-slice_fusion.7 = bf16[768,1152]{1,0:T(8,128)(2,1)} fusion(bf16[768,1152]{1,0:T(8,128)(2,1)} %constant_dynamic-update-slice_fusion.8, bf16[768,128]{1,0:T(8,128)(2,1)S(1)} %bitcast.100), kind=kLoop, calls=%fused_computation.53 | loop fusion | bytes 393216
  36.7 0.8 %constant_dynamic-update-slice_fusion.6 = bf16[768,1152]{1,0:T(8,128)(2,1)} fusion(bf16[768,1152]{1,0:T(8,128)(2,1)} %constant_dynamic-update-slice_fusion.7, bf16[768,128]{1,0:T(8,128)(2,1)S(1)} %bitcast.99), kind=kLoop, calls=%fused_computation.52 | loop fusion | bytes 393216
  37.4 0.7 %constant_dynamic-update-slice_fusion.5 = bf16[768,1152]{1,0:T(8,128)(2,1)} fusion(bf16[768,1152]{1,0:T(8,128)(2,1)} %constant_dynamic-update-slice_fusion.6, bf16[768,128]{1,0:T(8,128)(2,1)S(1)} %bitcast.98), kind=kLoop, calls=%fused_computation.51 | loop fusion | bytes 393216
  38.2 0.7 %constant_dynamic-update-slice_fusion.4 = bf16[768,1152]{1,0:T(8,128)(2,1)} fusion(bf16[768,1152]{1,0:T(8,128)(2,1)} %constant_dynamic-update-slice_fusion.5, bf16[768,128]{1,0:T(8,128)(2,1)S(1)} %bitcast.93), kind=kLoop, calls=%fused_computation.50 | loop fusion | bytes 393216
  38.9 0.7 %constant_dynamic-update-slice_fusion.3 = bf16[768,1152]{1,0:T(8,128)(2,1)} fusion(bf16[768,1152]{1,0:T(8,128)(2,1)} %constant_dynamic-update-slice_fusion.4, bf16[768,128]{1,0:T(8,128)(2,1)S(1)} %bitcast.97), kind=kLoop, calls=%fused_computation.49 | loop fusion | bytes 393216
  39.6 0.7 %constant_dynamic-update-slice_fusion.2 = bf16[768,1152]{1,0:T(8,128)(2,1)} fusion(bf16[768,1152]{1,0:T(8,128)(2,1)} %constant_dynamic-update-slice_fusion.3, bf16[768,128]{1,0:T(8,128)(2,1)S(1)} %bitcast.96), kind=kLoop, calls=%fused_computation.48 | loop fusion | bytes 393216
  40.3 0.7 %constant_dynamic-update-slice_fusion.1 = bf16[768,1152]{1,0:T(8,128)(2,1)} fusion(bf16[768,1152]{1,0:T(8,128)(2,1)} %constant_dynamic-update-slice_fusion.2, bf16[768,128]{1,0:T(8,128)(2,1)S(1)} %bitcast.95), kind=kLoop, calls=%fused_computation.47 | loop fusion | bytes 393216
  41.0 0.7 %constant_dynamic-update-slice_fusion = bf16[768,1152]{1,0:T(8,128)(2,1)} fusion(bf16[768,1152]{1,0:T(8,128)(2,1)} %constant_dynamic-update-slice_fusion.1, bf16[768,128]{1,0:T(8,128)(2,1)S(1)} %bitcast.94), kind=kLoop, calls=%fused_computation.46 | loop fusion | bytes 393216 | tf_op jit(solution)/shard_map/concatenate | solution.py:90
  41.7 3.2 %all-to-all-done.2 = bf16[4,192,256]{2,1,0:T(8,128)(2,1)S(1)} async-done(((bf16[4,192,256]{2,1,0:T(8,128)(2,1)}), bf16[4,192,256]{2,1,0:T(8,128)(2,1)S(1)}, u32[]{:S(2)}, u32[]{:S(2)}) %all-to-all-start.2) | async-done | bytes 393248 | tf_op jit(solution)/shard_map/all_to_all | solution.py:45
  44.8 3.0 %convolution_convert_fusion = bf16[1152,256]{0,1:T(8,128)(2,1)} fusion(bf16[768,1152]{1,0:T(8,128)(2,1)} %constant_dynamic-update-slice_fusion, bf16[768,256]{1,0:T(8,128)(2,1)S(1)} %bitcast.105), kind=kOutput, calls=%fused_computation | convolution fusion | flops 453279744 | bytes 2752512 | tf_op jit(solution)/shard_map/dot_general | solution.py:93
  47.9 3.7 %all-to-all-start.3 = ((bf16[8,32,1152]{2,1,0:T(8,128)(2,1)}), bf16[8,32,1152]{2,1,0:T(8,128)(2,1)S(1)}, u32[]{:S(2)}, u32[]{:S(2)}) async-start(bf16[8,32,1152]{2,1,0:T(8,128)(2,1)} %bitcast.31), calls=%async_computation.3 | async-start | bytes 1179648 | tf_op jit(solution)/shard_map/all_to_all | solution.py:100
  51.6 1.0 %constant_dynamic-slice_fusion = bf16[192,1152]{1,0:T(8,128)(2,1)S(1)} fusion(bf16[768,1152]{1,0:T(8,128)(2,1)} %constant_dynamic-update-slice_fusion, s32[]{:T(128)S(6)} %select_n.22), kind=kLoop, calls=%fused_computation.64 | loop fusion | bytes 884740 | tf_op jit(solution)/shard_map/dynamic_slice | solution.py:107
  52.7 1.1 %reshape.98 = bf16[6,32,9,128]{3,2,1,0:T(8,128)(2,1)} reshape(bf16[192,1152]{1,0:T(8,128)(2,1)S(1)} %constant_dynamic-slice_fusion) | data formatting | bytes 884736 | tf_op jit(solution)/shard_map/reshape.17
  53.8 3.0 %fusion.4 = f32[1,6,32,1024]{3,2,1,0:T(8,128)} fusion(bf16[1024,9,128]{2,0,1:T(8,128)(2,1)S(1)} %copy-done, bf16[6,32,9,128]{3,2,1,0:T(8,128)(2,1)} %reshape.98), kind=kOutput, calls=%fused_computation.5 | convolution fusion | flops 452984832 | bytes 3588096 | tf_op jit(solution)/shard_map/dot_general | solution.py:108
  56.8 5.3 %all-to-all-done.3 = bf16[8,32,1152]{2,1,0:T(8,128)(2,1)S(1)} async-done(((bf16[8,32,1152]{2,1,0:T(8,128)(2,1)}), bf16[8,32,1152]{2,1,0:T(8,128)(2,1)S(1)}, u32[]{:S(2)}, u32[]{:S(2)}) %all-to-all-start.3) | async-done | bytes 589856 | tf_op jit(solution)/shard_map/all_to_all | solution.py:100
  62.1 0.1 convert_reduce_fusion
  62.2 0.7 %div.24 = f32[288,128]{1,0:T(8,128)} reshape(f32[32,1152]{1,0:T(8,128)S(1)} %broadcast_multiply_fusion) | data formatting | bytes 294912 | tf_op jit(solution)/shard_map/div | solution.py:101
  (12 shorter events, 0.2 us)
Async XLA Ops:
  0.6 1.7 %copy-start = (bf16[1024,9,128]{2,0,1:T(8,128)(2,1)S(1)}, bf16[1024,9,128]{2,0,1:T(8,128)(2,1)}, u32[]{:S(2)}) copy-start(bf16[1024,9,128]{2,0,1:T(8,128)(2,1)} %param.9) | copy-start | bytes 7077892
  4.0 7.4 %copy-start.2 = (s32[1,6,32]{2,0,1:T(1,128)S(1)}, s32[1,6,32]{2,0,1:T(1,128)}, u32[]{:S(2)}) copy-start(s32[1,6,32]{2,0,1:T(1,128)} %param.8) | copy-start | bytes 2308
  4.0 7.5 %copy-start.3 = (s32[1,6,32]{2,0,1:T(1,128)S(1)}, s32[1,6,32]{2,0,1:T(1,128)}, u32[]{:S(2)}) copy-start(s32[1,6,32]{2,0,1:T(1,128)} %param.7) | copy-start | bytes 2308
  4.1 15.0 %copy-start.4 = (f32[128]{0:T(128)S(1)}, f32[128]{0:T(128)}, u32[]{:S(2)}) copy-start(f32[128]{0:T(128)} %param.10) | copy-start | bytes 1540
  4.1 15.0 %copy-start.5 = (bf16[128,3]{0,1:T(4,128)(2,1)S(1)}, bf16[128,3]{0,1:T(4,128)(2,1)}, u32[]{:S(2)}) copy-start(bf16[128,3]{0,1:T(4,128)(2,1)} %param.11) | copy-start | bytes 2308
  4.3 19.5 %copy-start.1 = (bf16[1,6,32,1024]{3,2,1,0:T(8,128)(2,1)S(1)}, bf16[1,6,32,1024]{3,2,1,0:T(8,128)(2,1)}, u32[]{:S(2)}) copy-start(bf16[1,6,32,1024]{3,2,1,0:T(8,128)(2,1)} %param.6) | copy-start | bytes 1179652
  5.1 13.8 %all-to-all-start = ((bf16[4,6,32,128]{3,2,1,0:T(8,128)(2,1)}), bf16[4,6,32,128]{3,2,1,0:T(8,128)(2,1)S(1)}, u32[]{:S(2)}, u32[]{:S(2)}) async-start(bf16[4,6,32,128]{3,2,1,0:T(8,128)(2,1)} %select_select_fusion), calls=%async_computation | async-start | bytes 393216 | tf_op jit(solution)/shard_map/all_to_all | solution.py:60
  20.4 9.6 %all-to-all-start.1 = ((bf16[4,192,128]{2,1,0:T(8,128)(2,1)}), bf16[4,192,128]{2,1,0:T(8,128)(2,1)S(1)}, u32[]{:S(2)}, u32[]{:S(2)}) async-start(bf16[4,192,128]{2,1,0:T(8,128)(2,1)} %broadcast_in_dim.54), calls=%async_computation.1 | async-start | bytes 393216 | tf_op jit(solution)/shard_map/all_to_all | solution.py:81
  30.0 14.9 %all-to-all-start.2 = ((bf16[4,192,256]{2,1,0:T(8,128)(2,1)}), bf16[4,192,256]{2,1,0:T(8,128)(2,1)S(1)}, u32[]{:S(2)}, u32[]{:S(2)}) async-start(bf16[4,192,256]{2,1,0:T(8,128)(2,1)} %copy.58), calls=%async_computation.2 | async-start | bytes 786432 | tf_op jit(solution)/shard_map/all_to_all | solution.py:45
  47.9 14.2 %all-to-all-start.3 = ((bf16[8,32,1152]{2,1,0:T(8,128)(2,1)}), bf16[8,32,1152]{2,1,0:T(8,128)(2,1)S(1)}, u32[]{:S(2)}, u32[]{:S(2)}) async-start(bf16[8,32,1152]{2,1,0:T(8,128)(2,1)} %bitcast.31), calls=%async_computation.3 | async-start | bytes 1179648 | tf_op jit(solution)/shard_map/all_to_all | solution.py:100

commit v2 on v1

v2 whole, which is shorter than its diff:
```python
import functools

import jax
import jax.numpy as jnp
from jax import lax
from jax.experimental import pallas as pl
from jax.experimental.pallas import tpu as pltpu
from jax.sharding import PartitionSpec as P

DILATION_SIZE = 6
VMEM_LIMIT = 48 * 1024 * 1024


def channel_plan(channels, taps, replicas, bands):
    rows = channels * taps // (replicas * bands)
    starts = [[(d * bands + s) * rows // taps for d in range(replicas)] for s in range(bands)]
    offsets = [[(d * bands + s) * rows % taps for d in range(replicas)] for s in range(bands)]
    cover = max(-(-(off + rows) // taps) for line in offsets for off in line)
    picks = [[min(c + k, channels - 1) for c in line for k in range(cover)] for line in starts]
    return rows, cover, picks, offsets


def shift_columns(array, by, columns):
    if by == 0:
        return array
    size = array.shape[0]
    column = lax.broadcasted_iota(jnp.int32, array.shape, 0) % columns + by
    moved = pltpu.roll(array, (-by) % size, 0)
    return jnp.where((column >= 0) & (column < columns), moved, 0.0)


def forward_kernel(columns, reach, x_ref, w_ref, middle_ref, halo_ref):
    step = pl.program_id(0)
    band = lax.axis_index("space")
    bands = halo_ref.shape[0]
    pixels = x_ref.shape[0]
    width = w_ref.shape[2]
    edge = reach * columns
    weight = jnp.concatenate([w_ref[b] for b in range(3)], axis=1)
    product = jnp.dot(x_ref[...], weight, preferred_element_type=jnp.float32)
    part = sum(
        shift_columns(product[:, b * width : (b + 1) * width], (b - 1) * reach, columns)
        for b in range(3)
    )

    @pl.when(step == 0)
    def _():
        halo_ref[...] = jnp.zeros_like(halo_ref)
        if pixels > edge:
            middle_ref[:edge] = jnp.zeros((edge, width), jnp.float32)
            middle_ref[edge:] = part[: pixels - edge]

        @pl.when(band + 1 < bands)
        def _():
            halo_ref[jnp.minimum(band + 1, bands - 1)] = part[pixels - edge :].astype(halo_ref.dtype)

    @pl.when(step == 1)
    def _():
        if pixels > edge:
            middle_ref[...] += part
        else:
            middle_ref[...] = part

    @pl.when(step == 2)
    def _():
        if pixels > edge:
            middle_ref[: pixels - edge] += part[edge:]

        @pl.when(band > 0)
        def _():
            halo_ref[jnp.maximum(band - 1, 0)] = part[:edge].astype(halo_ref.dtype)


def forward(flat, weight, bands, columns, reach):
    pixels, channels = flat.shape
    taps, _, width = weight.shape
    return pl.pallas_call(
        functools.partial(forward_kernel, columns, reach),
        grid=(3,),
        in_specs=[
            pl.BlockSpec((pixels, channels), lambda i: (0, 0)),
            pl.BlockSpec((3, channels, width), lambda i: (i, 0, 0)),
        ],
        out_specs=[
            pl.BlockSpec((pixels, width), lambda i: (0, 0)),
            pl.BlockSpec((bands, reach * columns, width), lambda i: (0, 0, 0)),
        ],
        out_shape=[
            jax.ShapeDtypeStruct((pixels, width), jnp.float32),
            jax.ShapeDtypeStruct((bands, reach * columns, width), jnp.bfloat16),
        ],
        compiler_params=pltpu.CompilerParams(vmem_limit_bytes=VMEM_LIMIT),
        cost_estimate=pl.CostEstimate(
            flops=2 * pixels * channels * taps * width,
            bytes_accessed=2 * taps * channels * width + 2 * pixels * channels,
            transcendentals=0,
        ),
        name="forward",
    )(flat, weight)


def arrange_kernel(replicas, cover, x_ref, out_ref):
    bands = out_ref.shape[0]
    x = x_ref[...]
    for s in range(bands):
        out_ref[s] = jnp.concatenate(
            [x[:, (d * bands + s) * cover : (d * bands + s + 1) * cover] for d in range(replicas)],
            axis=1,
        )


def arrange(flat, bands, replicas, cover):
    pixels, channels = flat.shape
    return pl.pallas_call(
        functools.partial(arrange_kernel, replicas, cover),
        out_shape=jax.ShapeDtypeStruct((bands, pixels, replicas * cover), flat.dtype),
        compiler_params=pltpu.CompilerParams(vmem_limit_bytes=VMEM_LIMIT),
        cost_estimate=pl.CostEstimate(
            flops=0, bytes_accessed=4 * pixels * channels, transcendentals=0
        ),
        name="arrange",
    )(flat)


def pointwise_kernel(
    edge, middle_ref, halo_ref, bias_ref, class_ref, label_ref, scale_ref, feature_ref, out_ref
):
    band = lax.axis_index("space")
    bands = halo_ref.shape[0]
    pixels, width = middle_ref.shape
    above = halo_ref[jnp.maximum(band - 1, 0)].astype(jnp.float32)
    below = halo_ref[jnp.minimum(band + 1, bands - 1)].astype(jnp.float32)
    above = jnp.where(band > 0, above, 0.0)
    below = jnp.where(band + 1 < bands, below, 0.0)
    if pixels > edge:
        none = jnp.zeros((pixels - edge, width), jnp.float32)
        above = jnp.concatenate([above, none], axis=0)
        below = jnp.concatenate([none, below], axis=0)
    preact = middle_ref[...] + above + below + bias_ref[...]
    sigmoid_z = jax.nn.sigmoid(preact)
    hidden = (preact * sigmoid_z).astype(jnp.bfloat16)
    classes = class_ref[...]
    logits = lax.dot_general(
        hidden, classes, (((1,), (1,)), ((), ())), preferred_element_type=jnp.float32
    )
    exponent = jnp.exp(logits)
    chances = exponent / jnp.sum(exponent, axis=1, keepdims=True)
    index = lax.broadcasted_iota(jnp.int32, chances.shape, 1)
    onehot = jnp.where(label_ref[...] == index, 1.0, 0.0)
    grad_logits = scale_ref[...].astype(jnp.float32) * (chances - onehot)
    wide = classes.astype(jnp.float32)
    hidden_grad = sum(
        grad_logits[:, k : k + 1] * wide[k : k + 1] for k in range(classes.shape[0])
    )
    gradient = hidden_grad * sigmoid_z * (1.0 + preact * (1.0 - sigmoid_z))
    gradient = gradient.astype(out_ref.dtype)
    for s in range(bands):
        out_ref[s, :, :width] = gradient
        out_ref[s, :, width:] = feature_ref[s]


def pointwise(middle, halo, bias, classes, labels, scale, features):
    pixels, width = middle.shape
    bands, edge, _ = halo.shape
    extra = features.shape[2]
    return pl.pallas_call(
        functools.partial(pointwise_kernel, edge),
        out_shape=jax.ShapeDtypeStruct((bands, pixels, width + extra), jnp.bfloat16),
        compiler_params=pltpu.CompilerParams(vmem_limit_bytes=VMEM_LIMIT),
        cost_estimate=pl.CostEstimate(
            flops=30 * pixels * width,
            bytes_accessed=4 * bands * pixels * (width + extra),
            transcendentals=pixels * width,
        ),
        name="pointwise",
    )(middle, halo, bias, classes, labels, scale, features)


def shifted_taps(gradient, columns, reach):
    wide = gradient.astype(jnp.float32)
    return jnp.concatenate(
        [shift_columns(wide, (1 - b) * reach, columns).astype(jnp.bfloat16) for b in range(3)],
        axis=1,
    )


def kernel_grad_kernel(columns, reach, in_ref, out_ref):
    width = out_ref.shape[1] // 9
    bands, pixels, lanes = in_ref.shape
    together = in_ref[...].reshape(bands * pixels, lanes)
    total = bands * pixels
    edge = reach * columns
    shifted = shifted_taps(together[:, :width], columns, reach)
    features = together[:, width:]
    contract = (((0,), (0,)), ((), ()))
    for a in range(3):
        if a == 0:
            left, right = features[: total - edge], shifted[edge:]
        elif a == 1:
            left, right = features, shifted
        else:
            left, right = features[edge:], shifted[: total - edge]
        block = lax.dot_general(left, right, contract, preferred_element_type=jnp.float32)
        out_ref[:, 3 * a * width : 3 * (a + 1) * width] = block.astype(out_ref.dtype)


def kernel_grad(gathered, width, columns, reach):
    bands, pixels, lanes = gathered.shape
    extra = lanes - width
    return pl.pallas_call(
        functools.partial(kernel_grad_kernel, columns, reach),
        out_shape=jax.ShapeDtypeStruct((extra, 9 * width), jnp.bfloat16),
        compiler_params=pltpu.CompilerParams(vmem_limit_bytes=VMEM_LIMIT),
        cost_estimate=pl.CostEstimate(
            flops=18 * bands * pixels * extra * width,
            bytes_accessed=2 * bands * pixels * lanes + 18 * extra * width,
            transcendentals=0,
        ),
        name="kernel_grad",
    )(gathered)


def feature_grad_kernel(columns, reach, g_ref, w_ref, out_ref):
    band = lax.axis_index("space")
    bands, pixels, width = g_ref.shape
    edge = reach * columns
    own = g_ref[band]
    above = g_ref[jnp.maximum(band - 1, 0)][pixels - edge :]
    below = g_ref[jnp.minimum(band + 1, bands - 1)][:edge]
    above = jnp.where(band > 0, above, jnp.zeros_like(above))
    below = jnp.where(band + 1 < bands, below, jnp.zeros_like(below))
    stack = shifted_taps(jnp.concatenate([above, own, below], axis=0), columns, reach)
    taps = jnp.concatenate(
        [stack[(2 - a) * edge : (2 - a) * edge + pixels] for a in range(3)], axis=1
    )
    weight = jnp.concatenate([w_ref[t] for t in range(9)], axis=1)
    out_ref[...] = lax.dot_general(
        taps, weight, (((1,), (1,)), ((), ())), preferred_element_type=jnp.float32
    )


def feature_grad(gathered, weight, columns, reach):
    bands, pixels, _ = gathered.shape
    taps, channels, width = weight.shape
    step = 256 if channels % 256 == 0 else channels
    return pl.pallas_call(
        functools.partial(feature_grad_kernel, columns, reach),
        grid=(channels // step,),
        in_specs=[
            pl.BlockSpec((bands, pixels, width), lambda i: (0, 0, 0)),
            pl.BlockSpec((taps, step, width), lambda i: (0, i, 0)),
        ],
        out_specs=pl.BlockSpec((pixels, step), lambda i: (0, i)),
        out_shape=jax.ShapeDtypeStruct((pixels, channels), jnp.float32),
        compiler_params=pltpu.CompilerParams(vmem_limit_bytes=VMEM_LIMIT),
        cost_estimate=pl.CostEstimate(
            flops=2 * pixels * taps * channels * width,
            bytes_accessed=2 * taps * channels * width + 4 * pixels * channels,
            transcendentals=0,
        ),
        name="feature_grad",
    )(gathered, weight)


def final_kernel(in_ref, out_ref):
    replicas, cover, lanes = in_ref.shape
    width = out_ref.shape[1]
    taps = lanes // width
    total = in_ref[0].astype(jnp.float32)
    for d in range(1, replicas):
        total += in_ref[d].astype(jnp.float32)
    total = total / replicas
    for t in range(taps):
        out_ref[pl.ds(t, cover, stride=taps), :] = total[:, t * width : (t + 1) * width]


def final(came, width):
    replicas, cover, lanes = came.shape
    return pl.pallas_call(
        final_kernel,
        out_shape=jax.ShapeDtypeStruct((cover * lanes // width, width), jnp.float32),
        compiler_params=pltpu.CompilerParams(vmem_limit_bytes=VMEM_LIMIT),
        name="final_sum",
    )(came)


def on_device(features, labels, pixel_weight, conv_weight, conv_bias, class_weight):
    image = features[0]
    band_rows, columns, channels = image.shape
    taps, width = conv_weight.shape[1:]
    pixels = band_rows * columns
    replicas = lax.axis_size("dp")
    bands = lax.axis_size("space")
    reach = DILATION_SIZE

    flat = image.reshape(pixels, channels)
    weight = conv_weight.transpose(1, 0, 2)
    middle, halo = forward(flat, weight, bands, columns, reach)
    halo = lax.all_to_all(halo, "space", 0, 0)

    block_rows, cover, picks, offsets = channel_plan(channels, taps, replicas, bands)
    if block_rows % taps == 0:
        split = arrange(flat, bands, replicas, cover)
    else:
        order = jnp.array([c for line in picks for c in line], jnp.int32)
        split = jnp.take(flat, order, axis=1)
        split = split.reshape(pixels, bands, replicas * cover).transpose(1, 0, 2)

    packed = pointwise(
        middle,
        halo,
        conv_bias.reshape(1, width),
        class_weight.T,
        labels.reshape(pixels, 1),
        pixel_weight.reshape(pixels, 1),
        split,
    )
    gathered = lax.all_to_all(packed, "space", 0, 0)
    partial_grad = kernel_grad(gathered, width, columns, reach)
    came = lax.all_to_all(partial_grad.reshape(replicas, cover, taps * width), "dp", 0, 0)
    weight_grad = final(came, width)
    if block_rows % taps:
        start = jnp.array(offsets)[lax.axis_index("space"), lax.axis_index("dp")]
        weight_grad = lax.dynamic_slice_in_dim(weight_grad, start, block_rows)

    grad = feature_grad(gathered[:, :, :width], weight, columns, reach)
    return grad.reshape(1, band_rows, columns, channels), weight_grad


def solution(mesh):
    placed = (
        P("dp", "space", None, None),
        P("dp", "space", None),
        P("dp", "space", None),
        P(),
        P(),
        P(),
    )
    return jax.shard_map(
        on_device,
        mesh=mesh,
        in_specs=placed,
        out_specs=(P("dp", "space", None, None), P(("dp", "space"), None)),
        check_vma=False,
    )
```

time: 63.5 us -> 54.3 us (0.86)
  blocking collectives: 0 us -> 17.9 us
  local copies, waits for them, and re-layouts: 18.3 us -> 3.77 us
  starting transfers between devices: 18.4 us -> 10 us
  matrix products: 8.16 us -> 0 us
  Pallas kernels: 0 us -> 6.8 us
  other arithmetic: 1.24 us -> 0.03 us
  waiting for transfers between devices: 15.8 us -> 14.6 us
    all_to_all x0 -> x1, blocking collectives: none -> 17.9 us  [on_device(): gathered = lax.all_to_all(packed, 'space', 0, 0)]
    all_to_all x4 -> x2, starting transfers between devices: 18.4 us -> 10 us  [the longest x1 6.32 us: on_device(): halo = lax.all_to_all(halo, 'space', 0, 0)]
    dot_general x5 -> x0, matrix products: 8.16 us -> none  [the longest x1 3.04 us: on_device(): lax.dot_general(whole.reshape(bands * pixels, replicas * cover), shifted,...]
    pallas_call x0 -> x6, Pallas kernels: none -> 6.8 us  [the longest x1 2.63 us: feature_grad(): pl.pallas_call(functools.partial(feature_grad_kernel, columns, reach), gr...]
    unnamed x20 -> x18, local copies, waits for them, and re-layouts: 7.42 us -> 3.51 us
    another operation x2 -> x0, local copies, waits for them, and re-layouts: 3.52 us -> none  [the longest x1 2.39 us: on_device(): split = flat.reshape(pixels, replicas, bands, cover).transpose(2, 0, 1, 3)]
    transpose x1 -> x0, local copies, waits for them, and re-layouts: 2.81 us -> none  [on_device(): split = flat.reshape(pixels, replicas, bands, cover).transpose(2, 0, 1, 3)]
    all_to_all x4 -> x2, waiting for transfers between devices: 15.8 us -> 14.6 us  [the longest x1 7.77 us: on_device(): lax.all_to_all(partial_grad.reshape(replicas, cover, taps * width), 'dp',...]
  transfers between devices with their start and end apart: 4 -> 2, of which waited for: 3 -> 2; matrix products, arithmetic and copies ran while one was open for 29% -> 1% of each run, Pallas kernels for 0% -> 6%
where the time goes in v2:
time: 54.3 us; the launch traced here: 53.9 us
  blocking collectives  17.9 us (33%)
  waiting for transfers between devices  14.6 us (27%)
  starting transfers between devices  10 us (18%)
  Pallas kernels  6.8 us (13%)
  local copies, waits for them, and re-layouts  3.77 us (7%)
  between operations  0.75 us (1%)
    all_to_all x1, blocking collectives, on_device(): gathered = lax.all_to_all(packed, 'space', 0, 0)  17.9 us
    all_to_all x1, waiting for transfers between devices, on_device(): lax.all_to_all(partial_grad.reshape(replicas, cover, taps * width), 'dp',...  7.77 us
    all_to_all x1, waiting for transfers between devices, on_device(): halo = lax.all_to_all(halo, 'space', 0, 0)  6.82 us
    all_to_all x1, starting transfers between devices, on_device(): halo = lax.all_to_all(halo, 'space', 0, 0)  6.32 us
    all_to_all x1, starting transfers between devices, on_device(): lax.all_to_all(partial_grad.reshape(replicas, cover, taps * width), 'dp',...  3.73 us
    unnamed x18, local copies, waits for them, and re-layouts  3.51 us
    pallas_call x1, Pallas kernels, feature_grad(): pl.pallas_call(functools.partial(feature_grad_kernel, columns, reach), gr...  2.63 us
    pallas_call x1, Pallas kernels, forward(): pl.pallas_call(functools.partial(forward_kernel, columns, reach), grid=(3...  1.85 us
  transfers between devices with their start and end apart: 2, of which 2 were waited for; matrix products, arithmetic and copies ran while one was open for 1% of the time, Pallas kernels for 6%

profile of v2, /device:TPU:0, one launch (start us, length us, event | category | flops | bytes accessed | tf_op | source)
XLA Modules:
  0.0 53.9 jit_solution(14863026382817817406)
XLA Ops:
  0.6 0.0 copy-start.5
  0.6 0.0 copy-start.6
  0.7 0.0 copy-start
  0.7 1.7 %copy-done = bf16[1024,9,128]{2,0,1:T(8,128)(2,1)S(1)} copy-done((bf16[1024,9,128]{2,0,1:T(8,128)(2,1)S(1)}, bf16[1024,9,128]{2,0,1:T(8,128)(2,1)}, u32[]{:S(2)}) %copy-start) | copy-done | bytes 2359320
  2.3 0.0 copy-start.2
  2.3 1.0 %copy-done.2 = bf16[1,6,32,1024]{3,2,1,0:T(8,128)(2,1)S(1)} copy-done((bf16[1,6,32,1024]{3,2,1,0:T(8,128)(2,1)S(1)}, bf16[1,6,32,1024]{3,2,1,0:T(8,128)(2,1)}, u32[]{:S(2)}) %copy-start.2) | copy-done | bytes 393240
  3.3 0.0 copy-start.3
  3.3 0.0 copy-start.7
  3.3 0.0 copy-start.8
  3.3 1.9 %forward.1 = (f32[192,128]{1,0:T(8,128)S(1)}, bf16[4,192,128]{2,1,0:T(8,128)(2,1)}) custom-call(bf16[192,1024]{1,0:T(8,128)(2,1)S(1)} %bitcast.8, bf16[9,1024,128]{2,1,0:T(8,128)(2,1)S(1)} %bitcast.6), custom_call_target="tpu_custom_call" | custom-call | flops 452984832 | bytes 2752512 | tf_op jit(solution)/shard_map/forward/pallas_call | solution.py:77
  5.2 6.3 %all-to-all-start = ((bf16[4,192,128]{2,1,0:T(8,128)(2,1)}), bf16[4,192,128]{2,1,0:T(8,128)(2,1)S(1)}, u32[]{:S(2)}, u32[]{:S(2)}) async-start(bf16[4,192,128]{2,1,0:T(8,128)(2,1)} %get-tuple-element.5), calls=%async_computation | async-start | bytes 393216 | tf_op jit(solution)/shard_map/all_to_all | solution.py:299
  11.5 0.0 copy-done.3
  11.5 0.4 arrange.1.feature_ref
  11.9 0.0 copy-done.7
  11.9 0.0 copy-done.8
  12.0 0.1 reshape.25.scale_ref
  12.1 0.1 reshape.24.label_ref
  12.2 6.8 %all-to-all-done.halo_ref = bf16[4,192,128]{2,1,0:T(8,128)(2,1)S(1)} async-done(((bf16[4,192,128]{2,1,0:T(8,128)(2,1)}), bf16[4,192,128]{2,1,0:T(8,128)(2,1)S(1)}, u32[]{:S(2)}, u32[]{:S(2)}) %all-to-all-start) | async-done | bytes 196640 | tf_op jit(solution)/shard_map/all_to_all | solution.py:299
  19.0 0.0 copy-done.5
  19.0 0.0 copy-done.6
  19.0 0.4 pointwise.1
  19.4 0.0 copy-start.1
  19.5 17.9 %all_to_all.15.in_ref = bf16[4,192,384]{2,1,0:T(8,128)(2,1)S(1)} all-to-all(bf16[4,192,384]{2,1,0:T(8,128)(2,1)S(1)} %pointwise.1), channel_id=1, replica_groups=mesh['dp'=8,'space'=4] {'space'}, dimensions={0} | all-to-all | bytes 1179648 | tf_op jit(solution)/shard_map/all_to_all | solution.py:318
  37.4 0.8 %kernel_grad.1 = bf16[256,1152]{1,0:T(8,128)(2,1)S(1)} custom-call(bf16[4,192,384]{2,1,0:T(8,128)(2,1)S(1)} %all_to_all.15.in_ref), custom_call_target="tpu_custom_call" | custom-call | flops 452984832 | bytes 1179648 | tf_op jit(solution)/shard_map/kernel_grad/pallas_call | solution.py:210
  38.2 0.0 copy-start.4
  38.2 0.8 %copy-done.4 = bf16[256,1152]{1,0:T(8,128)(2,1)} copy-done((bf16[256,1152]{1,0:T(8,128)(2,1)}, bf16[256,1152]{1,0:T(8,128)(2,1)S(1)}, u32[]{:S(2)}) %copy-start.4) | copy-done | bytes 589848
  39.0 3.7 %all-to-all-start.2 = ((bf16[8,32,1152]{2,1,0:T(8,128)(2,1)}), bf16[8,32,1152]{2,1,0:T(8,128)(2,1)S(1)}, u32[]{:S(2)}, u32[]{:S(2)}) async-start(bf16[8,32,1152]{2,1,0:T(8,128)(2,1)} %bitcast.10), calls=%async_computation.2 | async-start | bytes 1179648 | tf_op jit(solution)/shard_map/all_to_all | solution.py:320
  42.8 0.0 copy-done.1
  42.8 2.6 %feature_grad.1 = f32[192,1024]{1,0:T(8,128)} custom-call(bf16[4,192,128]{2,1,0:T(8,128)(2,1)S(1)} %slice.4.g_ref, bf16[9,1024,128]{2,1,0:T(8,128)(2,1)S(1)} %bitcast.7), custom_call_target="tpu_custom_call" | custom-call | flops 452984832 | bytes 3145728 | tf_op jit(solution)/shard_map/feature_grad/pallas_call | solution.py:246
  45.4 7.8 %all-to-all-done.2.in_ref = bf16[8,32,1152]{2,1,0:T(8,128)(2,1)S(1)} async-done(((bf16[8,32,1152]{2,1,0:T(8,128)(2,1)}), bf16[8,32,1152]{2,1,0:T(8,128)(2,1)S(1)}, u32[]{:S(2)}, u32[]{:S(2)}) %all-to-all-start.2) | async-done | bytes 589856 | tf_op jit(solution)/shard_map/all_to_all | solution.py:320
  53.2 0.7 %final_sum.1 = f32[288,128]{1,0:T(8,128)} custom-call(bf16[8,32,1152]{2,1,0:T(8,128)(2,1)S(1)} %all-to-all-done.2.in_ref), custom_call_target="tpu_custom_call" | custom-call | tf_op jit(solution)/shard_map/final_sum/pallas_call | solution.py:279
  (3 shorter events, 0.1 us)
Async XLA Ops:
  0.6 18.4 %copy-start.5 = (bf16[128,3]{0,1:T(4,128)(2,1)S(1)}, bf16[128,3]{0,1:T(4,128)(2,1)}, u32[]{:S(2)}) copy-start(bf16[128,3]{0,1:T(4,128)(2,1)} %param.11) | copy-start | bytes 2308
  0.6 18.4 %copy-start.6 = (f32[128]{0:T(128)S(1)}, f32[128]{0:T(128)}, u32[]{:S(2)}) copy-start(f32[128]{0:T(128)} %param.10) | copy-start | bytes 1540
  0.7 1.7 %copy-start = (bf16[1024,9,128]{2,0,1:T(8,128)(2,1)S(1)}, bf16[1024,9,128]{2,0,1:T(8,128)(2,1)}, u32[]{:S(2)}) copy-start(bf16[1024,9,128]{2,0,1:T(8,128)(2,1)} %param.9) | copy-start | bytes 7077892
  2.3 1.0 %copy-start.2 = (bf16[1,6,32,1024]{3,2,1,0:T(8,128)(2,1)S(1)}, bf16[1,6,32,1024]{3,2,1,0:T(8,128)(2,1)}, u32[]{:S(2)}) copy-start(bf16[1,6,32,1024]{3,2,1,0:T(8,128)(2,1)} %param.6) | copy-start | bytes 1179652
  3.3 8.2 %copy-start.3 = (bf16[1,6,32,1024]{3,2,1,0:T(8,128)(2,1)S(1)}, bf16[1,6,32,1024]{3,2,1,0:T(8,128)(2,1)}, u32[]{:S(2)}) copy-start(bf16[1,6,32,1024]{3,2,1,0:T(8,128)(2,1)} %param.6) | copy-start | bytes 1179652
  3.3 8.6 %copy-start.7 = (s32[1,6,32]{2,0,1:T(1,128)S(1)}, s32[1,6,32]{2,0,1:T(1,128)}, u32[]{:S(2)}) copy-start(s32[1,6,32]{2,0,1:T(1,128)} %param.7) | copy-start | bytes 2308
  3.3 8.6 %copy-start.8 = (s32[1,6,32]{2,0,1:T(1,128)S(1)}, s32[1,6,32]{2,0,1:T(1,128)}, u32[]{:S(2)}) copy-start(s32[1,6,32]{2,0,1:T(1,128)} %param.8) | copy-start | bytes 2308
  5.2 13.8 %all-to-all-start = ((bf16[4,192,128]{2,1,0:T(8,128)(2,1)}), bf16[4,192,128]{2,1,0:T(8,128)(2,1)S(1)}, u32[]{:S(2)}, u32[]{:S(2)}) async-start(bf16[4,192,128]{2,1,0:T(8,128)(2,1)} %get-tuple-element.5), calls=%async_computation | async-start | bytes 393216 | tf_op jit(solution)/shard_map/all_to_all | solution.py:299
  19.4 23.3 %copy-start.1 = (bf16[1024,9,128]{2,0,1:T(8,128)(2,1)S(1)}, bf16[1024,9,128]{2,0,1:T(8,128)(2,1)}, u32[]{:S(2)}) copy-start(bf16[1024,9,128]{2,0,1:T(8,128)(2,1)} %param.9) | copy-start | bytes 7077892
  38.2 0.8 %copy-start.4 = (bf16[256,1152]{1,0:T(8,128)(2,1)}, bf16[256,1152]{1,0:T(8,128)(2,1)S(1)}, u32[]{:S(2)}) copy-start(bf16[256,1152]{1,0:T(8,128)(2,1)S(1)} %kernel_grad.1) | copy-start | bytes 1769476
  39.0 14.2 %all-to-all-start.2 = ((bf16[8,32,1152]{2,1,0:T(8,128)(2,1)}), bf16[8,32,1152]{2,1,0:T(8,128)(2,1)S(1)}, u32[]{:S(2)}, u32[]{:S(2)}) async-start(bf16[8,32,1152]{2,1,0:T(8,128)(2,1)} %bitcast.10), calls=%async_computation.2 | async-start | bytes 1179648 | tf_op jit(solution)/shard_map/all_to_all | solution.py:320

commit v3 on v2

--- a/solution.py
+++ b/solution.py
@@ -8,7 +8,8 @@
 from jax.sharding import PartitionSpec as P
 
 DILATION_SIZE = 6
-VMEM_LIMIT = 48 * 1024 * 1024
+VMEM_LIMIT = 16 * 1024 * 1024
+VMEM_WHOLE = 60 * 1024 * 1024
 
 
 def channel_plan(channels, taps, replicas, bands):
@@ -89,7 +90,7 @@
             jax.ShapeDtypeStruct((pixels, width), jnp.float32),
             jax.ShapeDtypeStruct((bands, reach * columns, width), jnp.bfloat16),
         ],
-        compiler_params=pltpu.CompilerParams(vmem_limit_bytes=VMEM_LIMIT),
+        compiler_params=pltpu.CompilerParams(vmem_limit_bytes=VMEM_WHOLE),
         cost_estimate=pl.CostEstimate(
             flops=2 * pixels * channels * taps * width,
             bytes_accessed=2 * taps * channels * width + 2 * pixels * channels,
@@ -99,7 +100,8 @@
     )(flat, weight)
 
 
-def arrange_kernel(replicas, cover, x_ref, out_ref):
+def arrange_kernel(replicas, cover, x_ref, after_ref, out_ref):
+    del after_ref
     bands = out_ref.shape[0]
     x = x_ref[...]
     for s in range(bands):
@@ -109,21 +111,22 @@
         )
 
 
-def arrange(flat, bands, replicas, cover):
+def arrange(flat, after, bands, replicas, cover):
     pixels, channels = flat.shape
     return pl.pallas_call(
         functools.partial(arrange_kernel, replicas, cover),
+        in_specs=[pl.BlockSpec(memory_space=pltpu.VMEM), pl.BlockSpec(memory_space=pl.ANY)],
         out_shape=jax.ShapeDtypeStruct((bands, pixels, replicas * cover), flat.dtype),
         compiler_params=pltpu.CompilerParams(vmem_limit_bytes=VMEM_LIMIT),
         cost_estimate=pl.CostEstimate(
             flops=0, bytes_accessed=4 * pixels * channels, transcendentals=0
         ),
         name="arrange",
-    )(flat)
+    )(flat, after)
 
 
 def pointwise_kernel(
-    edge, middle_ref, halo_ref, bias_ref, class_ref, label_ref, scale_ref, feature_ref, out_ref
+    edge, middle_ref, halo_ref, bias_ref, class_ref, label_ref, scale_ref, out_ref
 ):
     band = lax.axis_index("space")
     bands = halo_ref.shape[0]
@@ -155,25 +158,23 @@
     gradient = hidden_grad * sigmoid_z * (1.0 + preact * (1.0 - sigmoid_z))
     gradient = gradient.astype(out_ref.dtype)
     for s in range(bands):
-        out_ref[s, :, :width] = gradient
-        out_ref[s, :, width:] = feature_ref[s]
-
-
-def pointwise(middle, halo, bias, classes, labels, scale, features):
+        out_ref[s] = gradient
+
+
+def pointwise(middle, halo, bias, classes, labels, scale):
     pixels, width = middle.shape
     bands, edge, _ = halo.shape
-    extra = features.shape[2]
     return pl.pallas_call(
         functools.partial(pointwise_kernel, edge),
-        out_shape=jax.ShapeDtypeStruct((bands, pixels, width + extra), jnp.bfloat16),
+        out_shape=jax.ShapeDtypeStruct((bands, pixels, width), jnp.bfloat16),
         compiler_params=pltpu.CompilerParams(vmem_limit_bytes=VMEM_LIMIT),
         cost_estimate=pl.CostEstimate(
             flops=30 * pixels * width,
-            bytes_accessed=4 * bands * pixels * (width + extra),
+            bytes_accessed=2 * bands * pixels * width + 4 * pixels * width,
             transcendentals=pixels * width,
         ),
         name="pointwise",
-    )(middle, halo, bias, classes, labels, scale, features)
+    )(middle, halo, bias, classes, labels, scale)
 
 
 def shifted_taps(gradient, columns, reach):
@@ -184,40 +185,45 @@
     )
 
 
-def kernel_grad_kernel(columns, reach, in_ref, out_ref):
-    width = out_ref.shape[1] // 9
-    bands, pixels, lanes = in_ref.shape
-    together = in_ref[...].reshape(bands * pixels, lanes)
+def kernel_grad_kernel(columns, reach, g_ref, *refs):
+    out_ref, padded = refs[-2:]
+    bands, pixels, width = g_ref.shape
+    edge = reach * columns
     total = bands * pixels
+    band = lax.axis_index("space")
+    shifted = shifted_taps(g_ref[...].reshape(total, width), columns, reach)
+    padded[:edge] = jnp.zeros((edge, 3 * width), padded.dtype)
+    padded[edge : edge + total] = shifted
+    padded[edge + total :] = jnp.zeros((edge, 3 * width), padded.dtype)
+    grad = None
+    for k in range(bands):
+        first = lax.rem(band + bands - k, bands) * pixels
+        right = jnp.concatenate(
+            [padded[pl.ds(pl.multiple_of(first + (2 - a) * edge, 16), pixels)] for a in range(3)], axis=1
+        )
+        term = lax.dot_general(
+            refs[k][...], right, (((0,), (0,)), ((), ())), preferred_element_type=jnp.float32
+        )
+        grad = term if grad is None else grad + term
+    out_ref[...] = grad.astype(out_ref.dtype)
+
+
+def kernel_grad(gathered, blocks, columns, reach):
+    bands, pixels, width = gathered.shape
+    extra = blocks[0].shape[1]
     edge = reach * columns
-    shifted = shifted_taps(together[:, :width], columns, reach)
-    features = together[:, width:]
-    contract = (((0,), (0,)), ((), ()))
-    for a in range(3):
-        if a == 0:
-            left, right = features[: total - edge], shifted[edge:]
-        elif a == 1:
-            left, right = features, shifted
-        else:
-            left, right = features[edge:], shifted[: total - edge]
-        block = lax.dot_general(left, right, contract, preferred_element_type=jnp.float32)
-        out_ref[:, 3 * a * width : 3 * (a + 1) * width] = block.astype(out_ref.dtype)
-
-
-def kernel_grad(gathered, width, columns, reach):
-    bands, pixels, lanes = gathered.shape
-    extra = lanes - width
     return pl.pallas_call(
         functools.partial(kernel_grad_kernel, columns, reach),
         out_shape=jax.ShapeDtypeStruct((extra, 9 * width), jnp.bfloat16),
+        scratch_shapes=[pltpu.VMEM((bands * pixels + 2 * edge, 3 * width), jnp.bfloat16)],
         compiler_params=pltpu.CompilerParams(vmem_limit_bytes=VMEM_LIMIT),
         cost_estimate=pl.CostEstimate(
             flops=18 * bands * pixels * extra * width,
-            bytes_accessed=2 * bands * pixels * lanes + 18 * extra * width,
+            bytes_accessed=2 * bands * pixels * (width + extra) + 18 * extra * width,
             transcendentals=0,
         ),
         name="kernel_grad",
-    )(gathered)
+    )(gathered, *blocks)
 
 
 def feature_grad_kernel(columns, reach, g_ref, w_ref, out_ref):
@@ -296,34 +302,40 @@
     flat = image.reshape(pixels, channels)
     weight = conv_weight.transpose(1, 0, 2)
     middle, halo = forward(flat, weight, bands, columns, reach)
-    halo = lax.all_to_all(halo, "space", 0, 0)
+    came = lax.all_to_all(halo, "space", 0, 0)
 
     block_rows, cover, picks, offsets = channel_plan(channels, taps, replicas, bands)
     if block_rows % taps == 0:
-        split = arrange(flat, bands, replicas, cover)
+        split = arrange(flat, middle, bands, replicas, cover)
     else:
         order = jnp.array([c for line in picks for c in line], jnp.int32)
         split = jnp.take(flat, order, axis=1)
         split = split.reshape(pixels, bands, replicas * cover).transpose(1, 0, 2)
-
-    packed = pointwise(
+    band = lax.axis_index("space")
+    blocks = []
+    for k in range(bands):
+        block = lax.dynamic_index_in_dim(split, (band + k) % bands, keepdims=False)
+        if k:
+            block = lax.ppermute(block, "space", [(i, (i + k) % bands) for i in range(bands)])
+        blocks.append(block)
+
+    gradient = pointwise(
         middle,
-        halo,
+        came,
         conv_bias.reshape(1, width),
         class_weight.T,
         labels.reshape(pixels, 1),
         pixel_weight.reshape(pixels, 1),
-        split,
-    )
-    gathered = lax.all_to_all(packed, "space", 0, 0)
-    partial_grad = kernel_grad(gathered, width, columns, reach)
+    )
+    gathered = lax.all_to_all(gradient, "space", 0, 0)
+    partial_grad = kernel_grad(gathered, blocks, columns, reach)
     came = lax.all_to_all(partial_grad.reshape(replicas, cover, taps * width), "dp", 0, 0)
     weight_grad = final(came, width)
     if block_rows % taps:
-        start = jnp.array(offsets)[lax.axis_index("space"), lax.axis_index("dp")]
+        start = jnp.array(offsets)[band, lax.axis_index("dp")]
         weight_grad = lax.dynamic_slice_in_dim(weight_grad, start, block_rows)
 
-    grad = feature_grad(gathered[:, :, :width], weight, columns, reach)
+    grad = feature_grad(gathered, weight, columns, reach)
     return grad.reshape(1, band_rows, columns, channels), weight_grad
 
 

time: 54.3 us -> 55.8 us (1.028)
  blocking collectives: 17.9 us -> 0 us
  waiting for transfers between devices: 14.6 us -> 23.2 us
  starting transfers between devices: 10 us -> 18.3 us
  Pallas kernels: 6.8 us -> 9.79 us
  local copies, waits for them, and re-layouts: 3.77 us -> 3.04 us
    all_to_all x1 -> x0, blocking collectives: 17.9 us -> none  [on_device(): gathered = lax.all_to_all(packed, 'space', 0, 0)]
    ppermute x0 -> x3, waiting for transfers between devices: none -> 8.2 us  [on_device(): lax.ppermute(block, 'space', [(i, (i + k) % bands) for i in range(bands)])]
    ppermute x0 -> x3, starting transfers between devices: none -> 4.89 us  [on_device(): lax.ppermute(block, 'space', [(i, (i + k) % bands) for i in range(bands)])]
    all_to_all x1 -> x2, starting transfers between devices: 6.32 us -> 9.69 us  [the longest x1 6.32 us: on_device(): came = lax.all_to_all(halo, 'space', 0, 0)]
    pallas_call x1, Pallas kernels: 1.85 us -> 3.95 us  [forward(): pl.pallas_call(functools.partial(forward_kernel, columns, reach), grid=(3...]
    unnamed x18, local copies, waits for them, and re-layouts: 3.51 us -> 2.77 us
    pallas_call x1, Pallas kernels: 0.42 us -> 1.1 us  [pointwise(): pl.pallas_call(functools.partial(pointwise_kernel, edge), out_shape=jax.S...]
    all_to_all x1 -> x2, waiting for transfers between devices: 6.82 us -> 7.22 us  [the longest x1 7.22 us: on_device(): came = lax.all_to_all(halo, 'space', 0, 0)]
  transfers between devices with their start and end apart: 2 -> 6, of which waited for: 2 -> 4; matrix products, arithmetic and copies ran while one was open for 1% -> 1% of each run, Pallas kernels for 6% -> 5%
where the time goes in v3:
time: 55.8 us; the launch traced here: 55.3 us
  waiting for transfers between devices  23.2 us (42%)
  starting transfers between devices  18.3 us (33%)
  Pallas kernels  9.79 us (18%)
  local copies, waits for them, and re-layouts  3.04 us (5%)
  between operations  0.85 us (2%)
    ppermute x3, waiting for transfers between devices, on_device(): lax.ppermute(block, 'space', [(i, (i + k) % bands) for i in range(bands)])  8.2 us
    all_to_all x1, waiting for transfers between devices, on_device(): lax.all_to_all(partial_grad.reshape(replicas, cover, taps * width), 'dp',...  7.82 us
    all_to_all x1, waiting for transfers between devices, on_device(): came = lax.all_to_all(halo, 'space', 0, 0)  7.22 us
    all_to_all x1, starting transfers between devices, on_device(): came = lax.all_to_all(halo, 'space', 0, 0)  6.32 us
    ppermute x3, starting transfers between devices, on_device(): lax.ppermute(block, 'space', [(i, (i + k) % bands) for i in range(bands)])  4.89 us
    pallas_call x1, Pallas kernels, forward(): pl.pallas_call(functools.partial(forward_kernel, columns, reach), grid=(3...  3.95 us
    all_to_all x1, starting transfers between devices, on_device(): lax.all_to_all(partial_grad.reshape(replicas, cover, taps * width), 'dp',...  3.73 us
    all_to_all x1, starting transfers between devices, on_device(): gathered = lax.all_to_all(gradient, 'space', 0, 0)  3.37 us
  transfers between devices with their start and end apart: 6, of which 4 were waited for; matrix products, arithmetic and copies ran while one was open for 1% of the time, Pallas kernels for 5%

profile of v3, /device:TPU:0, one launch (start us, length us, event | category | flops | bytes accessed | tf_op | source)
XLA Modules:
  0.0 55.3 jit_solution(11765815300291961364)
XLA Ops:
  0.6 0.0 copy-start.1
  0.6 0.0 copy-start.7
  0.7 0.0 copy-start.8
  0.7 0.0 copy-start.5
  0.7 0.0 copy-start.6
  0.7 3.9 %forward.1 = (f32[192,128]{1,0:T(8,128)}, bf16[4,192,128]{2,1,0:T(8,128)(2,1)}) custom-call(bf16[192,1024]{1,0:T(8,128)(2,1)} %bitcast.16, bf16[9,1024,128]{2,1,0:T(8,128)(2,1)} %bitcast.14), custom_call_target="tpu_custom_call" | custom-call | flops 452984832 | bytes 2752512 | tf_op jit(solution)/shard_map/forward/pallas_call | solution.py:78
  4.6 6.3 %all-to-all-start = ((bf16[4,192,128]{2,1,0:T(8,128)(2,1)}), bf16[4,192,128]{2,1,0:T(8,128)(2,1)S(1)}, u32[]{:S(2)}, u32[]{:S(2)}) async-start(bf16[4,192,128]{2,1,0:T(8,128)(2,1)} %get-tuple-element.5), calls=%async_computation | async-start | bytes 393216 | tf_op jit(solution)/shard_map/all_to_all | solution.py:305
  10.9 0.0 copy-done.7
  11.0 0.0 copy-done.8
  11.0 0.1 reshape.25.scale_ref
  11.1 0.1 reshape.24.label_ref
  11.2 7.2 %all-to-all-done.halo_ref = bf16[4,192,128]{2,1,0:T(8,128)(2,1)S(1)} async-done(((bf16[4,192,128]{2,1,0:T(8,128)(2,1)}), bf16[4,192,128]{2,1,0:T(8,128)(2,1)S(1)}, u32[]{:S(2)}, u32[]{:S(2)}) %all-to-all-start) | async-done | bytes 196640 | tf_op jit(solution)/shard_map/all_to_all | solution.py:305
  18.5 0.0 copy-done.5
  18.5 0.0 copy-done.6
  18.5 0.0 copy-start.3
  18.5 0.9 %copy-done.3 = f32[192,128]{1,0:T(8,128)S(1)} copy-done((f32[192,128]{1,0:T(8,128)S(1)}, f32[192,128]{1,0:T(8,128)}, u32[]{:S(2)}) %copy-start.3) | copy-done | bytes 98328
  19.4 1.1 %pointwise.1 = bf16[4,192,128]{2,1,0:T(8,128)(2,1)} custom-call(f32[192,128]{1,0:T(8,128)S(1)} %copy-done.3, bf16[4,192,128]{2,1,0:T(8,128)(2,1)S(1)} %all-to-all-done.halo_ref, f32[1,128]{1,0:T(1,128)S(1)} %bitcast.20, bf16[3,128]{1,0:T(4,128)(2,1)S(1)} %bitcast.19, s32[192,1]{1,0:T(8,128)S(1)} %reshape.24.label_ref, s32[192,1]{1,0:T(8,128)S(1)} %reshape.25.scale_ref), custom_call_target="tpu_custom_call" | custom-call | flops 737280 | bytes 294912 | tf_op jit(solution)/shard_map/pointwise/pallas_call | solution.py:167
  20.5 3.4 %all-to-all-start.1 = ((bf16[4,192,128]{2,1,0:T(8,128)(2,1)}), bf16[4,192,128]{2,1,0:T(8,128)(2,1)S(1)}, u32[]{:S(2)}, u32[]{:S(2)}) async-start(bf16[4,192,128]{2,1,0:T(8,128)(2,1)} %pointwise.1), calls=%async_computation.1 | async-start | bytes 393216 | tf_op jit(solution)/shard_map/all_to_all | solution.py:330
  23.8 0.0 copy-start
  23.9 0.0 copy-done.1
  23.9 0.0 copy-start.4
  23.9 1.0 %copy-done.4 = f32[192,128]{1,0:T(8,128)S(1)} copy-done((f32[192,128]{1,0:T(8,128)S(1)}, f32[192,128]{1,0:T(8,128)}, u32[]{:S(2)}) %copy-start.4) | copy-done | bytes 98328
  24.9 0.4 arrange.1
  25.4 3.8 %collective-permute-start.2 = (bf16[192,256]{1,0:T(8,128)(2,1)S(1)}, bf16[192,256]{1,0:T(8,128)(2,1)S(1)}, u32[]{:S(2)}, u32[]{:S(2)}) collective-permute-start(bf16[192,256]{1,0:T(8,128)(2,1)S(1)} %get-tuple-element.6), channel_id=1, source_target_pairs={{0,3},{1,0},{2,1},{3,2},{4,7},{5,4},{6,5},{7,6},{8,11},{9,8},{10,9... | collective-permute-start | bytes 294920 | tf_op jit(solution)/shard_map/ppermute | solution.py:319
  29.2 0.0 collective-permute-start.1
  29.2 1.1 %collective-permute-start = (bf16[192,256]{1,0:T(8,128)(2,1)S(1)}, bf16[192,256]{1,0:T(8,128)(2,1)S(1)}, u32[]{:S(2)}, u32[]{:S(2)}) collective-permute-start(bf16[192,256]{1,0:T(8,128)(2,1)S(1)} %get-tuple-element.8), channel_id=1, source_target_pairs={{0,1},{1,2},{2,3},{3,0},{4,5},{5,6},{6,7},{7,4},{8,9},{9,10},{10,1... | collective-permute-start | bytes 294920 | tf_op jit(solution)/shard_map/ppermute | solution.py:319
  30.3 1.3 %collective-permute-done.2.refs_3_ = bf16[192,256]{1,0:T(8,128)(2,1)S(1)} collective-permute-done((bf16[192,256]{1,0:T(8,128)(2,1)S(1)}, bf16[192,256]{1,0:T(8,128)(2,1)S(1)}, u32[]{:S(2)}, u32[]{:S(2)}) %collective-permute-start.2) | collective-permute-done | bytes 98336 | tf_op jit(solution)/shard_map/ppermute | solution.py:319
  31.6 6.9 %collective-permute-done.1.refs_2_ = bf16[192,256]{1,0:T(8,128)(2,1)S(1)} collective-permute-done((bf16[192,256]{1,0:T(8,128)(2,1)S(1)}, bf16[192,256]{1,0:T(8,128)(2,1)S(1)}, u32[]{:S(2)}, u32[]{:S(2)}) %collective-permute-start.1) | collective-permute-done | bytes 98336 | tf_op jit(solution)/shard_map/ppermute | solution.py:319
  38.5 0.0 collective-permute-done.refs_1_
  38.5 0.0 all-to-all-done.1.g_ref
  38.5 1.0 %kernel_grad.1 = bf16[256,1152]{1,0:T(8,128)(2,1)S(1)} custom-call(bf16[4,192,128]{2,1,0:T(8,128)(2,1)S(1)} %all-to-all-done.1.g_ref, bf16[192,256]{1,0:T(8,128)(2,1)S(1)} %get-tuple-element.9.refs_0_, bf16[192,256]{1,0:T(8,128)(2,1)S(1)} %collective-permute-done.refs_1_, bf16[192,256]{1,0:T(8,128)(2,1)S(1)} %collective-permute-done.1.refs_2_, ...), custom_call_target="tpu_custom_call" | custom-call | flops 452984832 | bytes 1179648 | tf_op jit(solution)/shard_map/kernel_grad/pallas_call | solution.py:215
  39.5 0.0 copy-start.2
  39.5 0.8 %copy-done.2 = bf16[256,1152]{1,0:T(8,128)(2,1)} copy-done((bf16[256,1152]{1,0:T(8,128)(2,1)}, bf16[256,1152]{1,0:T(8,128)(2,1)S(1)}, u32[]{:S(2)}) %copy-start.2) | copy-done | bytes 589848
  40.3 3.7 %all-to-all-start.2 = ((bf16[8,32,1152]{2,1,0:T(8,128)(2,1)}), bf16[8,32,1152]{2,1,0:T(8,128)(2,1)S(1)}, u32[]{:S(2)}, u32[]{:S(2)}) async-start(bf16[8,32,1152]{2,1,0:T(8,128)(2,1)} %bitcast.18), calls=%async_computation.2 | async-start | bytes 1179648 | tf_op jit(solution)/shard_map/all_to_all | solution.py:332
  44.1 0.0 copy-done
  44.1 2.6 %feature_grad.1 = f32[192,1024]{1,0:T(8,128)} custom-call(bf16[4,192,128]{2,1,0:T(8,128)(2,1)S(1)} %all-to-all-done.1.g_ref, bf16[9,1024,128]{2,1,0:T(8,128)(2,1)S(1)} %bitcast.15), custom_call_target="tpu_custom_call" | custom-call | flops 452984832 | bytes 3145728 | tf_op jit(solution)/shard_map/feature_grad/pallas_call | solution.py:252
  46.7 7.8 %all-to-all-done.2.in_ref = bf16[8,32,1152]{2,1,0:T(8,128)(2,1)S(1)} async-done(((bf16[8,32,1152]{2,1,0:T(8,128)(2,1)}), bf16[8,32,1152]{2,1,0:T(8,128)(2,1)S(1)}, u32[]{:S(2)}, u32[]{:S(2)}) %all-to-all-start.2) | async-done | bytes 589856 | tf_op jit(solution)/shard_map/all_to_all | solution.py:332
  54.5 0.7 %final_sum.1 = f32[288,128]{1,0:T(8,128)} custom-call(bf16[8,32,1152]{2,1,0:T(8,128)(2,1)S(1)} %all-to-all-done.2.in_ref), custom_call_target="tpu_custom_call" | custom-call | tf_op jit(solution)/shard_map/final_sum/pallas_call | solution.py:285
  (3 shorter events, 0.1 us)
Async XLA Ops:
  0.6 23.3 %copy-start.1 = (bf16[1,6,32,1024]{3,2,1,0:T(8,128)(2,1)S(1)}, bf16[1,6,32,1024]{3,2,1,0:T(8,128)(2,1)}, u32[]{:S(2)}) copy-start(bf16[1,6,32,1024]{3,2,1,0:T(8,128)(2,1)} %param.6) | copy-start | bytes 1179652
  0.6 10.3 %copy-start.7 = (s32[1,6,32]{2,0,1:T(1,128)S(1)}, s32[1,6,32]{2,0,1:T(1,128)}, u32[]{:S(2)}) copy-start(s32[1,6,32]{2,0,1:T(1,128)} %param.7) | copy-start | bytes 2308
  0.7 10.3 %copy-start.8 = (s32[1,6,32]{2,0,1:T(1,128)S(1)}, s32[1,6,32]{2,0,1:T(1,128)}, u32[]{:S(2)}) copy-start(s32[1,6,32]{2,0,1:T(1,128)} %param.8) | copy-start | bytes 2308
  0.7 17.8 %copy-start.5 = (bf16[128,3]{0,1:T(4,128)(2,1)S(1)}, bf16[128,3]{0,1:T(4,128)(2,1)}, u32[]{:S(2)}) copy-start(bf16[128,3]{0,1:T(4,128)(2,1)} %param.11) | copy-start | bytes 2308
  0.7 17.8 %copy-start.6 = (f32[128]{0:T(128)S(1)}, f32[128]{0:T(128)}, u32[]{:S(2)}) copy-start(f32[128]{0:T(128)} %param.10) | copy-start | bytes 1540
  4.6 13.8 %all-to-all-start = ((bf16[4,192,128]{2,1,0:T(8,128)(2,1)}), bf16[4,192,128]{2,1,0:T(8,128)(2,1)S(1)}, u32[]{:S(2)}, u32[]{:S(2)}) async-start(bf16[4,192,128]{2,1,0:T(8,128)(2,1)} %get-tuple-element.5), calls=%async_computation | async-start | bytes 393216 | tf_op jit(solution)/shard_map/all_to_all | solution.py:305
  18.5 0.9 %copy-start.3 = (f32[192,128]{1,0:T(8,128)S(1)}, f32[192,128]{1,0:T(8,128)}, u32[]{:S(2)}) copy-start(f32[192,128]{1,0:T(8,128)} %get-tuple-element.4.middle_ref.after_ref) | copy-start | bytes 294916
  20.5 18.0 %all-to-all-start.1 = ((bf16[4,192,128]{2,1,0:T(8,128)(2,1)}), bf16[4,192,128]{2,1,0:T(8,128)(2,1)S(1)}, u32[]{:S(2)}, u32[]{:S(2)}) async-start(bf16[4,192,128]{2,1,0:T(8,128)(2,1)} %pointwise.1), calls=%async_computation.1 | async-start | bytes 393216 | tf_op jit(solution)/shard_map/all_to_all | solution.py:330
  23.8 20.2 %copy-start = (bf16[1024,9,128]{2,0,1:T(8,128)(2,1)S(1)}, bf16[1024,9,128]{2,0,1:T(8,128)(2,1)}, u32[]{:S(2)}) copy-start(bf16[1024,9,128]{2,0,1:T(8,128)(2,1)} %param.9) | copy-start | bytes 7077892
  23.9 1.0 %copy-start.4 = (f32[192,128]{1,0:T(8,128)S(1)}, f32[192,128]{1,0:T(8,128)}, u32[]{:S(2)}) copy-start(f32[192,128]{1,0:T(8,128)} %get-tuple-element.4.middle_ref.after_ref) | copy-start | bytes 294916
  25.4 6.2 %collective-permute-start.2 = (bf16[192,256]{1,0:T(8,128)(2,1)S(1)}, bf16[192,256]{1,0:T(8,128)(2,1)S(1)}, u32[]{:S(2)}, u32[]{:S(2)}) collective-permute-start(bf16[192,256]{1,0:T(8,128)(2,1)S(1)} %get-tuple-element.6), channel_id=1, source_target_pairs={{0,3},{1,0},{2,1},{3,2},{4,7},{5,4},{6,5},{7,6},{8,11},{9,8},{10,9... | collective-permute-start | bytes 294920 | tf_op jit(solution)/shard_map/ppermute | solution.py:319
  29.2 9.3 %collective-permute-start.1 = (bf16[192,256]{1,0:T(8,128)(2,1)S(1)}, bf16[192,256]{1,0:T(8,128)(2,1)S(1)}, u32[]{:S(2)}, u32[]{:S(2)}) collective-permute-start(bf16[192,256]{1,0:T(8,128)(2,1)S(1)} %get-tuple-element.7), channel_id=1, source_target_pairs={{0,2},{1,3},{2,0},{3,1},{4,6},{5,7},{6,4},{7,5},{8,10},{9,11},{10,... | collective-permute-start | bytes 294920 | tf_op jit(solution)/shard_map/ppermute | solution.py:319
  29.2 9.3 %collective-permute-start = (bf16[192,256]{1,0:T(8,128)(2,1)S(1)}, bf16[192,256]{1,0:T(8,128)(2,1)S(1)}, u32[]{:S(2)}, u32[]{:S(2)}) collective-permute-start(bf16[192,256]{1,0:T(8,128)(2,1)S(1)} %get-tuple-element.8), channel_id=1, source_target_pairs={{0,1},{1,2},{2,3},{3,0},{4,5},{5,6},{6,7},{7,4},{8,9},{9,10},{10,1... | collective-permute-start | bytes 294920 | tf_op jit(solution)/shard_map/ppermute | solution.py:319
  39.5 0.8 %copy-start.2 = (bf16[256,1152]{1,0:T(8,128)(2,1)}, bf16[256,1152]{1,0:T(8,128)(2,1)S(1)}, u32[]{:S(2)}) copy-start(bf16[256,1152]{1,0:T(8,128)(2,1)S(1)} %kernel_grad.1) | copy-start | bytes 1769476
  40.3 14.2 %all-to-all-start.2 = ((bf16[8,32,1152]{2,1,0:T(8,128)(2,1)}), bf16[8,32,1152]{2,1,0:T(8,128)(2,1)S(1)}, u32[]{:S(2)}, u32[]{:S(2)}) async-start(bf16[8,32,1152]{2,1,0:T(8,128)(2,1)} %bitcast.18), calls=%async_computation.2 | async-start | bytes 1179648 | tf_op jit(solution)/shard_map/all_to_all | solution.py:332

commit v4 on v2

v4 whole, which is shorter than its diff:
```python
import functools

import jax
import jax.numpy as jnp
from jax import lax
from jax.experimental import pallas as pl
from jax.experimental.pallas import tpu as pltpu
from jax.sharding import PartitionSpec as P

DILATION_SIZE = 6
VMEM_LIMIT = 16 * 1024 * 1024


def channel_plan(channels, taps, replicas, bands):
    rows = channels * taps // (replicas * bands)
    starts = [[(d * bands + s) * rows // taps for d in range(replicas)] for s in range(bands)]
    offsets = [[(d * bands + s) * rows % taps for d in range(replicas)] for s in range(bands)]
    cover = max(-(-(off + rows) // taps) for line in offsets for off in line)
    picks = [[min(c + k, channels - 1) for c in line for k in range(cover)] for line in starts]
    return rows, cover, picks, offsets


def shift_columns(array, by, columns):
    if by == 0:
        return array
    size = array.shape[0]
    column = lax.broadcasted_iota(jnp.int32, array.shape, 0) % columns + by
    moved = pltpu.roll(array, (-by) % size, 0)
    return jnp.where((column >= 0) & (column < columns), moved, 0.0)


def tap_row(x, w_ref, a, columns, reach):
    width = w_ref.shape[2]
    weight = jnp.concatenate([w_ref[3 * a + b] for b in range(3)], axis=1)
    product = jnp.dot(x, weight, preferred_element_type=jnp.float32)
    return sum(
        shift_columns(product[:, b * width : (b + 1) * width], (b - 1) * reach, columns)
        for b in range(3)
    )


def halo_kernel(columns, reach, x_ref, w_ref, after_ref, down_ref, up_ref):
    del after_ref
    pixels, edge = x_ref.shape[0], reach * columns
    down_ref[...] = tap_row(x_ref[pixels - edge :], w_ref, 0, columns, reach).astype(down_ref.dtype)
    up_ref[...] = tap_row(x_ref[:edge], w_ref, 2, columns, reach).astype(up_ref.dtype)


def halo(flat, weight, after, columns, reach):
    pixels, channels = flat.shape
    width = weight.shape[2]
    edge = reach * columns
    vmem = pl.BlockSpec(memory_space=pltpu.VMEM)
    return pl.pallas_call(
        functools.partial(halo_kernel, columns, reach),
        in_specs=[vmem, vmem, pl.BlockSpec(memory_space=pltpu.HBM)],
        out_shape=[jax.ShapeDtypeStruct((edge, width), jnp.bfloat16)] * 2,
        compiler_params=pltpu.CompilerParams(vmem_limit_bytes=VMEM_LIMIT),
        cost_estimate=pl.CostEstimate(
            flops=12 * edge * channels * width,
            bytes_accessed=12 * channels * width + 2 * pixels * channels,
            transcendentals=0,
        ),
        name="halo",
    )(flat, weight, after)


def middle_kernel(columns, reach, x_ref, w_ref, after_ref, out_ref):
    del after_ref
    pixels, edge = x_ref.shape[0], reach * columns
    out_ref[...] = tap_row(x_ref[...], w_ref, 1, columns, reach)
    if pixels > edge:
        out_ref[edge:] += tap_row(x_ref[: pixels - edge], w_ref, 0, columns, reach)
        out_ref[: pixels - edge] += tap_row(x_ref[edge:], w_ref, 2, columns, reach)


def middle_taps(flat, weight, after, columns, reach):
    pixels, channels = flat.shape
    width = weight.shape[2]
    vmem = pl.BlockSpec(memory_space=pltpu.VMEM)
    return pl.pallas_call(
        functools.partial(middle_kernel, columns, reach),
        in_specs=[vmem, vmem, pl.BlockSpec(memory_space=pl.ANY)],
        out_shape=jax.ShapeDtypeStruct((pixels, width), jnp.float32),
        compiler_params=pltpu.CompilerParams(vmem_limit_bytes=VMEM_LIMIT),
        cost_estimate=pl.CostEstimate(
            flops=6 * pixels * channels * width,
            bytes_accessed=6 * channels * width + 2 * pixels * channels,
            transcendentals=0,
        ),
        name="middle_taps",
    )(flat, weight, after)


def arrange_kernel(replicas, cover, x_ref, out_ref, room, sems):
    bands = out_ref.shape[0]
    x = x_ref[...]
    copies = [pltpu.make_async_copy(room.at[s], out_ref.at[s], sems.at[s]) for s in range(bands)]
    for s in range(bands):
        room[s] = jnp.concatenate(
            [x[:, (d * bands + s) * cover : (d * bands + s + 1) * cover] for d in range(replicas)],
            axis=1,
        )
        copies[s].start()
    for copy in copies:
        copy.wait()


def arrange(flat, bands, replicas, cover):
    pixels, channels = flat.shape
    shape = (bands, pixels, replicas * cover)
    return pl.pallas_call(
        functools.partial(arrange_kernel, replicas, cover),
        in_specs=[pl.BlockSpec(memory_space=pltpu.VMEM)],
        out_specs=pl.BlockSpec(memory_space=pltpu.HBM),
        out_shape=jax.ShapeDtypeStruct(shape, flat.dtype),
        scratch_shapes=[pltpu.VMEM(shape, flat.dtype), pltpu.SemaphoreType.DMA((bands,))],
        compiler_params=pltpu.CompilerParams(vmem_limit_bytes=VMEM_LIMIT),
        cost_estimate=pl.CostEstimate(
            flops=0, bytes_accessed=4 * pixels * channels, transcendentals=0
        ),
        name="arrange",
    )(flat)


def pointwise_kernel(
    middle_ref, above_ref, below_ref, bias_ref, class_ref, label_ref, scale_ref, after_ref,
    out_ref, room, sems
):
    del after_ref
    bands = out_ref.shape[0]
    pixels, width = middle_ref.shape
    edge = above_ref.shape[0]
    above = above_ref[...].astype(jnp.float32)
    below = below_ref[...].astype(jnp.float32)
    if pixels > edge:
        none = jnp.zeros((pixels - edge, width), jnp.float32)
        above = jnp.concatenate([above, none], axis=0)
        below = jnp.concatenate([none, below], axis=0)
    preact = middle_ref[...] + above + below + bias_ref[...]
    sigmoid_z = jax.nn.sigmoid(preact)
    hidden = (preact * sigmoid_z).astype(jnp.bfloat16)
    classes = class_ref[...]
    logits = lax.dot_general(
        hidden, classes, (((1,), (1,)), ((), ())), preferred_element_type=jnp.float32
    )
    exponent = jnp.exp(logits)
    chances = exponent / jnp.sum(exponent, axis=1, keepdims=True)
    index = lax.broadcasted_iota(jnp.int32, chances.shape, 1)
    onehot = jnp.where(label_ref[...] == index, 1.0, 0.0)
    grad_logits = scale_ref[...].astype(jnp.float32) * (chances - onehot)
    wide = classes.astype(jnp.float32)
    hidden_grad = sum(
        grad_logits[:, k : k + 1] * wide[k : k + 1] for k in range(classes.shape[0])
    )
    gradient = hidden_grad * sigmoid_z * (1.0 + preact * (1.0 - sigmoid_z))
    room[...] = gradient.astype(out_ref.dtype)
    copies = [pltpu.make_async_copy(room, out_ref.at[s], sems.at[s]) for s in range(bands)]
    for copy in copies:
        copy.start()
    for copy in copies:
        copy.wait()


def pointwise(middle, above, below, bias, classes, labels, scale, after, bands):
    pixels, width = middle.shape
    vmem = pl.BlockSpec(memory_space=pltpu.VMEM)
    return pl.pallas_call(
        pointwise_kernel,
        in_specs=[vmem] * 7 + [pl.BlockSpec(memory_space=pl.ANY)],
        out_specs=pl.BlockSpec(memory_space=pltpu.HBM),
        out_shape=jax.ShapeDtypeStruct((bands, pixels, width), jnp.bfloat16),
        scratch_shapes=[
            pltpu.VMEM((pixels, width), jnp.bfloat16),
            pltpu.SemaphoreType.DMA((bands,)),
        ],
        compiler_params=pltpu.CompilerParams(vmem_limit_bytes=VMEM_LIMIT),
        cost_estimate=pl.CostEstimate(
            flops=30 * pixels * width,
            bytes_accessed=2 * bands * pixels * width + 8 * pixels * width,
            transcendentals=pixels * width,
        ),
        name="pointwise",
    )(middle, above, below, bias, classes, labels, scale, after)


def shifted_taps(gradient, columns, reach):
    wide = gradient.astype(jnp.float32)
    return jnp.concatenate(
        [shift_columns(wide, (1 - b) * reach, columns).astype(jnp.bfloat16) for b in range(3)],
        axis=1,
    )


def kernel_grad_kernel(columns, reach, g_ref, x_ref, out_ref, room, sems):
    bands, pixels, width = g_ref.shape
    total = bands * pixels
    edge = reach * columns
    shifted = shifted_taps(g_ref[...].reshape(total, width), columns, reach)
    features = x_ref[...].reshape(total, x_ref.shape[2])
    copies = []
    for a in range(3):
        if a == 0:
            left, right = features[: total - edge], shifted[edge:]
        elif a == 1:
            left, right = features, shifted
        else:
            left, right = features[edge:], shifted[: total - edge]
        block = lax.dot_general(
            left, right, (((0,), (0,)), ((), ())), preferred_element_type=jnp.float32
        )
        room[a] = block.astype(room.dtype)
        lanes = pl.ds(3 * a * width, 3 * width)
        copies.append(pltpu.make_async_copy(room.at[a], out_ref.at[:, lanes], sems.at[a]))
        copies[-1].start()
    for copy in copies:
        copy.wait()


def kernel_grad(gathered, features, columns, reach):
    bands, pixels, width = gathered.shape
    extra = features.shape[2]
    vmem = pl.BlockSpec(memory_space=pltpu.VMEM)
    return pl.pallas_call(
        functools.partial(kernel_grad_kernel, columns, reach),
        in_specs=[vmem, vmem],
        out_specs=pl.BlockSpec(memory_space=pltpu.HBM),
        out_shape=jax.ShapeDtypeStruct((extra, 9 * width), jnp.bfloat16),
        scratch_shapes=[
            pltpu.VMEM((3, extra, 3 * width), jnp.bfloat16),
            pltpu.SemaphoreType.DMA((3,)),
        ],
        compiler_params=pltpu.CompilerParams(vmem_limit_bytes=VMEM_LIMIT),
        cost_estimate=pl.CostEstimate(
            flops=18 * bands * pixels * extra * width,
            bytes_accessed=2 * bands * pixels * (width + extra) + 18 * extra * width,
            transcendentals=0,
        ),
        name="kernel_grad",
    )(gathered, features)


def feature_grad_kernel(columns, reach, g_ref, w_ref, out_ref):
    band = lax.axis_index("space")
    bands, pixels, width = g_ref.shape
    edge = reach * columns
    own = g_ref[band]
    above = g_ref[jnp.maximum(band - 1, 0)][pixels - edge :]
    below = g_ref[jnp.minimum(band + 1, bands - 1)][:edge]
    above = jnp.where(band > 0, above, jnp.zeros_like(above))
    below = jnp.where(band + 1 < bands, below, jnp.zeros_like(below))
    stack = shifted_taps(jnp.concatenate([above, own, below], axis=0), columns, reach)
    taps = jnp.concatenate(
        [stack[(2 - a) * edge : (2 - a) * edge + pixels] for a in range(3)], axis=1
    )
    weight = jnp.concatenate([w_ref[t] for t in range(9)], axis=1)
    out_ref[...] = lax.dot_general(
        taps, weight, (((1,), (1,)), ((), ())), preferred_element_type=jnp.float32
    )


def feature_grad(gathered, weight, columns, reach):
    bands, pixels, _ = gathered.shape
    taps, channels, width = weight.shape
    step = 256 if channels % 256 == 0 else channels
    return pl.pallas_call(
        functools.partial(feature_grad_kernel, columns, reach),
        grid=(channels // step,),
        in_specs=[
            pl.BlockSpec((bands, pixels, width), lambda i: (0, 0, 0)),
            pl.BlockSpec((taps, step, width), lambda i: (0, i, 0)),
        ],
        out_specs=pl.BlockSpec((pixels, step), lambda i: (0, i)),
        out_shape=jax.ShapeDtypeStruct((pixels, channels), jnp.float32),
        compiler_params=pltpu.CompilerParams(vmem_limit_bytes=VMEM_LIMIT),
        cost_estimate=pl.CostEstimate(
            flops=2 * pixels * taps * channels * width,
            bytes_accessed=2 * taps * channels * width + 4 * pixels * channels,
            transcendentals=0,
        ),
        name="feature_grad",
    )(gathered, weight)


def final_kernel(in_ref, out_ref):
    replicas, cover, lanes = in_ref.shape
    width = out_ref.shape[1]
    taps = lanes // width
    total = in_ref[0].astype(jnp.float32)
    for d in range(1, replicas):
        total += in_ref[d].astype(jnp.float32)
    total = total / replicas
    for t in range(taps):
        out_ref[pl.ds(t, cover, stride=taps), :] = total[:, t * width : (t + 1) * width]


def final(came, width):
    replicas, cover, lanes = came.shape
    return pl.pallas_call(
        final_kernel,
        out_shape=jax.ShapeDtypeStruct((cover * lanes // width, width), jnp.float32),
        compiler_params=pltpu.CompilerParams(vmem_limit_bytes=VMEM_LIMIT),
        name="final_sum",
    )(came)


def on_device(features, labels, pixel_weight, conv_weight, conv_bias, class_weight):
    image = features[0]
    band_rows, columns, channels = image.shape
    taps, width = conv_weight.shape[1:]
    pixels = band_rows * columns
    replicas = lax.axis_size("dp")
    bands = lax.axis_size("space")
    reach = DILATION_SIZE

    flat = image.reshape(pixels, channels)
    weight = conv_weight.transpose(1, 0, 2)
    block_rows, cover, picks, offsets = channel_plan(channels, taps, replicas, bands)
    if block_rows % taps == 0:
        split = arrange(flat, bands, replicas, cover)
    else:
        order = jnp.array([c for line in picks for c in line], jnp.int32)
        split = jnp.take(flat, order, axis=1)
        split = split.reshape(pixels, bands, replicas * cover).transpose(1, 0, 2)
    whole = lax.all_to_all(split, "space", 0, 0)

    down, up = halo(flat, weight, split, columns, reach)
    above = lax.ppermute(down, "space", [(i, i + 1) for i in range(bands - 1)])
    below = lax.ppermute(up, "space", [(i + 1, i) for i in range(bands - 1)])
    middle = middle_taps(flat, weight, up, columns, reach)

    gradient = pointwise(
        middle,
        above,
        below,
        conv_bias.reshape(1, width),
        class_weight.T,
        labels.reshape(pixels, 1),
        pixel_weight.reshape(pixels, 1),
        whole,
        bands,
    )
    gathered = lax.all_to_all(gradient, "space", 0, 0)
    partial_grad = kernel_grad(gathered, whole, columns, reach)
    came = lax.all_to_all(partial_grad.reshape(replicas, cover, taps * width), "dp", 0, 0)
    weight_grad = final(came, width)
    if block_rows % taps:
        start = jnp.array(offsets)[lax.axis_index("space"), lax.axis_index("dp")]
        weight_grad = lax.dynamic_slice_in_dim(weight_grad, start, block_rows)

    grad = feature_grad(gathered, weight, columns, reach)
    return grad.reshape(1, band_rows, columns, channels), weight_grad


def solution(mesh):
    placed = (
        P("dp", "space", None, None),
        P("dp", "space", None),
        P("dp", "space", None),
        P(),
        P(),
        P(),
    )
    return jax.shard_map(
        on_device,
        mesh=mesh,
        in_specs=placed,
        out_specs=(P("dp", "space", None, None), P(("dp", "space"), None)),
        check_vma=False,
    )
```

time: 54.3 us -> 51.4 us (0.947)
  blocking collectives: 17.9 us -> 10.2 us
  starting transfers between devices: 10 us -> 15.3 us
  waiting for transfers between devices: 14.6 us -> 12 us
  Pallas kernels: 6.8 us -> 7.95 us
  local copies, waits for them, and re-layouts: 3.77 us -> 4.7 us
    all_to_all x1, blocking collectives: 17.9 us -> 10.2 us  [on_device(): gathered = lax.all_to_all(gradient, 'space', 0, 0)]
    all_to_all x1, waiting for transfers between devices: 6.82 us -> 0.01 us  [on_device(): whole = lax.all_to_all(split, 'space', 0, 0)]
    ppermute x0 -> x2, starting transfers between devices: none -> 5.21 us  [the longest x1 3.92 us: on_device(): above = lax.ppermute(down, 'space', [(i, i + 1) for i in range(bands - 1)])]
    ppermute x0 -> x2, waiting for transfers between devices: none -> 4.2 us  [the longest x1 4.15 us: on_device(): below = lax.ppermute(up, 'space', [(i + 1, i) for i in range(bands - 1)])]
    pallas_call x4 -> x5, Pallas kernels: 3.43 us -> 4.59 us  [the longest x1 1.29 us: kernel_grad(): pl.pallas_call(functools.partial(kernel_grad_kernel, columns, reach), in_...]
    unnamed x18 -> x20, local copies, waits for them, and re-layouts: 3.51 us -> 4.47 us
  transfers between devices with their start and end apart: 2 -> 4, of which waited for: 2 -> 2; matrix products, arithmetic and copies ran while one was open for 1% -> 1% of each run, Pallas kernels for 6% -> 8%
where the time goes in v4:
time: 51.4 us; the launch traced here: 51 us
  starting transfers between devices  15.3 us (30%)
  waiting for transfers between devices  12 us (23%)
  blocking collectives  10.2 us (20%)
  Pallas kernels  7.95 us (15%)
  local copies, waits for them, and re-layouts  4.7 us (9%)
  between operations  0.77 us (1%)
    all_to_all x1, blocking collectives, on_device(): gathered = lax.all_to_all(gradient, 'space', 0, 0)  10.2 us
    all_to_all x1, waiting for transfers between devices, on_device(): lax.all_to_all(partial_grad.reshape(replicas, cover, taps * width), 'dp',...  7.83 us
    all_to_all x1, starting transfers between devices, on_device(): whole = lax.all_to_all(split, 'space', 0, 0)  6.33 us
    unnamed x20, local copies, waits for them, and re-layouts  4.47 us
    ppermute x1, waiting for transfers between devices, on_device(): below = lax.ppermute(up, 'space', [(i + 1, i) for i in range(bands - 1)])  4.15 us
    ppermute x1, starting transfers between devices, on_device(): above = lax.ppermute(down, 'space', [(i, i + 1) for i in range(bands - 1)])  3.92 us
    all_to_all x1, starting transfers between devices, on_device(): lax.all_to_all(partial_grad.reshape(replicas, cover, taps * width), 'dp',...  3.73 us
    pallas_call x1, Pallas kernels, feature_grad(): pl.pallas_call(functools.partial(feature_grad_kernel, columns, reach), gr...  2.62 us
  transfers between devices with their start and end apart: 4, of which 2 were waited for; matrix products, arithmetic and copies ran while one was open for 1% of the time, Pallas kernels for 8%

profile of v4, /device:TPU:0, one launch (start us, length us, event | category | flops | bytes accessed | tf_op | source)
XLA Modules:
  0.0 51.0 jit_solution(1101922659525028853)
XLA Ops:
  0.6 0.0 copy-start.2
  0.6 1.0 %copy-done.2 = bf16[1,6,32,1024]{3,2,1,0:T(8,128)(2,1)S(1)} copy-done((bf16[1,6,32,1024]{3,2,1,0:T(8,128)(2,1)S(1)}, bf16[1,6,32,1024]{3,2,1,0:T(8,128)(2,1)}, u32[]{:S(2)}) %copy-start.2) | copy-done | bytes 393240
  1.6 0.0 copy-start.8
  1.6 0.0 copy-start.9
  1.6 0.0 copy-start.4
  1.6 1.0 %arrange.1.after_ref = bf16[4,192,256]{2,1,0:T(8,128)(2,1)} custom-call(bf16[192,1024]{1,0:T(8,128)(2,1)S(1)} %bitcast.9), custom_call_target="tpu_custom_call" | custom-call | bytes 786432 | tf_op jit(solution)/shard_map/arrange/pallas_call | solution.py:112
  2.7 6.3 %all-to-all-start = ((bf16[4,192,256]{2,1,0:T(8,128)(2,1)}), bf16[4,192,256]{2,1,0:T(8,128)(2,1)S(1)}, u32[]{:S(2)}, u32[]{:S(2)}) async-start(bf16[4,192,256]{2,1,0:T(8,128)(2,1)} %arrange.1.after_ref), calls=%async_computation | async-start | bytes 786432 | tf_op jit(solution)/shard_map/all_to_all | solution.py:325
  9.0 0.0 copy-start
  9.0 1.7 %copy-done = bf16[1024,9,128]{2,0,1:T(8,128)(2,1)S(1)} copy-done((bf16[1024,9,128]{2,0,1:T(8,128)(2,1)S(1)}, bf16[1024,9,128]{2,0,1:T(8,128)(2,1)}, u32[]{:S(2)}) %copy-start) | copy-done | bytes 2359320
  10.7 0.0 copy-start.3
  10.7 1.0 %copy-done.3 = bf16[1,6,32,1024]{3,2,1,0:T(8,128)(2,1)S(1)} copy-done((bf16[1,6,32,1024]{3,2,1,0:T(8,128)(2,1)S(1)}, bf16[1,6,32,1024]{3,2,1,0:T(8,128)(2,1)}, u32[]{:S(2)}) %copy-start.3) | copy-done | bytes 393240
  11.7 0.0 copy-start.1
  11.7 0.0 copy-start.6
  11.7 0.0 copy-start.7
  11.7 1.2 %halo.1 = (bf16[192,128]{1,0:T(8,128)(2,1)}, bf16[192,128]{1,0:T(8,128)(2,1)}) custom-call(bf16[192,1024]{1,0:T(8,128)(2,1)S(1)} %bitcast.10, bf16[9,1024,128]{2,1,0:T(8,128)(2,1)S(1)} %bitcast.6, bf16[4,192,256]{2,1,0:T(8,128)(2,1)} %arrange.1.after_ref), custom_call_target="tpu_custom_call" | custom-call | flops 301989888 | bytes 1966080 | tf_op jit(solution)/shard_map/halo/pallas_call | solution.py:54
  12.9 3.9 %collective-permute-start = (bf16[192,128]{1,0:T(8,128)(2,1)}, bf16[192,128]{1,0:T(8,128)(2,1)S(1)}, u32[]{:S(2)}, u32[]{:S(2)}) collective-permute-start(bf16[192,128]{1,0:T(8,128)(2,1)} %get-tuple-element.5), channel_id=1, source_target_pairs={{0,1},{1,2},{2,3},{4,5},{5,6},{6,7},{8,9},{9,10},{10,11},{12,13},{... | collective-permute-start | bytes 147464 | tf_op jit(solution)/shard_map/ppermute | solution.py:328
  16.8 1.3 %collective-permute-start.1 = (bf16[192,128]{1,0:T(8,128)(2,1)}, bf16[192,128]{1,0:T(8,128)(2,1)S(1)}, u32[]{:S(2)}, u32[]{:S(2)}) collective-permute-start(bf16[192,128]{1,0:T(8,128)(2,1)} %get-tuple-element.4.after_ref), channel_id=1, source_target_pairs={{1,0},{2,1},{3,2},{5,4},{6,5},{7,6},{9,8},{10,9},{11,10},{13,12},{... | collective-permute-start | bytes 147464 | tf_op jit(solution)/shard_map/ppermute | solution.py:329
  18.1 0.0 copy-done.8
  18.1 0.0 copy-done.9
  18.2 0.1 reshape.25.scale_ref
  18.3 0.1 reshape.24.label_ref
  18.4 0.0 copy-done.4
  18.4 0.0 copy-done.1
  18.4 0.4 middle_taps.1.middle_ref
  18.8 0.1 collective-permute-done.above_ref
  18.8 4.1 %collective-permute-done.1.below_ref = bf16[192,128]{1,0:T(8,128)(2,1)S(1)} collective-permute-done((bf16[192,128]{1,0:T(8,128)(2,1)}, bf16[192,128]{1,0:T(8,128)(2,1)S(1)}, u32[]{:S(2)}, u32[]{:S(2)}) %collective-permute-start.1) | collective-permute-done | bytes 49184 | tf_op jit(solution)/shard_map/ppermute | solution.py:329
  23.0 0.0 all-to-all-done.after_ref.x_ref
  23.0 0.0 copy-done.6
  23.0 0.0 copy-done.7
  23.0 0.7 %pointwise.1 = bf16[4,192,128]{2,1,0:T(8,128)(2,1)S(1)} custom-call(f32[192,128]{1,0:T(8,128)S(1)} %middle_taps.1.middle_ref, bf16[192,128]{1,0:T(8,128)(2,1)S(1)} %collective-permute-done.above_ref, bf16[192,128]{1,0:T(8,128)(2,1)S(1)} %collective-permute-done.1.below_ref, f32[1,128]{1,0:T(1,128)S(1)} %bitcast.14, bf16[3,128]{1,0:T(4,128)(2,1)S(1)} %bitcast.13, ...), custom_call_target="tpu_custom_call" | custom-call | flops 737280 | bytes 393216 | tf_op jit(solution)/shard_map/pointwise/pallas_call | solution.py:168
  23.7 10.2 %all_to_all.15.g_ref = bf16[4,192,128]{2,1,0:T(8,128)(2,1)S(1)} all-to-all(bf16[4,192,128]{2,1,0:T(8,128)(2,1)S(1)} %pointwise.1), channel_id=1, replica_groups=mesh['dp'=8,'space'=4] {'space'}, dimensions={0} | all-to-all | bytes 393216 | tf_op jit(solution)/shard_map/all_to_all | solution.py:343
  34.0 1.3 %kernel_grad.1 = bf16[256,1152]{1,0:T(8,128)(2,1)S(1)} custom-call(bf16[4,192,128]{2,1,0:T(8,128)(2,1)S(1)} %all_to_all.15.g_ref, bf16[4,192,256]{2,1,0:T(8,128)(2,1)S(1)} %all-to-all-done.after_ref.x_ref), custom_call_target="tpu_custom_call" | custom-call | flops 452984832 | bytes 1179648 | tf_op jit(solution)/shard_map/kernel_grad/pallas_call | solution.py:224
  35.3 0.0 copy-start.5
  35.3 0.8 %copy-done.5 = bf16[256,1152]{1,0:T(8,128)(2,1)} copy-done((bf16[256,1152]{1,0:T(8,128)(2,1)}, bf16[256,1152]{1,0:T(8,128)(2,1)S(1)}, u32[]{:S(2)}) %copy-start.5) | copy-done | bytes 589848
  36.1 3.7 %all-to-all-start.2 = ((bf16[8,32,1152]{2,1,0:T(8,128)(2,1)}), bf16[8,32,1152]{2,1,0:T(8,128)(2,1)S(1)}, u32[]{:S(2)}, u32[]{:S(2)}) async-start(bf16[8,32,1152]{2,1,0:T(8,128)(2,1)} %bitcast.12), calls=%async_computation.2 | async-start | bytes 1179648 | tf_op jit(solution)/shard_map/all_to_all | solution.py:345
  39.8 2.6 %feature_grad.1 = f32[192,1024]{1,0:T(8,128)} custom-call(bf16[4,192,128]{2,1,0:T(8,128)(2,1)S(1)} %all_to_all.15.g_ref, bf16[9,1024,128]{2,1,0:T(8,128)(2,1)S(1)} %bitcast.8), custom_call_target="tpu_custom_call" | custom-call | flops 452984832 | bytes 3145728 | tf_op jit(solution)/shard_map/feature_grad/pallas_call | solution.py:266
  42.4 7.8 %all-to-all-done.2.in_ref = bf16[8,32,1152]{2,1,0:T(8,128)(2,1)S(1)} async-done(((bf16[8,32,1152]{2,1,0:T(8,128)(2,1)}), bf16[8,32,1152]{2,1,0:T(8,128)(2,1)S(1)}, u32[]{:S(2)}, u32[]{:S(2)}) %all-to-all-start.2) | async-done | bytes 589856 | tf_op jit(solution)/shard_map/all_to_all | solution.py:345
  50.2 0.7 %final_sum.1 = f32[288,128]{1,0:T(8,128)} custom-call(bf16[8,32,1152]{2,1,0:T(8,128)(2,1)S(1)} %all-to-all-done.2.in_ref), custom_call_target="tpu_custom_call" | custom-call | tf_op jit(solution)/shard_map/final_sum/pallas_call | solution.py:299
  (2 shorter events, 0.0 us)
Async XLA Ops:
  0.6 1.0 %copy-start.2 = (bf16[1,6,32,1024]{3,2,1,0:T(8,128)(2,1)S(1)}, bf16[1,6,32,1024]{3,2,1,0:T(8,128)(2,1)}, u32[]{:S(2)}) copy-start(bf16[1,6,32,1024]{3,2,1,0:T(8,128)(2,1)} %param.6) | copy-start | bytes 1179652
  1.6 16.5 %copy-start.8 = (s32[1,6,32]{2,0,1:T(1,128)S(1)}, s32[1,6,32]{2,0,1:T(1,128)}, u32[]{:S(2)}) copy-start(s32[1,6,32]{2,0,1:T(1,128)} %param.7) | copy-start | bytes 2308
  1.6 16.5 %copy-start.9 = (s32[1,6,32]{2,0,1:T(1,128)S(1)}, s32[1,6,32]{2,0,1:T(1,128)}, u32[]{:S(2)}) copy-start(s32[1,6,32]{2,0,1:T(1,128)} %param.8) | copy-start | bytes 2308
  1.6 16.8 %copy-start.4 = (bf16[1,6,32,1024]{3,2,1,0:T(8,128)(2,1)S(1)}, bf16[1,6,32,1024]{3,2,1,0:T(8,128)(2,1)}, u32[]{:S(2)}) copy-start(bf16[1,6,32,1024]{3,2,1,0:T(8,128)(2,1)} %param.6) | copy-start | bytes 1179652
  2.7 20.3 %all-to-all-start = ((bf16[4,192,256]{2,1,0:T(8,128)(2,1)}), bf16[4,192,256]{2,1,0:T(8,128)(2,1)S(1)}, u32[]{:S(2)}, u32[]{:S(2)}) async-start(bf16[4,192,256]{2,1,0:T(8,128)(2,1)} %arrange.1.after_ref), calls=%async_computation | async-start | bytes 786432 | tf_op jit(solution)/shard_map/all_to_all | solution.py:325
  9.0 1.7 %copy-start = (bf16[1024,9,128]{2,0,1:T(8,128)(2,1)S(1)}, bf16[1024,9,128]{2,0,1:T(8,128)(2,1)}, u32[]{:S(2)}) copy-start(bf16[1024,9,128]{2,0,1:T(8,128)(2,1)} %param.9) | copy-start | bytes 7077892
  10.7 1.0 %copy-start.3 = (bf16[1,6,32,1024]{3,2,1,0:T(8,128)(2,1)S(1)}, bf16[1,6,32,1024]{3,2,1,0:T(8,128)(2,1)}, u32[]{:S(2)}) copy-start(bf16[1,6,32,1024]{3,2,1,0:T(8,128)(2,1)} %param.6) | copy-start | bytes 1179652
  11.7 6.7 %copy-start.1 = (bf16[1024,9,128]{2,0,1:T(8,128)(2,1)S(1)}, bf16[1024,9,128]{2,0,1:T(8,128)(2,1)}, u32[]{:S(2)}) copy-start(bf16[1024,9,128]{2,0,1:T(8,128)(2,1)} %param.9) | copy-start | bytes 7077892
  11.7 11.3 %copy-start.6 = (bf16[128,3]{0,1:T(4,128)(2,1)S(1)}, bf16[128,3]{0,1:T(4,128)(2,1)}, u32[]{:S(2)}) copy-start(bf16[128,3]{0,1:T(4,128)(2,1)} %param.11) | copy-start | bytes 2308
  11.7 11.3 %copy-start.7 = (f32[128]{0:T(128)S(1)}, f32[128]{0:T(128)}, u32[]{:S(2)}) copy-start(f32[128]{0:T(128)} %param.10) | copy-start | bytes 1540
  12.9 6.0 %collective-permute-start = (bf16[192,128]{1,0:T(8,128)(2,1)}, bf16[192,128]{1,0:T(8,128)(2,1)S(1)}, u32[]{:S(2)}, u32[]{:S(2)}) collective-permute-start(bf16[192,128]{1,0:T(8,128)(2,1)} %get-tuple-element.5), channel_id=1, source_target_pairs={{0,1},{1,2},{2,3},{4,5},{5,6},{6,7},{8,9},{9,10},{10,11},{12,13},{... | collective-permute-start | bytes 147464 | tf_op jit(solution)/shard_map/ppermute | solution.py:328
  16.8 6.2 %collective-permute-start.1 = (bf16[192,128]{1,0:T(8,128)(2,1)}, bf16[192,128]{1,0:T(8,128)(2,1)S(1)}, u32[]{:S(2)}, u32[]{:S(2)}) collective-permute-start(bf16[192,128]{1,0:T(8,128)(2,1)} %get-tuple-element.4.after_ref), channel_id=1, source_target_pairs={{1,0},{2,1},{3,2},{5,4},{6,5},{7,6},{9,8},{10,9},{11,10},{13,12},{... | collective-permute-start | bytes 147464 | tf_op jit(solution)/shard_map/ppermute | solution.py:329
  35.3 0.8 %copy-start.5 = (bf16[256,1152]{1,0:T(8,128)(2,1)}, bf16[256,1152]{1,0:T(8,128)(2,1)S(1)}, u32[]{:S(2)}) copy-start(bf16[256,1152]{1,0:T(8,128)(2,1)S(1)} %kernel_grad.1) | copy-start | bytes 1769476
  36.1 14.2 %all-to-all-start.2 = ((bf16[8,32,1152]{2,1,0:T(8,128)(2,1)}), bf16[8,32,1152]{2,1,0:T(8,128)(2,1)S(1)}, u32[]{:S(2)}, u32[]{:S(2)}) async-start(bf16[8,32,1152]{2,1,0:T(8,128)(2,1)} %bitcast.12), calls=%async_computation.2 | async-start | bytes 1179648 | tf_op jit(solution)/shard_map/all_to_all | solution.py:345

commit v5 on v4

--- a/solution.py
+++ b/solution.py
@@ -9,6 +9,7 @@
 
 DILATION_SIZE = 6
 VMEM_LIMIT = 16 * 1024 * 1024
+VMEM_WHOLE = 62 * 1024 * 1024
 
 
 def channel_plan(channels, taps, replicas, bands):
@@ -39,30 +40,75 @@
     )
 
 
-def halo_kernel(columns, reach, x_ref, w_ref, after_ref, down_ref, up_ref):
-    del after_ref
+def prepare_kernel(
+    columns, reach, replicas, cover, x_hbm, w_hbm, *refs
+):
+    outs, (x_ref, w_ref, room, halo, x_sem, w_sems, out_sems, halo_sems) = refs[:-8], refs[-8:]
+    down_hbm, up_hbm = outs[:2]
     pixels, edge = x_ref.shape[0], reach * columns
-    down_ref[...] = tap_row(x_ref[pixels - edge :], w_ref, 0, columns, reach).astype(down_ref.dtype)
-    up_ref[...] = tap_row(x_ref[:edge], w_ref, 2, columns, reach).astype(up_ref.dtype)
-
-
-def halo(flat, weight, after, columns, reach):
+    load = pltpu.make_async_copy(x_hbm, x_ref, x_sem)
+    load.start()
+    rows = [0, 2]
+    loads = [
+        pltpu.make_async_copy(w_hbm.at[pl.ds(3 * a, 3)], w_ref.at[pl.ds(3 * a, 3)], w_sems.at[a])
+        for a in rows
+    ]
+    for copy in loads:
+        copy.start()
+    load.wait()
+    copies = []
+    if len(outs) == 3:
+        x = x_ref[...]
+        bands = room.shape[0]
+        for s in range(bands):
+            room[s] = jnp.concatenate(
+                [x[:, (d * bands + s) * cover : (d * bands + s + 1) * cover] for d in range(replicas)],
+                axis=1,
+            )
+            copies.append(pltpu.make_async_copy(room.at[s], outs[2].at[s], out_sems.at[s]))
+            copies[-1].start()
+    for k, a in enumerate(rows):
+        loads[k].wait()
+        x = x_ref[pixels - edge :] if a == 0 else x_ref[:edge]
+        halo[k] = tap_row(x, w_ref, a, columns, reach).astype(halo.dtype)
+        copies.append(pltpu.make_async_copy(halo.at[k], (down_hbm, up_hbm)[k], halo_sems.at[k]))
+        copies[-1].start()
+    for copy in copies:
+        copy.wait()
+
+
+def prepare(flat, weight, columns, reach, bands, replicas, cover, blocks):
     pixels, channels = flat.shape
-    width = weight.shape[2]
+    taps, _, width = weight.shape
     edge = reach * columns
-    vmem = pl.BlockSpec(memory_space=pltpu.VMEM)
-    return pl.pallas_call(
-        functools.partial(halo_kernel, columns, reach),
-        in_specs=[vmem, vmem, pl.BlockSpec(memory_space=pltpu.HBM)],
-        out_shape=[jax.ShapeDtypeStruct((edge, width), jnp.bfloat16)] * 2,
-        compiler_params=pltpu.CompilerParams(vmem_limit_bytes=VMEM_LIMIT),
+    hbm = pl.BlockSpec(memory_space=pltpu.HBM)
+    shape = (bands, pixels, replicas * cover)
+    out_shape = [jax.ShapeDtypeStruct((edge, width), jnp.bfloat16)] * 2
+    if blocks:
+        out_shape.append(jax.ShapeDtypeStruct(shape, flat.dtype))
+    return pl.pallas_call(
+        functools.partial(prepare_kernel, columns, reach, replicas, cover),
+        in_specs=[hbm, hbm],
+        out_specs=[hbm] * len(out_shape),
+        out_shape=out_shape,
+        scratch_shapes=[
+            pltpu.VMEM((pixels, channels), flat.dtype),
+            pltpu.VMEM((taps, channels, width), weight.dtype),
+            pltpu.VMEM(shape, flat.dtype),
+            pltpu.VMEM((2, edge, width), jnp.bfloat16),
+            pltpu.SemaphoreType.DMA,
+            pltpu.SemaphoreType.DMA((3,)),
+            pltpu.SemaphoreType.DMA((bands,)),
+            pltpu.SemaphoreType.DMA((2,)),
+        ],
+        compiler_params=pltpu.CompilerParams(vmem_limit_bytes=VMEM_WHOLE),
         cost_estimate=pl.CostEstimate(
             flops=12 * edge * channels * width,
-            bytes_accessed=12 * channels * width + 2 * pixels * channels,
+            bytes_accessed=12 * channels * width + 6 * pixels * channels,
             transcendentals=0,
         ),
-        name="halo",
-    )(flat, weight, after)
+        name="prepare",
+    )(flat, weight)
 
 
 def middle_kernel(columns, reach, x_ref, w_ref, after_ref, out_ref):
@@ -90,37 +136,6 @@
         ),
         name="middle_taps",
     )(flat, weight, after)
-
-
-def arrange_kernel(replicas, cover, x_ref, out_ref, room, sems):
-    bands = out_ref.shape[0]
-    x = x_ref[...]
-    copies = [pltpu.make_async_copy(room.at[s], out_ref.at[s], sems.at[s]) for s in range(bands)]
-    for s in range(bands):
-        room[s] = jnp.concatenate(
-            [x[:, (d * bands + s) * cover : (d * bands + s + 1) * cover] for d in range(replicas)],
-            axis=1,
-        )
-        copies[s].start()
-    for copy in copies:
-        copy.wait()
-
-
-def arrange(flat, bands, replicas, cover):
-    pixels, channels = flat.shape
-    shape = (bands, pixels, replicas * cover)
-    return pl.pallas_call(
-        functools.partial(arrange_kernel, replicas, cover),
-        in_specs=[pl.BlockSpec(memory_space=pltpu.VMEM)],
-        out_specs=pl.BlockSpec(memory_space=pltpu.HBM),
-        out_shape=jax.ShapeDtypeStruct(shape, flat.dtype),
-        scratch_shapes=[pltpu.VMEM(shape, flat.dtype), pltpu.SemaphoreType.DMA((bands,))],
-        compiler_params=pltpu.CompilerParams(vmem_limit_bytes=VMEM_LIMIT),
-        cost_estimate=pl.CostEstimate(
-            flops=0, bytes_accessed=4 * pixels * channels, transcendentals=0
-        ),
-        name="arrange",
-    )(flat)
 
 
 def pointwise_kernel(
@@ -192,13 +207,12 @@
     )
 
 
-def kernel_grad_kernel(columns, reach, g_ref, x_ref, out_ref, room, sems):
+def kernel_grad_kernel(columns, reach, g_ref, x_ref, out_ref):
     bands, pixels, width = g_ref.shape
     total = bands * pixels
     edge = reach * columns
     shifted = shifted_taps(g_ref[...].reshape(total, width), columns, reach)
     features = x_ref[...].reshape(total, x_ref.shape[2])
-    copies = []
     for a in range(3):
         if a == 0:
             left, right = features[: total - edge], shifted[edge:]
@@ -209,27 +223,15 @@
         block = lax.dot_general(
             left, right, (((0,), (0,)), ((), ())), preferred_element_type=jnp.float32
         )
-        room[a] = block.astype(room.dtype)
-        lanes = pl.ds(3 * a * width, 3 * width)
-        copies.append(pltpu.make_async_copy(room.at[a], out_ref.at[:, lanes], sems.at[a]))
-        copies[-1].start()
-    for copy in copies:
-        copy.wait()
+        out_ref[:, 3 * a * width : 3 * (a + 1) * width] = block.astype(out_ref.dtype)
 
 
 def kernel_grad(gathered, features, columns, reach):
     bands, pixels, width = gathered.shape
     extra = features.shape[2]
-    vmem = pl.BlockSpec(memory_space=pltpu.VMEM)
     return pl.pallas_call(
         functools.partial(kernel_grad_kernel, columns, reach),
-        in_specs=[vmem, vmem],
-        out_specs=pl.BlockSpec(memory_space=pltpu.HBM),
         out_shape=jax.ShapeDtypeStruct((extra, 9 * width), jnp.bfloat16),
-        scratch_shapes=[
-            pltpu.VMEM((3, extra, 3 * width), jnp.bfloat16),
-            pltpu.SemaphoreType.DMA((3,)),
-        ],
         compiler_params=pltpu.CompilerParams(vmem_limit_bytes=VMEM_LIMIT),
         cost_estimate=pl.CostEstimate(
             flops=18 * bands * pixels * extra * width,
@@ -316,15 +318,14 @@
     flat = image.reshape(pixels, channels)
     weight = conv_weight.transpose(1, 0, 2)
     block_rows, cover, picks, offsets = channel_plan(channels, taps, replicas, bands)
-    if block_rows % taps == 0:
-        split = arrange(flat, bands, replicas, cover)
-    else:
+    even = block_rows % taps == 0
+    down, up, *split = prepare(flat, weight, columns, reach, bands, replicas, cover, even)
+    if not even:
         order = jnp.array([c for line in picks for c in line], jnp.int32)
-        split = jnp.take(flat, order, axis=1)
-        split = split.reshape(pixels, bands, replicas * cover).transpose(1, 0, 2)
-    whole = lax.all_to_all(split, "space", 0, 0)
-
-    down, up = halo(flat, weight, split, columns, reach)
+        blocks = jnp.take(flat, order, axis=1).reshape(pixels, bands, replicas * cover)
+        split = [blocks.transpose(1, 0, 2)]
+    whole = lax.all_to_all(split[0], "space", 0, 0)
+
     above = lax.ppermute(down, "space", [(i, i + 1) for i in range(bands - 1)])
     below = lax.ppermute(up, "space", [(i + 1, i) for i in range(bands - 1)])
     middle = middle_taps(flat, weight, up, columns, reach)
@@ -344,7 +345,7 @@
     partial_grad = kernel_grad(gathered, whole, columns, reach)
     came = lax.all_to_all(partial_grad.reshape(replicas, cover, taps * width), "dp", 0, 0)
     weight_grad = final(came, width)
-    if block_rows % taps:
+    if not even:
         start = jnp.array(offsets)[lax.axis_index("space"), lax.axis_index("dp")]
         weight_grad = lax.dynamic_slice_in_dim(weight_grad, start, block_rows)
 

time: 51.4 us -> 49.4 us (0.961)
  local copies, waits for them, and re-layouts: 4.7 us -> 3.52 us
  blocking collectives: 10.2 us -> 9.33 us
    ppermute x1, waiting for transfers between devices: 4.15 us -> 1.89 us  [on_device(): below = lax.ppermute(up, 'space', [(i + 1, i) for i in range(bands - 1)])]
    all_to_all x1, waiting for transfers between devices: 0.01 us -> 1.91 us  [on_device(): whole = lax.all_to_all(split[0], 'space', 0, 0)]
    unnamed x20 -> x18, local copies, waits for them, and re-layouts: 4.47 us -> 3.3 us
    all_to_all x1, blocking collectives: 10.2 us -> 9.33 us  [on_device(): gathered = lax.all_to_all(gradient, 'space', 0, 0)]
    pallas_call x3 -> x2, Pallas kernels: 3.52 us -> 3.94 us  [the longest x1 3.15 us: prepare(): pl.pallas_call(functools.partial(prepare_kernel, columns, reach, replicas...]
  transfers between devices with their start and end apart: 4 -> 4, of which waited for: 2 -> 3; matrix products, arithmetic and copies ran while one was open for 1% -> 1% of each run, Pallas kernels for 8% -> 6%
where the time goes in v5:
time: 49.4 us; the launch traced here: 49 us
  starting transfers between devices  15.3 us (31%)
  waiting for transfers between devices  11.6 us (23%)
  blocking collectives  9.33 us (19%)
  Pallas kernels  8.38 us (17%)
  local copies, waits for them, and re-layouts  3.52 us (7%)
  between operations  0.81 us (2%)
    all_to_all x1, blocking collectives, on_device(): gathered = lax.all_to_all(gradient, 'space', 0, 0)  9.33 us
    all_to_all x1, waiting for transfers between devices, on_device(): lax.all_to_all(partial_grad.reshape(replicas, cover, taps * width), 'dp',...  7.82 us
    all_to_all x1, starting transfers between devices, on_device(): whole = lax.all_to_all(split[0], 'space', 0, 0)  6.33 us
    ppermute x1, starting transfers between devices, on_device(): above = lax.ppermute(down, 'space', [(i, i + 1) for i in range(bands - 1)])  3.92 us
    all_to_all x1, starting transfers between devices, on_device(): lax.all_to_all(partial_grad.reshape(replicas, cover, taps * width), 'dp',...  3.72 us
    unnamed x18, local copies, waits for them, and re-layouts  3.3 us
    pallas_call x1, Pallas kernels, prepare(): pl.pallas_call(functools.partial(prepare_kernel, columns, reach, replicas...  3.15 us
    pallas_call x1, Pallas kernels, feature_grad(): pl.pallas_call(functools.partial(feature_grad_kernel, columns, reach), gr...  2.62 us
  transfers between devices with their start and end apart: 4, of which 3 were waited for; matrix products, arithmetic and copies ran while one was open for 1% of the time, Pallas kernels for 6%

profile of v5, /device:TPU:0, one launch (start us, length us, event | category | flops | bytes accessed | tf_op | source)
XLA Modules:
  0.0 49.0 jit_solution(8161853599163490198)
XLA Ops:
  0.6 0.0 copy-start.2
  0.6 0.0 copy-start.7
  0.6 0.0 copy-start.8
  0.7 3.2 %prepare.1 = (bf16[192,128]{1,0:T(8,128)(2,1)}, bf16[192,128]{1,0:T(8,128)(2,1)}, bf16[4,192,256]{2,1,0:T(8,128)(2,1)}) custom-call(bf16[192,1024]{1,0:T(8,128)(2,1)} %bitcast.9, bf16[9,1024,128]{2,1,0:T(8,128)(2,1)} %bitcast.6), custom_call_target="tpu_custom_call" | custom-call | flops 301989888 | bytes 2752512 | tf_op jit(solution)/shard_map/prepare/pallas_call | solution.py:89
  3.8 0.0 copy-start.5
  3.8 0.0 copy-start.6
  3.8 6.3 %all-to-all-start = ((bf16[4,192,256]{2,1,0:T(8,128)(2,1)}), bf16[4,192,256]{2,1,0:T(8,128)(2,1)S(1)}, u32[]{:S(2)}, u32[]{:S(2)}) async-start(bf16[4,192,256]{2,1,0:T(8,128)(2,1)} %get-tuple-element.7), calls=%async_computation | async-start | bytes 786432 | tf_op jit(solution)/shard_map/all_to_all | solution.py:327
  10.2 3.9 %collective-permute-start = (bf16[192,128]{1,0:T(8,128)(2,1)}, bf16[192,128]{1,0:T(8,128)(2,1)S(1)}, u32[]{:S(2)}, u32[]{:S(2)}) collective-permute-start(bf16[192,128]{1,0:T(8,128)(2,1)} %get-tuple-element.6), channel_id=1, source_target_pairs={{0,1},{1,2},{2,3},{4,5},{5,6},{6,7},{8,9},{9,10},{10,11},{12,13},{... | collective-permute-start | bytes 147464 | tf_op jit(solution)/shard_map/ppermute | solution.py:329
  14.1 1.3 %collective-permute-start.1 = (bf16[192,128]{1,0:T(8,128)(2,1)}, bf16[192,128]{1,0:T(8,128)(2,1)S(1)}, u32[]{:S(2)}, u32[]{:S(2)}) collective-permute-start(bf16[192,128]{1,0:T(8,128)(2,1)} %get-tuple-element.5.after_ref), channel_id=1, source_target_pairs={{1,0},{2,1},{3,2},{5,4},{6,5},{7,6},{9,8},{10,9},{11,10},{13,12},{... | collective-permute-start | bytes 147464 | tf_op jit(solution)/shard_map/ppermute | solution.py:330
  15.4 0.0 copy-done.7
  15.4 0.0 copy-done.8
  15.5 0.1 reshape.25.scale_ref
  15.6 0.1 reshape.24.label_ref
  15.7 0.0 copy-done.2
  15.7 0.0 copy-start
  15.7 1.7 %copy-done = bf16[1024,9,128]{2,0,1:T(8,128)(2,1)S(1)} copy-done((bf16[1024,9,128]{2,0,1:T(8,128)(2,1)S(1)}, bf16[1024,9,128]{2,0,1:T(8,128)(2,1)}, u32[]{:S(2)}) %copy-start) | copy-done | bytes 2359320
  17.4 0.0 copy-start.4
  17.4 0.8 %copy-done.4 = bf16[192,128]{1,0:T(8,128)(2,1)S(1)} copy-done((bf16[192,128]{1,0:T(8,128)(2,1)S(1)}, bf16[192,128]{1,0:T(8,128)(2,1)}, u32[]{:S(2)}) %copy-start.4) | copy-done | bytes 49176
  18.2 0.4 middle_taps.1.middle_ref
  18.6 0.0 copy-start.1
  18.6 0.0 collective-permute-done.above_ref
  18.6 1.9 %collective-permute-done.1.below_ref = bf16[192,128]{1,0:T(8,128)(2,1)S(1)} collective-permute-done((bf16[192,128]{1,0:T(8,128)(2,1)}, bf16[192,128]{1,0:T(8,128)(2,1)S(1)}, u32[]{:S(2)}, u32[]{:S(2)}) %collective-permute-start.1) | collective-permute-done | bytes 49184 | tf_op jit(solution)/shard_map/ppermute | solution.py:330
  20.5 1.9 %all-to-all-done.after_ref.x_ref = bf16[4,192,256]{2,1,0:T(8,128)(2,1)S(1)} async-done(((bf16[4,192,256]{2,1,0:T(8,128)(2,1)}), bf16[4,192,256]{2,1,0:T(8,128)(2,1)S(1)}, u32[]{:S(2)}, u32[]{:S(2)}) %all-to-all-start) | async-done | bytes 393248 | tf_op jit(solution)/shard_map/all_to_all | solution.py:327
  22.4 0.0 copy-done.5
  22.4 0.0 copy-done.6
  22.4 0.7 %pointwise.1 = bf16[4,192,128]{2,1,0:T(8,128)(2,1)S(1)} custom-call(f32[192,128]{1,0:T(8,128)S(1)} %middle_taps.1.middle_ref, bf16[192,128]{1,0:T(8,128)(2,1)S(1)} %collective-permute-done.above_ref, bf16[192,128]{1,0:T(8,128)(2,1)S(1)} %collective-permute-done.1.below_ref, f32[1,128]{1,0:T(1,128)S(1)} %bitcast.13, bf16[3,128]{1,0:T(4,128)(2,1)S(1)} %bitcast.12, ...), custom_call_target="tpu_custom_call" | custom-call | flops 737280 | bytes 393216 | tf_op jit(solution)/shard_map/pointwise/pallas_call | solution.py:183
  23.1 9.3 %all_to_all.15.g_ref = bf16[4,192,128]{2,1,0:T(8,128)(2,1)S(1)} all-to-all(bf16[4,192,128]{2,1,0:T(8,128)(2,1)S(1)} %pointwise.1), channel_id=1, replica_groups=mesh['dp'=8,'space'=4] {'space'}, dimensions={0} | all-to-all | bytes 393216 | tf_op jit(solution)/shard_map/all_to_all | solution.py:344
  32.4 0.8 %kernel_grad.1 = bf16[256,1152]{1,0:T(8,128)(2,1)S(1)} custom-call(bf16[4,192,128]{2,1,0:T(8,128)(2,1)S(1)} %all_to_all.15.g_ref, bf16[4,192,256]{2,1,0:T(8,128)(2,1)S(1)} %all-to-all-done.after_ref.x_ref), custom_call_target="tpu_custom_call" | custom-call | flops 452984832 | bytes 1179648 | tf_op jit(solution)/shard_map/kernel_grad/pallas_call | solution.py:232
  33.2 0.0 copy-start.3
  33.2 0.8 %copy-done.3 = bf16[256,1152]{1,0:T(8,128)(2,1)} copy-done((bf16[256,1152]{1,0:T(8,128)(2,1)}, bf16[256,1152]{1,0:T(8,128)(2,1)S(1)}, u32[]{:S(2)}) %copy-start.3) | copy-done | bytes 589848
  34.0 3.7 %all-to-all-start.2 = ((bf16[8,32,1152]{2,1,0:T(8,128)(2,1)}), bf16[8,32,1152]{2,1,0:T(8,128)(2,1)S(1)}, u32[]{:S(2)}, u32[]{:S(2)}) async-start(bf16[8,32,1152]{2,1,0:T(8,128)(2,1)} %bitcast.11), calls=%async_computation.2 | async-start | bytes 1179648 | tf_op jit(solution)/shard_map/all_to_all | solution.py:346
  37.8 0.0 copy-done.1
  37.8 2.6 %feature_grad.1 = f32[192,1024]{1,0:T(8,128)} custom-call(bf16[4,192,128]{2,1,0:T(8,128)(2,1)S(1)} %all_to_all.15.g_ref, bf16[9,1024,128]{2,1,0:T(8,128)(2,1)S(1)} %bitcast.8), custom_call_target="tpu_custom_call" | custom-call | flops 452984832 | bytes 3145728 | tf_op jit(solution)/shard_map/feature_grad/pallas_call | solution.py:268
  40.4 7.8 %all-to-all-done.2.in_ref = bf16[8,32,1152]{2,1,0:T(8,128)(2,1)S(1)} async-done(((bf16[8,32,1152]{2,1,0:T(8,128)(2,1)}), bf16[8,32,1152]{2,1,0:T(8,128)(2,1)S(1)}, u32[]{:S(2)}, u32[]{:S(2)}) %all-to-all-start.2) | async-done | bytes 589856 | tf_op jit(solution)/shard_map/all_to_all | solution.py:346
  48.2 0.7 %final_sum.1 = f32[288,128]{1,0:T(8,128)} custom-call(bf16[8,32,1152]{2,1,0:T(8,128)(2,1)S(1)} %all-to-all-done.2.in_ref), custom_call_target="tpu_custom_call" | custom-call | tf_op jit(solution)/shard_map/final_sum/pallas_call | solution.py:301
  (2 shorter events, 0.0 us)
Async XLA Ops:
  0.6 15.1 %copy-start.2 = (bf16[1,6,32,1024]{3,2,1,0:T(8,128)(2,1)S(1)}, bf16[1,6,32,1024]{3,2,1,0:T(8,128)(2,1)}, u32[]{:S(2)}) copy-start(bf16[1,6,32,1024]{3,2,1,0:T(8,128)(2,1)} %param.6) | copy-start | bytes 1179652
  0.6 14.8 %copy-start.7 = (s32[1,6,32]{2,0,1:T(1,128)S(1)}, s32[1,6,32]{2,0,1:T(1,128)}, u32[]{:S(2)}) copy-start(s32[1,6,32]{2,0,1:T(1,128)} %param.7) | copy-start | bytes 2308
  0.6 14.8 %copy-start.8 = (s32[1,6,32]{2,0,1:T(1,128)S(1)}, s32[1,6,32]{2,0,1:T(1,128)}, u32[]{:S(2)}) copy-start(s32[1,6,32]{2,0,1:T(1,128)} %param.8) | copy-start | bytes 2308
  3.8 18.6 %copy-start.5 = (bf16[128,3]{0,1:T(4,128)(2,1)S(1)}, bf16[128,3]{0,1:T(4,128)(2,1)}, u32[]{:S(2)}) copy-start(bf16[128,3]{0,1:T(4,128)(2,1)} %param.11) | copy-start | bytes 2308
  3.8 18.6 %copy-start.6 = (f32[128]{0:T(128)S(1)}, f32[128]{0:T(128)}, u32[]{:S(2)}) copy-start(f32[128]{0:T(128)} %param.10) | copy-start | bytes 1540
  3.8 18.5 %all-to-all-start = ((bf16[4,192,256]{2,1,0:T(8,128)(2,1)}), bf16[4,192,256]{2,1,0:T(8,128)(2,1)S(1)}, u32[]{:S(2)}, u32[]{:S(2)}) async-start(bf16[4,192,256]{2,1,0:T(8,128)(2,1)} %get-tuple-element.7), calls=%async_computation | async-start | bytes 786432 | tf_op jit(solution)/shard_map/all_to_all | solution.py:327
  10.2 8.4 %collective-permute-start = (bf16[192,128]{1,0:T(8,128)(2,1)}, bf16[192,128]{1,0:T(8,128)(2,1)S(1)}, u32[]{:S(2)}, u32[]{:S(2)}) collective-permute-start(bf16[192,128]{1,0:T(8,128)(2,1)} %get-tuple-element.6), channel_id=1, source_target_pairs={{0,1},{1,2},{2,3},{4,5},{5,6},{6,7},{8,9},{9,10},{10,11},{12,13},{... | collective-permute-start | bytes 147464 | tf_op jit(solution)/shard_map/ppermute | solution.py:329
  14.1 6.4 %collective-permute-start.1 = (bf16[192,128]{1,0:T(8,128)(2,1)}, bf16[192,128]{1,0:T(8,128)(2,1)S(1)}, u32[]{:S(2)}, u32[]{:S(2)}) collective-permute-start(bf16[192,128]{1,0:T(8,128)(2,1)} %get-tuple-element.5.after_ref), channel_id=1, source_target_pairs={{1,0},{2,1},{3,2},{5,4},{6,5},{7,6},{9,8},{10,9},{11,10},{13,12},{... | collective-permute-start | bytes 147464 | tf_op jit(solution)/shard_map/ppermute | solution.py:330
  15.7 1.7 %copy-start = (bf16[1024,9,128]{2,0,1:T(8,128)(2,1)S(1)}, bf16[1024,9,128]{2,0,1:T(8,128)(2,1)}, u32[]{:S(2)}) copy-start(bf16[1024,9,128]{2,0,1:T(8,128)(2,1)} %param.9) | copy-start | bytes 7077892
  17.4 0.8 %copy-start.4 = (bf16[192,128]{1,0:T(8,128)(2,1)S(1)}, bf16[192,128]{1,0:T(8,128)(2,1)}, u32[]{:S(2)}) copy-start(bf16[192,128]{1,0:T(8,128)(2,1)} %get-tuple-element.5.after_ref) | copy-start | bytes 147460
  18.6 19.2 %copy-start.1 = (bf16[1024,9,128]{2,0,1:T(8,128)(2,1)S(1)}, bf16[1024,9,128]{2,0,1:T(8,128)(2,1)}, u32[]{:S(2)}) copy-start(bf16[1024,9,128]{2,0,1:T(8,128)(2,1)} %param.9) | copy-start | bytes 7077892
  33.2 0.8 %copy-start.3 = (bf16[256,1152]{1,0:T(8,128)(2,1)}, bf16[256,1152]{1,0:T(8,128)(2,1)S(1)}, u32[]{:S(2)}) copy-start(bf16[256,1152]{1,0:T(8,128)(2,1)S(1)} %kernel_grad.1) | copy-start | bytes 1769476
  34.0 14.2 %all-to-all-start.2 = ((bf16[8,32,1152]{2,1,0:T(8,128)(2,1)}), bf16[8,32,1152]{2,1,0:T(8,128)(2,1)S(1)}, u32[]{:S(2)}, u32[]{:S(2)}) async-start(bf16[8,32,1152]{2,1,0:T(8,128)(2,1)} %bitcast.11), calls=%async_computation.2 | async-start | bytes 1179648 | tf_op jit(solution)/shard_map/all_to_all | solution.py:346

commit v6 on v5

--- a/solution.py
+++ b/solution.py
@@ -111,6 +111,22 @@
     )(flat, weight)
 
 
+def pass_on_kernel(x_ref, after_ref, out_ref):
+    del x_ref, after_ref, out_ref
+
+
+def pass_on(x, after):
+    hbm = pl.BlockSpec(memory_space=pltpu.HBM)
+    return pl.pallas_call(
+        pass_on_kernel,
+        in_specs=[hbm, pl.BlockSpec(memory_space=pl.ANY)],
+        out_specs=hbm,
+        out_shape=jax.ShapeDtypeStruct(x.shape, x.dtype),
+        input_output_aliases={0: 0},
+        name="pass_on",
+    )(x, after)
+
+
 def middle_kernel(columns, reach, x_ref, w_ref, after_ref, out_ref):
     del after_ref
     pixels, edge = x_ref.shape[0], reach * columns
@@ -139,11 +155,8 @@
 
 
 def pointwise_kernel(
-    middle_ref, above_ref, below_ref, bias_ref, class_ref, label_ref, scale_ref, after_ref,
-    out_ref, room, sems
+    middle_ref, above_ref, below_ref, bias_ref, class_ref, label_ref, scale_ref, out_ref
 ):
-    del after_ref
-    bands = out_ref.shape[0]
     pixels, width = middle_ref.shape
     edge = above_ref.shape[0]
     above = above_ref[...].astype(jnp.float32)
@@ -169,34 +182,22 @@
         grad_logits[:, k : k + 1] * wide[k : k + 1] for k in range(classes.shape[0])
     )
     gradient = hidden_grad * sigmoid_z * (1.0 + preact * (1.0 - sigmoid_z))
-    room[...] = gradient.astype(out_ref.dtype)
-    copies = [pltpu.make_async_copy(room, out_ref.at[s], sems.at[s]) for s in range(bands)]
-    for copy in copies:
-        copy.start()
-    for copy in copies:
-        copy.wait()
-
-
-def pointwise(middle, above, below, bias, classes, labels, scale, after, bands):
+    out_ref[...] = gradient.astype(out_ref.dtype)
+
+
+def pointwise(middle, above, below, bias, classes, labels, scale):
     pixels, width = middle.shape
-    vmem = pl.BlockSpec(memory_space=pltpu.VMEM)
     return pl.pallas_call(
         pointwise_kernel,
-        in_specs=[vmem] * 7 + [pl.BlockSpec(memory_space=pl.ANY)],
-        out_specs=pl.BlockSpec(memory_space=pltpu.HBM),
-        out_shape=jax.ShapeDtypeStruct((bands, pixels, width), jnp.bfloat16),
-        scratch_shapes=[
-            pltpu.VMEM((pixels, width), jnp.bfloat16),
-            pltpu.SemaphoreType.DMA((bands,)),
-        ],
+        out_shape=jax.ShapeDtypeStruct((pixels, width), jnp.bfloat16),
         compiler_params=pltpu.CompilerParams(vmem_limit_bytes=VMEM_LIMIT),
         cost_estimate=pl.CostEstimate(
             flops=30 * pixels * width,
-            bytes_accessed=2 * bands * pixels * width + 8 * pixels * width,
+            bytes_accessed=10 * pixels * width,
             transcendentals=pixels * width,
         ),
         name="pointwise",
-    )(middle, above, below, bias, classes, labels, scale, after)
+    )(middle, above, below, bias, classes, labels, scale)
 
 
 def shifted_taps(gradient, columns, reach):
@@ -207,31 +208,37 @@
     )
 
 
-def kernel_grad_kernel(columns, reach, g_ref, x_ref, out_ref):
-    bands, pixels, width = g_ref.shape
+def kernel_grad_kernel(columns, reach, x_ref, *refs):
+    *g_refs, out_ref, taps = refs
+    bands, pixels, _ = x_ref.shape
+    width = g_refs[0].shape[1]
     total = bands * pixels
     edge = reach * columns
-    shifted = shifted_taps(g_ref[...].reshape(total, width), columns, reach)
+    band = lax.axis_index("space")
+    for k, g_ref in enumerate(g_refs):
+        first = lax.rem(band + bands - k, bands) * pixels
+        taps[pl.ds(pl.multiple_of(first, 16), pixels)] = shifted_taps(g_ref[...], columns, reach)
     features = x_ref[...].reshape(total, x_ref.shape[2])
     for a in range(3):
         if a == 0:
-            left, right = features[: total - edge], shifted[edge:]
+            left, right = features[: total - edge], taps[edge:]
         elif a == 1:
-            left, right = features, shifted
+            left, right = features, taps[...]
         else:
-            left, right = features[edge:], shifted[: total - edge]
+            left, right = features[edge:], taps[: total - edge]
         block = lax.dot_general(
             left, right, (((0,), (0,)), ((), ())), preferred_element_type=jnp.float32
         )
         out_ref[:, 3 * a * width : 3 * (a + 1) * width] = block.astype(out_ref.dtype)
 
 
-def kernel_grad(gathered, features, columns, reach):
-    bands, pixels, width = gathered.shape
-    extra = features.shape[2]
+def kernel_grad(features, gradients, columns, reach):
+    bands, pixels, extra = features.shape
+    width = gradients[0].shape[1]
     return pl.pallas_call(
         functools.partial(kernel_grad_kernel, columns, reach),
         out_shape=jax.ShapeDtypeStruct((extra, 9 * width), jnp.bfloat16),
+        scratch_shapes=[pltpu.VMEM((bands * pixels, 3 * width), jnp.bfloat16)],
         compiler_params=pltpu.CompilerParams(vmem_limit_bytes=VMEM_LIMIT),
         cost_estimate=pl.CostEstimate(
             flops=18 * bands * pixels * extra * width,
@@ -239,16 +246,16 @@
             transcendentals=0,
         ),
         name="kernel_grad",
-    )(gathered, features)
-
-
-def feature_grad_kernel(columns, reach, g_ref, w_ref, out_ref):
+    )(features, *gradients)
+
+
+def feature_grad_kernel(columns, reach, bands, own_ref, above_ref, below_ref, w_ref, out_ref):
     band = lax.axis_index("space")
-    bands, pixels, width = g_ref.shape
+    pixels, width = own_ref.shape
     edge = reach * columns
-    own = g_ref[band]
-    above = g_ref[jnp.maximum(band - 1, 0)][pixels - edge :]
-    below = g_ref[jnp.minimum(band + 1, bands - 1)][:edge]
+    own = own_ref[...]
+    above = above_ref[pixels - edge :]
+    below = below_ref[:edge]
     above = jnp.where(band > 0, above, jnp.zeros_like(above))
     below = jnp.where(band + 1 < bands, below, jnp.zeros_like(below))
     stack = shifted_taps(jnp.concatenate([above, own, below], axis=0), columns, reach)
@@ -261,17 +268,15 @@
     )
 
 
-def feature_grad(gathered, weight, columns, reach):
-    bands, pixels, _ = gathered.shape
+def feature_grad(own, above, below, weight, columns, reach, bands):
+    pixels, _ = own.shape
     taps, channels, width = weight.shape
     step = 256 if channels % 256 == 0 else channels
-    return pl.pallas_call(
-        functools.partial(feature_grad_kernel, columns, reach),
+    whole = pl.BlockSpec((pixels, width), lambda i: (0, 0))
+    return pl.pallas_call(
+        functools.partial(feature_grad_kernel, columns, reach, bands),
         grid=(channels // step,),
-        in_specs=[
-            pl.BlockSpec((bands, pixels, width), lambda i: (0, 0, 0)),
-            pl.BlockSpec((taps, step, width), lambda i: (0, i, 0)),
-        ],
+        in_specs=[whole, whole, whole, pl.BlockSpec((taps, step, width), lambda i: (0, i, 0))],
         out_specs=pl.BlockSpec((pixels, step), lambda i: (0, i)),
         out_shape=jax.ShapeDtypeStruct((pixels, channels), jnp.float32),
         compiler_params=pltpu.CompilerParams(vmem_limit_bytes=VMEM_LIMIT),
@@ -281,7 +286,7 @@
             transcendentals=0,
         ),
         name="feature_grad",
-    )(gathered, weight)
+    )(own, above, below, weight)
 
 
 def final_kernel(in_ref, out_ref):
@@ -324,11 +329,10 @@
         order = jnp.array([c for line in picks for c in line], jnp.int32)
         blocks = jnp.take(flat, order, axis=1).reshape(pixels, bands, replicas * cover)
         split = [blocks.transpose(1, 0, 2)]
-    whole = lax.all_to_all(split[0], "space", 0, 0)
-
     above = lax.ppermute(down, "space", [(i, i + 1) for i in range(bands - 1)])
     below = lax.ppermute(up, "space", [(i + 1, i) for i in range(bands - 1)])
     middle = middle_taps(flat, weight, up, columns, reach)
+    whole = lax.all_to_all(pass_on(split[0], above), "space", 0, 0)
 
     gradient = pointwise(
         middle,
@@ -338,18 +342,19 @@
         class_weight.T,
         labels.reshape(pixels, 1),
         pixel_weight.reshape(pixels, 1),
-        whole,
-        bands,
-    )
-    gathered = lax.all_to_all(gradient, "space", 0, 0)
-    partial_grad = kernel_grad(gathered, whole, columns, reach)
+    )
+    gradients = [gradient] + [
+        lax.ppermute(gradient, "space", [(i, (i + k) % bands) for i in range(bands)])
+        for k in range(1, bands)
+    ]
+    partial_grad = kernel_grad(whole, gradients, columns, reach)
     came = lax.all_to_all(partial_grad.reshape(replicas, cover, taps * width), "dp", 0, 0)
     weight_grad = final(came, width)
     if not even:
         start = jnp.array(offsets)[lax.axis_index("space"), lax.axis_index("dp")]
         weight_grad = lax.dynamic_slice_in_dim(weight_grad, start, block_rows)
 
-    grad = feature_grad(gathered, weight, columns, reach)
+    grad = feature_grad(gradient, gradients[1 % bands], gradients[-1], weight, columns, reach, bands)
     return grad.reshape(1, band_rows, columns, channels), weight_grad
 
 

time: 49.4 us -> 55.6 us (1.13)
  blocking collectives: 9.33 us -> 0 us
  waiting for transfers between devices: 11.6 us -> 19.7 us
  starting transfers between devices: 15.3 us -> 22.3 us
  Pallas kernels: 8.38 us -> 9.05 us
    all_to_all x1 -> x0, blocking collectives: 9.33 us -> none  [on_device(): gathered = lax.all_to_all(gradient, 'space', 0, 0)]
    ppermute x0 -> x3, starting transfers between devices: none -> 6.75 us  [on_device(): lax.ppermute(gradient, 'space', [(i, (i + k) % bands) for i in range(band...]
    ppermute x0 -> x3, waiting for transfers between devices: none -> 5.88 us  [on_device(): lax.ppermute(gradient, 'space', [(i, (i + k) % bands) for i in range(band...]
    ppermute x1, waiting for transfers between devices: 0.01 us -> 2.05 us  [on_device(): above = lax.ppermute(down, 'space', [(i, i + 1) for i in range(bands - 1)])]
    ppermute x1, waiting for transfers between devices: 1.89 us -> 3.9 us  [on_device(): below = lax.ppermute(up, 'space', [(i + 1, i) for i in range(bands - 1)])]
    all_to_all x1, waiting for transfers between devices: 1.91 us -> 0.01 us  [on_device(): whole = lax.all_to_all(pass_on(split[0], above), 'space', 0, 0)]
    ppermute x1, starting transfers between devices: 3.92 us -> 4.93 us  [on_device(): above = lax.ppermute(down, 'space', [(i, i + 1) for i in range(bands - 1)])]
    pallas_call x1, Pallas kernels: 0.79 us -> 1.76 us  [kernel_grad(): pl.pallas_call(functools.partial(kernel_grad_kernel, columns, reach), out...]
  transfers between devices with their start and end apart: 4 -> 7, of which waited for: 3 -> 5; matrix products, arithmetic and copies ran while one was open for 1% -> 0% of each run, Pallas kernels for 6% -> 6%
where the time goes in v6:
time: 55.6 us; the launch traced here: 55.2 us
  starting transfers between devices  22.3 us (40%)
  waiting for transfers between devices  19.7 us (35%)
  Pallas kernels  9.05 us (16%)
  local copies, waits for them, and re-layouts  3.34 us (6%)
  between operations  0.78 us (1%)
    all_to_all x1, waiting for transfers between devices, on_device(): lax.all_to_all(partial_grad.reshape(replicas, cover, taps * width), 'dp',...  7.82 us
    ppermute x3, starting transfers between devices, on_device(): lax.ppermute(gradient, 'space', [(i, (i + k) % bands) for i in range(band...  6.75 us
    ppermute x3, waiting for transfers between devices, on_device(): lax.ppermute(gradient, 'space', [(i, (i + k) % bands) for i in range(band...  5.88 us
    all_to_all x1, starting transfers between devices, on_device(): whole = lax.all_to_all(pass_on(split[0], above), 'space', 0, 0)  5.66 us
    ppermute x1, starting transfers between devices, on_device(): above = lax.ppermute(down, 'space', [(i, i + 1) for i in range(bands - 1)])  4.93 us
    ppermute x1, waiting for transfers between devices, on_device(): below = lax.ppermute(up, 'space', [(i + 1, i) for i in range(bands - 1)])  3.9 us
    all_to_all x1, starting transfers between devices, on_device(): lax.all_to_all(partial_grad.reshape(replicas, cover, taps * width), 'dp',...  3.72 us
    pallas_call x1, Pallas kernels, prepare(): pl.pallas_call(functools.partial(prepare_kernel, columns, reach, replicas...  3.15 us
  transfers between devices with their start and end apart: 7, of which 5 were waited for; matrix products, arithmetic and copies ran while one was open for 0% of the time, Pallas kernels for 6%

profile of v6, /device:TPU:0, one launch (start us, length us, event | category | flops | bytes accessed | tf_op | source)
XLA Modules:
  0.0 55.2 jit_solution(800864849828639480)
XLA Ops:
  0.6 0.0 copy-start.2
  0.6 0.0 copy-start.8
  0.6 0.0 copy-start.9
  0.7 3.1 %prepare.1 = (bf16[192,128]{1,0:T(8,128)(2,1)}, bf16[192,128]{1,0:T(8,128)(2,1)}, bf16[4,192,256]{2,1,0:T(8,128)(2,1)}) custom-call(bf16[192,1024]{1,0:T(8,128)(2,1)} %bitcast.9, bf16[9,1024,128]{2,1,0:T(8,128)(2,1)} %bitcast.6), custom_call_target="tpu_custom_call" | custom-call | flops 301989888 | bytes 2752512 | tf_op jit(solution)/shard_map/prepare/pallas_call | solution.py:89
  3.8 4.9 %collective-permute-start = (bf16[192,128]{1,0:T(8,128)(2,1)}, bf16[192,128]{1,0:T(8,128)(2,1)S(1)}, u32[]{:S(2)}, u32[]{:S(2)}) collective-permute-start(bf16[192,128]{1,0:T(8,128)(2,1)} %get-tuple-element.6), channel_id=1, source_target_pairs={{0,1},{1,2},{2,3},{4,5},{5,6},{6,7},{8,9},{9,10},{10,11},{12,13},{... | collective-permute-start | bytes 147464 | tf_op jit(solution)/shard_map/ppermute | solution.py:332
  8.8 2.0 %collective-permute-done.above_ref.after_ref = bf16[192,128]{1,0:T(8,128)(2,1)S(1)} collective-permute-done((bf16[192,128]{1,0:T(8,128)(2,1)}, bf16[192,128]{1,0:T(8,128)(2,1)S(1)}, u32[]{:S(2)}, u32[]{:S(2)}) %collective-permute-start) | collective-permute-done | bytes 49184 | tf_op jit(solution)/shard_map/ppermute | solution.py:332
  10.8 0.0 copy-start.3
  10.8 0.6 %copy-done.3 = bf16[192,128]{1,0:T(8,128)(2,1)} copy-done((bf16[192,128]{1,0:T(8,128)(2,1)}, bf16[192,128]{1,0:T(8,128)(2,1)S(1)}, u32[]{:S(2)}) %copy-start.3) | copy-done | bytes 49176
  11.4 0.0 copy-start.6
  11.4 0.0 copy-start.7
  11.4 0.0 copy-start.4
  11.4 5.7 %all-to-all-start = ((bf16[4,192,256]{2,1,0:T(8,128)(2,1)}), bf16[4,192,256]{2,1,0:T(8,128)(2,1)S(1)}, u32[]{:S(2)}, u32[]{:S(2)}) async-start(bf16[4,192,256]{2,1,0:T(8,128)(2,1)} %pass_on.1), calls=%async_computation | async-start | bytes 786432 | tf_op jit(solution)/shard_map/all_to_all | solution.py:335
  17.1 1.3 %collective-permute-start.1 = (bf16[192,128]{1,0:T(8,128)(2,1)}, bf16[192,128]{1,0:T(8,128)(2,1)S(1)}, u32[]{:S(2)}, u32[]{:S(2)}) collective-permute-start(bf16[192,128]{1,0:T(8,128)(2,1)} %get-tuple-element.5.after_ref), channel_id=1, source_target_pairs={{1,0},{2,1},{3,2},{5,4},{6,5},{7,6},{9,8},{10,9},{11,10},{13,12},{... | collective-permute-start | bytes 147464 | tf_op jit(solution)/shard_map/ppermute | solution.py:333
  18.4 0.0 copy-done.8
  18.4 0.0 copy-done.9
  18.4 0.1 reshape.25.scale_ref
  18.6 0.1 reshape.24.label_ref
  18.7 0.0 copy-done.2
  18.7 0.0 copy-start
  18.7 1.7 %copy-done = bf16[1024,9,128]{2,0,1:T(8,128)(2,1)S(1)} copy-done((bf16[1024,9,128]{2,0,1:T(8,128)(2,1)S(1)}, bf16[1024,9,128]{2,0,1:T(8,128)(2,1)}, u32[]{:S(2)}) %copy-start) | copy-done | bytes 2359320
  20.4 0.0 copy-start.5
  20.4 0.8 %copy-done.5 = bf16[192,128]{1,0:T(8,128)(2,1)S(1)} copy-done((bf16[192,128]{1,0:T(8,128)(2,1)S(1)}, bf16[192,128]{1,0:T(8,128)(2,1)}, u32[]{:S(2)}) %copy-start.5) | copy-done | bytes 49176
  21.2 0.4 middle_taps.1.middle_ref
  21.5 0.0 copy-start.1
  21.5 3.9 %collective-permute-done.1.below_ref = bf16[192,128]{1,0:T(8,128)(2,1)S(1)} collective-permute-done((bf16[192,128]{1,0:T(8,128)(2,1)}, bf16[192,128]{1,0:T(8,128)(2,1)S(1)}, u32[]{:S(2)}, u32[]{:S(2)}) %collective-permute-start.1) | collective-permute-done | bytes 49184 | tf_op jit(solution)/shard_map/ppermute | solution.py:333
  25.4 0.0 copy-done.6
  25.4 0.0 copy-done.7
  25.5 0.0 copy-done.4
  25.5 0.4 pointwise.1.own_ref.refs_0_
  25.9 3.5 %collective-permute-start.4 = (bf16[192,128]{1,0:T(8,128)(2,1)S(1)}, bf16[192,128]{1,0:T(8,128)(2,1)S(1)}, u32[]{:S(2)}, u32[]{:S(2)}) collective-permute-start(bf16[192,128]{1,0:T(8,128)(2,1)S(1)} %pointwise.1.own_ref.refs_0_), channel_id=1, source_target_pairs={{0,2},{1,3},{2,0},{3,1},{4,6},{5,7},{6,4},{7,5},{8,10},{9,11},{10,... | collective-permute-start | bytes 147464 | tf_op jit(solution)/shard_map/ppermute | solution.py:347
  29.3 3.3 %collective-permute-start.3 = (bf16[192,128]{1,0:T(8,128)(2,1)S(1)}, bf16[192,128]{1,0:T(8,128)(2,1)S(1)}, u32[]{:S(2)}, u32[]{:S(2)}) collective-permute-start(bf16[192,128]{1,0:T(8,128)(2,1)S(1)} %pointwise.1.own_ref.refs_0_), channel_id=1, source_target_pairs={{0,3},{1,0},{2,1},{3,2},{4,7},{5,4},{6,5},{7,6},{8,11},{9,8},{10,9... | collective-permute-start | bytes 147464 | tf_op jit(solution)/shard_map/ppermute | solution.py:347
  32.6 0.0 collective-permute-start.2
  32.6 0.0 collective-permute-done.4.refs_2_
  32.6 1.7 %collective-permute-done.3.below_ref.refs_3_ = bf16[192,128]{1,0:T(8,128)(2,1)S(1)} collective-permute-done((bf16[192,128]{1,0:T(8,128)(2,1)S(1)}, bf16[192,128]{1,0:T(8,128)(2,1)S(1)}, u32[]{:S(2)}, u32[]{:S(2)}) %collective-permute-start.3) | collective-permute-done | bytes 49184 | tf_op jit(solution)/shard_map/ppermute | solution.py:347
  34.4 4.1 %collective-permute-done.2.above_ref.refs_1_ = bf16[192,128]{1,0:T(8,128)(2,1)S(1)} collective-permute-done((bf16[192,128]{1,0:T(8,128)(2,1)S(1)}, bf16[192,128]{1,0:T(8,128)(2,1)S(1)}, u32[]{:S(2)}, u32[]{:S(2)}) %collective-permute-start.2) | collective-permute-done | bytes 49184 | tf_op jit(solution)/shard_map/ppermute | solution.py:347
  38.5 0.0 all-to-all-done.x_ref
  38.5 1.8 %kernel_grad.1 = bf16[256,1152]{1,0:T(8,128)(2,1)} custom-call(bf16[4,192,256]{2,1,0:T(8,128)(2,1)S(1)} %all-to-all-done.x_ref, bf16[192,128]{1,0:T(8,128)(2,1)S(1)} %pointwise.1.own_ref.refs_0_, bf16[192,128]{1,0:T(8,128)(2,1)S(1)} %collective-permute-done.2.above_ref.refs_1_, bf16[192,128]{1,0:T(8,128)(2,1)S(1)} %collective-permute-done.4.refs_2_, ...), custom_call_target="tpu_custom_call" | custom-call | flops 452984832 | bytes 1179648 | tf_op jit(solution)/shard_map/kernel_grad/pallas_call | solution.py:238
  40.3 3.7 %all-to-all-start.1 = ((bf16[8,32,1152]{2,1,0:T(8,128)(2,1)}), bf16[8,32,1152]{2,1,0:T(8,128)(2,1)S(1)}, u32[]{:S(2)}, u32[]{:S(2)}) async-start(bf16[8,32,1152]{2,1,0:T(8,128)(2,1)} %bitcast.5), calls=%async_computation.1 | async-start | bytes 1179648 | tf_op jit(solution)/shard_map/all_to_all | solution.py:351
  44.0 0.0 copy-done.1
  44.0 2.6 %feature_grad.1 = f32[192,1024]{1,0:T(8,128)} custom-call(bf16[192,128]{1,0:T(8,128)(2,1)S(1)} %pointwise.1.own_ref.refs_0_, bf16[192,128]{1,0:T(8,128)(2,1)S(1)} %collective-permute-done.2.above_ref.refs_1_, bf16[192,128]{1,0:T(8,128)(2,1)S(1)} %collective-permute-done.3.below_ref.refs_3_, bf16[9,1024,128]{2,1,0:T(8,128)(2,1)S(1)} %bitcast.8), custom_call_target="tpu_custom_call" | custom-call | flops 452984832 | bytes 3145728 | tf_op jit(solution)/shard_map/feature_grad/pallas_call | solution.py:276
  46.6 7.8 %all-to-all-done.1.in_ref = bf16[8,32,1152]{2,1,0:T(8,128)(2,1)S(1)} async-done(((bf16[8,32,1152]{2,1,0:T(8,128)(2,1)}), bf16[8,32,1152]{2,1,0:T(8,128)(2,1)S(1)}, u32[]{:S(2)}, u32[]{:S(2)}) %all-to-all-start.1) | async-done | bytes 589856 | tf_op jit(solution)/shard_map/all_to_all | solution.py:351
  54.4 0.7 %final_sum.1 = f32[288,128]{1,0:T(8,128)} custom-call(bf16[8,32,1152]{2,1,0:T(8,128)(2,1)S(1)} %all-to-all-done.1.in_ref), custom_call_target="tpu_custom_call" | custom-call | tf_op jit(solution)/shard_map/final_sum/pallas_call | solution.py:306
  (3 shorter events, 0.0 us)
Async XLA Ops:
  0.6 18.1 %copy-start.2 = (bf16[1,6,32,1024]{3,2,1,0:T(8,128)(2,1)S(1)}, bf16[1,6,32,1024]{3,2,1,0:T(8,128)(2,1)}, u32[]{:S(2)}) copy-start(bf16[1,6,32,1024]{3,2,1,0:T(8,128)(2,1)} %param.6) | copy-start | bytes 1179652
  0.6 17.7 %copy-start.8 = (s32[1,6,32]{2,0,1:T(1,128)S(1)}, s32[1,6,32]{2,0,1:T(1,128)}, u32[]{:S(2)}) copy-start(s32[1,6,32]{2,0,1:T(1,128)} %param.7) | copy-start | bytes 2308
  0.6 17.8 %copy-start.9 = (s32[1,6,32]{2,0,1:T(1,128)S(1)}, s32[1,6,32]{2,0,1:T(1,128)}, u32[]{:S(2)}) copy-start(s32[1,6,32]{2,0,1:T(1,128)} %param.8) | copy-start | bytes 2308
  3.8 7.0 %collective-permute-start = (bf16[192,128]{1,0:T(8,128)(2,1)}, bf16[192,128]{1,0:T(8,128)(2,1)S(1)}, u32[]{:S(2)}, u32[]{:S(2)}) collective-permute-start(bf16[192,128]{1,0:T(8,128)(2,1)} %get-tuple-element.6), channel_id=1, source_target_pairs={{0,1},{1,2},{2,3},{4,5},{5,6},{6,7},{8,9},{9,10},{10,11},{12,13},{... | collective-permute-start | bytes 147464 | tf_op jit(solution)/shard_map/ppermute | solution.py:332
  10.8 0.6 %copy-start.3 = (bf16[192,128]{1,0:T(8,128)(2,1)}, bf16[192,128]{1,0:T(8,128)(2,1)S(1)}, u32[]{:S(2)}) copy-start(bf16[192,128]{1,0:T(8,128)(2,1)S(1)} %collective-permute-done.above_ref.after_ref) | copy-start | bytes 147460
  11.4 14.0 %copy-start.6 = (bf16[128,3]{0,1:T(4,128)(2,1)S(1)}, bf16[128,3]{0,1:T(4,128)(2,1)}, u32[]{:S(2)}) copy-start(bf16[128,3]{0,1:T(4,128)(2,1)} %param.11) | copy-start | bytes 2308
  11.4 14.0 %copy-start.7 = (f32[128]{0:T(128)S(1)}, f32[128]{0:T(128)}, u32[]{:S(2)}) copy-start(f32[128]{0:T(128)} %param.10) | copy-start | bytes 1540
  11.4 14.0 %copy-start.4 = (bf16[192,128]{1,0:T(8,128)(2,1)S(1)}, bf16[192,128]{1,0:T(8,128)(2,1)}, u32[]{:S(2)}) copy-start(bf16[192,128]{1,0:T(8,128)(2,1)} %copy-done.3) | copy-start | bytes 147460
  11.4 27.1 %all-to-all-start = ((bf16[4,192,256]{2,1,0:T(8,128)(2,1)}), bf16[4,192,256]{2,1,0:T(8,128)(2,1)S(1)}, u32[]{:S(2)}, u32[]{:S(2)}) async-start(bf16[4,192,256]{2,1,0:T(8,128)(2,1)} %pass_on.1), calls=%async_computation | async-start | bytes 786432 | tf_op jit(solution)/shard_map/all_to_all | solution.py:335
  17.1 8.4 %collective-permute-start.1 = (bf16[192,128]{1,0:T(8,128)(2,1)}, bf16[192,128]{1,0:T(8,128)(2,1)S(1)}, u32[]{:S(2)}, u32[]{:S(2)}) collective-permute-start(bf16[192,128]{1,0:T(8,128)(2,1)} %get-tuple-element.5.after_ref), channel_id=1, source_target_pairs={{1,0},{2,1},{3,2},{5,4},{6,5},{7,6},{9,8},{10,9},{11,10},{13,12},{... | collective-permute-start | bytes 147464 | tf_op jit(solution)/shard_map/ppermute | solution.py:333
  18.7 1.7 %copy-start = (bf16[1024,9,128]{2,0,1:T(8,128)(2,1)S(1)}, bf16[1024,9,128]{2,0,1:T(8,128)(2,1)}, u32[]{:S(2)}) copy-start(bf16[1024,9,128]{2,0,1:T(8,128)(2,1)} %param.9) | copy-start | bytes 7077892
  20.4 0.8 %copy-start.5 = (bf16[192,128]{1,0:T(8,128)(2,1)S(1)}, bf16[192,128]{1,0:T(8,128)(2,1)}, u32[]{:S(2)}) copy-start(bf16[192,128]{1,0:T(8,128)(2,1)} %get-tuple-element.5.after_ref) | copy-start | bytes 147460
  21.5 22.5 %copy-start.1 = (bf16[1024,9,128]{2,0,1:T(8,128)(2,1)S(1)}, bf16[1024,9,128]{2,0,1:T(8,128)(2,1)}, u32[]{:S(2)}) copy-start(bf16[1024,9,128]{2,0,1:T(8,128)(2,1)} %param.9) | copy-start | bytes 7077892
  25.9 6.8 %collective-permute-start.4 = (bf16[192,128]{1,0:T(8,128)(2,1)S(1)}, bf16[192,128]{1,0:T(8,128)(2,1)S(1)}, u32[]{:S(2)}, u32[]{:S(2)}) collective-permute-start(bf16[192,128]{1,0:T(8,128)(2,1)S(1)} %pointwise.1.own_ref.refs_0_), channel_id=1, source_target_pairs={{0,2},{1,3},{2,0},{3,1},{4,6},{5,7},{6,4},{7,5},{8,10},{9,11},{10,... | collective-permute-start | bytes 147464 | tf_op jit(solution)/shard_map/ppermute | solution.py:347
  29.3 5.0 %collective-permute-start.3 = (bf16[192,128]{1,0:T(8,128)(2,1)S(1)}, bf16[192,128]{1,0:T(8,128)(2,1)S(1)}, u32[]{:S(2)}, u32[]{:S(2)}) collective-permute-start(bf16[192,128]{1,0:T(8,128)(2,1)S(1)} %pointwise.1.own_ref.refs_0_), channel_id=1, source_target_pairs={{0,3},{1,0},{2,1},{3,2},{4,7},{5,4},{6,5},{7,6},{8,11},{9,8},{10,9... | collective-permute-start | bytes 147464 | tf_op jit(solution)/shard_map/ppermute | solution.py:347
  32.6 5.9 %collective-permute-start.2 = (bf16[192,128]{1,0:T(8,128)(2,1)S(1)}, bf16[192,128]{1,0:T(8,128)(2,1)S(1)}, u32[]{:S(2)}, u32[]{:S(2)}) collective-permute-start(bf16[192,128]{1,0:T(8,128)(2,1)S(1)} %pointwise.1.own_ref.refs_0_), channel_id=1, source_target_pairs={{0,1},{1,2},{2,3},{3,0},{4,5},{5,6},{6,7},{7,4},{8,9},{9,10},{10,1... | collective-permute-start | bytes 147464 | tf_op jit(solution)/shard_map/ppermute | solution.py:347
  40.3 14.2 %all-to-all-start.1 = ((bf16[8,32,1152]{2,1,0:T(8,128)(2,1)}), bf16[8,32,1152]{2,1,0:T(8,128)(2,1)S(1)}, u32[]{:S(2)}, u32[]{:S(2)}) async-start(bf16[8,32,1152]{2,1,0:T(8,128)(2,1)} %bitcast.5), calls=%async_computation.1 | async-start | bytes 1179648 | tf_op jit(solution)/shard_map/all_to_all | solution.py:351

commit v7 on v6

--- a/solution.py
+++ b/solution.py
@@ -17,8 +17,17 @@
     starts = [[(d * bands + s) * rows // taps for d in range(replicas)] for s in range(bands)]
     offsets = [[(d * bands + s) * rows % taps for d in range(replicas)] for s in range(bands)]
     cover = max(-(-(off + rows) // taps) for line in offsets for off in line)
-    picks = [[min(c + k, channels - 1) for c in line for k in range(cover)] for line in starts]
+    picks = [
+        [min(line[d] + k, channels - 1) for d in replica_order(replicas) for k in range(cover)]
+        for line in starts
+    ]
     return rows, cover, picks, offsets
+
+
+def replica_order(replicas):
+    if replicas % 2:
+        return list(range(replicas))
+    return list(range(0, replicas, 2)) + list(range(1, replicas, 2))
 
 
 def shift_columns(array, by, columns):
@@ -62,7 +71,10 @@
         bands = room.shape[0]
         for s in range(bands):
             room[s] = jnp.concatenate(
-                [x[:, (d * bands + s) * cover : (d * bands + s + 1) * cover] for d in range(replicas)],
+                [
+                    x[:, (d * bands + s) * cover : (d * bands + s + 1) * cover]
+                    for d in replica_order(replicas)
+                ],
                 axis=1,
             )
             copies.append(pltpu.make_async_copy(room.at[s], outs[2].at[s], out_sems.at[s]))
@@ -111,20 +123,20 @@
     )(flat, weight)
 
 
-def pass_on_kernel(x_ref, after_ref, out_ref):
-    del x_ref, after_ref, out_ref
-
-
-def pass_on(x, after):
+def pass_on_kernel(*refs):
+    del refs
+
+
+def pass_on(x, *after):
     hbm = pl.BlockSpec(memory_space=pltpu.HBM)
     return pl.pallas_call(
         pass_on_kernel,
-        in_specs=[hbm, pl.BlockSpec(memory_space=pl.ANY)],
+        in_specs=[hbm] + [pl.BlockSpec(memory_space=pl.ANY)] * len(after),
         out_specs=hbm,
         out_shape=jax.ShapeDtypeStruct(x.shape, x.dtype),
         input_output_aliases={0: 0},
         name="pass_on",
-    )(x, after)
+    )(x, *after)
 
 
 def middle_kernel(columns, reach, x_ref, w_ref, after_ref, out_ref):
@@ -208,17 +220,25 @@
     )
 
 
-def kernel_grad_kernel(columns, reach, x_ref, *refs):
+def kernel_grad_kernel(columns, reach, parts, other, x_ref, *refs):
     *g_refs, out_ref, taps = refs
-    bands, pixels, _ = x_ref.shape
+    bands, pixels, lanes = x_ref.shape
     width = g_refs[0].shape[1]
     total = bands * pixels
     edge = reach * columns
+    extra = lanes // parts
     band = lax.axis_index("space")
     for k, g_ref in enumerate(g_refs):
         first = lax.rem(band + bands - k, bands) * pixels
         taps[pl.ds(pl.multiple_of(first, 16), pixels)] = shifted_taps(g_ref[...], columns, reach)
-    features = x_ref[...].reshape(total, x_ref.shape[2])
+    part = lax.rem(lax.axis_index("dp") + other, parts)
+    if extra % 128 == 0:
+        features = x_ref[:, :, pl.ds(pl.multiple_of(part * extra, 128), extra)]
+    else:
+        features = x_ref[:, :, :extra]
+        for k in range(1, parts):
+            features = jnp.where(part == k, x_ref[:, :, k * extra : (k + 1) * extra], features)
+    features = features.reshape(total, extra)
     for a in range(3):
         if a == 0:
             left, right = features[: total - edge], taps[edge:]
@@ -232,12 +252,13 @@
         out_ref[:, 3 * a * width : 3 * (a + 1) * width] = block.astype(out_ref.dtype)
 
 
-def kernel_grad(features, gradients, columns, reach):
-    bands, pixels, extra = features.shape
+def kernel_grad(features, gradients, columns, reach, parts, other, dtype):
+    bands, pixels, lanes = features.shape
+    extra = lanes // parts
     width = gradients[0].shape[1]
     return pl.pallas_call(
-        functools.partial(kernel_grad_kernel, columns, reach),
-        out_shape=jax.ShapeDtypeStruct((extra, 9 * width), jnp.bfloat16),
+        functools.partial(kernel_grad_kernel, columns, reach, parts, other),
+        out_shape=jax.ShapeDtypeStruct((extra, 9 * width), dtype),
         scratch_shapes=[pltpu.VMEM((bands * pixels, 3 * width), jnp.bfloat16)],
         compiler_params=pltpu.CompilerParams(vmem_limit_bytes=VMEM_LIMIT),
         cost_estimate=pl.CostEstimate(
@@ -247,6 +268,19 @@
         ),
         name="kernel_grad",
     )(features, *gradients)
+
+
+def add_kernel(a_ref, b_ref, out_ref):
+    out_ref[...] = (a_ref[...] + b_ref[...].astype(jnp.float32)).astype(out_ref.dtype)
+
+
+def add_up(own, came):
+    return pl.pallas_call(
+        add_kernel,
+        out_shape=jax.ShapeDtypeStruct(came.shape, came.dtype),
+        compiler_params=pltpu.CompilerParams(vmem_limit_bytes=VMEM_LIMIT),
+        name="add_up",
+    )(own, came)
 
 
 def feature_grad_kernel(columns, reach, bands, own_ref, above_ref, below_ref, w_ref, out_ref):
@@ -289,22 +323,22 @@
     )(own, above, below, weight)
 
 
-def final_kernel(in_ref, out_ref):
-    replicas, cover, lanes = in_ref.shape
+def final_kernel(replicas, in_ref, out_ref):
+    blocks, cover, lanes = in_ref.shape
     width = out_ref.shape[1]
     taps = lanes // width
     total = in_ref[0].astype(jnp.float32)
-    for d in range(1, replicas):
+    for d in range(1, blocks):
         total += in_ref[d].astype(jnp.float32)
     total = total / replicas
     for t in range(taps):
         out_ref[pl.ds(t, cover, stride=taps), :] = total[:, t * width : (t + 1) * width]
 
 
-def final(came, width):
-    replicas, cover, lanes = came.shape
-    return pl.pallas_call(
-        final_kernel,
+def final(came, width, replicas):
+    _, cover, lanes = came.shape
+    return pl.pallas_call(
+        functools.partial(final_kernel, replicas),
         out_shape=jax.ShapeDtypeStruct((cover * lanes // width, width), jnp.float32),
         compiler_params=pltpu.CompilerParams(vmem_limit_bytes=VMEM_LIMIT),
         name="final_sum",
@@ -332,7 +366,7 @@
     above = lax.ppermute(down, "space", [(i, i + 1) for i in range(bands - 1)])
     below = lax.ppermute(up, "space", [(i + 1, i) for i in range(bands - 1)])
     middle = middle_taps(flat, weight, up, columns, reach)
-    whole = lax.all_to_all(pass_on(split[0], above), "space", 0, 0)
+    whole = lax.all_to_all(pass_on(split[0], above, below), "space", 0, 0)
 
     gradient = pointwise(
         middle,
@@ -347,9 +381,18 @@
         lax.ppermute(gradient, "space", [(i, (i + k) % bands) for i in range(bands)])
         for k in range(1, bands)
     ]
-    partial_grad = kernel_grad(whole, gradients, columns, reach)
-    came = lax.all_to_all(partial_grad.reshape(replicas, cover, taps * width), "dp", 0, 0)
-    weight_grad = final(came, width)
+    if replicas % 2 == 0:
+        theirs = kernel_grad(whole, gradients, columns, reach, 2, 1, jnp.bfloat16)
+        came = lax.ppermute(theirs, "dp", [(i, i ^ 1) for i in range(replicas)])
+        own = kernel_grad(whole, gradients, columns, reach, 2, 0, jnp.float32)
+        partial_grad = add_up(own, came)
+        groups = [list(range(c, replicas, 2)) for c in range(2)]
+    else:
+        partial_grad = kernel_grad(whole, gradients, columns, reach, 1, 0, jnp.bfloat16)
+        groups = None
+    partial_grad = partial_grad.reshape(-1, cover, taps * width)
+    came = lax.all_to_all(partial_grad, "dp", 0, 0, axis_index_groups=groups)
+    weight_grad = final(came, width, replicas)
     if not even:
         start = jnp.array(offsets)[lax.axis_index("space"), lax.axis_index("dp")]
         weight_grad = lax.dynamic_slice_in_dim(weight_grad, start, block_rows)

time: 55.6 us -> 47.5 us (0.85)
  waiting for transfers between devices: 19.7 us -> 14.5 us
  starting transfers between devices: 22.3 us -> 19 us
    all_to_all x2, waiting for transfers between devices: 7.82 us -> 3.32 us  [the longest x1 3.31 us: on_device(): came = lax.all_to_all(partial_grad, 'dp', 0, 0, axis_index_groups=groups)]
    ppermute x3, starting transfers between devices: 6.75 us -> 5.01 us  [on_device(): lax.ppermute(gradient, 'space', [(i, (i + k) % bands) for i in range(band...]
    all_to_all x2, starting transfers between devices: 9.38 us -> 7.72 us  [the longest x1 4 us: on_device(): whole = lax.all_to_all(pass_on(split[0], above, below), 'space', 0, 0)]
    ppermute x1, waiting for transfers between devices: 2.05 us -> 0.75 us  [on_device(): above = lax.ppermute(down, 'space', [(i, i + 1) for i in range(bands - 1)])]
    ppermute x0 -> x1, waiting for transfers between devices: none -> 0.91 us  [on_device(): came = lax.ppermute(theirs, 'dp', [(i, i ^ 1) for i in range(replicas)])]
    pallas_call x3 -> x5, Pallas kernels: 2.5 us -> 2.77 us  [the longest x2 1.31 us: kernel_grad(): pl.pallas_call(functools.partial(kernel_grad_kernel, columns, reach, part...]
    unnamed x20 -> x24, local copies, waits for them, and re-layouts: 3.11 us -> 3.1 us
  transfers between devices with their start and end apart: 7 -> 8, of which waited for: 5 -> 6; matrix products, arithmetic and copies ran while one was open for 0% -> 1% of each run, Pallas kernels for 6% -> 9%
where the time goes in v7:
time: 47.5 us; the launch traced here: 47.1 us
  starting transfers between devices  19 us (40%)
  waiting for transfers between devices  14.5 us (31%)
  Pallas kernels  9.31 us (20%)
  local copies, waits for them, and re-layouts  3.33 us (7%)
  between operations  0.81 us (2%)
    ppermute x3, waiting for transfers between devices, on_device(): lax.ppermute(gradient, 'space', [(i, (i + k) % bands) for i in range(band...  5.43 us
    ppermute x3, starting transfers between devices, on_device(): lax.ppermute(gradient, 'space', [(i, (i + k) % bands) for i in range(band...  5.01 us
    ppermute x1, starting transfers between devices, on_device(): above = lax.ppermute(down, 'space', [(i, i + 1) for i in range(bands - 1)])  4.93 us
    ppermute x1, waiting for transfers between devices, on_device(): below = lax.ppermute(up, 'space', [(i + 1, i) for i in range(bands - 1)])  4.14 us
    all_to_all x1, starting transfers between devices, on_device(): whole = lax.all_to_all(pass_on(split[0], above, below), 'space', 0, 0)  4 us
    all_to_all x1, starting transfers between devices, on_device(): came = lax.all_to_all(partial_grad, 'dp', 0, 0, axis_index_groups=groups)  3.71 us
    all_to_all x1, waiting for transfers between devices, on_device(): came = lax.all_to_all(partial_grad, 'dp', 0, 0, axis_index_groups=groups)  3.31 us
    pallas_call x1, Pallas kernels, prepare(): pl.pallas_call(functools.partial(prepare_kernel, columns, reach, replicas...  3.16 us
  transfers between devices with their start and end apart: 8, of which 6 were waited for; matrix products, arithmetic and copies ran while one was open for 1% of the time, Pallas kernels for 9%

profile of v7, /device:TPU:0, one launch (start us, length us, event | category | flops | bytes accessed | tf_op | source)
XLA Modules:
  0.0 47.1 jit_solution(3547744543589220660)
XLA Ops:
  0.6 0.0 copy-start.2
  0.6 0.0 copy-start.10
  0.6 0.0 copy-start.11
  0.7 3.2 %prepare.1 = (bf16[192,128]{1,0:T(8,128)(2,1)}, bf16[192,128]{1,0:T(8,128)(2,1)}, bf16[4,192,256]{2,1,0:T(8,128)(2,1)}) custom-call(bf16[192,1024]{1,0:T(8,128)(2,1)} %bitcast.9, bf16[9,1024,128]{2,1,0:T(8,128)(2,1)} %bitcast.6), custom_call_target="tpu_custom_call" | custom-call | flops 301989888 | bytes 2752512 | tf_op jit(solution)/shard_map/prepare/pallas_call | solution.py:101
  3.8 4.9 %collective-permute-start = (bf16[192,128]{1,0:T(8,128)(2,1)}, bf16[192,128]{1,0:T(8,128)(2,1)S(1)}, u32[]{:S(2)}, u32[]{:S(2)}) collective-permute-start(bf16[192,128]{1,0:T(8,128)(2,1)} %get-tuple-element.6), channel_id=1, source_target_pairs={{0,1},{1,2},{2,3},{4,5},{5,6},{6,7},{8,9},{9,10},{10,11},{12,13},{... | collective-permute-start | bytes 147464 | tf_op jit(solution)/shard_map/ppermute | solution.py:366
  8.8 1.3 %collective-permute-start.1 = (bf16[192,128]{1,0:T(8,128)(2,1)}, bf16[192,128]{1,0:T(8,128)(2,1)S(1)}, u32[]{:S(2)}, u32[]{:S(2)}) collective-permute-start(bf16[192,128]{1,0:T(8,128)(2,1)} %get-tuple-element.5.after_ref), channel_id=1, source_target_pairs={{1,0},{2,1},{3,2},{5,4},{6,5},{7,6},{9,8},{10,9},{11,10},{13,12},{... | collective-permute-start | bytes 147464 | tf_op jit(solution)/shard_map/ppermute | solution.py:367
  10.1 0.7 %collective-permute-done.above_ref.refs_1_ = bf16[192,128]{1,0:T(8,128)(2,1)S(1)} collective-permute-done((bf16[192,128]{1,0:T(8,128)(2,1)}, bf16[192,128]{1,0:T(8,128)(2,1)S(1)}, u32[]{:S(2)}, u32[]{:S(2)}) %collective-permute-start) | collective-permute-done | bytes 49184 | tf_op jit(solution)/shard_map/ppermute | solution.py:366
  10.8 0.0 copy-start.3
  10.8 4.1 %collective-permute-done.1.below_ref.refs_2_ = bf16[192,128]{1,0:T(8,128)(2,1)S(1)} collective-permute-done((bf16[192,128]{1,0:T(8,128)(2,1)}, bf16[192,128]{1,0:T(8,128)(2,1)S(1)}, u32[]{:S(2)}, u32[]{:S(2)}) %collective-permute-start.1) | collective-permute-done | bytes 49184 | tf_op jit(solution)/shard_map/ppermute | solution.py:367
  15.0 0.0 copy-start.5
  15.0 0.0 copy-done.3
  15.0 0.6 %copy-done.5 = bf16[192,128]{1,0:T(8,128)(2,1)} copy-done((bf16[192,128]{1,0:T(8,128)(2,1)}, bf16[192,128]{1,0:T(8,128)(2,1)S(1)}, u32[]{:S(2)}) %copy-start.5) | copy-done | bytes 49176
  15.6 0.0 copy-start.8
  15.6 0.0 copy-start.9
  15.6 0.0 copy-start.4
  15.6 4.0 %all-to-all-start = ((bf16[4,192,256]{2,1,0:T(8,128)(2,1)}), bf16[4,192,256]{2,1,0:T(8,128)(2,1)S(1)}, u32[]{:S(2)}, u32[]{:S(2)}) async-start(bf16[4,192,256]{2,1,0:T(8,128)(2,1)} %pass_on.1), calls=%async_computation | async-start | bytes 786432 | tf_op jit(solution)/shard_map/all_to_all | solution.py:369
  19.6 0.0 copy-done.10
  19.6 0.0 copy-done.11
  19.6 0.1 reshape.25.scale_ref
  19.8 0.1 reshape.24.label_ref
  19.9 0.0 copy-done.2
  19.9 0.0 copy-start
  19.9 1.7 %copy-done = bf16[1024,9,128]{2,0,1:T(8,128)(2,1)S(1)} copy-done((bf16[1024,9,128]{2,0,1:T(8,128)(2,1)S(1)}, bf16[1024,9,128]{2,0,1:T(8,128)(2,1)}, u32[]{:S(2)}) %copy-start) | copy-done | bytes 2359320
  21.6 0.8 %copy-done.7 = bf16[192,128]{1,0:T(8,128)(2,1)S(1)} copy-done((bf16[192,128]{1,0:T(8,128)(2,1)S(1)}, bf16[192,128]{1,0:T(8,128)(2,1)}, u32[]{:S(2)}) %copy-start.7) | copy-done | bytes 49176
  22.4 0.4 middle_taps.1.middle_ref
  22.7 0.0 copy-start.1
  22.7 0.0 copy-done.8
  22.7 0.0 copy-done.9
  22.8 0.0 copy-done.4
  22.8 0.0 copy-done.6
  22.8 0.4 pointwise.1.own_ref.refs_0_
  23.2 3.0 %collective-permute-start.4 = (bf16[192,128]{1,0:T(8,128)(2,1)S(1)}, bf16[192,128]{1,0:T(8,128)(2,1)S(1)}, u32[]{:S(2)}, u32[]{:S(2)}) collective-permute-start(bf16[192,128]{1,0:T(8,128)(2,1)S(1)} %pointwise.1.own_ref.refs_0_), channel_id=1, source_target_pairs={{0,2},{1,3},{2,0},{3,1},{4,6},{5,7},{6,4},{7,5},{8,10},{9,11},{10,... | collective-permute-start | bytes 147464 | tf_op jit(solution)/shard_map/ppermute | solution.py:381
  26.2 1.5 %collective-permute-start.3 = (bf16[192,128]{1,0:T(8,128)(2,1)S(1)}, bf16[192,128]{1,0:T(8,128)(2,1)S(1)}, u32[]{:S(2)}, u32[]{:S(2)}) collective-permute-start(bf16[192,128]{1,0:T(8,128)(2,1)S(1)} %pointwise.1.own_ref.refs_0_), channel_id=1, source_target_pairs={{0,3},{1,0},{2,1},{3,2},{4,7},{5,4},{6,5},{7,6},{8,11},{9,8},{10,9... | collective-permute-start | bytes 147464 | tf_op jit(solution)/shard_map/ppermute | solution.py:381
  27.6 0.6 %collective-permute-start.2 = (bf16[192,128]{1,0:T(8,128)(2,1)S(1)}, bf16[192,128]{1,0:T(8,128)(2,1)S(1)}, u32[]{:S(2)}, u32[]{:S(2)}) collective-permute-start(bf16[192,128]{1,0:T(8,128)(2,1)S(1)} %pointwise.1.own_ref.refs_0_), channel_id=1, source_target_pairs={{0,1},{1,2},{2,3},{3,0},{4,5},{5,6},{6,7},{7,4},{8,9},{9,10},{10,1... | collective-permute-start | bytes 147464 | tf_op jit(solution)/shard_map/ppermute | solution.py:381
  28.2 4.8 %collective-permute-done.4.refs_2_ = bf16[192,128]{1,0:T(8,128)(2,1)S(1)} collective-permute-done((bf16[192,128]{1,0:T(8,128)(2,1)S(1)}, bf16[192,128]{1,0:T(8,128)(2,1)S(1)}, u32[]{:S(2)}, u32[]{:S(2)}) %collective-permute-start.4) | collective-permute-done | bytes 49184 | tf_op jit(solution)/shard_map/ppermute | solution.py:381
  33.0 0.0 collective-permute-done.3.below_ref.refs_3_
  33.0 0.6 %collective-permute-done.2.above_ref.refs_1_ = bf16[192,128]{1,0:T(8,128)(2,1)S(1)} collective-permute-done((bf16[192,128]{1,0:T(8,128)(2,1)S(1)}, bf16[192,128]{1,0:T(8,128)(2,1)S(1)}, u32[]{:S(2)}, u32[]{:S(2)}) %collective-permute-start.2) | collective-permute-done | bytes 49184 | tf_op jit(solution)/shard_map/ppermute | solution.py:381
  33.6 0.0 all-to-all-done.x_ref
  33.6 0.7 %kernel_grad.3 = bf16[128,1152]{1,0:T(8,128)(2,1)S(1)} custom-call(bf16[4,192,256]{2,1,0:T(8,128)(2,1)S(1)} %all-to-all-done.x_ref, bf16[192,128]{1,0:T(8,128)(2,1)S(1)} %pointwise.1.own_ref.refs_0_, bf16[192,128]{1,0:T(8,128)(2,1)S(1)} %collective-permute-done.2.above_ref.refs_1_, bf16[192,128]{1,0:T(8,128)(2,1)S(1)} %collective-permute-done.4.refs_2_, ...), custom_call_target="tpu_custom_call" | custom-call | flops 226492416 | bytes 688128 | tf_op jit(solution)/shard_map/kernel_grad/pallas_call | solution.py:259
  34.3 0.1 collective-permute-start.5
  34.4 0.7 %kernel_grad.2.a_ref = f32[128,1152]{1,0:T(8,128)S(1)} custom-call(bf16[4,192,256]{2,1,0:T(8,128)(2,1)S(1)} %all-to-all-done.x_ref, bf16[192,128]{1,0:T(8,128)(2,1)S(1)} %pointwise.1.own_ref.refs_0_, bf16[192,128]{1,0:T(8,128)(2,1)S(1)} %collective-permute-done.2.above_ref.refs_1_, bf16[192,128]{1,0:T(8,128)(2,1)S(1)} %collective-permute-done.4.refs_2_, ...), custom_call_target="tpu_custom_call" | custom-call | flops 226492416 | bytes 688128 | tf_op jit(solution)/shard_map/kernel_grad/pallas_call | solution.py:259
  35.0 0.9 %collective-permute-done.5.b_ref = bf16[128,1152]{1,0:T(8,128)(2,1)S(1)} collective-permute-done((bf16[128,1152]{1,0:T(8,128)(2,1)S(1)}, bf16[128,1152]{1,0:T(8,128)(2,1)S(1)}, u32[]{:S(2)}, u32[]{:S(2)}) %collective-permute-start.5) | collective-permute-done | bytes 294944 | tf_op jit(solution)/shard_map/ppermute | solution.py:386
  35.9 0.8 %add_up.1 = bf16[128,1152]{1,0:T(8,128)(2,1)} custom-call(f32[128,1152]{1,0:T(8,128)S(1)} %kernel_grad.2.a_ref, bf16[128,1152]{1,0:T(8,128)(2,1)S(1)} %collective-permute-done.5.b_ref), custom_call_target="tpu_custom_call" | custom-call | tf_op jit(solution)/shard_map/add_up/pallas_call | solution.py:278
  36.7 3.7 %all-to-all-start.1 = ((bf16[4,32,1152]{2,1,0:T(8,128)(2,1)}), bf16[4,32,1152]{2,1,0:T(8,128)(2,1)S(1)}, u32[]{:S(2)}, u32[]{:S(2)}) async-start(bf16[4,32,1152]{2,1,0:T(8,128)(2,1)} %bitcast.5), calls=%async_computation.1 | async-start | bytes 589824 | tf_op jit(solution)/shard_map/all_to_all | solution.py:394
  40.4 0.0 copy-done.1
  40.4 2.6 %feature_grad.1 = f32[192,1024]{1,0:T(8,128)} custom-call(bf16[192,128]{1,0:T(8,128)(2,1)S(1)} %pointwise.1.own_ref.refs_0_, bf16[192,128]{1,0:T(8,128)(2,1)S(1)} %collective-permute-done.2.above_ref.refs_1_, bf16[192,128]{1,0:T(8,128)(2,1)S(1)} %collective-permute-done.3.below_ref.refs_3_, bf16[9,1024,128]{2,1,0:T(8,128)(2,1)S(1)} %bitcast.8), custom_call_target="tpu_custom_call" | custom-call | flops 452984832 | bytes 3145728 | tf_op jit(solution)/shard_map/feature_grad/pallas_call | solution.py:310
  43.0 3.3 %all-to-all-done.1.in_ref = bf16[4,32,1152]{2,1,0:T(8,128)(2,1)S(1)} async-done(((bf16[4,32,1152]{2,1,0:T(8,128)(2,1)}), bf16[4,32,1152]{2,1,0:T(8,128)(2,1)S(1)}, u32[]{:S(2)}, u32[]{:S(2)}) %all-to-all-start.1) | async-done | bytes 294944 | tf_op jit(solution)/shard_map/all_to_all | solution.py:394
  46.3 0.7 %final_sum.1 = f32[288,128]{1,0:T(8,128)} custom-call(bf16[4,32,1152]{2,1,0:T(8,128)(2,1)S(1)} %all-to-all-done.1.in_ref), custom_call_target="tpu_custom_call" | custom-call | tf_op jit(solution)/shard_map/final_sum/pallas_call | solution.py:340
  (5 shorter events, 0.0 us)
Async XLA Ops:
  0.6 19.2 %copy-start.2 = (bf16[1,6,32,1024]{3,2,1,0:T(8,128)(2,1)S(1)}, bf16[1,6,32,1024]{3,2,1,0:T(8,128)(2,1)}, u32[]{:S(2)}) copy-start(bf16[1,6,32,1024]{3,2,1,0:T(8,128)(2,1)} %param.6) | copy-start | bytes 1179652
  0.6 18.9 %copy-start.10 = (s32[1,6,32]{2,0,1:T(1,128)S(1)}, s32[1,6,32]{2,0,1:T(1,128)}, u32[]{:S(2)}) copy-start(s32[1,6,32]{2,0,1:T(1,128)} %param.7) | copy-start | bytes 2308
  0.6 19.0 %copy-start.11 = (s32[1,6,32]{2,0,1:T(1,128)S(1)}, s32[1,6,32]{2,0,1:T(1,128)}, u32[]{:S(2)}) copy-start(s32[1,6,32]{2,0,1:T(1,128)} %param.8) | copy-start | bytes 2308
  3.8 7.0 %collective-permute-start = (bf16[192,128]{1,0:T(8,128)(2,1)}, bf16[192,128]{1,0:T(8,128)(2,1)S(1)}, u32[]{:S(2)}, u32[]{:S(2)}) collective-permute-start(bf16[192,128]{1,0:T(8,128)(2,1)} %get-tuple-element.6), channel_id=1, source_target_pairs={{0,1},{1,2},{2,3},{4,5},{5,6},{6,7},{8,9},{9,10},{10,11},{12,13},{... | collective-permute-start | bytes 147464 | tf_op jit(solution)/shard_map/ppermute | solution.py:366
  8.8 6.2 %collective-permute-start.1 = (bf16[192,128]{1,0:T(8,128)(2,1)}, bf16[192,128]{1,0:T(8,128)(2,1)S(1)}, u32[]{:S(2)}, u32[]{:S(2)}) collective-permute-start(bf16[192,128]{1,0:T(8,128)(2,1)} %get-tuple-element.5.after_ref), channel_id=1, source_target_pairs={{1,0},{2,1},{3,2},{5,4},{6,5},{7,6},{9,8},{10,9},{11,10},{13,12},{... | collective-permute-start | bytes 147464 | tf_op jit(solution)/shard_map/ppermute | solution.py:367
  10.8 4.2 %copy-start.3 = (bf16[192,128]{1,0:T(8,128)(2,1)}, bf16[192,128]{1,0:T(8,128)(2,1)S(1)}, u32[]{:S(2)}) copy-start(bf16[192,128]{1,0:T(8,128)(2,1)S(1)} %collective-permute-done.above_ref.refs_1_) | copy-start | bytes 147460
  15.0 0.6 %copy-start.5 = (bf16[192,128]{1,0:T(8,128)(2,1)}, bf16[192,128]{1,0:T(8,128)(2,1)S(1)}, u32[]{:S(2)}) copy-start(bf16[192,128]{1,0:T(8,128)(2,1)S(1)} %collective-permute-done.1.below_ref.refs_2_) | copy-start | bytes 147460
  15.6 7.2 %copy-start.8 = (bf16[128,3]{0,1:T(4,128)(2,1)S(1)}, bf16[128,3]{0,1:T(4,128)(2,1)}, u32[]{:S(2)}) copy-start(bf16[128,3]{0,1:T(4,128)(2,1)} %param.11) | copy-start | bytes 2308
  15.6 7.2 %copy-start.9 = (f32[128]{0:T(128)S(1)}, f32[128]{0:T(128)}, u32[]{:S(2)}) copy-start(f32[128]{0:T(128)} %param.10) | copy-start | bytes 1540
  15.6 7.2 %copy-start.4 = (bf16[192,128]{1,0:T(8,128)(2,1)S(1)}, bf16[192,128]{1,0:T(8,128)(2,1)}, u32[]{:S(2)}) copy-start(bf16[192,128]{1,0:T(8,128)(2,1)} %copy-done.3) | copy-start | bytes 147460
  15.6 7.2 %copy-start.6 = (bf16[192,128]{1,0:T(8,128)(2,1)S(1)}, bf16[192,128]{1,0:T(8,128)(2,1)}, u32[]{:S(2)}) copy-start(bf16[192,128]{1,0:T(8,128)(2,1)} %copy-done.5) | copy-start | bytes 147460
  15.6 18.1 %all-to-all-start = ((bf16[4,192,256]{2,1,0:T(8,128)(2,1)}), bf16[4,192,256]{2,1,0:T(8,128)(2,1)S(1)}, u32[]{:S(2)}, u32[]{:S(2)}) async-start(bf16[4,192,256]{2,1,0:T(8,128)(2,1)} %pass_on.1), calls=%async_computation | async-start | bytes 786432 | tf_op jit(solution)/shard_map/all_to_all | solution.py:369
  19.9 1.7 %copy-start = (bf16[1024,9,128]{2,0,1:T(8,128)(2,1)S(1)}, bf16[1024,9,128]{2,0,1:T(8,128)(2,1)}, u32[]{:S(2)}) copy-start(bf16[1024,9,128]{2,0,1:T(8,128)(2,1)} %param.9) | copy-start | bytes 7077892
  21.6 0.8 %copy-start.7 = (bf16[192,128]{1,0:T(8,128)(2,1)S(1)}, bf16[192,128]{1,0:T(8,128)(2,1)}, u32[]{:S(2)}) copy-start(bf16[192,128]{1,0:T(8,128)(2,1)} %get-tuple-element.5.after_ref) | copy-start | bytes 147460
  22.7 17.7 %copy-start.1 = (bf16[1024,9,128]{2,0,1:T(8,128)(2,1)S(1)}, bf16[1024,9,128]{2,0,1:T(8,128)(2,1)}, u32[]{:S(2)}) copy-start(bf16[1024,9,128]{2,0,1:T(8,128)(2,1)} %param.9) | copy-start | bytes 7077892
  23.2 9.8 %collective-permute-start.4 = (bf16[192,128]{1,0:T(8,128)(2,1)S(1)}, bf16[192,128]{1,0:T(8,128)(2,1)S(1)}, u32[]{:S(2)}, u32[]{:S(2)}) collective-permute-start(bf16[192,128]{1,0:T(8,128)(2,1)S(1)} %pointwise.1.own_ref.refs_0_), channel_id=1, source_target_pairs={{0,2},{1,3},{2,0},{3,1},{4,6},{5,7},{6,4},{7,5},{8,10},{9,11},{10,... | collective-permute-start | bytes 147464 | tf_op jit(solution)/shard_map/ppermute | solution.py:381
  26.2 6.8 %collective-permute-start.3 = (bf16[192,128]{1,0:T(8,128)(2,1)S(1)}, bf16[192,128]{1,0:T(8,128)(2,1)S(1)}, u32[]{:S(2)}, u32[]{:S(2)}) collective-permute-start(bf16[192,128]{1,0:T(8,128)(2,1)S(1)} %pointwise.1.own_ref.refs_0_), channel_id=1, source_target_pairs={{0,3},{1,0},{2,1},{3,2},{4,7},{5,4},{6,5},{7,6},{8,11},{9,8},{10,9... | collective-permute-start | bytes 147464 | tf_op jit(solution)/shard_map/ppermute | solution.py:381
  27.6 6.0 %collective-permute-start.2 = (bf16[192,128]{1,0:T(8,128)(2,1)S(1)}, bf16[192,128]{1,0:T(8,128)(2,1)S(1)}, u32[]{:S(2)}, u32[]{:S(2)}) collective-permute-start(bf16[192,128]{1,0:T(8,128)(2,1)S(1)} %pointwise.1.own_ref.refs_0_), channel_id=1, source_target_pairs={{0,1},{1,2},{2,3},{3,0},{4,5},{5,6},{6,7},{7,4},{8,9},{9,10},{10,1... | collective-permute-start | bytes 147464 | tf_op jit(solution)/shard_map/ppermute | solution.py:381
  34.3 1.6 %collective-permute-start.5 = (bf16[128,1152]{1,0:T(8,128)(2,1)S(1)}, bf16[128,1152]{1,0:T(8,128)(2,1)S(1)}, u32[]{:S(2)}, u32[]{:S(2)}) collective-permute-start(bf16[128,1152]{1,0:T(8,128)(2,1)S(1)} %kernel_grad.3), channel_id=1, source_target_pairs={{0,4},{4,0},{8,12},{12,8},{16,20},{20,16},{24,28},{28,24},{1,5},{5... | collective-permute-start | bytes 884744 | tf_op jit(solution)/shard_map/ppermute | solution.py:386
  36.7 9.6 %all-to-all-start.1 = ((bf16[4,32,1152]{2,1,0:T(8,128)(2,1)}), bf16[4,32,1152]{2,1,0:T(8,128)(2,1)S(1)}, u32[]{:S(2)}, u32[]{:S(2)}) async-start(bf16[4,32,1152]{2,1,0:T(8,128)(2,1)} %bitcast.5), calls=%async_computation.1 | async-start | bytes 589824 | tf_op jit(solution)/shard_map/all_to_all | solution.py:394

commit v8 on v6

--- a/solution.py
+++ b/solution.py
@@ -17,8 +17,17 @@
     starts = [[(d * bands + s) * rows // taps for d in range(replicas)] for s in range(bands)]
     offsets = [[(d * bands + s) * rows % taps for d in range(replicas)] for s in range(bands)]
     cover = max(-(-(off + rows) // taps) for line in offsets for off in line)
-    picks = [[min(c + k, channels - 1) for c in line for k in range(cover)] for line in starts]
+    picks = [
+        [min(line[d] + k, channels - 1) for d in replica_order(replicas) for k in range(cover)]
+        for line in starts
+    ]
     return rows, cover, picks, offsets
+
+
+def replica_order(replicas):
+    if replicas % 2:
+        return list(range(replicas))
+    return list(range(0, replicas, 2)) + list(range(1, replicas, 2))
 
 
 def shift_columns(array, by, columns):
@@ -40,91 +49,107 @@
     )
 
 
-def prepare_kernel(
-    columns, reach, replicas, cover, x_hbm, w_hbm, *refs
-):
-    outs, (x_ref, w_ref, room, halo, x_sem, w_sems, out_sems, halo_sems) = refs[:-8], refs[-8:]
-    down_hbm, up_hbm = outs[:2]
-    pixels, edge = x_ref.shape[0], reach * columns
-    load = pltpu.make_async_copy(x_hbm, x_ref, x_sem)
-    load.start()
-    rows = [0, 2]
-    loads = [
-        pltpu.make_async_copy(w_hbm.at[pl.ds(3 * a, 3)], w_ref.at[pl.ds(3 * a, 3)], w_sems.at[a])
-        for a in rows
-    ]
-    for copy in loads:
-        copy.start()
-    load.wait()
+def load_kernel(replicas, cover, x_hbm, w_hbm, *refs):
+    x_ref, w_ref, *outs = refs[: len(refs) - 4]
+    room, x_sem, w_sem, out_sems = refs[len(refs) - 4 :]
+    x_load = pltpu.make_async_copy(x_hbm, x_ref, x_sem)
+    w_load = pltpu.make_async_copy(w_hbm, w_ref, w_sem)
+    x_load.start()
+    w_load.start()
+    x_load.wait()
     copies = []
-    if len(outs) == 3:
+    if outs:
+        parts, bands, _, lanes = room.shape
         x = x_ref[...]
-        bands = room.shape[0]
-        for s in range(bands):
-            room[s] = jnp.concatenate(
-                [x[:, (d * bands + s) * cover : (d * bands + s + 1) * cover] for d in range(replicas)],
-                axis=1,
-            )
-            copies.append(pltpu.make_async_copy(room.at[s], outs[2].at[s], out_sems.at[s]))
+        order = replica_order(replicas)
+        for p in range(parts):
+            for s in range(bands):
+                blocks = order[p * (replicas // parts) : (p + 1) * (replicas // parts)]
+                room[p, s] = jnp.concatenate(
+                    [x[:, (d * bands + s) * cover : (d * bands + s + 1) * cover] for d in blocks],
+                    axis=1,
+                )
+        for k, out in enumerate(outs):
+            part = lax.rem(lax.axis_index("dp") + parts - 1 - k, parts)
+            copies.append(pltpu.make_async_copy(room.at[part], out, out_sems.at[k]))
             copies[-1].start()
-    for k, a in enumerate(rows):
-        loads[k].wait()
-        x = x_ref[pixels - edge :] if a == 0 else x_ref[:edge]
-        halo[k] = tap_row(x, w_ref, a, columns, reach).astype(halo.dtype)
-        copies.append(pltpu.make_async_copy(halo.at[k], (down_hbm, up_hbm)[k], halo_sems.at[k]))
-        copies[-1].start()
+    w_load.wait()
     for copy in copies:
         copy.wait()
 
 
-def prepare(flat, weight, columns, reach, bands, replicas, cover, blocks):
+def load(flat, weight, bands, replicas, cover, parts, blocks):
     pixels, channels = flat.shape
-    taps, _, width = weight.shape
+    hbm = pl.BlockSpec(memory_space=pltpu.HBM)
+    vmem = pl.BlockSpec(memory_space=pltpu.VMEM)
+    shape = (bands, pixels, replicas // parts * cover)
+    count = parts if blocks else 0
+    return pl.pallas_call(
+        functools.partial(load_kernel, replicas, cover),
+        in_specs=[hbm, hbm],
+        out_specs=[vmem, vmem] + [hbm] * count,
+        out_shape=[
+            pltpu.VMEM(flat.shape, flat.dtype),
+            pltpu.VMEM(weight.shape, weight.dtype),
+        ]
+        + [pltpu.HBM(shape, flat.dtype)] * count,
+        scratch_shapes=[
+            pltpu.VMEM((parts,) + shape, flat.dtype),
+            pltpu.SemaphoreType.DMA,
+            pltpu.SemaphoreType.DMA,
+            pltpu.SemaphoreType.DMA((parts,)),
+        ],
+        compiler_params=pltpu.CompilerParams(vmem_limit_bytes=VMEM_LIMIT),
+        cost_estimate=pl.CostEstimate(
+            flops=0,
+            bytes_accessed=2 * weight.size + 4 * pixels * channels,
+            transcendentals=0,
+        ),
+        name="load",
+    )(
+        pltpu.with_memory_space_constraint(flat, pltpu.HBM),
+        pltpu.with_memory_space_constraint(weight, pltpu.HBM),
+    )
+
+
+def halo_kernel(columns, reach, x_ref, w_ref, down_ref, up_ref):
+    pixels, edge = x_ref.shape[0], reach * columns
+    down_ref[...] = tap_row(x_ref[pixels - edge :], w_ref, 0, columns, reach).astype(down_ref.dtype)
+    up_ref[...] = tap_row(x_ref[:edge], w_ref, 2, columns, reach).astype(up_ref.dtype)
+
+
+def halo(flat, weight, columns, reach):
+    _, channels = flat.shape
+    width = weight.shape[2]
     edge = reach * columns
+    return pl.pallas_call(
+        functools.partial(halo_kernel, columns, reach),
+        out_shape=[jax.ShapeDtypeStruct((edge, width), jnp.bfloat16)] * 2,
+        compiler_params=pltpu.CompilerParams(vmem_limit_bytes=VMEM_LIMIT),
+        cost_estimate=pl.CostEstimate(
+            flops=12 * edge * channels * width,
+            bytes_accessed=12 * channels * width + 2 * edge * channels,
+            transcendentals=0,
+        ),
+        name="halo",
+    )(flat, weight)
+
+
+def pass_on_kernel(*refs):
+    del refs
+
+
+def pass_on(x, *after):
     hbm = pl.BlockSpec(memory_space=pltpu.HBM)
-    shape = (bands, pixels, replicas * cover)
-    out_shape = [jax.ShapeDtypeStruct((edge, width), jnp.bfloat16)] * 2
-    if blocks:
-        out_shape.append(jax.ShapeDtypeStruct(shape, flat.dtype))
-    return pl.pallas_call(
-        functools.partial(prepare_kernel, columns, reach, replicas, cover),
-        in_specs=[hbm, hbm],
-        out_specs=[hbm] * len(out_shape),
-        out_shape=out_shape,
-        scratch_shapes=[
-            pltpu.VMEM((pixels, channels), flat.dtype),
-            pltpu.VMEM((taps, channels, width), weight.dtype),
-            pltpu.VMEM(shape, flat.dtype),
-            pltpu.VMEM((2, edge, width), jnp.bfloat16),
-            pltpu.SemaphoreType.DMA,
-            pltpu.SemaphoreType.DMA((3,)),
-            pltpu.SemaphoreType.DMA((bands,)),
-            pltpu.SemaphoreType.DMA((2,)),
-        ],
-        compiler_params=pltpu.CompilerParams(vmem_limit_bytes=VMEM_WHOLE),
-        cost_estimate=pl.CostEstimate(
-            flops=12 * edge * channels * width,
-            bytes_accessed=12 * channels * width + 6 * pixels * channels,
-            transcendentals=0,
-        ),
-        name="prepare",
-    )(flat, weight)
-
-
-def pass_on_kernel(x_ref, after_ref, out_ref):
-    del x_ref, after_ref, out_ref
-
-
-def pass_on(x, after):
-    hbm = pl.BlockSpec(memory_space=pltpu.HBM)
     return pl.pallas_call(
         pass_on_kernel,
-        in_specs=[hbm, pl.BlockSpec(memory_space=pl.ANY)],
+        in_specs=[hbm] + [pl.BlockSpec(memory_space=pltpu.VMEM)] * len(after),
         out_specs=hbm,
-        out_shape=jax.ShapeDtypeStruct(x.shape, x.dtype),
+        out_shape=pltpu.HBM(x.shape, x.dtype),
         input_output_aliases={0: 0},
+        compiler_params=pltpu.CompilerParams(vmem_limit_bytes=VMEM_LIMIT),
         name="pass_on",
-    )(x, after)
+    )(pltpu.with_memory_space_constraint(x, pltpu.HBM), *after)
 
 
 def middle_kernel(columns, reach, x_ref, w_ref, after_ref, out_ref):
@@ -142,7 +167,7 @@
     vmem = pl.BlockSpec(memory_space=pltpu.VMEM)
     return pl.pallas_call(
         functools.partial(middle_kernel, columns, reach),
-        in_specs=[vmem, vmem, pl.BlockSpec(memory_space=pl.ANY)],
+        in_specs=[vmem, vmem, vmem],
         out_shape=jax.ShapeDtypeStruct((pixels, width), jnp.float32),
         compiler_params=pltpu.CompilerParams(vmem_limit_bytes=VMEM_LIMIT),
         cost_estimate=pl.CostEstimate(
@@ -210,7 +235,7 @@
 
 def kernel_grad_kernel(columns, reach, x_ref, *refs):
     *g_refs, out_ref, taps = refs
-    bands, pixels, _ = x_ref.shape
+    bands, pixels, extra = x_ref.shape
     width = g_refs[0].shape[1]
     total = bands * pixels
     edge = reach * columns
@@ -218,7 +243,7 @@
     for k, g_ref in enumerate(g_refs):
         first = lax.rem(band + bands - k, bands) * pixels
         taps[pl.ds(pl.multiple_of(first, 16), pixels)] = shifted_taps(g_ref[...], columns, reach)
-    features = x_ref[...].reshape(total, x_ref.shape[2])
+    features = x_ref[...].reshape(total, extra)
     for a in range(3):
         if a == 0:
             left, right = features[: total - edge], taps[edge:]
@@ -232,12 +257,12 @@
         out_ref[:, 3 * a * width : 3 * (a + 1) * width] = block.astype(out_ref.dtype)
 
 
-def kernel_grad(features, gradients, columns, reach):
+def kernel_grad(features, gradients, columns, reach, dtype):
     bands, pixels, extra = features.shape
     width = gradients[0].shape[1]
     return pl.pallas_call(
         functools.partial(kernel_grad_kernel, columns, reach),
-        out_shape=jax.ShapeDtypeStruct((extra, 9 * width), jnp.bfloat16),
+        out_shape=jax.ShapeDtypeStruct((extra, 9 * width), dtype),
         scratch_shapes=[pltpu.VMEM((bands * pixels, 3 * width), jnp.bfloat16)],
         compiler_params=pltpu.CompilerParams(vmem_limit_bytes=VMEM_LIMIT),
         cost_estimate=pl.CostEstimate(
@@ -247,6 +272,60 @@
         ),
         name="kernel_grad",
     )(features, *gradients)
+
+
+def partner(i, k, count):
+    return i ^ k if count & (count - 1) == 0 else (i + k) % count
+
+
+def split_kernel(parts, terms, *refs):
+    ins, outs = refs[:terms], refs[terms:]
+    count = len(outs)
+    cover = outs[0].shape[0]
+    me = lax.axis_index("dp") // parts
+    for k, out in enumerate(outs):
+        if count == 1:
+            rows = pl.ds(0, cover)
+        else:
+            block = jnp.bitwise_xor(me, k) if count & (count - 1) == 0 else lax.rem(me + k, count)
+            rows = pl.ds(pl.multiple_of(block * cover, cover), cover)
+        total = ins[0][rows, :].astype(jnp.float32)
+        for ref in ins[1:]:
+            total += ref[rows, :].astype(jnp.float32)
+        out[...] = total.astype(out.dtype)
+
+
+def split_up(terms, parts, count):
+    rows, lanes = terms[0].shape
+    return pl.pallas_call(
+        functools.partial(split_kernel, parts, len(terms)),
+        out_shape=[jax.ShapeDtypeStruct((rows // count, lanes), jnp.bfloat16)] * count,
+        compiler_params=pltpu.CompilerParams(vmem_limit_bytes=VMEM_LIMIT),
+        name="split_up",
+    )(*terms)
+
+
+def final_kernel(replicas, *refs):
+    *ins, out_ref = refs
+    cover, lanes = ins[0].shape
+    width = out_ref.shape[1]
+    taps = lanes // width
+    total = ins[0][...].astype(jnp.float32)
+    for ref in ins[1:]:
+        total += ref[...].astype(jnp.float32)
+    total = total / replicas
+    for t in range(taps):
+        out_ref[pl.ds(t, cover, stride=taps), :] = total[:, t * width : (t + 1) * width]
+
+
+def final(blocks, width, replicas):
+    cover, lanes = blocks[0].shape
+    return pl.pallas_call(
+        functools.partial(final_kernel, replicas),
+        out_shape=jax.ShapeDtypeStruct((cover * lanes // width, width), jnp.float32),
+        compiler_params=pltpu.CompilerParams(vmem_limit_bytes=VMEM_LIMIT),
+        name="final_sum",
+    )(*blocks)
 
 
 def feature_grad_kernel(columns, reach, bands, own_ref, above_ref, below_ref, w_ref, out_ref):
@@ -289,28 +368,6 @@
     )(own, above, below, weight)
 
 
-def final_kernel(in_ref, out_ref):
-    replicas, cover, lanes = in_ref.shape
-    width = out_ref.shape[1]
-    taps = lanes // width
-    total = in_ref[0].astype(jnp.float32)
-    for d in range(1, replicas):
-        total += in_ref[d].astype(jnp.float32)
-    total = total / replicas
-    for t in range(taps):
-        out_ref[pl.ds(t, cover, stride=taps), :] = total[:, t * width : (t + 1) * width]
-
-
-def final(came, width):
-    replicas, cover, lanes = came.shape
-    return pl.pallas_call(
-        final_kernel,
-        out_shape=jax.ShapeDtypeStruct((cover * lanes // width, width), jnp.float32),
-        compiler_params=pltpu.CompilerParams(vmem_limit_bytes=VMEM_LIMIT),
-        name="final_sum",
-    )(came)
-
-
 def on_device(features, labels, pixel_weight, conv_weight, conv_bias, class_weight):
     image = features[0]
     band_rows, columns, channels = image.shape
@@ -324,15 +381,26 @@
     weight = conv_weight.transpose(1, 0, 2)
     block_rows, cover, picks, offsets = channel_plan(channels, taps, replicas, bands)
     even = block_rows % taps == 0
-    down, up, *split = prepare(flat, weight, columns, reach, bands, replicas, cover, even)
+    parts = 2 if replicas % 2 == 0 else 1
+    count = replicas // parts
+    flat, weight, *split = load(flat, weight, bands, replicas, cover, parts, even)
     if not even:
         order = jnp.array([c for line in picks for c in line], jnp.int32)
-        blocks = jnp.take(flat, order, axis=1).reshape(pixels, bands, replicas * cover)
-        split = [blocks.transpose(1, 0, 2)]
+        blocks = jnp.take(flat, order, axis=1).reshape(pixels, bands, parts, count * cover)
+        blocks = blocks.transpose(2, 1, 0, 3)
+        me = lax.axis_index("dp")
+        split = [
+            lax.dynamic_index_in_dim(blocks, (me + parts - 1 - k) % parts, keepdims=False)
+            for k in range(parts)
+        ]
+    whole = [lax.all_to_all(split[0], "space", 0, 0)]
+    down, up = halo(flat, weight, columns, reach)
     above = lax.ppermute(down, "space", [(i, i + 1) for i in range(bands - 1)])
     below = lax.ppermute(up, "space", [(i + 1, i) for i in range(bands - 1)])
     middle = middle_taps(flat, weight, up, columns, reach)
-    whole = lax.all_to_all(pass_on(split[0], above), "space", 0, 0)
+    for blocks in split[1:]:
+        held = pass_on(blocks, above, below, middle, whole[0])
+        whole.append(lax.all_to_all(held, "space", 0, 0))
 
     gradient = pointwise(
         middle,
@@ -347,9 +415,21 @@
         lax.ppermute(gradient, "space", [(i, (i + k) % bands) for i in range(bands)])
         for k in range(1, bands)
     ]
-    partial_grad = kernel_grad(whole, gradients, columns, reach)
-    came = lax.all_to_all(partial_grad.reshape(replicas, cover, taps * width), "dp", 0, 0)
-    weight_grad = final(came, width)
+    terms = [kernel_grad(whole[-1], gradients, columns, reach, jnp.float32)]
+    if parts == 2:
+        theirs = kernel_grad(whole[0], gradients, columns, reach, jnp.bfloat16)
+        terms.append(lax.ppermute(theirs, "dp", [(i, i ^ 1) for i in range(replicas)]))
+    if cover % 16 == 0 and count <= 8:
+        blocks = split_up(terms, parts, count)
+        came = [blocks[0]]
+        for k in range(1, count):
+            pairs = [(i, parts * partner(i // parts, k, count) + i % parts) for i in range(replicas)]
+            came.append(lax.ppermute(blocks[k], "dp", pairs))
+    else:
+        blocks = split_up(terms, parts, 1)[0].reshape(count, cover, taps * width)
+        groups = [list(range(c, replicas, parts)) for c in range(parts)]
+        came = list(lax.all_to_all(blocks, "dp", 0, 0, axis_index_groups=groups))
+    weight_grad = final(came, width, replicas)
     if not even:
         start = jnp.array(offsets)[lax.axis_index("space"), lax.axis_index("dp")]
         weight_grad = lax.dynamic_slice_in_dim(weight_grad, start, block_rows)

time: 55.6 us -> 45.5 us (0.82)
  waiting for transfers between devices: 19.7 us -> 11.7 us
  local copies, waits for them, and re-layouts: 3.34 us -> 0.24 us
  starting transfers between devices: 22.3 us -> 24.2 us
  Pallas kernels: 9.05 us -> 8.21 us
    ppermute x3, waiting for transfers between devices: 5.88 us -> 0.82 us  [on_device(): lax.ppermute(gradient, 'space', [(i, (i + k) % bands) for i in range(band...]
    ppermute x0 -> x4, starting transfers between devices: none -> 3.62 us  [the longest x3 3.55 us: on_device(): came.append(lax.ppermute(blocks[k], 'dp', pairs))]
    all_to_all x2, waiting for transfers between devices: 7.82 us -> 4.69 us  [the longest x1 4.68 us: on_device(): whole.append(lax.all_to_all(held, 'space', 0, 0))]
    unnamed x20 -> x8, local copies, waits for them, and re-layouts: 3.11 us -> 0.02 us
    ppermute x3, starting transfers between devices: 6.75 us -> 4.45 us  [on_device(): lax.ppermute(gradient, 'space', [(i, (i + k) % bands) for i in range(band...]
    ppermute x0 -> x4, waiting for transfers between devices: none -> 2.17 us  [the longest x3 2.16 us: on_device(): came.append(lax.ppermute(blocks[k], 'dp', pairs))]
    ppermute x1, waiting for transfers between devices: 2.05 us -> 0.01 us  [on_device(): above = lax.ppermute(down, 'space', [(i, i + 1) for i in range(bands - 1)])]
    all_to_all x2, starting transfers between devices: 9.38 us -> 10.9 us  [the longest x1 6.33 us: on_device(): whole = [lax.all_to_all(split[0], 'space', 0, 0)]]
  transfers between devices with their start and end apart: 7 -> 11, of which waited for: 5 -> 4; matrix products, arithmetic and copies ran while one was open for 0% -> 1% of each run, Pallas kernels for 6% -> 12%
where the time goes in v8:
time: 45.5 us; the launch traced here: 45.1 us
  starting transfers between devices  24.2 us (53%)
  waiting for transfers between devices  11.7 us (26%)
  Pallas kernels  8.21 us (18%)
  between operations  0.78 us (2%)
    all_to_all x1, starting transfers between devices, on_device(): whole = [lax.all_to_all(split[0], 'space', 0, 0)]  6.33 us
    all_to_all x1, waiting for transfers between devices, on_device(): whole.append(lax.all_to_all(held, 'space', 0, 0))  4.68 us
    all_to_all x1, starting transfers between devices, on_device(): whole.append(lax.all_to_all(held, 'space', 0, 0))  4.53 us
    ppermute x3, starting transfers between devices, on_device(): lax.ppermute(gradient, 'space', [(i, (i + k) % bands) for i in range(band...  4.45 us
    ppermute x1, waiting for transfers between devices, on_device(): below = lax.ppermute(up, 'space', [(i + 1, i) for i in range(bands - 1)])  4 us
    ppermute x1, starting transfers between devices, on_device(): above = lax.ppermute(down, 'space', [(i, i + 1) for i in range(bands - 1)])  3.93 us
    ppermute x3, starting transfers between devices, on_device(): came.append(lax.ppermute(blocks[k], 'dp', pairs))  3.55 us
    pallas_call x1, Pallas kernels, feature_grad(): pl.pallas_call(functools.partial(feature_grad_kernel, columns, reach, ban...  2.61 us
  transfers between devices with their start and end apart: 11, of which 4 were waited for; matrix products, arithmetic and copies ran while one was open for 1% of the time, Pallas kernels for 12%

profile of v8, /device:TPU:0, one launch (start us, length us, event | category | flops | bytes accessed | tf_op | source)
XLA Modules:
  0.0 45.1 jit_solution(6283125982094152519)
XLA Ops:
  0.6 0.0 copy-start.2
  0.6 0.0 copy-start.3
  0.7 2.2 %load.1 = (bf16[192,1024]{1,0:T(8,128)(2,1)S(1)}, bf16[9,1024,128]{2,1,0:T(8,128)(2,1)S(1)}, bf16[4,192,128]{2,1,0:T(8,128)(2,1)}, bf16[4,192,128]{2,1,0:T(8,128)(2,1)}) custom-call(bf16[192,1024]{1,0:T(8,128)(2,1)} %bitcast.9, bf16[9,1024,128]{2,1,0:T(8,128)(2,1)} %bitcast.7), custom_call_target="tpu_custom_call" | custom-call | bytes 3145728 | tf_op jit(solution)/shard_map/load/pallas_call | solution.py:87
  2.8 6.3 %all-to-all-start = ((bf16[4,192,128]{2,1,0:T(8,128)(2,1)}), bf16[4,192,128]{2,1,0:T(8,128)(2,1)S(1)}, u32[]{:S(2)}, u32[]{:S(2)}) async-start(bf16[4,192,128]{2,1,0:T(8,128)(2,1)} %get-tuple-element.17), calls=%async_computation | async-start | bytes 393216 | tf_op jit(solution)/shard_map/all_to_all | solution.py:396
  9.2 0.0 copy-start
  9.2 0.0 copy-start.1
  9.2 0.6 %halo.1 = (bf16[192,128]{1,0:T(8,128)(2,1)S(1)}, bf16[192,128]{1,0:T(8,128)(2,1)S(1)}) custom-call(bf16[192,1024]{1,0:T(8,128)(2,1)S(1)} %get-tuple-element.12.x_ref, bf16[9,1024,128]{2,1,0:T(8,128)(2,1)S(1)} %get-tuple-element.13.w_ref), custom_call_target="tpu_custom_call" | custom-call | flops 301989888 | bytes 1966080 | tf_op jit(solution)/shard_map/halo/pallas_call | solution.py:125
  9.7 3.9 %collective-permute-start = (bf16[192,128]{1,0:T(8,128)(2,1)S(1)}, bf16[192,128]{1,0:T(8,128)(2,1)S(1)}, u32[]{:S(2)}, u32[]{:S(2)}) collective-permute-start(bf16[192,128]{1,0:T(8,128)(2,1)S(1)} %get-tuple-element.15), channel_id=1, source_target_pairs={{0,1},{1,2},{2,3},{4,5},{5,6},{6,7},{8,9},{9,10},{10,11},{12,13},{... | collective-permute-start | bytes 147464 | tf_op jit(solution)/shard_map/ppermute | solution.py:398
  13.7 1.3 %collective-permute-start.1 = (bf16[192,128]{1,0:T(8,128)(2,1)S(1)}, bf16[192,128]{1,0:T(8,128)(2,1)S(1)}, u32[]{:S(2)}, u32[]{:S(2)}) collective-permute-start(bf16[192,128]{1,0:T(8,128)(2,1)S(1)} %get-tuple-element.14.after_ref), channel_id=1, source_target_pairs={{1,0},{2,1},{3,2},{5,4},{6,5},{7,6},{9,8},{10,9},{11,10},{13,12},{... | collective-permute-start | bytes 147464 | tf_op jit(solution)/shard_map/ppermute | solution.py:399
  15.0 0.0 copy-done.2
  15.0 0.0 copy-done.3
  15.0 0.1 reshape.21.scale_ref
  15.2 0.1 reshape.20.label_ref
  15.3 0.4 middle_taps.1.middle_ref.refs_3_
  15.6 0.0 collective-permute-done.above_ref.refs_1_
  15.7 4.0 %collective-permute-done.1.below_ref.refs_2_ = bf16[192,128]{1,0:T(8,128)(2,1)S(1)} collective-permute-done((bf16[192,128]{1,0:T(8,128)(2,1)S(1)}, bf16[192,128]{1,0:T(8,128)(2,1)S(1)}, u32[]{:S(2)}, u32[]{:S(2)}) %collective-permute-start.1) | collective-permute-done | bytes 49184 | tf_op jit(solution)/shard_map/ppermute | solution.py:399
  19.7 0.0 copy-done
  19.7 0.0 copy-done.1
  19.7 0.4 pointwise.1.own_ref.refs_0_
  20.1 2.4 %collective-permute-start.4 = (bf16[192,128]{1,0:T(8,128)(2,1)S(1)}, bf16[192,128]{1,0:T(8,128)(2,1)S(1)}, u32[]{:S(2)}, u32[]{:S(2)}) collective-permute-start(bf16[192,128]{1,0:T(8,128)(2,1)S(1)} %pointwise.1.own_ref.refs_0_), channel_id=1, source_target_pairs={{0,2},{1,3},{2,0},{3,1},{4,6},{5,7},{6,4},{7,5},{8,10},{9,11},{10,... | collective-permute-start | bytes 147464 | tf_op jit(solution)/shard_map/ppermute | solution.py:415
  22.5 1.5 %collective-permute-start.3 = (bf16[192,128]{1,0:T(8,128)(2,1)S(1)}, bf16[192,128]{1,0:T(8,128)(2,1)S(1)}, u32[]{:S(2)}, u32[]{:S(2)}) collective-permute-start(bf16[192,128]{1,0:T(8,128)(2,1)S(1)} %pointwise.1.own_ref.refs_0_), channel_id=1, source_target_pairs={{0,3},{1,0},{2,1},{3,2},{4,7},{5,4},{6,5},{7,6},{8,11},{9,8},{10,9... | collective-permute-start | bytes 147464 | tf_op jit(solution)/shard_map/ppermute | solution.py:415
  24.0 0.6 %collective-permute-start.2 = (bf16[192,128]{1,0:T(8,128)(2,1)S(1)}, bf16[192,128]{1,0:T(8,128)(2,1)S(1)}, u32[]{:S(2)}, u32[]{:S(2)}) collective-permute-start(bf16[192,128]{1,0:T(8,128)(2,1)S(1)} %pointwise.1.own_ref.refs_0_), channel_id=1, source_target_pairs={{0,1},{1,2},{2,3},{3,0},{4,5},{5,6},{6,7},{7,4},{8,9},{9,10},{10,1... | collective-permute-start | bytes 147464 | tf_op jit(solution)/shard_map/ppermute | solution.py:415
  24.5 0.0 all-to-all-done.refs_4_.x_ref
  24.5 4.5 %all-to-all-start.1 = ((bf16[4,192,128]{2,1,0:T(8,128)(2,1)}), bf16[4,192,128]{2,1,0:T(8,128)(2,1)S(1)}, u32[]{:S(2)}, u32[]{:S(2)}) async-start(bf16[4,192,128]{2,1,0:T(8,128)(2,1)} %pass_on.1), calls=%async_computation.1 | async-start | bytes 393216 | tf_op jit(solution)/shard_map/all_to_all | solution.py:403
  29.1 0.0 collective-permute-done.4.refs_2_
  29.1 0.0 collective-permute-done.3.below_ref.refs_3_
  29.1 0.8 %collective-permute-done.2.above_ref.refs_1_ = bf16[192,128]{1,0:T(8,128)(2,1)S(1)} collective-permute-done((bf16[192,128]{1,0:T(8,128)(2,1)S(1)}, bf16[192,128]{1,0:T(8,128)(2,1)S(1)}, u32[]{:S(2)}, u32[]{:S(2)}) %collective-permute-start.2) | collective-permute-done | bytes 49184 | tf_op jit(solution)/shard_map/ppermute | solution.py:415
  29.9 0.7 %kernel_grad.3 = bf16[128,1152]{1,0:T(8,128)(2,1)S(1)} custom-call(bf16[4,192,128]{2,1,0:T(8,128)(2,1)S(1)} %all-to-all-done.refs_4_.x_ref, bf16[192,128]{1,0:T(8,128)(2,1)S(1)} %pointwise.1.own_ref.refs_0_, bf16[192,128]{1,0:T(8,128)(2,1)S(1)} %collective-permute-done.2.above_ref.refs_1_, bf16[192,128]{1,0:T(8,128)(2,1)S(1)} %collective-permute-done.4.refs_2_, ...), custom_call_target="tpu_custom_call" | custom-call | flops 226492416 | bytes 688128 | tf_op jit(solution)/shard_map/kernel_grad/pallas_call | solution.py:263
  30.6 0.1 collective-permute-start.5
  30.6 4.7 %all-to-all-done.1.x_ref = bf16[4,192,128]{2,1,0:T(8,128)(2,1)S(1)} async-done(((bf16[4,192,128]{2,1,0:T(8,128)(2,1)}), bf16[4,192,128]{2,1,0:T(8,128)(2,1)S(1)}, u32[]{:S(2)}, u32[]{:S(2)}) %all-to-all-start.1) | async-done | bytes 196640 | tf_op jit(solution)/shard_map/all_to_all | solution.py:403
  35.3 0.7 %kernel_grad.2.refs_0_ = f32[128,1152]{1,0:T(8,128)S(1)} custom-call(bf16[4,192,128]{2,1,0:T(8,128)(2,1)S(1)} %all-to-all-done.1.x_ref, bf16[192,128]{1,0:T(8,128)(2,1)S(1)} %pointwise.1.own_ref.refs_0_, bf16[192,128]{1,0:T(8,128)(2,1)S(1)} %collective-permute-done.2.above_ref.refs_1_, bf16[192,128]{1,0:T(8,128)(2,1)S(1)} %collective-permute-done.4.refs_2_, ...), custom_call_target="tpu_custom_call" | custom-call | flops 226492416 | bytes 688128 | tf_op jit(solution)/shard_map/kernel_grad/pallas_call | solution.py:263
  36.0 0.0 collective-permute-done.5.refs_1_
  36.0 0.1 split_up.1
  36.1 1.6 %collective-permute-start.6 = (bf16[32,1152]{1,0:T(8,128)(2,1)S(1)}, bf16[32,1152]{1,0:T(8,128)(2,1)S(1)}, u32[]{:S(2)}, u32[]{:S(2)}) collective-permute-start(bf16[32,1152]{1,0:T(8,128)(2,1)S(1)} %get-tuple-element.19), channel_id=1, source_target_pairs={{0,8},{4,12},{8,0},{12,4},{16,24},{20,28},{24,16},{28,20},{1,9},{5... | collective-permute-start | bytes 221192 | tf_op jit(solution)/shard_map/ppermute | solution.py:427
  37.6 1.5 %collective-permute-start.7 = (bf16[32,1152]{1,0:T(8,128)(2,1)S(1)}, bf16[32,1152]{1,0:T(8,128)(2,1)S(1)}, u32[]{:S(2)}, u32[]{:S(2)}) collective-permute-start(bf16[32,1152]{1,0:T(8,128)(2,1)S(1)} %get-tuple-element.20), channel_id=1, source_target_pairs={{0,16},{4,20},{8,24},{12,28},{16,0},{20,4},{24,8},{28,12},{1,17},{... | collective-permute-start | bytes 221192 | tf_op jit(solution)/shard_map/ppermute | solution.py:427
  39.1 0.5 %collective-permute-start.8 = (bf16[32,1152]{1,0:T(8,128)(2,1)S(1)}, bf16[32,1152]{1,0:T(8,128)(2,1)S(1)}, u32[]{:S(2)}, u32[]{:S(2)}) collective-permute-start(bf16[32,1152]{1,0:T(8,128)(2,1)S(1)} %get-tuple-element.21), channel_id=1, source_target_pairs={{0,24},{4,28},{8,16},{12,20},{16,8},{20,12},{24,0},{28,4},{1,25},{... | collective-permute-start | bytes 221192 | tf_op jit(solution)/shard_map/ppermute | solution.py:427
  39.6 2.6 %feature_grad.1 = f32[192,1024]{1,0:T(8,128)} custom-call(bf16[192,128]{1,0:T(8,128)(2,1)S(1)} %pointwise.1.own_ref.refs_0_, bf16[192,128]{1,0:T(8,128)(2,1)S(1)} %collective-permute-done.2.above_ref.refs_1_, bf16[192,128]{1,0:T(8,128)(2,1)S(1)} %collective-permute-done.3.below_ref.refs_3_, bf16[9,1024,128]{2,1,0:T(8,128)(2,1)S(1)} %get-tuple-element.13.w_ref), custom_call_target="tpu_custom_call" | custom-call | flops 452984832 | bytes 3145728 | tf_op jit(solution)/shard_map/feature_grad/pallas_call | solution.py:355
  42.2 0.0 collective-permute-done.6.refs_1_
  42.2 0.0 collective-permute-done.7.refs_2_
  42.2 2.2 %collective-permute-done.8.refs_3_ = bf16[32,1152]{1,0:T(8,128)(2,1)S(1)} collective-permute-done((bf16[32,1152]{1,0:T(8,128)(2,1)S(1)}, bf16[32,1152]{1,0:T(8,128)(2,1)S(1)}, u32[]{:S(2)}, u32[]{:S(2)}) %collective-permute-start.8) | collective-permute-done | bytes 73760 | tf_op jit(solution)/shard_map/ppermute | solution.py:427
  44.4 0.7 %final_sum.1 = f32[288,128]{1,0:T(8,128)} custom-call(bf16[32,1152]{1,0:T(8,128)(2,1)S(1)} %get-tuple-element.18.refs_0_, bf16[32,1152]{1,0:T(8,128)(2,1)S(1)} %collective-permute-done.6.refs_1_, bf16[32,1152]{1,0:T(8,128)(2,1)S(1)} %collective-permute-done.7.refs_2_, bf16[32,1152]{1,0:T(8,128)(2,1)S(1)} %collective-permute-done.8.refs_3_), custom_call_target="tpu_custom_call" | custom-call | tf_op jit(solution)/shard_map/final_sum/pallas_call | solution.py:323
  (3 shorter events, 0.0 us)
Async XLA Ops:
  0.6 14.3 %copy-start.2 = (s32[1,6,32]{2,0,1:T(1,128)S(1)}, s32[1,6,32]{2,0,1:T(1,128)}, u32[]{:S(2)}) copy-start(s32[1,6,32]{2,0,1:T(1,128)} %param.7) | copy-start | bytes 2308
  0.6 14.4 %copy-start.3 = (s32[1,6,32]{2,0,1:T(1,128)S(1)}, s32[1,6,32]{2,0,1:T(1,128)}, u32[]{:S(2)}) copy-start(s32[1,6,32]{2,0,1:T(1,128)} %param.8) | copy-start | bytes 2308
  2.8 21.7 %all-to-all-start = ((bf16[4,192,128]{2,1,0:T(8,128)(2,1)}), bf16[4,192,128]{2,1,0:T(8,128)(2,1)S(1)}, u32[]{:S(2)}, u32[]{:S(2)}) async-start(bf16[4,192,128]{2,1,0:T(8,128)(2,1)} %get-tuple-element.17), calls=%async_computation | async-start | bytes 393216 | tf_op jit(solution)/shard_map/all_to_all | solution.py:396
  9.2 10.5 %copy-start = (bf16[128,3]{0,1:T(4,128)(2,1)S(1)}, bf16[128,3]{0,1:T(4,128)(2,1)}, u32[]{:S(2)}) copy-start(bf16[128,3]{0,1:T(4,128)(2,1)} %param.11) | copy-start | bytes 2308
  9.2 10.5 %copy-start.1 = (f32[128]{0:T(128)S(1)}, f32[128]{0:T(128)}, u32[]{:S(2)}) copy-start(f32[128]{0:T(128)} %param.10) | copy-start | bytes 1540
  9.7 5.9 %collective-permute-start = (bf16[192,128]{1,0:T(8,128)(2,1)S(1)}, bf16[192,128]{1,0:T(8,128)(2,1)S(1)}, u32[]{:S(2)}, u32[]{:S(2)}) collective-permute-start(bf16[192,128]{1,0:T(8,128)(2,1)S(1)} %get-tuple-element.15), channel_id=1, source_target_pairs={{0,1},{1,2},{2,3},{4,5},{5,6},{6,7},{8,9},{9,10},{10,11},{12,13},{... | collective-permute-start | bytes 147464 | tf_op jit(solution)/shard_map/ppermute | solution.py:398
  13.7 6.0 %collective-permute-start.1 = (bf16[192,128]{1,0:T(8,128)(2,1)S(1)}, bf16[192,128]{1,0:T(8,128)(2,1)S(1)}, u32[]{:S(2)}, u32[]{:S(2)}) collective-permute-start(bf16[192,128]{1,0:T(8,128)(2,1)S(1)} %get-tuple-element.14.after_ref), channel_id=1, source_target_pairs={{1,0},{2,1},{3,2},{5,4},{6,5},{7,6},{9,8},{10,9},{11,10},{13,12},{... | collective-permute-start | bytes 147464 | tf_op jit(solution)/shard_map/ppermute | solution.py:399
  20.1 9.0 %collective-permute-start.4 = (bf16[192,128]{1,0:T(8,128)(2,1)S(1)}, bf16[192,128]{1,0:T(8,128)(2,1)S(1)}, u32[]{:S(2)}, u32[]{:S(2)}) collective-permute-start(bf16[192,128]{1,0:T(8,128)(2,1)S(1)} %pointwise.1.own_ref.refs_0_), channel_id=1, source_target_pairs={{0,2},{1,3},{2,0},{3,1},{4,6},{5,7},{6,4},{7,5},{8,10},{9,11},{10,... | collective-permute-start | bytes 147464 | tf_op jit(solution)/shard_map/ppermute | solution.py:415
  22.5 6.6 %collective-permute-start.3 = (bf16[192,128]{1,0:T(8,128)(2,1)S(1)}, bf16[192,128]{1,0:T(8,128)(2,1)S(1)}, u32[]{:S(2)}, u32[]{:S(2)}) collective-permute-start(bf16[192,128]{1,0:T(8,128)(2,1)S(1)} %pointwise.1.own_ref.refs_0_), channel_id=1, source_target_pairs={{0,3},{1,0},{2,1},{3,2},{4,7},{5,4},{6,5},{7,6},{8,11},{9,8},{10,9... | collective-permute-start | bytes 147464 | tf_op jit(solution)/shard_map/ppermute | solution.py:415
  24.0 5.9 %collective-permute-start.2 = (bf16[192,128]{1,0:T(8,128)(2,1)S(1)}, bf16[192,128]{1,0:T(8,128)(2,1)S(1)}, u32[]{:S(2)}, u32[]{:S(2)}) collective-permute-start(bf16[192,128]{1,0:T(8,128)(2,1)S(1)} %pointwise.1.own_ref.refs_0_), channel_id=1, source_target_pairs={{0,1},{1,2},{2,3},{3,0},{4,5},{5,6},{6,7},{7,4},{8,9},{9,10},{10,1... | collective-permute-start | bytes 147464 | tf_op jit(solution)/shard_map/ppermute | solution.py:415
  24.5 10.8 %all-to-all-start.1 = ((bf16[4,192,128]{2,1,0:T(8,128)(2,1)}), bf16[4,192,128]{2,1,0:T(8,128)(2,1)S(1)}, u32[]{:S(2)}, u32[]{:S(2)}) async-start(bf16[4,192,128]{2,1,0:T(8,128)(2,1)} %pass_on.1), calls=%async_computation.1 | async-start | bytes 393216 | tf_op jit(solution)/shard_map/all_to_all | solution.py:403
  30.6 5.4 %collective-permute-start.5 = (bf16[128,1152]{1,0:T(8,128)(2,1)S(1)}, bf16[128,1152]{1,0:T(8,128)(2,1)S(1)}, u32[]{:S(2)}, u32[]{:S(2)}) collective-permute-start(bf16[128,1152]{1,0:T(8,128)(2,1)S(1)} %kernel_grad.3), channel_id=1, source_target_pairs={{0,4},{4,0},{8,12},{12,8},{16,20},{20,16},{24,28},{28,24},{1,5},{5... | collective-permute-start | bytes 884744 | tf_op jit(solution)/shard_map/ppermute | solution.py:421
  36.1 6.2 %collective-permute-start.6 = (bf16[32,1152]{1,0:T(8,128)(2,1)S(1)}, bf16[32,1152]{1,0:T(8,128)(2,1)S(1)}, u32[]{:S(2)}, u32[]{:S(2)}) collective-permute-start(bf16[32,1152]{1,0:T(8,128)(2,1)S(1)} %get-tuple-element.19), channel_id=1, source_target_pairs={{0,8},{4,12},{8,0},{12,4},{16,24},{20,28},{24,16},{28,20},{1,9},{5... | collective-permute-start | bytes 221192 | tf_op jit(solution)/shard_map/ppermute | solution.py:427
  37.6 4.6 %collective-permute-start.7 = (bf16[32,1152]{1,0:T(8,128)(2,1)S(1)}, bf16[32,1152]{1,0:T(8,128)(2,1)S(1)}, u32[]{:S(2)}, u32[]{:S(2)}) collective-permute-start(bf16[32,1152]{1,0:T(8,128)(2,1)S(1)} %get-tuple-element.20), channel_id=1, source_target_pairs={{0,16},{4,20},{8,24},{12,28},{16,0},{20,4},{24,8},{28,12},{1,17},{... | collective-permute-start | bytes 221192 | tf_op jit(solution)/shard_map/ppermute | solution.py:427
  39.1 5.3 %collective-permute-start.8 = (bf16[32,1152]{1,0:T(8,128)(2,1)S(1)}, bf16[32,1152]{1,0:T(8,128)(2,1)S(1)}, u32[]{:S(2)}, u32[]{:S(2)}) collective-permute-start(bf16[32,1152]{1,0:T(8,128)(2,1)S(1)} %get-tuple-element.21), channel_id=1, source_target_pairs={{0,24},{4,28},{8,16},{12,20},{16,8},{20,12},{24,0},{28,4},{1,25},{... | collective-permute-start | bytes 221192 | tf_op jit(solution)/shard_map/ppermute | solution.py:427

commit v9 on v8

--- a/solution.py
+++ b/solution.py
@@ -49,41 +49,38 @@
     )
 
 
-def load_kernel(replicas, cover, x_hbm, w_hbm, *refs):
-    x_ref, w_ref, *outs = refs[: len(refs) - 4]
-    room, x_sem, w_sem, out_sems = refs[len(refs) - 4 :]
+def load_kernel(replicas, cover, x_hbm, w_hbm, x_ref, w_ref, *refs):
+    *outs, room, x_sem, w_sem, out_sems = refs
     x_load = pltpu.make_async_copy(x_hbm, x_ref, x_sem)
     w_load = pltpu.make_async_copy(w_hbm, w_ref, w_sem)
     x_load.start()
     w_load.start()
     x_load.wait()
     copies = []
-    if outs:
-        parts, bands, _, lanes = room.shape
+    for out in outs:
+        bands = room.shape[0]
         x = x_ref[...]
-        order = replica_order(replicas)
-        for p in range(parts):
-            for s in range(bands):
-                blocks = order[p * (replicas // parts) : (p + 1) * (replicas // parts)]
-                room[p, s] = jnp.concatenate(
-                    [x[:, (d * bands + s) * cover : (d * bands + s + 1) * cover] for d in blocks],
-                    axis=1,
-                )
-        for k, out in enumerate(outs):
-            part = lax.rem(lax.axis_index("dp") + parts - 1 - k, parts)
-            copies.append(pltpu.make_async_copy(room.at[part], out, out_sems.at[k]))
+        for s in range(bands):
+            room[s] = jnp.concatenate(
+                [
+                    x[:, (d * bands + s) * cover : (d * bands + s + 1) * cover]
+                    for d in replica_order(replicas)
+                ],
+                axis=1,
+            )
+            copies.append(pltpu.make_async_copy(room.at[s], out.at[s], out_sems.at[s]))
             copies[-1].start()
     w_load.wait()
     for copy in copies:
         copy.wait()
 
 
-def load(flat, weight, bands, replicas, cover, parts, blocks):
+def load(flat, weight, bands, replicas, cover, blocks):
     pixels, channels = flat.shape
     hbm = pl.BlockSpec(memory_space=pltpu.HBM)
     vmem = pl.BlockSpec(memory_space=pltpu.VMEM)
-    shape = (bands, pixels, replicas // parts * cover)
-    count = parts if blocks else 0
+    shape = (bands, pixels, replicas * cover)
+    count = 1 if blocks else 0
     return pl.pallas_call(
         functools.partial(load_kernel, replicas, cover),
         in_specs=[hbm, hbm],
@@ -94,10 +91,10 @@
         ]
         + [pltpu.HBM(shape, flat.dtype)] * count,
         scratch_shapes=[
-            pltpu.VMEM((parts,) + shape, flat.dtype),
+            pltpu.VMEM(shape, flat.dtype),
             pltpu.SemaphoreType.DMA,
             pltpu.SemaphoreType.DMA,
-            pltpu.SemaphoreType.DMA((parts,)),
+            pltpu.SemaphoreType.DMA((bands,)),
         ],
         compiler_params=pltpu.CompilerParams(vmem_limit_bytes=VMEM_LIMIT),
         cost_estimate=pl.CostEstimate(
@@ -133,23 +130,6 @@
         ),
         name="halo",
     )(flat, weight)
-
-
-def pass_on_kernel(*refs):
-    del refs
-
-
-def pass_on(x, *after):
-    hbm = pl.BlockSpec(memory_space=pltpu.HBM)
-    return pl.pallas_call(
-        pass_on_kernel,
-        in_specs=[hbm] + [pl.BlockSpec(memory_space=pltpu.VMEM)] * len(after),
-        out_specs=hbm,
-        out_shape=pltpu.HBM(x.shape, x.dtype),
-        input_output_aliases={0: 0},
-        compiler_params=pltpu.CompilerParams(vmem_limit_bytes=VMEM_LIMIT),
-        name="pass_on",
-    )(pltpu.with_memory_space_constraint(x, pltpu.HBM), *after)
 
 
 def middle_kernel(columns, reach, x_ref, w_ref, after_ref, out_ref):
@@ -180,8 +160,9 @@
 
 
 def pointwise_kernel(
-    middle_ref, above_ref, below_ref, bias_ref, class_ref, label_ref, scale_ref, out_ref
+    middle_ref, above_ref, below_ref, bias_ref, class_ref, label_ref, scale_ref, after_ref, out_ref
 ):
+    del after_ref
     pixels, width = middle_ref.shape
     edge = above_ref.shape[0]
     above = above_ref[...].astype(jnp.float32)
@@ -210,10 +191,12 @@
     out_ref[...] = gradient.astype(out_ref.dtype)
 
 
-def pointwise(middle, above, below, bias, classes, labels, scale):
+def pointwise(middle, above, below, bias, classes, labels, scale, after):
     pixels, width = middle.shape
+    vmem = pl.BlockSpec(memory_space=pltpu.VMEM)
     return pl.pallas_call(
         pointwise_kernel,
+        in_specs=[vmem] * 7 + [pl.BlockSpec(memory_space=pl.ANY)],
         out_shape=jax.ShapeDtypeStruct((pixels, width), jnp.bfloat16),
         compiler_params=pltpu.CompilerParams(vmem_limit_bytes=VMEM_LIMIT),
         cost_estimate=pl.CostEstimate(
@@ -222,7 +205,7 @@
             transcendentals=pixels * width,
         ),
         name="pointwise",
-    )(middle, above, below, bias, classes, labels, scale)
+    )(middle, above, below, bias, classes, labels, scale, after)
 
 
 def shifted_taps(gradient, columns, reach):
@@ -233,17 +216,25 @@
     )
 
 
-def kernel_grad_kernel(columns, reach, x_ref, *refs):
+def kernel_grad_kernel(columns, reach, parts, other, x_ref, *refs):
     *g_refs, out_ref, taps = refs
-    bands, pixels, extra = x_ref.shape
+    bands, pixels, lanes = x_ref.shape
     width = g_refs[0].shape[1]
     total = bands * pixels
     edge = reach * columns
+    extra = lanes // parts
     band = lax.axis_index("space")
     for k, g_ref in enumerate(g_refs):
         first = lax.rem(band + bands - k, bands) * pixels
         taps[pl.ds(pl.multiple_of(first, 16), pixels)] = shifted_taps(g_ref[...], columns, reach)
-    features = x_ref[...].reshape(total, extra)
+    part = lax.rem(lax.axis_index("dp") + other, parts)
+    if extra % 128 == 0:
+        features = x_ref[:, :, pl.ds(pl.multiple_of(part * extra, 128), extra)]
+    else:
+        features = x_ref[:, :, :extra]
+        for k in range(1, parts):
+            features = jnp.where(part == k, x_ref[:, :, k * extra : (k + 1) * extra], features)
+    features = features.reshape(total, extra)
     for a in range(3):
         if a == 0:
             left, right = features[: total - edge], taps[edge:]
@@ -257,11 +248,12 @@
         out_ref[:, 3 * a * width : 3 * (a + 1) * width] = block.astype(out_ref.dtype)
 
 
-def kernel_grad(features, gradients, columns, reach, dtype):
-    bands, pixels, extra = features.shape
+def kernel_grad(features, gradients, columns, reach, parts, other, dtype):
+    bands, pixels, lanes = features.shape
+    extra = lanes // parts
     width = gradients[0].shape[1]
     return pl.pallas_call(
-        functools.partial(kernel_grad_kernel, columns, reach),
+        functools.partial(kernel_grad_kernel, columns, reach, parts, other),
         out_shape=jax.ShapeDtypeStruct((extra, 9 * width), dtype),
         scratch_shapes=[pltpu.VMEM((bands * pixels, 3 * width), jnp.bfloat16)],
         compiler_params=pltpu.CompilerParams(vmem_limit_bytes=VMEM_LIMIT),
@@ -383,24 +375,16 @@
     even = block_rows % taps == 0
     parts = 2 if replicas % 2 == 0 else 1
     count = replicas // parts
-    flat, weight, *split = load(flat, weight, bands, replicas, cover, parts, even)
+    flat, weight, *split = load(flat, weight, bands, replicas, cover, even)
     if not even:
         order = jnp.array([c for line in picks for c in line], jnp.int32)
-        blocks = jnp.take(flat, order, axis=1).reshape(pixels, bands, parts, count * cover)
-        blocks = blocks.transpose(2, 1, 0, 3)
-        me = lax.axis_index("dp")
-        split = [
-            lax.dynamic_index_in_dim(blocks, (me + parts - 1 - k) % parts, keepdims=False)
-            for k in range(parts)
-        ]
-    whole = [lax.all_to_all(split[0], "space", 0, 0)]
+        blocks = jnp.take(flat, order, axis=1).reshape(pixels, bands, replicas * cover)
+        split = [blocks.transpose(1, 0, 2)]
+    whole = lax.all_to_all(split[0], "space", 0, 0)
     down, up = halo(flat, weight, columns, reach)
     above = lax.ppermute(down, "space", [(i, i + 1) for i in range(bands - 1)])
     below = lax.ppermute(up, "space", [(i + 1, i) for i in range(bands - 1)])
     middle = middle_taps(flat, weight, up, columns, reach)
-    for blocks in split[1:]:
-        held = pass_on(blocks, above, below, middle, whole[0])
-        whole.append(lax.all_to_all(held, "space", 0, 0))
 
     gradient = pointwise(
         middle,
@@ -410,14 +394,15 @@
         class_weight.T,
         labels.reshape(pixels, 1),
         pixel_weight.reshape(pixels, 1),
+        whole,
     )
     gradients = [gradient] + [
         lax.ppermute(gradient, "space", [(i, (i + k) % bands) for i in range(bands)])
         for k in range(1, bands)
     ]
-    terms = [kernel_grad(whole[-1], gradients, columns, reach, jnp.float32)]
+    terms = [kernel_grad(whole, gradients, columns, reach, parts, 0, jnp.float32)]
     if parts == 2:
-        theirs = kernel_grad(whole[0], gradients, columns, reach, jnp.bfloat16)
+        theirs = kernel_grad(whole, gradients, columns, reach, parts, 1, jnp.bfloat16)
         terms.append(lax.ppermute(theirs, "dp", [(i, i ^ 1) for i in range(replicas)]))
     if cover % 16 == 0 and count <= 8:
         blocks = split_up(terms, parts, count)

time: 45.5 us -> 42.4 us (0.932)
  starting transfers between devices: 24.2 us -> 19 us
  Pallas kernels: 8.21 us -> 9.5 us
  waiting for transfers between devices: 11.7 us -> 12.4 us
    all_to_all x2 -> x1, starting transfers between devices: 10.9 us -> 6.33 us  [on_device(): whole = lax.all_to_all(split[0], 'space', 0, 0)]
    all_to_all x2 -> x1, waiting for transfers between devices: 4.69 us -> 0.52 us  [on_device(): whole = lax.all_to_all(split[0], 'space', 0, 0)]
    ppermute x3, waiting for transfers between devices: 0.82 us -> 4.98 us  [on_device(): lax.ppermute(gradient, 'space', [(i, (i + k) % bands) for i in range(band...]
    ppermute x1, waiting for transfers between devices: 0.01 us -> 0.91 us  [on_device(): lax.ppermute(theirs, 'dp', [(i, i ^ 1) for i in range(replicas)])]
    pallas_call x1, Pallas kernels: 0.36 us -> 1.16 us  [middle_taps(): pl.pallas_call(functools.partial(middle_kernel, columns, reach), in_specs...]
    pallas_call x1, Pallas kernels: 0.57 us -> 1.18 us  [halo(): pl.pallas_call(functools.partial(halo_kernel, columns, reach), out_shape=...]
    ppermute x3, starting transfers between devices: 4.45 us -> 3.88 us  [on_device(): lax.ppermute(gradient, 'space', [(i, (i + k) % bands) for i in range(band...]
    pallas_call x4 -> x3, Pallas kernels: 1.72 us -> 1.71 us  [the longest x2 1.3 us: kernel_grad(): pl.pallas_call(functools.partial(kernel_grad_kernel, columns, reach, part...]
  transfers between devices with their start and end apart: 11 -> 10, of which waited for: 4 -> 6; matrix products, arithmetic and copies ran while one was open for 1% -> 1% of each run, Pallas kernels for 12% -> 13%
where the time goes in v9:
time: 42.4 us; the launch traced here: 42 us
  starting transfers between devices  19 us (45%)
  waiting for transfers between devices  12.4 us (29%)
  Pallas kernels  9.5 us (22%)
  between operations  0.76 us (2%)
    all_to_all x1, starting transfers between devices, on_device(): whole = lax.all_to_all(split[0], 'space', 0, 0)  6.33 us
    ppermute x3, waiting for transfers between devices, on_device(): lax.ppermute(gradient, 'space', [(i, (i + k) % bands) for i in range(band...  4.98 us
    ppermute x1, starting transfers between devices, on_device(): above = lax.ppermute(down, 'space', [(i, i + 1) for i in range(bands - 1)])  3.92 us
    ppermute x3, starting transfers between devices, on_device(): lax.ppermute(gradient, 'space', [(i, (i + k) % bands) for i in range(band...  3.88 us
    ppermute x1, waiting for transfers between devices, on_device(): below = lax.ppermute(up, 'space', [(i + 1, i) for i in range(bands - 1)])  3.86 us
    ppermute x3, starting transfers between devices, on_device(): came.append(lax.ppermute(blocks[k], 'dp', pairs))  3.55 us
    pallas_call x1, Pallas kernels, feature_grad(): pl.pallas_call(functools.partial(feature_grad_kernel, columns, reach, ban...  2.61 us
    ppermute x3, waiting for transfers between devices, on_device(): came.append(lax.ppermute(blocks[k], 'dp', pairs))  2.16 us
  transfers between devices with their start and end apart: 10, of which 6 were waited for; matrix products, arithmetic and copies ran while one was open for 1% of the time, Pallas kernels for 13%

profile of v9, /device:TPU:0, one launch (start us, length us, event | category | flops | bytes accessed | tf_op | source)
XLA Modules:
  0.0 42.0 jit_solution(6653590897763238392)
XLA Ops:
  0.6 2.1 %load.1 = (bf16[192,1024]{1,0:T(8,128)(2,1)S(1)}, bf16[9,1024,128]{2,1,0:T(8,128)(2,1)S(1)}, bf16[4,192,256]{2,1,0:T(8,128)(2,1)}) custom-call(bf16[192,1024]{1,0:T(8,128)(2,1)} %bitcast.9, bf16[9,1024,128]{2,1,0:T(8,128)(2,1)} %bitcast.7), custom_call_target="tpu_custom_call" | custom-call | bytes 3145728 | tf_op jit(solution)/shard_map/load/pallas_call | solution.py:84
  2.7 0.0 copy-start.2
  2.7 0.0 copy-start.3
  2.7 6.3 %all-to-all-start = ((bf16[4,192,256]{2,1,0:T(8,128)(2,1)}), bf16[4,192,256]{2,1,0:T(8,128)(2,1)S(1)}, u32[]{:S(2)}, u32[]{:S(2)}) async-start(bf16[4,192,256]{2,1,0:T(8,128)(2,1)} %get-tuple-element.15), calls=%async_computation | async-start | bytes 786432 | tf_op jit(solution)/shard_map/all_to_all | solution.py:383
  9.1 0.0 copy-start
  9.1 0.0 copy-start.1
  9.1 1.2 %halo.1 = (bf16[192,128]{1,0:T(8,128)(2,1)}, bf16[192,128]{1,0:T(8,128)(2,1)}) custom-call(bf16[192,1024]{1,0:T(8,128)(2,1)S(1)} %get-tuple-element.11.x_ref, bf16[9,1024,128]{2,1,0:T(8,128)(2,1)S(1)} %get-tuple-element.12.w_ref), custom_call_target="tpu_custom_call" | custom-call | flops 301989888 | bytes 1966080 | tf_op jit(solution)/shard_map/halo/pallas_call | solution.py:122
  10.2 3.9 %collective-permute-start = (bf16[192,128]{1,0:T(8,128)(2,1)}, bf16[192,128]{1,0:T(8,128)(2,1)S(1)}, u32[]{:S(2)}, u32[]{:S(2)}) collective-permute-start(bf16[192,128]{1,0:T(8,128)(2,1)} %get-tuple-element.14), channel_id=1, source_target_pairs={{0,1},{1,2},{2,3},{4,5},{5,6},{6,7},{8,9},{9,10},{10,11},{12,13},{... | collective-permute-start | bytes 147464 | tf_op jit(solution)/shard_map/ppermute | solution.py:385
  14.2 1.3 %collective-permute-start.1 = (bf16[192,128]{1,0:T(8,128)(2,1)}, bf16[192,128]{1,0:T(8,128)(2,1)S(1)}, u32[]{:S(2)}, u32[]{:S(2)}) collective-permute-start(bf16[192,128]{1,0:T(8,128)(2,1)} %get-tuple-element.13.after_ref), channel_id=1, source_target_pairs={{1,0},{2,1},{3,2},{5,4},{6,5},{7,6},{9,8},{10,9},{11,10},{13,12},{... | collective-permute-start | bytes 147464 | tf_op jit(solution)/shard_map/ppermute | solution.py:386
  15.5 0.0 copy-done.2
  15.5 0.1 reshape.20.label_ref
  15.6 0.0 copy-done.3
  15.7 0.1 reshape.21.scale_ref
  15.8 1.2 %middle_taps.1.middle_ref = f32[192,128]{1,0:T(8,128)S(1)} custom-call(bf16[192,1024]{1,0:T(8,128)(2,1)S(1)} %get-tuple-element.11.x_ref, bf16[9,1024,128]{2,1,0:T(8,128)(2,1)S(1)} %get-tuple-element.12.w_ref, bf16[192,128]{1,0:T(8,128)(2,1)} %get-tuple-element.13.after_ref), custom_call_target="tpu_custom_call" | custom-call | flops 150994944 | bytes 1179648 | tf_op jit(solution)/shard_map/middle_taps/pallas_call | solution.py:148
  16.9 0.0 collective-permute-done.above_ref
  17.0 3.9 %collective-permute-done.1.below_ref = bf16[192,128]{1,0:T(8,128)(2,1)S(1)} collective-permute-done((bf16[192,128]{1,0:T(8,128)(2,1)}, bf16[192,128]{1,0:T(8,128)(2,1)S(1)}, u32[]{:S(2)}, u32[]{:S(2)}) %collective-permute-start.1) | collective-permute-done | bytes 49184 | tf_op jit(solution)/shard_map/ppermute | solution.py:386
  20.8 0.5 %all-to-all-done.after_ref.x_ref = bf16[4,192,256]{2,1,0:T(8,128)(2,1)S(1)} async-done(((bf16[4,192,256]{2,1,0:T(8,128)(2,1)}), bf16[4,192,256]{2,1,0:T(8,128)(2,1)S(1)}, u32[]{:S(2)}, u32[]{:S(2)}) %all-to-all-start) | async-done | bytes 393248 | tf_op jit(solution)/shard_map/all_to_all | solution.py:383
  21.3 0.0 copy-done
  21.3 0.0 copy-done.1
  21.3 0.4 pointwise.1.own_ref.refs_0_
  21.8 1.1 %collective-permute-start.2 = (bf16[192,128]{1,0:T(8,128)(2,1)S(1)}, bf16[192,128]{1,0:T(8,128)(2,1)S(1)}, u32[]{:S(2)}, u32[]{:S(2)}) collective-permute-start(bf16[192,128]{1,0:T(8,128)(2,1)S(1)} %pointwise.1.own_ref.refs_0_), channel_id=1, source_target_pairs={{0,1},{1,2},{2,3},{3,0},{4,5},{5,6},{6,7},{7,4},{8,9},{9,10},{10,1... | collective-permute-start | bytes 147464 | tf_op jit(solution)/shard_map/ppermute | solution.py:400
  22.8 2.8 %collective-permute-start.3 = (bf16[192,128]{1,0:T(8,128)(2,1)S(1)}, bf16[192,128]{1,0:T(8,128)(2,1)S(1)}, u32[]{:S(2)}, u32[]{:S(2)}) collective-permute-start(bf16[192,128]{1,0:T(8,128)(2,1)S(1)} %pointwise.1.own_ref.refs_0_), channel_id=1, source_target_pairs={{0,3},{1,0},{2,1},{3,2},{4,7},{5,4},{6,5},{7,6},{8,11},{9,8},{10,9... | collective-permute-start | bytes 147464 | tf_op jit(solution)/shard_map/ppermute | solution.py:400
  25.6 0.0 collective-permute-start.4
  25.6 2.2 %collective-permute-done.2.above_ref.refs_1_ = bf16[192,128]{1,0:T(8,128)(2,1)S(1)} collective-permute-done((bf16[192,128]{1,0:T(8,128)(2,1)S(1)}, bf16[192,128]{1,0:T(8,128)(2,1)S(1)}, u32[]{:S(2)}, u32[]{:S(2)}) %collective-permute-start.2) | collective-permute-done | bytes 49184 | tf_op jit(solution)/shard_map/ppermute | solution.py:400
  27.8 0.0 collective-permute-done.3.below_ref.refs_3_
  27.8 2.8 %collective-permute-done.4.refs_2_ = bf16[192,128]{1,0:T(8,128)(2,1)S(1)} collective-permute-done((bf16[192,128]{1,0:T(8,128)(2,1)S(1)}, bf16[192,128]{1,0:T(8,128)(2,1)S(1)}, u32[]{:S(2)}, u32[]{:S(2)}) %collective-permute-start.4) | collective-permute-done | bytes 49184 | tf_op jit(solution)/shard_map/ppermute | solution.py:400
  30.6 0.6 %kernel_grad.3 = bf16[128,1152]{1,0:T(8,128)(2,1)S(1)} custom-call(bf16[4,192,256]{2,1,0:T(8,128)(2,1)S(1)} %all-to-all-done.after_ref.x_ref, bf16[192,128]{1,0:T(8,128)(2,1)S(1)} %pointwise.1.own_ref.refs_0_, bf16[192,128]{1,0:T(8,128)(2,1)S(1)} %collective-permute-done.2.above_ref.refs_1_, bf16[192,128]{1,0:T(8,128)(2,1)S(1)} %collective-permute-done.4.refs_2_, ...), custom_call_target="tpu_custom_call" | custom-call | flops 226492416 | bytes 688128 | tf_op jit(solution)/shard_map/kernel_grad/pallas_call | solution.py:255
  31.3 0.1 collective-permute-start.5
  31.4 0.7 %kernel_grad.2.refs_0_ = f32[128,1152]{1,0:T(8,128)S(1)} custom-call(bf16[4,192,256]{2,1,0:T(8,128)(2,1)S(1)} %all-to-all-done.after_ref.x_ref, bf16[192,128]{1,0:T(8,128)(2,1)S(1)} %pointwise.1.own_ref.refs_0_, bf16[192,128]{1,0:T(8,128)(2,1)S(1)} %collective-permute-done.2.above_ref.refs_1_, bf16[192,128]{1,0:T(8,128)(2,1)S(1)} %collective-permute-done.4.refs_2_, ...), custom_call_target="tpu_custom_call" | custom-call | flops 226492416 | bytes 688128 | tf_op jit(solution)/shard_map/kernel_grad/pallas_call | solution.py:255
  32.0 0.9 %collective-permute-done.5.refs_1_ = bf16[128,1152]{1,0:T(8,128)(2,1)S(1)} collective-permute-done((bf16[128,1152]{1,0:T(8,128)(2,1)S(1)}, bf16[128,1152]{1,0:T(8,128)(2,1)S(1)}, u32[]{:S(2)}, u32[]{:S(2)}) %collective-permute-start.5) | collective-permute-done | bytes 294944 | tf_op jit(solution)/shard_map/ppermute | solution.py:406
  32.9 0.1 split_up.1
  33.0 1.6 %collective-permute-start.6 = (bf16[32,1152]{1,0:T(8,128)(2,1)S(1)}, bf16[32,1152]{1,0:T(8,128)(2,1)S(1)}, u32[]{:S(2)}, u32[]{:S(2)}) collective-permute-start(bf16[32,1152]{1,0:T(8,128)(2,1)S(1)} %get-tuple-element.17), channel_id=1, source_target_pairs={{0,8},{4,12},{8,0},{12,4},{16,24},{20,28},{24,16},{28,20},{1,9},{5... | collective-permute-start | bytes 221192 | tf_op jit(solution)/shard_map/ppermute | solution.py:412
  34.6 1.5 %collective-permute-start.7 = (bf16[32,1152]{1,0:T(8,128)(2,1)S(1)}, bf16[32,1152]{1,0:T(8,128)(2,1)S(1)}, u32[]{:S(2)}, u32[]{:S(2)}) collective-permute-start(bf16[32,1152]{1,0:T(8,128)(2,1)S(1)} %get-tuple-element.18), channel_id=1, source_target_pairs={{0,16},{4,20},{8,24},{12,28},{16,0},{20,4},{24,8},{28,12},{1,17},{... | collective-permute-start | bytes 221192 | tf_op jit(solution)/shard_map/ppermute | solution.py:412
  36.1 0.5 %collective-permute-start.8 = (bf16[32,1152]{1,0:T(8,128)(2,1)S(1)}, bf16[32,1152]{1,0:T(8,128)(2,1)S(1)}, u32[]{:S(2)}, u32[]{:S(2)}) collective-permute-start(bf16[32,1152]{1,0:T(8,128)(2,1)S(1)} %get-tuple-element.19), channel_id=1, source_target_pairs={{0,24},{4,28},{8,16},{12,20},{16,8},{20,12},{24,0},{28,4},{1,25},{... | collective-permute-start | bytes 221192 | tf_op jit(solution)/shard_map/ppermute | solution.py:412
  36.6 2.6 %feature_grad.1 = f32[192,1024]{1,0:T(8,128)} custom-call(bf16[192,128]{1,0:T(8,128)(2,1)S(1)} %pointwise.1.own_ref.refs_0_, bf16[192,128]{1,0:T(8,128)(2,1)S(1)} %collective-permute-done.2.above_ref.refs_1_, bf16[192,128]{1,0:T(8,128)(2,1)S(1)} %collective-permute-done.3.below_ref.refs_3_, bf16[9,1024,128]{2,1,0:T(8,128)(2,1)S(1)} %get-tuple-element.12.w_ref), custom_call_target="tpu_custom_call" | custom-call | flops 452984832 | bytes 3145728 | tf_op jit(solution)/shard_map/feature_grad/pallas_call | solution.py:347
  39.2 0.0 collective-permute-done.6.refs_1_
  39.2 0.0 collective-permute-done.7.refs_2_
  39.2 2.2 %collective-permute-done.8.refs_3_ = bf16[32,1152]{1,0:T(8,128)(2,1)S(1)} collective-permute-done((bf16[32,1152]{1,0:T(8,128)(2,1)S(1)}, bf16[32,1152]{1,0:T(8,128)(2,1)S(1)}, u32[]{:S(2)}, u32[]{:S(2)}) %collective-permute-start.8) | collective-permute-done | bytes 73760 | tf_op jit(solution)/shard_map/ppermute | solution.py:412
  41.3 0.7 %final_sum.1 = f32[288,128]{1,0:T(8,128)} custom-call(bf16[32,1152]{1,0:T(8,128)(2,1)S(1)} %get-tuple-element.16.refs_0_, bf16[32,1152]{1,0:T(8,128)(2,1)S(1)} %collective-permute-done.6.refs_1_, bf16[32,1152]{1,0:T(8,128)(2,1)S(1)} %collective-permute-done.7.refs_2_, bf16[32,1152]{1,0:T(8,128)(2,1)S(1)} %collective-permute-done.8.refs_3_), custom_call_target="tpu_custom_call" | custom-call | tf_op jit(solution)/shard_map/final_sum/pallas_call | solution.py:315
  (2 shorter events, 0.0 us)
Async XLA Ops:
  2.7 12.8 %copy-start.2 = (s32[1,6,32]{2,0,1:T(1,128)S(1)}, s32[1,6,32]{2,0,1:T(1,128)}, u32[]{:S(2)}) copy-start(s32[1,6,32]{2,0,1:T(1,128)} %param.7) | copy-start | bytes 2308
  2.7 12.9 %copy-start.3 = (s32[1,6,32]{2,0,1:T(1,128)S(1)}, s32[1,6,32]{2,0,1:T(1,128)}, u32[]{:S(2)}) copy-start(s32[1,6,32]{2,0,1:T(1,128)} %param.8) | copy-start | bytes 2308
  2.7 18.6 %all-to-all-start = ((bf16[4,192,256]{2,1,0:T(8,128)(2,1)}), bf16[4,192,256]{2,1,0:T(8,128)(2,1)S(1)}, u32[]{:S(2)}, u32[]{:S(2)}) async-start(bf16[4,192,256]{2,1,0:T(8,128)(2,1)} %get-tuple-element.15), calls=%async_computation | async-start | bytes 786432 | tf_op jit(solution)/shard_map/all_to_all | solution.py:383
  9.1 12.3 %copy-start = (bf16[128,3]{0,1:T(4,128)(2,1)S(1)}, bf16[128,3]{0,1:T(4,128)(2,1)}, u32[]{:S(2)}) copy-start(bf16[128,3]{0,1:T(4,128)(2,1)} %param.11) | copy-start | bytes 2308
  9.1 12.3 %copy-start.1 = (f32[128]{0:T(128)S(1)}, f32[128]{0:T(128)}, u32[]{:S(2)}) copy-start(f32[128]{0:T(128)} %param.10) | copy-start | bytes 1540
  10.2 6.7 %collective-permute-start = (bf16[192,128]{1,0:T(8,128)(2,1)}, bf16[192,128]{1,0:T(8,128)(2,1)S(1)}, u32[]{:S(2)}, u32[]{:S(2)}) collective-permute-start(bf16[192,128]{1,0:T(8,128)(2,1)} %get-tuple-element.14), channel_id=1, source_target_pairs={{0,1},{1,2},{2,3},{4,5},{5,6},{6,7},{8,9},{9,10},{10,11},{12,13},{... | collective-permute-start | bytes 147464 | tf_op jit(solution)/shard_map/ppermute | solution.py:385
  14.2 6.7 %collective-permute-start.1 = (bf16[192,128]{1,0:T(8,128)(2,1)}, bf16[192,128]{1,0:T(8,128)(2,1)S(1)}, u32[]{:S(2)}, u32[]{:S(2)}) collective-permute-start(bf16[192,128]{1,0:T(8,128)(2,1)} %get-tuple-element.13.after_ref), channel_id=1, source_target_pairs={{1,0},{2,1},{3,2},{5,4},{6,5},{7,6},{9,8},{10,9},{11,10},{13,12},{... | collective-permute-start | bytes 147464 | tf_op jit(solution)/shard_map/ppermute | solution.py:386
  21.8 6.0 %collective-permute-start.2 = (bf16[192,128]{1,0:T(8,128)(2,1)S(1)}, bf16[192,128]{1,0:T(8,128)(2,1)S(1)}, u32[]{:S(2)}, u32[]{:S(2)}) collective-permute-start(bf16[192,128]{1,0:T(8,128)(2,1)S(1)} %pointwise.1.own_ref.refs_0_), channel_id=1, source_target_pairs={{0,1},{1,2},{2,3},{3,0},{4,5},{5,6},{6,7},{7,4},{8,9},{9,10},{10,1... | collective-permute-start | bytes 147464 | tf_op jit(solution)/shard_map/ppermute | solution.py:400
  22.8 5.0 %collective-permute-start.3 = (bf16[192,128]{1,0:T(8,128)(2,1)S(1)}, bf16[192,128]{1,0:T(8,128)(2,1)S(1)}, u32[]{:S(2)}, u32[]{:S(2)}) collective-permute-start(bf16[192,128]{1,0:T(8,128)(2,1)S(1)} %pointwise.1.own_ref.refs_0_), channel_id=1, source_target_pairs={{0,3},{1,0},{2,1},{3,2},{4,7},{5,4},{6,5},{7,6},{8,11},{9,8},{10,9... | collective-permute-start | bytes 147464 | tf_op jit(solution)/shard_map/ppermute | solution.py:400
  25.6 5.0 %collective-permute-start.4 = (bf16[192,128]{1,0:T(8,128)(2,1)S(1)}, bf16[192,128]{1,0:T(8,128)(2,1)S(1)}, u32[]{:S(2)}, u32[]{:S(2)}) collective-permute-start(bf16[192,128]{1,0:T(8,128)(2,1)S(1)} %pointwise.1.own_ref.refs_0_), channel_id=1, source_target_pairs={{0,2},{1,3},{2,0},{3,1},{4,6},{5,7},{6,4},{7,5},{8,10},{9,11},{10,... | collective-permute-start | bytes 147464 | tf_op jit(solution)/shard_map/ppermute | solution.py:400
  31.3 1.6 %collective-permute-start.5 = (bf16[128,1152]{1,0:T(8,128)(2,1)S(1)}, bf16[128,1152]{1,0:T(8,128)(2,1)S(1)}, u32[]{:S(2)}, u32[]{:S(2)}) collective-permute-start(bf16[128,1152]{1,0:T(8,128)(2,1)S(1)} %kernel_grad.3), channel_id=1, source_target_pairs={{0,4},{4,0},{8,12},{12,8},{16,20},{20,16},{24,28},{28,24},{1,5},{5... | collective-permute-start | bytes 884744 | tf_op jit(solution)/shard_map/ppermute | solution.py:406
  33.0 6.2 %collective-permute-start.6 = (bf16[32,1152]{1,0:T(8,128)(2,1)S(1)}, bf16[32,1152]{1,0:T(8,128)(2,1)S(1)}, u32[]{:S(2)}, u32[]{:S(2)}) collective-permute-start(bf16[32,1152]{1,0:T(8,128)(2,1)S(1)} %get-tuple-element.17), channel_id=1, source_target_pairs={{0,8},{4,12},{8,0},{12,4},{16,24},{20,28},{24,16},{28,20},{1,9},{5... | collective-permute-start | bytes 221192 | tf_op jit(solution)/shard_map/ppermute | solution.py:412
  34.6 4.6 %collective-permute-start.7 = (bf16[32,1152]{1,0:T(8,128)(2,1)S(1)}, bf16[32,1152]{1,0:T(8,128)(2,1)S(1)}, u32[]{:S(2)}, u32[]{:S(2)}) collective-permute-start(bf16[32,1152]{1,0:T(8,128)(2,1)S(1)} %get-tuple-element.18), channel_id=1, source_target_pairs={{0,16},{4,20},{8,24},{12,28},{16,0},{20,4},{24,8},{28,12},{1,17},{... | collective-permute-start | bytes 221192 | tf_op jit(solution)/shard_map/ppermute | solution.py:412
  36.1 5.3 %collective-permute-start.8 = (bf16[32,1152]{1,0:T(8,128)(2,1)S(1)}, bf16[32,1152]{1,0:T(8,128)(2,1)S(1)}, u32[]{:S(2)}, u32[]{:S(2)}) collective-permute-start(bf16[32,1152]{1,0:T(8,128)(2,1)S(1)} %get-tuple-element.19), channel_id=1, source_target_pairs={{0,24},{4,28},{8,16},{12,20},{16,8},{20,12},{24,0},{28,4},{1,25},{... | collective-permute-start | bytes 221192 | tf_op jit(solution)/shard_map/ppermute | solution.py:412

commit v10 on v9

--- a/solution.py
+++ b/solution.py
@@ -49,17 +49,21 @@
     )
 
 
-def load_kernel(replicas, cover, x_hbm, w_hbm, x_ref, w_ref, *refs):
-    *outs, room, x_sem, w_sem, out_sems = refs
+def forward_kernel(columns, reach, replicas, cover, x_hbm, w_hbm, *refs):
+    w_ref, down_ref, up_ref, own_ref, *outs, x_ref, room, x_sem, w_sems, out_sems = refs
+    pixels, edge = x_ref.shape[0], reach * columns
     x_load = pltpu.make_async_copy(x_hbm, x_ref, x_sem)
-    w_load = pltpu.make_async_copy(w_hbm, w_ref, w_sem)
     x_load.start()
-    w_load.start()
+    w_loads = {}
+    for a in (0, 2, 1):
+        rows = pl.ds(3 * a, 3)
+        w_loads[a] = pltpu.make_async_copy(w_hbm.at[rows], w_ref.at[rows], w_sems.at[a])
+        w_loads[a].start()
     x_load.wait()
+    x = x_ref[...]
     copies = []
     for out in outs:
         bands = room.shape[0]
-        x = x_ref[...]
         for s in range(bands):
             room[s] = jnp.concatenate(
                 [
@@ -70,99 +74,100 @@
             )
             copies.append(pltpu.make_async_copy(room.at[s], out.at[s], out_sems.at[s]))
             copies[-1].start()
-    w_load.wait()
+    w_loads[0].wait()
+    part = tap_row(x, w_ref, 0, columns, reach)
+    down_ref[...] = part[pixels - edge :].astype(down_ref.dtype)
+    if pixels > edge:
+        none = jnp.zeros((edge, part.shape[1]), jnp.float32)
+        own_ref[...] = jnp.concatenate([none, part[: pixels - edge]], axis=0)
+    w_loads[2].wait()
+    part = tap_row(x, w_ref, 2, columns, reach)
+    up_ref[...] = part[:edge].astype(up_ref.dtype)
+    if pixels > edge:
+        own_ref[: pixels - edge] += part[edge:]
+    w_loads[1].wait()
+    part = tap_row(x, w_ref, 1, columns, reach)
+    if pixels > edge:
+        own_ref[...] += part
+    else:
+        own_ref[...] = part
     for copy in copies:
         copy.wait()
 
 
-def load(flat, weight, bands, replicas, cover, blocks):
+def forward(flat, weight, columns, reach, bands, replicas, cover, blocks):
     pixels, channels = flat.shape
+    taps, _, width = weight.shape
+    edge = reach * columns
     hbm = pl.BlockSpec(memory_space=pltpu.HBM)
     vmem = pl.BlockSpec(memory_space=pltpu.VMEM)
     shape = (bands, pixels, replicas * cover)
     count = 1 if blocks else 0
     return pl.pallas_call(
-        functools.partial(load_kernel, replicas, cover),
+        functools.partial(forward_kernel, columns, reach, replicas, cover),
         in_specs=[hbm, hbm],
-        out_specs=[vmem, vmem] + [hbm] * count,
+        out_specs=[vmem] * 4 + [hbm] * count,
         out_shape=[
-            pltpu.VMEM(flat.shape, flat.dtype),
             pltpu.VMEM(weight.shape, weight.dtype),
+            pltpu.VMEM((edge, width), jnp.bfloat16),
+            pltpu.VMEM((edge, width), jnp.bfloat16),
+            pltpu.VMEM((pixels, width), jnp.float32),
         ]
         + [pltpu.HBM(shape, flat.dtype)] * count,
         scratch_shapes=[
+            pltpu.VMEM(flat.shape, flat.dtype),
             pltpu.VMEM(shape, flat.dtype),
             pltpu.SemaphoreType.DMA,
-            pltpu.SemaphoreType.DMA,
+            pltpu.SemaphoreType.DMA((3,)),
             pltpu.SemaphoreType.DMA((bands,)),
         ],
         compiler_params=pltpu.CompilerParams(vmem_limit_bytes=VMEM_LIMIT),
         cost_estimate=pl.CostEstimate(
-            flops=0,
+            flops=2 * pixels * channels * taps * width,
             bytes_accessed=2 * weight.size + 4 * pixels * channels,
             transcendentals=0,
         ),
-        name="load",
+        name="forward",
     )(
         pltpu.with_memory_space_constraint(flat, pltpu.HBM),
         pltpu.with_memory_space_constraint(weight, pltpu.HBM),
     )
 
 
-def halo_kernel(columns, reach, x_ref, w_ref, down_ref, up_ref):
-    pixels, edge = x_ref.shape[0], reach * columns
-    down_ref[...] = tap_row(x_ref[pixels - edge :], w_ref, 0, columns, reach).astype(down_ref.dtype)
-    up_ref[...] = tap_row(x_ref[:edge], w_ref, 2, columns, reach).astype(up_ref.dtype)
-
-
-def halo(flat, weight, columns, reach):
-    _, channels = flat.shape
-    width = weight.shape[2]
-    edge = reach * columns
-    return pl.pallas_call(
-        functools.partial(halo_kernel, columns, reach),
-        out_shape=[jax.ShapeDtypeStruct((edge, width), jnp.bfloat16)] * 2,
-        compiler_params=pltpu.CompilerParams(vmem_limit_bytes=VMEM_LIMIT),
-        cost_estimate=pl.CostEstimate(
-            flops=12 * edge * channels * width,
-            bytes_accessed=12 * channels * width + 2 * edge * channels,
-            transcendentals=0,
-        ),
-        name="halo",
-    )(flat, weight)
-
-
-def middle_kernel(columns, reach, x_ref, w_ref, after_ref, out_ref):
-    del after_ref
-    pixels, edge = x_ref.shape[0], reach * columns
-    out_ref[...] = tap_row(x_ref[...], w_ref, 1, columns, reach)
-    if pixels > edge:
-        out_ref[edge:] += tap_row(x_ref[: pixels - edge], w_ref, 0, columns, reach)
-        out_ref[: pixels - edge] += tap_row(x_ref[edge:], w_ref, 2, columns, reach)
-
-
-def middle_taps(flat, weight, after, columns, reach):
-    pixels, channels = flat.shape
-    width = weight.shape[2]
-    vmem = pl.BlockSpec(memory_space=pltpu.VMEM)
-    return pl.pallas_call(
-        functools.partial(middle_kernel, columns, reach),
-        in_specs=[vmem, vmem, vmem],
-        out_shape=jax.ShapeDtypeStruct((pixels, width), jnp.float32),
-        compiler_params=pltpu.CompilerParams(vmem_limit_bytes=VMEM_LIMIT),
-        cost_estimate=pl.CostEstimate(
-            flops=6 * pixels * channels * width,
-            bytes_accessed=6 * channels * width + 2 * pixels * channels,
-            transcendentals=0,
-        ),
-        name="middle_taps",
-    )(flat, weight, after)
+def pass_on_kernel(*refs):
+    del refs
+
+
+def pass_on(x, *after):
+    hbm = pl.BlockSpec(memory_space=pltpu.HBM)
+    return pl.pallas_call(
+        pass_on_kernel,
+        in_specs=[hbm] + [pl.BlockSpec(memory_space=pltpu.VMEM)] * len(after),
+        out_specs=hbm,
+        out_shape=pltpu.HBM(x.shape, x.dtype),
+        input_output_aliases={0: 0},
+        compiler_params=pltpu.CompilerParams(vmem_limit_bytes=VMEM_LIMIT),
+        name="pass_on",
+    )(pltpu.with_memory_space_constraint(x, pltpu.HBM), *after)
+
+
+def as_column(rows_ref):
+    values = rows_ref[...].astype(jnp.float32)
+    rows, columns = values.shape
+    shape = (columns, columns)
+    same = lax.broadcasted_iota(jnp.int32, shape, 0) == lax.broadcasted_iota(jnp.int32, shape, 1)
+    return jnp.concatenate(
+        [
+            jnp.sum(jnp.where(same, values[r : r + 1], 0.0), axis=1, keepdims=True)
+            for r in range(rows)
+        ],
+        axis=0,
+    )
 
 
 def pointwise_kernel(
-    middle_ref, above_ref, below_ref, bias_ref, class_ref, label_ref, scale_ref, after_ref, out_ref
+    middle_ref, above_ref, below_ref, bias_ref, class_ref, label_ref, scale_ref, out_ref
 ):
-    del after_ref
     pixels, width = middle_ref.shape
     edge = above_ref.shape[0]
     above = above_ref[...].astype(jnp.float32)
@@ -180,9 +185,9 @@
     )
     exponent = jnp.exp(logits)
     chances = exponent / jnp.sum(exponent, axis=1, keepdims=True)
-    index = lax.broadcasted_iota(jnp.int32, chances.shape, 1)
-    onehot = jnp.where(label_ref[...] == index, 1.0, 0.0)
-    grad_logits = scale_ref[...].astype(jnp.float32) * (chances - onehot)
+    index = lax.broadcasted_iota(jnp.int32, chances.shape, 1).astype(jnp.float32)
+    onehot = jnp.where(as_column(label_ref) == index, 1.0, 0.0)
+    grad_logits = as_column(scale_ref) * (chances - onehot)
     wide = classes.astype(jnp.float32)
     hidden_grad = sum(
         grad_logits[:, k : k + 1] * wide[k : k + 1] for k in range(classes.shape[0])
@@ -191,12 +196,10 @@
     out_ref[...] = gradient.astype(out_ref.dtype)
 
 
-def pointwise(middle, above, below, bias, classes, labels, scale, after):
+def pointwise(middle, above, below, bias, classes, labels, scale):
     pixels, width = middle.shape
-    vmem = pl.BlockSpec(memory_space=pltpu.VMEM)
     return pl.pallas_call(
         pointwise_kernel,
-        in_specs=[vmem] * 7 + [pl.BlockSpec(memory_space=pl.ANY)],
         out_shape=jax.ShapeDtypeStruct((pixels, width), jnp.bfloat16),
         compiler_params=pltpu.CompilerParams(vmem_limit_bytes=VMEM_LIMIT),
         cost_estimate=pl.CostEstimate(
@@ -205,7 +208,7 @@
             transcendentals=pixels * width,
         ),
         name="pointwise",
-    )(middle, above, below, bias, classes, labels, scale, after)
+    )(middle, above, below, bias, classes, labels, scale)
 
 
 def shifted_taps(gradient, columns, reach):
@@ -375,16 +378,16 @@
     even = block_rows % taps == 0
     parts = 2 if replicas % 2 == 0 else 1
     count = replicas // parts
-    flat, weight, *split = load(flat, weight, bands, replicas, cover, even)
+    weight, down, up, middle, *split = forward(
+        flat, weight, columns, reach, bands, replicas, cover, even
+    )
     if not even:
         order = jnp.array([c for line in picks for c in line], jnp.int32)
         blocks = jnp.take(flat, order, axis=1).reshape(pixels, bands, replicas * cover)
         split = [blocks.transpose(1, 0, 2)]
-    whole = lax.all_to_all(split[0], "space", 0, 0)
-    down, up = halo(flat, weight, columns, reach)
     above = lax.ppermute(down, "space", [(i, i + 1) for i in range(bands - 1)])
     below = lax.ppermute(up, "space", [(i + 1, i) for i in range(bands - 1)])
-    middle = middle_taps(flat, weight, up, columns, reach)
+    whole = lax.all_to_all(pass_on(split[0], above), "space", 0, 0)
 
     gradient = pointwise(
         middle,
@@ -392,9 +395,8 @@
         below,
         conv_bias.reshape(1, width),
         class_weight.T,
-        labels.reshape(pixels, 1),
-        pixel_weight.reshape(pixels, 1),
-        whole,
+        labels.reshape(band_rows, columns),
+        pixel_weight.reshape(band_rows, columns),
     )
     gradients = [gradient] + [
         lax.ppermute(gradient, "space", [(i, (i + k) % bands) for i in range(bands)])

time: 42.4 us -> 49.1 us (1.16)
  waiting for transfers between devices: 12.4 us -> 17.5 us
  starting transfers between devices: 19 us -> 22.4 us
  Pallas kernels: 9.5 us -> 8.2 us
    ppermute x3, starting transfers between devices: 3.88 us -> 6.95 us  [on_device(): lax.ppermute(gradient, 'space', [(i, (i + k) % bands) for i in range(band...]
    ppermute x1, waiting for transfers between devices: 3.86 us -> 6.84 us  [on_device(): below = lax.ppermute(up, 'space', [(i + 1, i) for i in range(bands - 1)])]
    ppermute x1, waiting for transfers between devices: 0.01 us -> 1.73 us  [on_device(): above = lax.ppermute(down, 'space', [(i, i + 1) for i in range(bands - 1)])]
    pallas_call x4 -> x3, Pallas kernels: 4.82 us -> 3.5 us  [the longest x1 3.07 us: forward(): pl.pallas_call(functools.partial(forward_kernel, columns, reach, replicas...]
    ppermute x1, starting transfers between devices: 3.92 us -> 4.93 us  [on_device(): above = lax.ppermute(down, 'space', [(i, i + 1) for i in range(bands - 1)])]
    ppermute x3, waiting for transfers between devices: 4.98 us -> 5.88 us  [on_device(): lax.ppermute(gradient, 'space', [(i, (i + k) % bands) for i in range(band...]
    all_to_all x1, starting transfers between devices: 6.33 us -> 5.64 us  [on_device(): whole = lax.all_to_all(pass_on(split[0], above), 'space', 0, 0)]
    all_to_all x1, waiting for transfers between devices: 0.52 us -> 0.01 us  [on_device(): whole = lax.all_to_all(pass_on(split[0], above), 'space', 0, 0)]
  transfers between devices with their start and end apart: 10 -> 10, of which waited for: 6 -> 6; matrix products, arithmetic and copies ran while one was open for 1% -> 0% of each run, Pallas kernels for 13% -> 8%
where the time goes in v10:
time: 49.1 us; the launch traced here: 48.9 us
  starting transfers between devices  22.4 us (46%)
  waiting for transfers between devices  17.5 us (36%)
  Pallas kernels  8.2 us (17%)
  between operations  0.75 us (2%)
    ppermute x3, starting transfers between devices, on_device(): lax.ppermute(gradient, 'space', [(i, (i + k) % bands) for i in range(band...  6.95 us
    ppermute x1, waiting for transfers between devices, on_device(): below = lax.ppermute(up, 'space', [(i + 1, i) for i in range(bands - 1)])  6.84 us
    ppermute x3, waiting for transfers between devices, on_device(): lax.ppermute(gradient, 'space', [(i, (i + k) % bands) for i in range(band...  5.88 us
    all_to_all x1, starting transfers between devices, on_device(): whole = lax.all_to_all(pass_on(split[0], above), 'space', 0, 0)  5.64 us
    ppermute x1, starting transfers between devices, on_device(): above = lax.ppermute(down, 'space', [(i, i + 1) for i in range(bands - 1)])  4.93 us
    ppermute x3, starting transfers between devices, on_device(): came.append(lax.ppermute(blocks[k], 'dp', pairs))  3.55 us
    pallas_call x1, Pallas kernels, forward(): pl.pallas_call(functools.partial(forward_kernel, columns, reach, replicas...  3.07 us
    pallas_call x1, Pallas kernels, feature_grad(): pl.pallas_call(functools.partial(feature_grad_kernel, columns, reach, ban...  2.62 us
  transfers between devices with their start and end apart: 10, of which 6 were waited for; matrix products, arithmetic and copies ran while one was open for 0% of the time, Pallas kernels for 8%

profile of v10, /device:TPU:0, one launch (start us, length us, event | category | flops | bytes accessed | tf_op | source)
XLA Modules:
  0.0 48.9 jit_solution(8911422405071012733)
XLA Ops:
  0.6 0.0 copy-start.2
  0.6 0.0 copy-start.3
  0.7 0.0 copy-start
  0.7 0.0 copy-start.1
  0.7 3.1 %forward.1 = (bf16[9,1024,128]{2,1,0:T(8,128)(2,1)S(1)}, bf16[192,128]{1,0:T(8,128)(2,1)S(1)}, bf16[192,128]{1,0:T(8,128)(2,1)S(1)}, f32[192,128]{1,0:T(8,128)S(1)}, bf16[4,192,256]{2,1,0:T(8,128)(2,1)}) custom-call(bf16[192,1024]{1,0:T(8,128)(2,1)} %bitcast.13, bf16[9,1024,128]{2,1,0:T(8,128)(2,1)} %bitcast.11), custom_call_target="tpu_custom_call" | custom-call | flops 452984832 | bytes 3145728 | tf_op jit(solution)/shard_map/forward/pallas_call | solution.py:106
  3.8 4.9 %collective-permute-start = (bf16[192,128]{1,0:T(8,128)(2,1)S(1)}, bf16[192,128]{1,0:T(8,128)(2,1)S(1)}, u32[]{:S(2)}, u32[]{:S(2)}) collective-permute-start(bf16[192,128]{1,0:T(8,128)(2,1)S(1)} %get-tuple-element.12), channel_id=1, source_target_pairs={{0,1},{1,2},{2,3},{4,5},{5,6},{6,7},{8,9},{9,10},{10,11},{12,13},{... | collective-permute-start | bytes 147464 | tf_op jit(solution)/shard_map/ppermute | solution.py:388
  8.7 1.7 %collective-permute-done.above_ref.refs_1_ = bf16[192,128]{1,0:T(8,128)(2,1)S(1)} collective-permute-done((bf16[192,128]{1,0:T(8,128)(2,1)S(1)}, bf16[192,128]{1,0:T(8,128)(2,1)S(1)}, u32[]{:S(2)}, u32[]{:S(2)}) %collective-permute-start) | collective-permute-done | bytes 49184 | tf_op jit(solution)/shard_map/ppermute | solution.py:388
  10.4 5.6 %all-to-all-start = ((bf16[4,192,256]{2,1,0:T(8,128)(2,1)}), bf16[4,192,256]{2,1,0:T(8,128)(2,1)S(1)}, u32[]{:S(2)}, u32[]{:S(2)}) async-start(bf16[4,192,256]{2,1,0:T(8,128)(2,1)} %pass_on.1), calls=%async_computation | async-start | bytes 786432 | tf_op jit(solution)/shard_map/all_to_all | solution.py:390
  16.1 1.3 %collective-permute-start.1 = (bf16[192,128]{1,0:T(8,128)(2,1)S(1)}, bf16[192,128]{1,0:T(8,128)(2,1)S(1)}, u32[]{:S(2)}, u32[]{:S(2)}) collective-permute-start(bf16[192,128]{1,0:T(8,128)(2,1)S(1)} %get-tuple-element.13), channel_id=1, source_target_pairs={{1,0},{2,1},{3,2},{5,4},{6,5},{7,6},{9,8},{10,9},{11,10},{13,12},{... | collective-permute-start | bytes 147464 | tf_op jit(solution)/shard_map/ppermute | solution.py:389
  17.3 0.0 copy-done.2
  17.4 0.0 copy-done.3
  17.4 6.8 %collective-permute-done.1.below_ref = bf16[192,128]{1,0:T(8,128)(2,1)S(1)} collective-permute-done((bf16[192,128]{1,0:T(8,128)(2,1)S(1)}, bf16[192,128]{1,0:T(8,128)(2,1)S(1)}, u32[]{:S(2)}, u32[]{:S(2)}) %collective-permute-start.1) | collective-permute-done | bytes 49184 | tf_op jit(solution)/shard_map/ppermute | solution.py:389
  24.2 0.0 copy-done
  24.2 0.0 copy-done.1
  24.2 0.4 pointwise.1.own_ref.refs_0_
  24.7 3.6 %collective-permute-start.4 = (bf16[192,128]{1,0:T(8,128)(2,1)S(1)}, bf16[192,128]{1,0:T(8,128)(2,1)S(1)}, u32[]{:S(2)}, u32[]{:S(2)}) collective-permute-start(bf16[192,128]{1,0:T(8,128)(2,1)S(1)} %pointwise.1.own_ref.refs_0_), channel_id=1, source_target_pairs={{0,2},{1,3},{2,0},{3,1},{4,6},{5,7},{6,4},{7,5},{8,10},{9,11},{10,... | collective-permute-start | bytes 147464 | tf_op jit(solution)/shard_map/ppermute | solution.py:402
  28.2 3.4 %collective-permute-start.3 = (bf16[192,128]{1,0:T(8,128)(2,1)S(1)}, bf16[192,128]{1,0:T(8,128)(2,1)S(1)}, u32[]{:S(2)}, u32[]{:S(2)}) collective-permute-start(bf16[192,128]{1,0:T(8,128)(2,1)S(1)} %pointwise.1.own_ref.refs_0_), channel_id=1, source_target_pairs={{0,3},{1,0},{2,1},{3,2},{4,7},{5,4},{6,5},{7,6},{8,11},{9,8},{10,9... | collective-permute-start | bytes 147464 | tf_op jit(solution)/shard_map/ppermute | solution.py:402
  31.6 0.0 collective-permute-start.2
  31.6 0.0 collective-permute-done.4.refs_2_
  31.6 1.7 %collective-permute-done.3.below_ref.refs_3_ = bf16[192,128]{1,0:T(8,128)(2,1)S(1)} collective-permute-done((bf16[192,128]{1,0:T(8,128)(2,1)S(1)}, bf16[192,128]{1,0:T(8,128)(2,1)S(1)}, u32[]{:S(2)}, u32[]{:S(2)}) %collective-permute-start.3) | collective-permute-done | bytes 49184 | tf_op jit(solution)/shard_map/ppermute | solution.py:402
  33.4 4.1 %collective-permute-done.2.above_ref.refs_1_ = bf16[192,128]{1,0:T(8,128)(2,1)S(1)} collective-permute-done((bf16[192,128]{1,0:T(8,128)(2,1)S(1)}, bf16[192,128]{1,0:T(8,128)(2,1)S(1)}, u32[]{:S(2)}, u32[]{:S(2)}) %collective-permute-start.2) | collective-permute-done | bytes 49184 | tf_op jit(solution)/shard_map/ppermute | solution.py:402
  37.5 0.0 all-to-all-done.x_ref
  37.5 0.7 %kernel_grad.3 = bf16[128,1152]{1,0:T(8,128)(2,1)S(1)} custom-call(bf16[4,192,256]{2,1,0:T(8,128)(2,1)S(1)} %all-to-all-done.x_ref, bf16[192,128]{1,0:T(8,128)(2,1)S(1)} %pointwise.1.own_ref.refs_0_, bf16[192,128]{1,0:T(8,128)(2,1)S(1)} %collective-permute-done.2.above_ref.refs_1_, bf16[192,128]{1,0:T(8,128)(2,1)S(1)} %collective-permute-done.4.refs_2_, ...), custom_call_target="tpu_custom_call" | custom-call | flops 226492416 | bytes 688128 | tf_op jit(solution)/shard_map/kernel_grad/pallas_call | solution.py:258
  38.1 0.1 collective-permute-start.5
  38.2 0.7 %kernel_grad.2.refs_0_ = f32[128,1152]{1,0:T(8,128)S(1)} custom-call(bf16[4,192,256]{2,1,0:T(8,128)(2,1)S(1)} %all-to-all-done.x_ref, bf16[192,128]{1,0:T(8,128)(2,1)S(1)} %pointwise.1.own_ref.refs_0_, bf16[192,128]{1,0:T(8,128)(2,1)S(1)} %collective-permute-done.2.above_ref.refs_1_, bf16[192,128]{1,0:T(8,128)(2,1)S(1)} %collective-permute-done.4.refs_2_, ...), custom_call_target="tpu_custom_call" | custom-call | flops 226492416 | bytes 688128 | tf_op jit(solution)/shard_map/kernel_grad/pallas_call | solution.py:258
  38.9 0.9 %collective-permute-done.5.refs_1_ = bf16[128,1152]{1,0:T(8,128)(2,1)S(1)} collective-permute-done((bf16[128,1152]{1,0:T(8,128)(2,1)S(1)}, bf16[128,1152]{1,0:T(8,128)(2,1)S(1)}, u32[]{:S(2)}, u32[]{:S(2)}) %collective-permute-start.5) | collective-permute-done | bytes 294944 | tf_op jit(solution)/shard_map/ppermute | solution.py:408
  39.8 0.1 split_up.1
  39.9 1.6 %collective-permute-start.6 = (bf16[32,1152]{1,0:T(8,128)(2,1)S(1)}, bf16[32,1152]{1,0:T(8,128)(2,1)S(1)}, u32[]{:S(2)}, u32[]{:S(2)}) collective-permute-start(bf16[32,1152]{1,0:T(8,128)(2,1)S(1)} %get-tuple-element.17), channel_id=1, source_target_pairs={{0,8},{4,12},{8,0},{12,4},{16,24},{20,28},{24,16},{28,20},{1,9},{5... | collective-permute-start | bytes 221192 | tf_op jit(solution)/shard_map/ppermute | solution.py:414
  41.4 1.5 %collective-permute-start.7 = (bf16[32,1152]{1,0:T(8,128)(2,1)S(1)}, bf16[32,1152]{1,0:T(8,128)(2,1)S(1)}, u32[]{:S(2)}, u32[]{:S(2)}) collective-permute-start(bf16[32,1152]{1,0:T(8,128)(2,1)S(1)} %get-tuple-element.18), channel_id=1, source_target_pairs={{0,16},{4,20},{8,24},{12,28},{16,0},{20,4},{24,8},{28,12},{1,17},{... | collective-permute-start | bytes 221192 | tf_op jit(solution)/shard_map/ppermute | solution.py:414
  42.9 0.5 collective-permute-start.8
  43.4 2.6 %feature_grad.1 = f32[192,1024]{1,0:T(8,128)} custom-call(bf16[192,128]{1,0:T(8,128)(2,1)S(1)} %pointwise.1.own_ref.refs_0_, bf16[192,128]{1,0:T(8,128)(2,1)S(1)} %collective-permute-done.2.above_ref.refs_1_, bf16[192,128]{1,0:T(8,128)(2,1)S(1)} %collective-permute-done.3.below_ref.refs_3_, bf16[9,1024,128]{2,1,0:T(8,128)(2,1)S(1)} %get-tuple-element.14.w_ref), custom_call_target="tpu_custom_call" | custom-call | flops 452984832 | bytes 3145728 | tf_op jit(solution)/shard_map/feature_grad/pallas_call | solution.py:350
  46.0 0.0 collective-permute-done.6.refs_1_
  46.0 0.0 collective-permute-done.7.refs_2_
  46.0 2.1 %collective-permute-done.8.refs_3_ = bf16[32,1152]{1,0:T(8,128)(2,1)S(1)} collective-permute-done((bf16[32,1152]{1,0:T(8,128)(2,1)S(1)}, bf16[32,1152]{1,0:T(8,128)(2,1)S(1)}, u32[]{:S(2)}, u32[]{:S(2)}) %collective-permute-start.8) | collective-permute-done | bytes 73760 | tf_op jit(solution)/shard_map/ppermute | solution.py:414
  48.2 0.7 %final_sum.1 = f32[288,128]{1,0:T(8,128)} custom-call(bf16[32,1152]{1,0:T(8,128)(2,1)S(1)} %get-tuple-element.16.refs_0_, bf16[32,1152]{1,0:T(8,128)(2,1)S(1)} %collective-permute-done.6.refs_1_, bf16[32,1152]{1,0:T(8,128)(2,1)S(1)} %collective-permute-done.7.refs_2_, bf16[32,1152]{1,0:T(8,128)(2,1)S(1)} %collective-permute-done.8.refs_3_), custom_call_target="tpu_custom_call" | custom-call | tf_op jit(solution)/shard_map/final_sum/pallas_call | solution.py:318
  (2 shorter events, 0.0 us)
Async XLA Ops:
  0.6 16.7 %copy-start.2 = (s32[1,6,32]{2,0,1:T(1,128)S(1)}, s32[1,6,32]{2,0,1:T(1,128)}, u32[]{:S(2)}) copy-start(s32[1,6,32]{2,0,1:T(1,128)} %param.8) | copy-start | bytes 2308
  0.6 16.7 %copy-start.3 = (s32[1,6,32]{2,0,1:T(1,128)S(1)}, s32[1,6,32]{2,0,1:T(1,128)}, u32[]{:S(2)}) copy-start(s32[1,6,32]{2,0,1:T(1,128)} %param.7) | copy-start | bytes 2308
  0.7 23.6 %copy-start = (bf16[128,3]{0,1:T(4,128)(2,1)S(1)}, bf16[128,3]{0,1:T(4,128)(2,1)}, u32[]{:S(2)}) copy-start(bf16[128,3]{0,1:T(4,128)(2,1)} %param.11) | copy-start | bytes 2308
  0.7 23.6 %copy-start.1 = (f32[128]{0:T(128)S(1)}, f32[128]{0:T(128)}, u32[]{:S(2)}) copy-start(f32[128]{0:T(128)} %param.10) | copy-start | bytes 1540
  3.8 6.7 %collective-permute-start = (bf16[192,128]{1,0:T(8,128)(2,1)S(1)}, bf16[192,128]{1,0:T(8,128)(2,1)S(1)}, u32[]{:S(2)}, u32[]{:S(2)}) collective-permute-start(bf16[192,128]{1,0:T(8,128)(2,1)S(1)} %get-tuple-element.12), channel_id=1, source_target_pairs={{0,1},{1,2},{2,3},{4,5},{5,6},{6,7},{8,9},{9,10},{10,11},{12,13},{... | collective-permute-start | bytes 147464 | tf_op jit(solution)/shard_map/ppermute | solution.py:388
  10.4 27.1 %all-to-all-start = ((bf16[4,192,256]{2,1,0:T(8,128)(2,1)}), bf16[4,192,256]{2,1,0:T(8,128)(2,1)S(1)}, u32[]{:S(2)}, u32[]{:S(2)}) async-start(bf16[4,192,256]{2,1,0:T(8,128)(2,1)} %pass_on.1), calls=%async_computation | async-start | bytes 786432 | tf_op jit(solution)/shard_map/all_to_all | solution.py:390
  16.1 8.2 %collective-permute-start.1 = (bf16[192,128]{1,0:T(8,128)(2,1)S(1)}, bf16[192,128]{1,0:T(8,128)(2,1)S(1)}, u32[]{:S(2)}, u32[]{:S(2)}) collective-permute-start(bf16[192,128]{1,0:T(8,128)(2,1)S(1)} %get-tuple-element.13), channel_id=1, source_target_pairs={{1,0},{2,1},{3,2},{5,4},{6,5},{7,6},{9,8},{10,9},{11,10},{13,12},{... | collective-permute-start | bytes 147464 | tf_op jit(solution)/shard_map/ppermute | solution.py:389
  24.7 7.0 %collective-permute-start.4 = (bf16[192,128]{1,0:T(8,128)(2,1)S(1)}, bf16[192,128]{1,0:T(8,128)(2,1)S(1)}, u32[]{:S(2)}, u32[]{:S(2)}) collective-permute-start(bf16[192,128]{1,0:T(8,128)(2,1)S(1)} %pointwise.1.own_ref.refs_0_), channel_id=1, source_target_pairs={{0,2},{1,3},{2,0},{3,1},{4,6},{5,7},{6,4},{7,5},{8,10},{9,11},{10,... | collective-permute-start | bytes 147464 | tf_op jit(solution)/shard_map/ppermute | solution.py:402
  28.2 5.1 %collective-permute-start.3 = (bf16[192,128]{1,0:T(8,128)(2,1)S(1)}, bf16[192,128]{1,0:T(8,128)(2,1)S(1)}, u32[]{:S(2)}, u32[]{:S(2)}) collective-permute-start(bf16[192,128]{1,0:T(8,128)(2,1)S(1)} %pointwise.1.own_ref.refs_0_), channel_id=1, source_target_pairs={{0,3},{1,0},{2,1},{3,2},{4,7},{5,4},{6,5},{7,6},{8,11},{9,8},{10,9... | collective-permute-start | bytes 147464 | tf_op jit(solution)/shard_map/ppermute | solution.py:402
  31.6 5.9 %collective-permute-start.2 = (bf16[192,128]{1,0:T(8,128)(2,1)S(1)}, bf16[192,128]{1,0:T(8,128)(2,1)S(1)}, u32[]{:S(2)}, u32[]{:S(2)}) collective-permute-start(bf16[192,128]{1,0:T(8,128)(2,1)S(1)} %pointwise.1.own_ref.refs_0_), channel_id=1, source_target_pairs={{0,1},{1,2},{2,3},{3,0},{4,5},{5,6},{6,7},{7,4},{8,9},{9,10},{10,1... | collective-permute-start | bytes 147464 | tf_op jit(solution)/shard_map/ppermute | solution.py:402
  38.1 1.6 %collective-permute-start.5 = (bf16[128,1152]{1,0:T(8,128)(2,1)S(1)}, bf16[128,1152]{1,0:T(8,128)(2,1)S(1)}, u32[]{:S(2)}, u32[]{:S(2)}) collective-permute-start(bf16[128,1152]{1,0:T(8,128)(2,1)S(1)} %kernel_grad.3), channel_id=1, source_target_pairs={{0,4},{4,0},{8,12},{12,8},{16,20},{20,16},{24,28},{28,24},{1,5},{5... | collective-permute-start | bytes 884744 | tf_op jit(solution)/shard_map/ppermute | solution.py:408
  39.9 6.2 %collective-permute-start.6 = (bf16[32,1152]{1,0:T(8,128)(2,1)S(1)}, bf16[32,1152]{1,0:T(8,128)(2,1)S(1)}, u32[]{:S(2)}, u32[]{:S(2)}) collective-permute-start(bf16[32,1152]{1,0:T(8,128)(2,1)S(1)} %get-tuple-element.17), channel_id=1, source_target_pairs={{0,8},{4,12},{8,0},{12,4},{16,24},{20,28},{24,16},{28,20},{1,9},{5... | collective-permute-start | bytes 221192 | tf_op jit(solution)/shard_map/ppermute | solution.py:414
  41.4 4.6 %collective-permute-start.7 = (bf16[32,1152]{1,0:T(8,128)(2,1)S(1)}, bf16[32,1152]{1,0:T(8,128)(2,1)S(1)}, u32[]{:S(2)}, u32[]{:S(2)}) collective-permute-start(bf16[32,1152]{1,0:T(8,128)(2,1)S(1)} %get-tuple-element.18), channel_id=1, source_target_pairs={{0,16},{4,20},{8,24},{12,28},{16,0},{20,4},{24,8},{28,12},{1,17},{... | collective-permute-start | bytes 221192 | tf_op jit(solution)/shard_map/ppermute | solution.py:414
  42.9 5.3 %collective-permute-start.8 = (bf16[32,1152]{1,0:T(8,128)(2,1)S(1)}, bf16[32,1152]{1,0:T(8,128)(2,1)S(1)}, u32[]{:S(2)}, u32[]{:S(2)}) collective-permute-start(bf16[32,1152]{1,0:T(8,128)(2,1)S(1)} %get-tuple-element.19), channel_id=1, source_target_pairs={{0,24},{4,28},{8,16},{12,20},{16,8},{20,12},{24,0},{28,4},{1,25},{... | collective-permute-start | bytes 221192 | tf_op jit(solution)/shard_map/ppermute | solution.py:414

commit v11 on v9

--- a/solution.py
+++ b/solution.py
@@ -121,7 +121,7 @@
     edge = reach * columns
     return pl.pallas_call(
         functools.partial(halo_kernel, columns, reach),
-        out_shape=[jax.ShapeDtypeStruct((edge, width), jnp.bfloat16)] * 2,
+        out_shape=[pltpu.VMEM((edge, width), jnp.bfloat16)] * 2,
         compiler_params=pltpu.CompilerParams(vmem_limit_bytes=VMEM_LIMIT),
         cost_estimate=pl.CostEstimate(
             flops=12 * edge * channels * width,
@@ -148,7 +148,7 @@
     return pl.pallas_call(
         functools.partial(middle_kernel, columns, reach),
         in_specs=[vmem, vmem, vmem],
-        out_shape=jax.ShapeDtypeStruct((pixels, width), jnp.float32),
+        out_shape=pltpu.VMEM((pixels, width), jnp.float32),
         compiler_params=pltpu.CompilerParams(vmem_limit_bytes=VMEM_LIMIT),
         cost_estimate=pl.CostEstimate(
             flops=6 * pixels * channels * width,
@@ -159,10 +159,23 @@
     )(flat, weight, after)
 
 
+def as_column(rows_ref):
+    values = rows_ref[...].astype(jnp.float32)
+    rows, columns = values.shape
+    shape = (columns, columns)
+    same = lax.broadcasted_iota(jnp.int32, shape, 0) == lax.broadcasted_iota(jnp.int32, shape, 1)
+    return jnp.concatenate(
+        [
+            jnp.sum(jnp.where(same, values[r : r + 1], 0.0), axis=1, keepdims=True)
+            for r in range(rows)
+        ],
+        axis=0,
+    )
+
+
 def pointwise_kernel(
-    middle_ref, above_ref, below_ref, bias_ref, class_ref, label_ref, scale_ref, after_ref, out_ref
+    middle_ref, above_ref, below_ref, bias_ref, class_ref, label_ref, scale_ref, out_ref
 ):
-    del after_ref
     pixels, width = middle_ref.shape
     edge = above_ref.shape[0]
     above = above_ref[...].astype(jnp.float32)
@@ -180,9 +193,9 @@
     )
     exponent = jnp.exp(logits)
     chances = exponent / jnp.sum(exponent, axis=1, keepdims=True)
-    index = lax.broadcasted_iota(jnp.int32, chances.shape, 1)
-    onehot = jnp.where(label_ref[...] == index, 1.0, 0.0)
-    grad_logits = scale_ref[...].astype(jnp.float32) * (chances - onehot)
+    index = lax.broadcasted_iota(jnp.int32, chances.shape, 1).astype(jnp.float32)
+    onehot = jnp.where(as_column(label_ref) == index, 1.0, 0.0)
+    grad_logits = as_column(scale_ref) * (chances - onehot)
     wide = classes.astype(jnp.float32)
     hidden_grad = sum(
         grad_logits[:, k : k + 1] * wide[k : k + 1] for k in range(classes.shape[0])
@@ -191,12 +204,10 @@
     out_ref[...] = gradient.astype(out_ref.dtype)
 
 
-def pointwise(middle, above, below, bias, classes, labels, scale, after):
+def pointwise(middle, above, below, bias, classes, labels, scale):
     pixels, width = middle.shape
-    vmem = pl.BlockSpec(memory_space=pltpu.VMEM)
     return pl.pallas_call(
         pointwise_kernel,
-        in_specs=[vmem] * 7 + [pl.BlockSpec(memory_space=pl.ANY)],
         out_shape=jax.ShapeDtypeStruct((pixels, width), jnp.bfloat16),
         compiler_params=pltpu.CompilerParams(vmem_limit_bytes=VMEM_LIMIT),
         cost_estimate=pl.CostEstimate(
@@ -205,7 +216,7 @@
             transcendentals=pixels * width,
         ),
         name="pointwise",
-    )(middle, above, below, bias, classes, labels, scale, after)
+    )(middle, above, below, bias, classes, labels, scale)
 
 
 def shifted_taps(gradient, columns, reach):
@@ -392,9 +403,8 @@
         below,
         conv_bias.reshape(1, width),
         class_weight.T,
-        labels.reshape(pixels, 1),
-        pixel_weight.reshape(pixels, 1),
-        whole,
+        labels.reshape(band_rows, columns),
+        pixel_weight.reshape(band_rows, columns),
     )
     gradients = [gradient] + [
         lax.ppermute(gradient, "space", [(i, (i + k) % bands) for i in range(bands)])
@@ -407,7 +417,7 @@
     if cover % 16 == 0 and count <= 8:
         blocks = split_up(terms, parts, count)
         came = [blocks[0]]
-        for k in range(1, count):
+        for k in reversed(range(1, count)):
             pairs = [(i, parts * partner(i // parts, k, count) + i % parts) for i in range(replicas)]
             came.append(lax.ppermute(blocks[k], "dp", pairs))
     else:

time: 42.4 us -> 40.3 us (0.950)
  Pallas kernels: 9.5 us -> 8.1 us
  waiting for transfers between devices: 12.4 us -> 11.3 us
  starting transfers between devices: 19 us -> 19.9 us
    ppermute x1, waiting for transfers between devices: 0.01 us -> 1.31 us  [on_device(): above = lax.ppermute(down, 'space', [(i, i + 1) for i in range(bands - 1)])]
    ppermute x3, waiting for transfers between devices: 2.16 us -> 1.2 us  [on_device(): came.append(lax.ppermute(blocks[k], 'dp', pairs))]
    ppermute x3, starting transfers between devices: 3.88 us -> 4.71 us  [on_device(): lax.ppermute(gradient, 'space', [(i, (i + k) % bands) for i in range(band...]
    pallas_call x1, Pallas kernels: 1.16 us -> 0.36 us  [middle_taps(): pl.pallas_call(functools.partial(middle_kernel, columns, reach), in_specs...]
    ppermute x1, waiting for transfers between devices: 3.86 us -> 3.15 us  [on_device(): below = lax.ppermute(up, 'space', [(i + 1, i) for i in range(bands - 1)])]
    pallas_call x1, Pallas kernels: 1.18 us -> 0.57 us  [halo(): pl.pallas_call(functools.partial(halo_kernel, columns, reach), out_shape=...]
    all_to_all x1, waiting for transfers between devices: 0.52 us -> 0.01 us  [on_device(): whole = lax.all_to_all(split[0], 'space', 0, 0)]
  transfers between devices with their start and end apart: 10 -> 10, of which waited for: 6 -> 8; matrix products, arithmetic and copies ran while one was open for 1% -> 0% of each run, Pallas kernels for 13% -> 12%
where the time goes in v11:
time: 40.3 us; the launch traced here: 40 us
  starting transfers between devices  19.9 us (49%)
  waiting for transfers between devices  11.3 us (28%)
  Pallas kernels  8.1 us (20%)
  between operations  0.74 us (2%)
    all_to_all x1, starting transfers between devices, on_device(): whole = lax.all_to_all(split[0], 'space', 0, 0)  6.33 us
    ppermute x3, starting transfers between devices, on_device(): lax.ppermute(gradient, 'space', [(i, (i + k) % bands) for i in range(band...  4.71 us
    ppermute x3, waiting for transfers between devices, on_device(): lax.ppermute(gradient, 'space', [(i, (i + k) % bands) for i in range(band...  4.69 us
    ppermute x1, starting transfers between devices, on_device(): above = lax.ppermute(down, 'space', [(i, i + 1) for i in range(bands - 1)])  3.93 us
    ppermute x3, starting transfers between devices, on_device(): came.append(lax.ppermute(blocks[k], 'dp', pairs))  3.55 us
    ppermute x1, waiting for transfers between devices, on_device(): below = lax.ppermute(up, 'space', [(i + 1, i) for i in range(bands - 1)])  3.15 us
    pallas_call x1, Pallas kernels, feature_grad(): pl.pallas_call(functools.partial(feature_grad_kernel, columns, reach, ban...  2.61 us
    pallas_call x1, Pallas kernels, load(): pl.pallas_call(functools.partial(load_kernel, replicas, cover), in_specs=...  2.06 us
  transfers between devices with their start and end apart: 10, of which 8 were waited for; matrix products, arithmetic and copies ran while one was open for 0% of the time, Pallas kernels for 12%

profile of v11, /device:TPU:0, one launch (start us, length us, event | category | flops | bytes accessed | tf_op | source)
XLA Modules:
  0.0 40.0 jit_solution(5279057678811812576)
XLA Ops:
  0.6 2.1 %load.1 = (bf16[192,1024]{1,0:T(8,128)(2,1)S(1)}, bf16[9,1024,128]{2,1,0:T(8,128)(2,1)S(1)}, bf16[4,192,256]{2,1,0:T(8,128)(2,1)}) custom-call(bf16[192,1024]{1,0:T(8,128)(2,1)} %bitcast.13, bf16[9,1024,128]{2,1,0:T(8,128)(2,1)} %bitcast.11), custom_call_target="tpu_custom_call" | custom-call | bytes 3145728 | tf_op jit(solution)/shard_map/load/pallas_call | solution.py:84
  2.7 0.0 copy-start.2
  2.7 0.0 copy-start.3
  2.7 6.3 %all-to-all-start = ((bf16[4,192,256]{2,1,0:T(8,128)(2,1)}), bf16[4,192,256]{2,1,0:T(8,128)(2,1)S(1)}, u32[]{:S(2)}, u32[]{:S(2)}) async-start(bf16[4,192,256]{2,1,0:T(8,128)(2,1)} %get-tuple-element.15), calls=%async_computation | async-start | bytes 786432 | tf_op jit(solution)/shard_map/all_to_all | solution.py:394
  9.1 0.0 copy-start
  9.1 0.0 copy-start.1
  9.1 0.6 %halo.1 = (bf16[192,128]{1,0:T(8,128)(2,1)S(1)}, bf16[192,128]{1,0:T(8,128)(2,1)S(1)}) custom-call(bf16[192,1024]{1,0:T(8,128)(2,1)S(1)} %get-tuple-element.11.x_ref, bf16[9,1024,128]{2,1,0:T(8,128)(2,1)S(1)} %get-tuple-element.12.w_ref), custom_call_target="tpu_custom_call" | custom-call | flops 301989888 | bytes 1966080 | tf_op jit(solution)/shard_map/halo/pallas_call | solution.py:122
  9.6 3.9 %collective-permute-start = (bf16[192,128]{1,0:T(8,128)(2,1)S(1)}, bf16[192,128]{1,0:T(8,128)(2,1)S(1)}, u32[]{:S(2)}, u32[]{:S(2)}) collective-permute-start(bf16[192,128]{1,0:T(8,128)(2,1)S(1)} %get-tuple-element.14), channel_id=1, source_target_pairs={{0,1},{1,2},{2,3},{4,5},{5,6},{6,7},{8,9},{9,10},{10,11},{12,13},{... | collective-permute-start | bytes 147464 | tf_op jit(solution)/shard_map/ppermute | solution.py:396
  13.6 1.3 %collective-permute-start.1 = (bf16[192,128]{1,0:T(8,128)(2,1)S(1)}, bf16[192,128]{1,0:T(8,128)(2,1)S(1)}, u32[]{:S(2)}, u32[]{:S(2)}) collective-permute-start(bf16[192,128]{1,0:T(8,128)(2,1)S(1)} %get-tuple-element.13.after_ref), channel_id=1, source_target_pairs={{1,0},{2,1},{3,2},{5,4},{6,5},{7,6},{9,8},{10,9},{11,10},{13,12},{... | collective-permute-start | bytes 147464 | tf_op jit(solution)/shard_map/ppermute | solution.py:397
  14.9 0.0 copy-done.2
  14.9 0.0 copy-done.3
  14.9 0.4 middle_taps.1.middle_ref
  15.3 1.3 %collective-permute-done.above_ref = bf16[192,128]{1,0:T(8,128)(2,1)S(1)} collective-permute-done((bf16[192,128]{1,0:T(8,128)(2,1)S(1)}, bf16[192,128]{1,0:T(8,128)(2,1)S(1)}, u32[]{:S(2)}, u32[]{:S(2)}) %collective-permute-start) | collective-permute-done | bytes 49184 | tf_op jit(solution)/shard_map/ppermute | solution.py:396
  16.6 3.1 %collective-permute-done.1.below_ref = bf16[192,128]{1,0:T(8,128)(2,1)S(1)} collective-permute-done((bf16[192,128]{1,0:T(8,128)(2,1)S(1)}, bf16[192,128]{1,0:T(8,128)(2,1)S(1)}, u32[]{:S(2)}, u32[]{:S(2)}) %collective-permute-start.1) | collective-permute-done | bytes 49184 | tf_op jit(solution)/shard_map/ppermute | solution.py:397
  19.7 0.0 copy-done
  19.7 0.0 copy-done.1
  19.7 0.4 %pointwise.1.own_ref.refs_0_ = bf16[192,128]{1,0:T(8,128)(2,1)S(1)} custom-call(f32[192,128]{1,0:T(8,128)S(1)} %middle_taps.1.middle_ref, bf16[192,128]{1,0:T(8,128)(2,1)S(1)} %collective-permute-done.above_ref, bf16[192,128]{1,0:T(8,128)(2,1)S(1)} %collective-permute-done.1.below_ref, f32[1,128]{1,0:T(1,128)S(1)} %bitcast.10, bf16[3,128]{1,0:T(4,128)(2,1)S(1)} %bitcast.9, ...), custom_call_target="tpu_custom_call" | custom-call | flops 737280 | bytes 245760 | tf_op jit(solution)/shard_map/pointwise/pallas_call | solution.py:209
  20.2 2.7 %collective-permute-start.2 = (bf16[192,128]{1,0:T(8,128)(2,1)S(1)}, bf16[192,128]{1,0:T(8,128)(2,1)S(1)}, u32[]{:S(2)}, u32[]{:S(2)}) collective-permute-start(bf16[192,128]{1,0:T(8,128)(2,1)S(1)} %pointwise.1.own_ref.refs_0_), channel_id=1, source_target_pairs={{0,1},{1,2},{2,3},{3,0},{4,5},{5,6},{6,7},{7,4},{8,9},{9,10},{10,1... | collective-permute-start | bytes 147464 | tf_op jit(solution)/shard_map/ppermute | solution.py:410
  22.8 1.2 %collective-permute-start.3 = (bf16[192,128]{1,0:T(8,128)(2,1)S(1)}, bf16[192,128]{1,0:T(8,128)(2,1)S(1)}, u32[]{:S(2)}, u32[]{:S(2)}) collective-permute-start(bf16[192,128]{1,0:T(8,128)(2,1)S(1)} %pointwise.1.own_ref.refs_0_), channel_id=1, source_target_pairs={{0,3},{1,0},{2,1},{3,2},{4,7},{5,4},{6,5},{7,6},{8,11},{9,8},{10,9... | collective-permute-start | bytes 147464 | tf_op jit(solution)/shard_map/ppermute | solution.py:410
  24.1 0.8 %collective-permute-start.4 = (bf16[192,128]{1,0:T(8,128)(2,1)S(1)}, bf16[192,128]{1,0:T(8,128)(2,1)S(1)}, u32[]{:S(2)}, u32[]{:S(2)}) collective-permute-start(bf16[192,128]{1,0:T(8,128)(2,1)S(1)} %pointwise.1.own_ref.refs_0_), channel_id=1, source_target_pairs={{0,2},{1,3},{2,0},{3,1},{4,6},{5,7},{6,4},{7,5},{8,10},{9,11},{10,... | collective-permute-start | bytes 147464 | tf_op jit(solution)/shard_map/ppermute | solution.py:410
  24.9 1.4 %collective-permute-done.2.above_ref.refs_1_ = bf16[192,128]{1,0:T(8,128)(2,1)S(1)} collective-permute-done((bf16[192,128]{1,0:T(8,128)(2,1)S(1)}, bf16[192,128]{1,0:T(8,128)(2,1)S(1)}, u32[]{:S(2)}, u32[]{:S(2)}) %collective-permute-start.2) | collective-permute-done | bytes 49184 | tf_op jit(solution)/shard_map/ppermute | solution.py:410
  26.3 0.6 %collective-permute-done.3.below_ref.refs_3_ = bf16[192,128]{1,0:T(8,128)(2,1)S(1)} collective-permute-done((bf16[192,128]{1,0:T(8,128)(2,1)S(1)}, bf16[192,128]{1,0:T(8,128)(2,1)S(1)}, u32[]{:S(2)}, u32[]{:S(2)}) %collective-permute-start.3) | collective-permute-done | bytes 49184 | tf_op jit(solution)/shard_map/ppermute | solution.py:410
  26.9 2.6 %collective-permute-done.4.refs_2_ = bf16[192,128]{1,0:T(8,128)(2,1)S(1)} collective-permute-done((bf16[192,128]{1,0:T(8,128)(2,1)S(1)}, bf16[192,128]{1,0:T(8,128)(2,1)S(1)}, u32[]{:S(2)}, u32[]{:S(2)}) %collective-permute-start.4) | collective-permute-done | bytes 49184 | tf_op jit(solution)/shard_map/ppermute | solution.py:410
  29.6 0.0 all-to-all-done.x_ref
  29.6 0.7 %kernel_grad.3 = bf16[128,1152]{1,0:T(8,128)(2,1)S(1)} custom-call(bf16[4,192,256]{2,1,0:T(8,128)(2,1)S(1)} %all-to-all-done.x_ref, bf16[192,128]{1,0:T(8,128)(2,1)S(1)} %pointwise.1.own_ref.refs_0_, bf16[192,128]{1,0:T(8,128)(2,1)S(1)} %collective-permute-done.2.above_ref.refs_1_, bf16[192,128]{1,0:T(8,128)(2,1)S(1)} %collective-permute-done.4.refs_2_, ...), custom_call_target="tpu_custom_call" | custom-call | flops 226492416 | bytes 688128 | tf_op jit(solution)/shard_map/kernel_grad/pallas_call | solution.py:266
  30.2 0.1 collective-permute-start.5
  30.3 0.7 %kernel_grad.2.refs_0_ = f32[128,1152]{1,0:T(8,128)S(1)} custom-call(bf16[4,192,256]{2,1,0:T(8,128)(2,1)S(1)} %all-to-all-done.x_ref, bf16[192,128]{1,0:T(8,128)(2,1)S(1)} %pointwise.1.own_ref.refs_0_, bf16[192,128]{1,0:T(8,128)(2,1)S(1)} %collective-permute-done.2.above_ref.refs_1_, bf16[192,128]{1,0:T(8,128)(2,1)S(1)} %collective-permute-done.4.refs_2_, ...), custom_call_target="tpu_custom_call" | custom-call | flops 226492416 | bytes 688128 | tf_op jit(solution)/shard_map/kernel_grad/pallas_call | solution.py:266
  31.0 0.9 %collective-permute-done.5.refs_1_ = bf16[128,1152]{1,0:T(8,128)(2,1)S(1)} collective-permute-done((bf16[128,1152]{1,0:T(8,128)(2,1)S(1)}, bf16[128,1152]{1,0:T(8,128)(2,1)S(1)}, u32[]{:S(2)}, u32[]{:S(2)}) %collective-permute-start.5) | collective-permute-done | bytes 294944 | tf_op jit(solution)/shard_map/ppermute | solution.py:416
  31.9 0.1 split_up.1
  31.9 2.5 %collective-permute-start.6 = (bf16[32,1152]{1,0:T(8,128)(2,1)S(1)}, bf16[32,1152]{1,0:T(8,128)(2,1)S(1)}, u32[]{:S(2)}, u32[]{:S(2)}) collective-permute-start(bf16[32,1152]{1,0:T(8,128)(2,1)S(1)} %get-tuple-element.17), channel_id=1, source_target_pairs={{0,24},{4,28},{8,16},{12,20},{16,8},{20,12},{24,0},{28,4},{1,25},{... | collective-permute-start | bytes 221192 | tf_op jit(solution)/shard_map/ppermute | solution.py:422
  34.5 0.5 %collective-permute-start.7 = (bf16[32,1152]{1,0:T(8,128)(2,1)S(1)}, bf16[32,1152]{1,0:T(8,128)(2,1)S(1)}, u32[]{:S(2)}, u32[]{:S(2)}) collective-permute-start(bf16[32,1152]{1,0:T(8,128)(2,1)S(1)} %get-tuple-element.18), channel_id=1, source_target_pairs={{0,16},{4,20},{8,24},{12,28},{16,0},{20,4},{24,8},{28,12},{1,17},{... | collective-permute-start | bytes 221192 | tf_op jit(solution)/shard_map/ppermute | solution.py:422
  35.0 0.5 %collective-permute-start.8 = (bf16[32,1152]{1,0:T(8,128)(2,1)S(1)}, bf16[32,1152]{1,0:T(8,128)(2,1)S(1)}, u32[]{:S(2)}, u32[]{:S(2)}) collective-permute-start(bf16[32,1152]{1,0:T(8,128)(2,1)S(1)} %get-tuple-element.19), channel_id=1, source_target_pairs={{0,8},{4,12},{8,0},{12,4},{16,24},{20,28},{24,16},{28,20},{1,9},{5... | collective-permute-start | bytes 221192 | tf_op jit(solution)/shard_map/ppermute | solution.py:422
  35.5 2.6 %feature_grad.1 = f32[192,1024]{1,0:T(8,128)} custom-call(bf16[192,128]{1,0:T(8,128)(2,1)S(1)} %pointwise.1.own_ref.refs_0_, bf16[192,128]{1,0:T(8,128)(2,1)S(1)} %collective-permute-done.2.above_ref.refs_1_, bf16[192,128]{1,0:T(8,128)(2,1)S(1)} %collective-permute-done.3.below_ref.refs_3_, bf16[9,1024,128]{2,1,0:T(8,128)(2,1)S(1)} %get-tuple-element.12.w_ref), custom_call_target="tpu_custom_call" | custom-call | flops 452984832 | bytes 3145728 | tf_op jit(solution)/shard_map/feature_grad/pallas_call | solution.py:358
  38.1 0.0 collective-permute-done.6.refs_1_
  38.1 0.7 %collective-permute-done.7.refs_2_ = bf16[32,1152]{1,0:T(8,128)(2,1)S(1)} collective-permute-done((bf16[32,1152]{1,0:T(8,128)(2,1)S(1)}, bf16[32,1152]{1,0:T(8,128)(2,1)S(1)}, u32[]{:S(2)}, u32[]{:S(2)}) %collective-permute-start.7) | collective-permute-done | bytes 73760 | tf_op jit(solution)/shard_map/ppermute | solution.py:422
  38.8 0.5 %collective-permute-done.8.refs_3_ = bf16[32,1152]{1,0:T(8,128)(2,1)S(1)} collective-permute-done((bf16[32,1152]{1,0:T(8,128)(2,1)S(1)}, bf16[32,1152]{1,0:T(8,128)(2,1)S(1)}, u32[]{:S(2)}, u32[]{:S(2)}) %collective-permute-start.8) | collective-permute-done | bytes 73760 | tf_op jit(solution)/shard_map/ppermute | solution.py:422
  39.3 0.7 %final_sum.1 = f32[288,128]{1,0:T(8,128)} custom-call(bf16[32,1152]{1,0:T(8,128)(2,1)S(1)} %get-tuple-element.16.refs_0_, bf16[32,1152]{1,0:T(8,128)(2,1)S(1)} %collective-permute-done.6.refs_1_, bf16[32,1152]{1,0:T(8,128)(2,1)S(1)} %collective-permute-done.7.refs_2_, bf16[32,1152]{1,0:T(8,128)(2,1)S(1)} %collective-permute-done.8.refs_3_), custom_call_target="tpu_custom_call" | custom-call | tf_op jit(solution)/shard_map/final_sum/pallas_call | solution.py:326
  (1 shorter events, 0.0 us)
Async XLA Ops:
  2.7 12.2 %copy-start.2 = (s32[1,6,32]{2,0,1:T(1,128)S(1)}, s32[1,6,32]{2,0,1:T(1,128)}, u32[]{:S(2)}) copy-start(s32[1,6,32]{2,0,1:T(1,128)} %param.8) | copy-start | bytes 2308
  2.7 12.2 %copy-start.3 = (s32[1,6,32]{2,0,1:T(1,128)S(1)}, s32[1,6,32]{2,0,1:T(1,128)}, u32[]{:S(2)}) copy-start(s32[1,6,32]{2,0,1:T(1,128)} %param.7) | copy-start | bytes 2308
  2.7 26.8 %all-to-all-start = ((bf16[4,192,256]{2,1,0:T(8,128)(2,1)}), bf16[4,192,256]{2,1,0:T(8,128)(2,1)S(1)}, u32[]{:S(2)}, u32[]{:S(2)}) async-start(bf16[4,192,256]{2,1,0:T(8,128)(2,1)} %get-tuple-element.15), calls=%async_computation | async-start | bytes 786432 | tf_op jit(solution)/shard_map/all_to_all | solution.py:394
  9.1 10.7 %copy-start = (bf16[128,3]{0,1:T(4,128)(2,1)S(1)}, bf16[128,3]{0,1:T(4,128)(2,1)}, u32[]{:S(2)}) copy-start(bf16[128,3]{0,1:T(4,128)(2,1)} %param.11) | copy-start | bytes 2308
  9.1 10.7 %copy-start.1 = (f32[128]{0:T(128)S(1)}, f32[128]{0:T(128)}, u32[]{:S(2)}) copy-start(f32[128]{0:T(128)} %param.10) | copy-start | bytes 1540
  9.6 7.0 %collective-permute-start = (bf16[192,128]{1,0:T(8,128)(2,1)S(1)}, bf16[192,128]{1,0:T(8,128)(2,1)S(1)}, u32[]{:S(2)}, u32[]{:S(2)}) collective-permute-start(bf16[192,128]{1,0:T(8,128)(2,1)S(1)} %get-tuple-element.14), channel_id=1, source_target_pairs={{0,1},{1,2},{2,3},{4,5},{5,6},{6,7},{8,9},{9,10},{10,11},{12,13},{... | collective-permute-start | bytes 147464 | tf_op jit(solution)/shard_map/ppermute | solution.py:396
  13.6 6.2 %collective-permute-start.1 = (bf16[192,128]{1,0:T(8,128)(2,1)S(1)}, bf16[192,128]{1,0:T(8,128)(2,1)S(1)}, u32[]{:S(2)}, u32[]{:S(2)}) collective-permute-start(bf16[192,128]{1,0:T(8,128)(2,1)S(1)} %get-tuple-element.13.after_ref), channel_id=1, source_target_pairs={{1,0},{2,1},{3,2},{5,4},{6,5},{7,6},{9,8},{10,9},{11,10},{13,12},{... | collective-permute-start | bytes 147464 | tf_op jit(solution)/shard_map/ppermute | solution.py:397
  20.2 6.1 %collective-permute-start.2 = (bf16[192,128]{1,0:T(8,128)(2,1)S(1)}, bf16[192,128]{1,0:T(8,128)(2,1)S(1)}, u32[]{:S(2)}, u32[]{:S(2)}) collective-permute-start(bf16[192,128]{1,0:T(8,128)(2,1)S(1)} %pointwise.1.own_ref.refs_0_), channel_id=1, source_target_pairs={{0,1},{1,2},{2,3},{3,0},{4,5},{5,6},{6,7},{7,4},{8,9},{9,10},{10,1... | collective-permute-start | bytes 147464 | tf_op jit(solution)/shard_map/ppermute | solution.py:410
  22.8 4.1 %collective-permute-start.3 = (bf16[192,128]{1,0:T(8,128)(2,1)S(1)}, bf16[192,128]{1,0:T(8,128)(2,1)S(1)}, u32[]{:S(2)}, u32[]{:S(2)}) collective-permute-start(bf16[192,128]{1,0:T(8,128)(2,1)S(1)} %pointwise.1.own_ref.refs_0_), channel_id=1, source_target_pairs={{0,3},{1,0},{2,1},{3,2},{4,7},{5,4},{6,5},{7,6},{8,11},{9,8},{10,9... | collective-permute-start | bytes 147464 | tf_op jit(solution)/shard_map/ppermute | solution.py:410
  24.1 5.5 %collective-permute-start.4 = (bf16[192,128]{1,0:T(8,128)(2,1)S(1)}, bf16[192,128]{1,0:T(8,128)(2,1)S(1)}, u32[]{:S(2)}, u32[]{:S(2)}) collective-permute-start(bf16[192,128]{1,0:T(8,128)(2,1)S(1)} %pointwise.1.own_ref.refs_0_), channel_id=1, source_target_pairs={{0,2},{1,3},{2,0},{3,1},{4,6},{5,7},{6,4},{7,5},{8,10},{9,11},{10,... | collective-permute-start | bytes 147464 | tf_op jit(solution)/shard_map/ppermute | solution.py:410
  30.2 1.6 %collective-permute-start.5 = (bf16[128,1152]{1,0:T(8,128)(2,1)S(1)}, bf16[128,1152]{1,0:T(8,128)(2,1)S(1)}, u32[]{:S(2)}, u32[]{:S(2)}) collective-permute-start(bf16[128,1152]{1,0:T(8,128)(2,1)S(1)} %kernel_grad.3), channel_id=1, source_target_pairs={{0,4},{4,0},{8,12},{12,8},{16,20},{20,16},{24,28},{28,24},{1,5},{5... | collective-permute-start | bytes 884744 | tf_op jit(solution)/shard_map/ppermute | solution.py:416
  31.9 6.2 %collective-permute-start.6 = (bf16[32,1152]{1,0:T(8,128)(2,1)S(1)}, bf16[32,1152]{1,0:T(8,128)(2,1)S(1)}, u32[]{:S(2)}, u32[]{:S(2)}) collective-permute-start(bf16[32,1152]{1,0:T(8,128)(2,1)S(1)} %get-tuple-element.17), channel_id=1, source_target_pairs={{0,24},{4,28},{8,16},{12,20},{16,8},{20,12},{24,0},{28,4},{1,25},{... | collective-permute-start | bytes 221192 | tf_op jit(solution)/shard_map/ppermute | solution.py:422
  34.5 4.4 %collective-permute-start.7 = (bf16[32,1152]{1,0:T(8,128)(2,1)S(1)}, bf16[32,1152]{1,0:T(8,128)(2,1)S(1)}, u32[]{:S(2)}, u32[]{:S(2)}) collective-permute-start(bf16[32,1152]{1,0:T(8,128)(2,1)S(1)} %get-tuple-element.18), channel_id=1, source_target_pairs={{0,16},{4,20},{8,24},{12,28},{16,0},{20,4},{24,8},{28,12},{1,17},{... | collective-permute-start | bytes 221192 | tf_op jit(solution)/shard_map/ppermute | solution.py:422
  35.0 4.4 %collective-permute-start.8 = (bf16[32,1152]{1,0:T(8,128)(2,1)S(1)}, bf16[32,1152]{1,0:T(8,128)(2,1)S(1)}, u32[]{:S(2)}, u32[]{:S(2)}) collective-permute-start(bf16[32,1152]{1,0:T(8,128)(2,1)S(1)} %get-tuple-element.19), channel_id=1, source_target_pairs={{0,8},{4,12},{8,0},{12,4},{16,24},{20,28},{24,16},{28,20},{1,9},{5... | collective-permute-start | bytes 221192 | tf_op jit(solution)/shard_map/ppermute | solution.py:422

commit v12 on v11

--- a/solution.py
+++ b/solution.py
@@ -111,8 +111,24 @@
 
 def halo_kernel(columns, reach, x_ref, w_ref, down_ref, up_ref):
     pixels, edge = x_ref.shape[0], reach * columns
-    down_ref[...] = tap_row(x_ref[pixels - edge :], w_ref, 0, columns, reach).astype(down_ref.dtype)
-    up_ref[...] = tap_row(x_ref[:edge], w_ref, 2, columns, reach).astype(up_ref.dtype)
+    width = w_ref.shape[2]
+    if pixels > edge:
+        down = tap_row(x_ref[pixels - edge :], w_ref, 0, columns, reach)
+        up = tap_row(x_ref[:edge], w_ref, 2, columns, reach)
+    else:
+        weight = jnp.concatenate([w_ref[t] for t in (0, 1, 2, 6, 7, 8)], axis=1)
+        product = jnp.dot(x_ref[...], weight, preferred_element_type=jnp.float32)
+        down, up = [
+            sum(
+                shift_columns(
+                    product[:, (3 * k + b) * width : (3 * k + b + 1) * width], (b - 1) * reach, columns
+                )
+                for b in range(3)
+            )
+            for k in range(2)
+        ]
+    down_ref[...] = down.astype(down_ref.dtype)
+    up_ref[...] = up.astype(up_ref.dtype)
 
 
 def halo(flat, weight, columns, reach):
@@ -227,54 +243,60 @@
     )
 
 
-def kernel_grad_kernel(columns, reach, parts, other, x_ref, *refs):
-    *g_refs, out_ref, taps = refs
+def kernel_grad_kernel(columns, reach, parts, others, distances, before, x_ref, *refs):
+    count = len(distances)
+    g_refs, sums, outs = refs[:count], refs[count : count + before], refs[count + before : -1]
+    padded = refs[-1]
     bands, pixels, lanes = x_ref.shape
     width = g_refs[0].shape[1]
     total = bands * pixels
     edge = reach * columns
     extra = lanes // parts
     band = lax.axis_index("space")
-    for k, g_ref in enumerate(g_refs):
-        first = lax.rem(band + bands - k, bands) * pixels
-        taps[pl.ds(pl.multiple_of(first, 16), pixels)] = shifted_taps(g_ref[...], columns, reach)
-    part = lax.rem(lax.axis_index("dp") + other, parts)
-    if extra % 128 == 0:
-        features = x_ref[:, :, pl.ds(pl.multiple_of(part * extra, 128), extra)]
-    else:
-        features = x_ref[:, :, :extra]
-        for k in range(1, parts):
-            features = jnp.where(part == k, x_ref[:, :, k * extra : (k + 1) * extra], features)
-    features = features.reshape(total, extra)
-    for a in range(3):
-        if a == 0:
-            left, right = features[: total - edge], taps[edge:]
-        elif a == 1:
-            left, right = features, taps[...]
+    none = jnp.zeros((edge, padded.shape[1]), padded.dtype)
+    padded[:edge] = none
+    padded[edge + total :] = none
+    shifted = [shifted_taps(g_ref[...], columns, reach) for g_ref in g_refs]
+    for n, (other, out_ref) in enumerate(zip(others, outs)):
+        part = lax.rem(lax.axis_index("dp") + other, parts)
+        if extra % 128 == 0:
+            features = x_ref[:, :, pl.ds(pl.multiple_of(part * extra, 128), extra)]
         else:
-            left, right = features[edge:], taps[: total - edge]
-        block = lax.dot_general(
-            left, right, (((0,), (0,)), ((), ())), preferred_element_type=jnp.float32
-        )
-        out_ref[:, 3 * a * width : 3 * (a + 1) * width] = block.astype(out_ref.dtype)
-
-
-def kernel_grad(features, gradients, columns, reach, parts, other, dtype):
+            features = x_ref[:, :, :extra]
+            for k in range(1, parts):
+                features = jnp.where(part == k, x_ref[:, :, k * extra : (k + 1) * extra], features)
+        padded[edge : edge + total] = features.reshape(total, extra)
+        for a in range(3):
+            here = pl.ds(3 * a * width, 3 * width)
+            grad = sums[n][:, here] if before else None
+            for k, right in zip(distances, shifted):
+                first = lax.rem(band + bands - k, bands) * pixels + a * edge
+                left = padded[pl.ds(pl.multiple_of(first, 16), pixels)]
+                term = lax.dot_general(
+                    left, right, (((0,), (0,)), ((), ())), preferred_element_type=jnp.float32
+                )
+                grad = term if grad is None else grad + term
+            out_ref[:, here] = grad.astype(out_ref.dtype)
+
+
+def kernel_grad(features, gradients, sums, columns, reach, parts, others, dtype):
     bands, pixels, lanes = features.shape
     extra = lanes // parts
-    width = gradients[0].shape[1]
-    return pl.pallas_call(
-        functools.partial(kernel_grad_kernel, columns, reach, parts, other),
-        out_shape=jax.ShapeDtypeStruct((extra, 9 * width), dtype),
-        scratch_shapes=[pltpu.VMEM((bands * pixels, 3 * width), jnp.bfloat16)],
-        compiler_params=pltpu.CompilerParams(vmem_limit_bytes=VMEM_LIMIT),
-        cost_estimate=pl.CostEstimate(
-            flops=18 * bands * pixels * extra * width,
-            bytes_accessed=2 * bands * pixels * (width + extra) + 18 * extra * width,
-            transcendentals=0,
+    distances = tuple(gradients)
+    width = gradients[distances[0]].shape[1]
+    work = len(others) * len(distances) * pixels * extra * width
+    return pl.pallas_call(
+        functools.partial(
+            kernel_grad_kernel, columns, reach, parts, others, distances, len(sums)
+        ),
+        out_shape=[pltpu.VMEM((extra, 9 * width), dtype)] * len(others),
+        scratch_shapes=[pltpu.VMEM((bands * pixels + 2 * reach * columns, extra), features.dtype)],
+        compiler_params=pltpu.CompilerParams(vmem_limit_bytes=VMEM_LIMIT),
+        cost_estimate=pl.CostEstimate(
+            flops=18 * work, bytes_accessed=2 * bands * pixels * lanes, transcendentals=0
         ),
         name="kernel_grad",
-    )(features, *gradients)
+    )(features, *gradients.values(), *sums)
 
 
 def partner(i, k, count):
@@ -331,7 +353,7 @@
     )(*blocks)
 
 
-def feature_grad_kernel(columns, reach, bands, own_ref, above_ref, below_ref, w_ref, out_ref):
+def feature_grad_kernel(columns, reach, bands, own_ref, above_ref, below_ref, w_ref, out, room, sems):
     band = lax.axis_index("space")
     pixels, width = own_ref.shape
     edge = reach * columns
@@ -344,23 +366,34 @@
     taps = jnp.concatenate(
         [stack[(2 - a) * edge : (2 - a) * edge + pixels] for a in range(3)], axis=1
     )
-    weight = jnp.concatenate([w_ref[t] for t in range(9)], axis=1)
-    out_ref[...] = lax.dot_general(
-        taps, weight, (((1,), (1,)), ((), ())), preferred_element_type=jnp.float32
-    )
+    steps, _, step = room.shape
+    copies = []
+    for n in range(steps):
+        here = pl.ds(n * step, step)
+        weight = jnp.concatenate([w_ref[t, here, :] for t in range(w_ref.shape[0])], axis=1)
+        room[n] = lax.dot_general(
+            taps, weight, (((1,), (1,)), ((), ())), preferred_element_type=jnp.float32
+        )
+        copies.append(pltpu.make_async_copy(room.at[n], out.at[:, here], sems.at[n]))
+        copies[-1].start()
+    for copy in copies:
+        copy.wait()
 
 
 def feature_grad(own, above, below, weight, columns, reach, bands):
     pixels, _ = own.shape
     taps, channels, width = weight.shape
     step = 256 if channels % 256 == 0 else channels
-    whole = pl.BlockSpec((pixels, width), lambda i: (0, 0))
+    vmem = pl.BlockSpec(memory_space=pltpu.VMEM)
     return pl.pallas_call(
         functools.partial(feature_grad_kernel, columns, reach, bands),
-        grid=(channels // step,),
-        in_specs=[whole, whole, whole, pl.BlockSpec((taps, step, width), lambda i: (0, i, 0))],
-        out_specs=pl.BlockSpec((pixels, step), lambda i: (0, i)),
-        out_shape=jax.ShapeDtypeStruct((pixels, channels), jnp.float32),
+        in_specs=[vmem] * 4,
+        out_specs=pl.BlockSpec(memory_space=pltpu.HBM),
+        out_shape=pltpu.HBM((pixels, channels), jnp.float32),
+        scratch_shapes=[
+            pltpu.VMEM((channels // step, pixels, step), jnp.float32),
+            pltpu.SemaphoreType.DMA((channels // step,)),
+        ],
         compiler_params=pltpu.CompilerParams(vmem_limit_bytes=VMEM_LIMIT),
         cost_estimate=pl.CostEstimate(
             flops=2 * pixels * taps * channels * width,
@@ -410,10 +443,18 @@
         lax.ppermute(gradient, "space", [(i, (i + k) % bands) for i in range(bands)])
         for k in range(1, bands)
     ]
-    terms = [kernel_grad(whole, gradients, columns, reach, parts, 0, jnp.float32)]
+    late = bands // 2
+    early = {k: g for k, g in enumerate(gradients) if k != late or bands == 1}
+    others = (0, 1)[:parts]
+    terms = kernel_grad(whole, early, [], columns, reach, parts, others, jnp.float32)
+    if bands > 1:
+        last = {late: gradients[late]}
+        own, *theirs = terms
+        terms = kernel_grad(whole, last, [own], columns, reach, parts, (0,), jnp.float32)
+        terms += kernel_grad(whole, last, theirs, columns, reach, parts, (1,), jnp.bfloat16) if theirs else []
     if parts == 2:
-        theirs = kernel_grad(whole, gradients, columns, reach, parts, 1, jnp.bfloat16)
-        terms.append(lax.ppermute(theirs, "dp", [(i, i ^ 1) for i in range(replicas)]))
+        theirs = terms[1].astype(jnp.bfloat16)
+        terms = [terms[0], lax.ppermute(theirs, "dp", [(i, i ^ 1) for i in range(replicas)])]
     if cover % 16 == 0 and count <= 8:
         blocks = split_up(terms, parts, count)
         came = [blocks[0]]

time: 40.3 us -> 39.9 us (0.990)
  Pallas kernels: 8.1 us -> 7.42 us
    ppermute x3, waiting for transfers between devices: 4.69 us -> 3.7 us  [on_device(): lax.ppermute(gradient, 'space', [(i, (i + k) % bands) for i in range(band...]
    ppermute x3, waiting for transfers between devices: 1.2 us -> 2.1 us  [on_device(): came.append(lax.ppermute(blocks[k], 'dp', pairs))]
    pallas_call x1, Pallas kernels: 2.61 us -> 1.72 us  [feature_grad(): pl.pallas_call(functools.partial(feature_grad_kernel, columns, reach, ban...]
    pallas_call x2 -> x3, Pallas kernels: 1.31 us -> 1.59 us  [kernel_grad(): pl.pallas_call(functools.partial(kernel_grad_kernel, columns, reach, part...]
  transfers between devices with their start and end apart: 10 -> 10, of which waited for: 8 -> 9; matrix products, arithmetic and copies ran while one was open for 0% -> 0% of each run, Pallas kernels for 12% -> 11%
where the time goes in v12:
time: 39.9 us; the launch traced here: 39.6 us
  starting transfers between devices  20 us (50%)
  waiting for transfers between devices  11.5 us (29%)
  Pallas kernels  7.42 us (19%)
  between operations  0.76 us (2%)
    all_to_all x1, starting transfers between devices, on_device(): whole = lax.all_to_all(split[0], 'space', 0, 0)  6.33 us
    ppermute x3, starting transfers between devices, on_device(): lax.ppermute(gradient, 'space', [(i, (i + k) % bands) for i in range(band...  4.79 us
    ppermute x1, starting transfers between devices, on_device(): above = lax.ppermute(down, 'space', [(i, i + 1) for i in range(bands - 1)])  3.93 us
    ppermute x3, waiting for transfers between devices, on_device(): lax.ppermute(gradient, 'space', [(i, (i + k) % bands) for i in range(band...  3.7 us
    ppermute x3, starting transfers between devices, on_device(): came.append(lax.ppermute(blocks[k], 'dp', pairs))  3.55 us
    ppermute x1, waiting for transfers between devices, on_device(): below = lax.ppermute(up, 'space', [(i + 1, i) for i in range(bands - 1)])  3.06 us
    ppermute x3, waiting for transfers between devices, on_device(): came.append(lax.ppermute(blocks[k], 'dp', pairs))  2.1 us
    pallas_call x1, Pallas kernels, load(): pl.pallas_call(functools.partial(load_kernel, replicas, cover), in_specs=...  2.06 us
  transfers between devices with their start and end apart: 10, of which 9 were waited for; matrix products, arithmetic and copies ran while one was open for 0% of the time, Pallas kernels for 11%

profile of v12, /device:TPU:0, one launch (start us, length us, event | category | flops | bytes accessed | tf_op | source)
XLA Modules:
  0.0 39.6 jit_solution(4993683822383762420)
XLA Ops:
  0.6 2.1 %load.1 = (bf16[192,1024]{1,0:T(8,128)(2,1)S(1)}, bf16[9,1024,128]{2,1,0:T(8,128)(2,1)S(1)}, bf16[4,192,256]{2,1,0:T(8,128)(2,1)}) custom-call(bf16[192,1024]{1,0:T(8,128)(2,1)} %bitcast.13, bf16[9,1024,128]{2,1,0:T(8,128)(2,1)} %bitcast.11), custom_call_target="tpu_custom_call" | custom-call | bytes 3145728 | tf_op jit(solution)/shard_map/load/pallas_call | solution.py:84
  2.7 0.0 copy-start.2
  2.7 0.0 copy-start.3
  2.7 6.3 %all-to-all-start = ((bf16[4,192,256]{2,1,0:T(8,128)(2,1)}), bf16[4,192,256]{2,1,0:T(8,128)(2,1)S(1)}, u32[]{:S(2)}, u32[]{:S(2)}) async-start(bf16[4,192,256]{2,1,0:T(8,128)(2,1)} %get-tuple-element.17), calls=%async_computation | async-start | bytes 786432 | tf_op jit(solution)/shard_map/all_to_all | solution.py:427
  9.1 0.0 copy-start
  9.1 0.0 copy-start.1
  9.1 0.5 %halo.1 = (bf16[192,128]{1,0:T(8,128)(2,1)S(1)}, bf16[192,128]{1,0:T(8,128)(2,1)S(1)}) custom-call(bf16[192,1024]{1,0:T(8,128)(2,1)S(1)} %get-tuple-element.13.x_ref, bf16[9,1024,128]{2,1,0:T(8,128)(2,1)S(1)} %get-tuple-element.14.w_ref), custom_call_target="tpu_custom_call" | custom-call | flops 301989888 | bytes 1966080 | tf_op jit(solution)/shard_map/halo/pallas_call | solution.py:138
  9.5 3.9 %collective-permute-start = (bf16[192,128]{1,0:T(8,128)(2,1)S(1)}, bf16[192,128]{1,0:T(8,128)(2,1)S(1)}, u32[]{:S(2)}, u32[]{:S(2)}) collective-permute-start(bf16[192,128]{1,0:T(8,128)(2,1)S(1)} %get-tuple-element.16), channel_id=1, source_target_pairs={{0,1},{1,2},{2,3},{4,5},{5,6},{6,7},{8,9},{9,10},{10,11},{12,13},{... | collective-permute-start | bytes 147464 | tf_op jit(solution)/shard_map/ppermute | solution.py:429
  13.5 1.3 %collective-permute-start.1 = (bf16[192,128]{1,0:T(8,128)(2,1)S(1)}, bf16[192,128]{1,0:T(8,128)(2,1)S(1)}, u32[]{:S(2)}, u32[]{:S(2)}) collective-permute-start(bf16[192,128]{1,0:T(8,128)(2,1)S(1)} %get-tuple-element.15.after_ref), channel_id=1, source_target_pairs={{1,0},{2,1},{3,2},{5,4},{6,5},{7,6},{9,8},{10,9},{11,10},{13,12},{... | collective-permute-start | bytes 147464 | tf_op jit(solution)/shard_map/ppermute | solution.py:430
  14.8 0.0 copy-done.2
  14.8 0.0 copy-done.3
  14.8 0.4 middle_taps.1.middle_ref
  15.2 1.4 %collective-permute-done.above_ref = bf16[192,128]{1,0:T(8,128)(2,1)S(1)} collective-permute-done((bf16[192,128]{1,0:T(8,128)(2,1)S(1)}, bf16[192,128]{1,0:T(8,128)(2,1)S(1)}, u32[]{:S(2)}, u32[]{:S(2)}) %collective-permute-start) | collective-permute-done | bytes 49184 | tf_op jit(solution)/shard_map/ppermute | solution.py:429
  16.6 3.1 %collective-permute-done.1.below_ref = bf16[192,128]{1,0:T(8,128)(2,1)S(1)} collective-permute-done((bf16[192,128]{1,0:T(8,128)(2,1)S(1)}, bf16[192,128]{1,0:T(8,128)(2,1)S(1)}, u32[]{:S(2)}, u32[]{:S(2)}) %collective-permute-start.1) | collective-permute-done | bytes 49184 | tf_op jit(solution)/shard_map/ppermute | solution.py:430
  19.6 0.0 copy-done
  19.6 0.0 copy-done.1
  19.7 0.4 %pointwise.1.own_ref.refs_0_ = bf16[192,128]{1,0:T(8,128)(2,1)S(1)} custom-call(f32[192,128]{1,0:T(8,128)S(1)} %middle_taps.1.middle_ref, bf16[192,128]{1,0:T(8,128)(2,1)S(1)} %collective-permute-done.above_ref, bf16[192,128]{1,0:T(8,128)(2,1)S(1)} %collective-permute-done.1.below_ref, f32[1,128]{1,0:T(1,128)S(1)} %bitcast.10, bf16[3,128]{1,0:T(4,128)(2,1)S(1)} %bitcast.9, ...), custom_call_target="tpu_custom_call" | custom-call | flops 737280 | bytes 245760 | tf_op jit(solution)/shard_map/pointwise/pallas_call | solution.py:225
  20.1 2.8 %collective-permute-start.2 = (bf16[192,128]{1,0:T(8,128)(2,1)S(1)}, bf16[192,128]{1,0:T(8,128)(2,1)S(1)}, u32[]{:S(2)}, u32[]{:S(2)}) collective-permute-start(bf16[192,128]{1,0:T(8,128)(2,1)S(1)} %pointwise.1.own_ref.refs_0_), channel_id=1, source_target_pairs={{0,1},{1,2},{2,3},{3,0},{4,5},{5,6},{6,7},{7,4},{8,9},{9,10},{10,1... | collective-permute-start | bytes 147464 | tf_op jit(solution)/shard_map/ppermute | solution.py:443
  22.8 1.1 %collective-permute-start.3 = (bf16[192,128]{1,0:T(8,128)(2,1)S(1)}, bf16[192,128]{1,0:T(8,128)(2,1)S(1)}, u32[]{:S(2)}, u32[]{:S(2)}) collective-permute-start(bf16[192,128]{1,0:T(8,128)(2,1)S(1)} %pointwise.1.own_ref.refs_0_), channel_id=1, source_target_pairs={{0,3},{1,0},{2,1},{3,2},{4,7},{5,4},{6,5},{7,6},{8,11},{9,8},{10,9... | collective-permute-start | bytes 147464 | tf_op jit(solution)/shard_map/ppermute | solution.py:443
  24.0 0.9 %collective-permute-start.4 = (bf16[192,128]{1,0:T(8,128)(2,1)S(1)}, bf16[192,128]{1,0:T(8,128)(2,1)S(1)}, u32[]{:S(2)}, u32[]{:S(2)}) collective-permute-start(bf16[192,128]{1,0:T(8,128)(2,1)S(1)} %pointwise.1.own_ref.refs_0_), channel_id=1, source_target_pairs={{0,2},{1,3},{2,0},{3,1},{4,6},{5,7},{6,4},{7,5},{8,10},{9,11},{10,... | collective-permute-start | bytes 147464 | tf_op jit(solution)/shard_map/ppermute | solution.py:443
  24.9 1.2 %collective-permute-done.2.above_ref.refs_1_ = bf16[192,128]{1,0:T(8,128)(2,1)S(1)} collective-permute-done((bf16[192,128]{1,0:T(8,128)(2,1)S(1)}, bf16[192,128]{1,0:T(8,128)(2,1)S(1)}, u32[]{:S(2)}, u32[]{:S(2)}) %collective-permute-start.2) | collective-permute-done | bytes 49184 | tf_op jit(solution)/shard_map/ppermute | solution.py:443
  26.1 0.8 %collective-permute-done.3.below_ref.refs_2_ = bf16[192,128]{1,0:T(8,128)(2,1)S(1)} collective-permute-done((bf16[192,128]{1,0:T(8,128)(2,1)S(1)}, bf16[192,128]{1,0:T(8,128)(2,1)S(1)}, u32[]{:S(2)}, u32[]{:S(2)}) %collective-permute-start.3) | collective-permute-done | bytes 49184 | tf_op jit(solution)/shard_map/ppermute | solution.py:443
  26.9 0.0 all-to-all-done.x_ref
  26.9 0.9 %kernel_grad.3 = (f32[128,1152]{1,0:T(8,128)S(1)}, f32[128,1152]{1,0:T(8,128)S(1)}) custom-call(bf16[4,192,256]{2,1,0:T(8,128)(2,1)S(1)} %all-to-all-done.x_ref, bf16[192,128]{1,0:T(8,128)(2,1)S(1)} %pointwise.1.own_ref.refs_0_, bf16[192,128]{1,0:T(8,128)(2,1)S(1)} %collective-permute-done.2.above_ref.refs_1_, ...), custom_call_target="tpu_custom_call" | custom-call | flops 339738624 | bytes 393216 | tf_op jit(solution)/shard_map/kernel_grad/pallas_call | solution.py:288
  27.8 1.6 %collective-permute-done.4.refs_0_ = bf16[192,128]{1,0:T(8,128)(2,1)S(1)} collective-permute-done((bf16[192,128]{1,0:T(8,128)(2,1)S(1)}, bf16[192,128]{1,0:T(8,128)(2,1)S(1)}, u32[]{:S(2)}, u32[]{:S(2)}) %collective-permute-start.4) | collective-permute-done | bytes 49184 | tf_op jit(solution)/shard_map/ppermute | solution.py:443
  29.5 0.3 kernel_grad.5
  29.8 0.1 collective-permute-start.5
  29.9 0.3 kernel_grad.4.refs_0_
  30.3 1.2 %collective-permute-done.5.refs_1_ = bf16[128,1152]{1,0:T(8,128)(2,1)S(1)} collective-permute-done((bf16[128,1152]{1,0:T(8,128)(2,1)S(1)}, bf16[128,1152]{1,0:T(8,128)(2,1)S(1)}, u32[]{:S(2)}, u32[]{:S(2)}) %collective-permute-start.5) | collective-permute-done | bytes 294944 | tf_op jit(solution)/shard_map/ppermute | solution.py:457
  31.5 0.1 split_up.1
  31.5 2.5 %collective-permute-start.6 = (bf16[32,1152]{1,0:T(8,128)(2,1)S(1)}, bf16[32,1152]{1,0:T(8,128)(2,1)S(1)}, u32[]{:S(2)}, u32[]{:S(2)}) collective-permute-start(bf16[32,1152]{1,0:T(8,128)(2,1)S(1)} %get-tuple-element.21), channel_id=1, source_target_pairs={{0,24},{4,28},{8,16},{12,20},{16,8},{20,12},{24,0},{28,4},{1,25},{... | collective-permute-start | bytes 221192 | tf_op jit(solution)/shard_map/ppermute | solution.py:463
  34.1 0.5 %collective-permute-start.7 = (bf16[32,1152]{1,0:T(8,128)(2,1)S(1)}, bf16[32,1152]{1,0:T(8,128)(2,1)S(1)}, u32[]{:S(2)}, u32[]{:S(2)}) collective-permute-start(bf16[32,1152]{1,0:T(8,128)(2,1)S(1)} %get-tuple-element.22), channel_id=1, source_target_pairs={{0,16},{4,20},{8,24},{12,28},{16,0},{20,4},{24,8},{28,12},{1,17},{... | collective-permute-start | bytes 221192 | tf_op jit(solution)/shard_map/ppermute | solution.py:463
  34.6 0.5 %collective-permute-start.8 = (bf16[32,1152]{1,0:T(8,128)(2,1)S(1)}, bf16[32,1152]{1,0:T(8,128)(2,1)S(1)}, u32[]{:S(2)}, u32[]{:S(2)}) collective-permute-start(bf16[32,1152]{1,0:T(8,128)(2,1)S(1)} %get-tuple-element.23), channel_id=1, source_target_pairs={{0,8},{4,12},{8,0},{12,4},{16,24},{20,28},{24,16},{28,20},{1,9},{5... | collective-permute-start | bytes 221192 | tf_op jit(solution)/shard_map/ppermute | solution.py:463
  35.1 1.7 %feature_grad.1 = f32[192,1024]{1,0:T(8,128)} custom-call(bf16[192,128]{1,0:T(8,128)(2,1)S(1)} %pointwise.1.own_ref.refs_0_, bf16[192,128]{1,0:T(8,128)(2,1)S(1)} %collective-permute-done.2.above_ref.refs_1_, bf16[192,128]{1,0:T(8,128)(2,1)S(1)} %collective-permute-done.3.below_ref.refs_2_, bf16[9,1024,128]{2,1,0:T(8,128)(2,1)S(1)} %get-tuple-element.14.w_ref), custom_call_target="tpu_custom_call" | custom-call | flops 452984832 | bytes 3145728 | tf_op jit(solution)/shard_map/feature_grad/pallas_call | solution.py:388
  36.8 0.1 collective-permute-done.6.refs_1_
  36.9 1.5 %collective-permute-done.7.refs_2_ = bf16[32,1152]{1,0:T(8,128)(2,1)S(1)} collective-permute-done((bf16[32,1152]{1,0:T(8,128)(2,1)S(1)}, bf16[32,1152]{1,0:T(8,128)(2,1)S(1)}, u32[]{:S(2)}, u32[]{:S(2)}) %collective-permute-start.7) | collective-permute-done | bytes 73760 | tf_op jit(solution)/shard_map/ppermute | solution.py:463
  38.4 0.5 %collective-permute-done.8.refs_3_ = bf16[32,1152]{1,0:T(8,128)(2,1)S(1)} collective-permute-done((bf16[32,1152]{1,0:T(8,128)(2,1)S(1)}, bf16[32,1152]{1,0:T(8,128)(2,1)S(1)}, u32[]{:S(2)}, u32[]{:S(2)}) %collective-permute-start.8) | collective-permute-done | bytes 73760 | tf_op jit(solution)/shard_map/ppermute | solution.py:463
  38.9 0.7 %final_sum.1 = f32[288,128]{1,0:T(8,128)} custom-call(bf16[32,1152]{1,0:T(8,128)(2,1)S(1)} %get-tuple-element.20.refs_0_, bf16[32,1152]{1,0:T(8,128)(2,1)S(1)} %collective-permute-done.6.refs_1_, bf16[32,1152]{1,0:T(8,128)(2,1)S(1)} %collective-permute-done.7.refs_2_, bf16[32,1152]{1,0:T(8,128)(2,1)S(1)} %collective-permute-done.8.refs_3_), custom_call_target="tpu_custom_call" | custom-call | tf_op jit(solution)/shard_map/final_sum/pallas_call | solution.py:348
  (1 shorter events, 0.0 us)
Async XLA Ops:
  2.7 12.1 %copy-start.2 = (s32[1,6,32]{2,0,1:T(1,128)S(1)}, s32[1,6,32]{2,0,1:T(1,128)}, u32[]{:S(2)}) copy-start(s32[1,6,32]{2,0,1:T(1,128)} %param.8) | copy-start | bytes 2308
  2.7 12.1 %copy-start.3 = (s32[1,6,32]{2,0,1:T(1,128)S(1)}, s32[1,6,32]{2,0,1:T(1,128)}, u32[]{:S(2)}) copy-start(s32[1,6,32]{2,0,1:T(1,128)} %param.7) | copy-start | bytes 2308
  2.7 24.2 %all-to-all-start = ((bf16[4,192,256]{2,1,0:T(8,128)(2,1)}), bf16[4,192,256]{2,1,0:T(8,128)(2,1)S(1)}, u32[]{:S(2)}, u32[]{:S(2)}) async-start(bf16[4,192,256]{2,1,0:T(8,128)(2,1)} %get-tuple-element.17), calls=%async_computation | async-start | bytes 786432 | tf_op jit(solution)/shard_map/all_to_all | solution.py:427
  9.1 10.6 %copy-start = (bf16[128,3]{0,1:T(4,128)(2,1)S(1)}, bf16[128,3]{0,1:T(4,128)(2,1)}, u32[]{:S(2)}) copy-start(bf16[128,3]{0,1:T(4,128)(2,1)} %param.11) | copy-start | bytes 2308
  9.1 10.6 %copy-start.1 = (f32[128]{0:T(128)S(1)}, f32[128]{0:T(128)}, u32[]{:S(2)}) copy-start(f32[128]{0:T(128)} %param.10) | copy-start | bytes 1540
  9.5 7.0 %collective-permute-start = (bf16[192,128]{1,0:T(8,128)(2,1)S(1)}, bf16[192,128]{1,0:T(8,128)(2,1)S(1)}, u32[]{:S(2)}, u32[]{:S(2)}) collective-permute-start(bf16[192,128]{1,0:T(8,128)(2,1)S(1)} %get-tuple-element.16), channel_id=1, source_target_pairs={{0,1},{1,2},{2,3},{4,5},{5,6},{6,7},{8,9},{9,10},{10,11},{12,13},{... | collective-permute-start | bytes 147464 | tf_op jit(solution)/shard_map/ppermute | solution.py:429
  13.5 6.2 %collective-permute-start.1 = (bf16[192,128]{1,0:T(8,128)(2,1)S(1)}, bf16[192,128]{1,0:T(8,128)(2,1)S(1)}, u32[]{:S(2)}, u32[]{:S(2)}) collective-permute-start(bf16[192,128]{1,0:T(8,128)(2,1)S(1)} %get-tuple-element.15.after_ref), channel_id=1, source_target_pairs={{1,0},{2,1},{3,2},{5,4},{6,5},{7,6},{9,8},{10,9},{11,10},{13,12},{... | collective-permute-start | bytes 147464 | tf_op jit(solution)/shard_map/ppermute | solution.py:430
  20.1 6.0 %collective-permute-start.2 = (bf16[192,128]{1,0:T(8,128)(2,1)S(1)}, bf16[192,128]{1,0:T(8,128)(2,1)S(1)}, u32[]{:S(2)}, u32[]{:S(2)}) collective-permute-start(bf16[192,128]{1,0:T(8,128)(2,1)S(1)} %pointwise.1.own_ref.refs_0_), channel_id=1, source_target_pairs={{0,1},{1,2},{2,3},{3,0},{4,5},{5,6},{6,7},{7,4},{8,9},{9,10},{10,1... | collective-permute-start | bytes 147464 | tf_op jit(solution)/shard_map/ppermute | solution.py:443
  22.8 4.1 %collective-permute-start.3 = (bf16[192,128]{1,0:T(8,128)(2,1)S(1)}, bf16[192,128]{1,0:T(8,128)(2,1)S(1)}, u32[]{:S(2)}, u32[]{:S(2)}) collective-permute-start(bf16[192,128]{1,0:T(8,128)(2,1)S(1)} %pointwise.1.own_ref.refs_0_), channel_id=1, source_target_pairs={{0,3},{1,0},{2,1},{3,2},{4,7},{5,4},{6,5},{7,6},{8,11},{9,8},{10,9... | collective-permute-start | bytes 147464 | tf_op jit(solution)/shard_map/ppermute | solution.py:443
  24.0 5.5 %collective-permute-start.4 = (bf16[192,128]{1,0:T(8,128)(2,1)S(1)}, bf16[192,128]{1,0:T(8,128)(2,1)S(1)}, u32[]{:S(2)}, u32[]{:S(2)}) collective-permute-start(bf16[192,128]{1,0:T(8,128)(2,1)S(1)} %pointwise.1.own_ref.refs_0_), channel_id=1, source_target_pairs={{0,2},{1,3},{2,0},{3,1},{4,6},{5,7},{6,4},{7,5},{8,10},{9,11},{10,... | collective-permute-start | bytes 147464 | tf_op jit(solution)/shard_map/ppermute | solution.py:443
  29.8 1.6 %collective-permute-start.5 = (bf16[128,1152]{1,0:T(8,128)(2,1)S(1)}, bf16[128,1152]{1,0:T(8,128)(2,1)S(1)}, u32[]{:S(2)}, u32[]{:S(2)}) collective-permute-start(bf16[128,1152]{1,0:T(8,128)(2,1)S(1)} %kernel_grad.5), channel_id=1, source_target_pairs={{0,4},{4,0},{8,12},{12,8},{16,20},{20,16},{24,28},{28,24},{1,5},{5... | collective-permute-start | bytes 884744 | tf_op jit(solution)/shard_map/ppermute | solution.py:457
  31.5 5.4 %collective-permute-start.6 = (bf16[32,1152]{1,0:T(8,128)(2,1)S(1)}, bf16[32,1152]{1,0:T(8,128)(2,1)S(1)}, u32[]{:S(2)}, u32[]{:S(2)}) collective-permute-start(bf16[32,1152]{1,0:T(8,128)(2,1)S(1)} %get-tuple-element.21), channel_id=1, source_target_pairs={{0,24},{4,28},{8,16},{12,20},{16,8},{20,12},{24,0},{28,4},{1,25},{... | collective-permute-start | bytes 221192 | tf_op jit(solution)/shard_map/ppermute | solution.py:463
  34.1 4.4 %collective-permute-start.7 = (bf16[32,1152]{1,0:T(8,128)(2,1)S(1)}, bf16[32,1152]{1,0:T(8,128)(2,1)S(1)}, u32[]{:S(2)}, u32[]{:S(2)}) collective-permute-start(bf16[32,1152]{1,0:T(8,128)(2,1)S(1)} %get-tuple-element.22), channel_id=1, source_target_pairs={{0,16},{4,20},{8,24},{12,28},{16,0},{20,4},{24,8},{28,12},{1,17},{... | collective-permute-start | bytes 221192 | tf_op jit(solution)/shard_map/ppermute | solution.py:463
  34.6 4.4 %collective-permute-start.8 = (bf16[32,1152]{1,0:T(8,128)(2,1)S(1)}, bf16[32,1152]{1,0:T(8,128)(2,1)S(1)}, u32[]{:S(2)}, u32[]{:S(2)}) collective-permute-start(bf16[32,1152]{1,0:T(8,128)(2,1)S(1)} %get-tuple-element.23), channel_id=1, source_target_pairs={{0,8},{4,12},{8,0},{12,4},{16,24},{20,28},{24,16},{28,20},{1,9},{5... | collective-permute-start | bytes 221192 | tf_op jit(solution)/shard_map/ppermute | solution.py:463

commit v13 on v12

--- a/solution.py
+++ b/solution.py
@@ -49,29 +49,37 @@
     )
 
 
-def load_kernel(replicas, cover, x_hbm, w_hbm, x_ref, w_ref, *refs):
-    *outs, room, x_sem, w_sem, out_sems = refs
-    x_load = pltpu.make_async_copy(x_hbm, x_ref, x_sem)
-    w_load = pltpu.make_async_copy(w_hbm, w_ref, w_sem)
-    x_load.start()
-    w_load.start()
-    x_load.wait()
-    copies = []
-    for out in outs:
-        bands = room.shape[0]
-        x = x_ref[...]
-        for s in range(bands):
-            room[s] = jnp.concatenate(
-                [
-                    x[:, (d * bands + s) * cover : (d * bands + s + 1) * cover]
-                    for d in replica_order(replicas)
-                ],
-                axis=1,
-            )
-            copies.append(pltpu.make_async_copy(room.at[s], out.at[s], out_sems.at[s]))
-            copies[-1].start()
-    w_load.wait()
-    for copy in copies:
+def load_kernel(replicas, cover, chunks, x_hbm, w_hbm, x_ref, w_ref, *refs):
+    *outs, room, x_sems, w_sems, out_sems = refs
+    rows = x_ref.shape[0] // chunks
+    x_loads, w_loads, copies = [], [], []
+    for n in range(chunks):
+        here = pl.ds(n * rows, rows)
+        x_loads.append(pltpu.make_async_copy(x_hbm.at[here], x_ref.at[here], x_sems.at[n]))
+        x_loads[-1].start()
+    for a in range(3):
+        here = pl.ds(3 * a, 3)
+        w_loads.append(pltpu.make_async_copy(w_hbm.at[here], w_ref.at[here], w_sems.at[a]))
+        w_loads[-1].start()
+    for n in range(chunks):
+        x_loads[n].wait()
+        here = pl.ds(n * rows, rows)
+        for out in outs:
+            bands = room.shape[0]
+            x = x_ref[here]
+            for s in range(bands):
+                room[s, here] = jnp.concatenate(
+                    [
+                        x[:, (d * bands + s) * cover : (d * bands + s + 1) * cover]
+                        for d in replica_order(replicas)
+                    ],
+                    axis=1,
+                )
+                copies.append(
+                    pltpu.make_async_copy(room.at[s, here], out.at[s, here], out_sems.at[n, s])
+                )
+                copies[-1].start()
+    for copy in w_loads + copies:
         copy.wait()
 
 
@@ -81,8 +89,9 @@
     vmem = pl.BlockSpec(memory_space=pltpu.VMEM)
     shape = (bands, pixels, replicas * cover)
     count = 1 if blocks else 0
-    return pl.pallas_call(
-        functools.partial(load_kernel, replicas, cover),
+    chunks = 4 if pixels % 64 == 0 else 1
+    return pl.pallas_call(
+        functools.partial(load_kernel, replicas, cover, chunks),
         in_specs=[hbm, hbm],
         out_specs=[vmem, vmem] + [hbm] * count,
         out_shape=[
@@ -92,9 +101,9 @@
         + [pltpu.HBM(shape, flat.dtype)] * count,
         scratch_shapes=[
             pltpu.VMEM(shape, flat.dtype),
-            pltpu.SemaphoreType.DMA,
-            pltpu.SemaphoreType.DMA,
-            pltpu.SemaphoreType.DMA((bands,)),
+            pltpu.SemaphoreType.DMA((chunks,)),
+            pltpu.SemaphoreType.DMA((3,)),
+            pltpu.SemaphoreType.DMA((chunks, bands)),
         ],
         compiler_params=pltpu.CompilerParams(vmem_limit_bytes=VMEM_LIMIT),
         cost_estimate=pl.CostEstimate(
@@ -330,24 +339,38 @@
     )(*terms)
 
 
-def final_kernel(replicas, *refs):
-    *ins, out_ref = refs
+def final_kernel(replicas, chunks, *refs):
+    *ins, out, room, sems = refs
     cover, lanes = ins[0].shape
-    width = out_ref.shape[1]
+    width = out.shape[1]
     taps = lanes // width
-    total = ins[0][...].astype(jnp.float32)
-    for ref in ins[1:]:
-        total += ref[...].astype(jnp.float32)
-    total = total / replicas
-    for t in range(taps):
-        out_ref[pl.ds(t, cover, stride=taps), :] = total[:, t * width : (t + 1) * width]
+    step = cover // chunks
+    copies = []
+    for n in range(chunks):
+        here = slice(n * step, (n + 1) * step)
+        total = ins[0][here].astype(jnp.float32)
+        for ref in ins[1:]:
+            total += ref[here].astype(jnp.float32)
+        total = total / replicas
+        for t in range(taps):
+            rows = pl.ds(n * step * taps + t, step, stride=taps)
+            room[rows, :] = total[:, t * width : (t + 1) * width]
+        rows = pl.ds(n * step * taps, step * taps)
+        copies.append(pltpu.make_async_copy(room.at[rows], out.at[rows], sems.at[n]))
+        copies[-1].start()
+    for copy in copies:
+        copy.wait()
 
 
 def final(blocks, width, replicas):
     cover, lanes = blocks[0].shape
-    return pl.pallas_call(
-        functools.partial(final_kernel, replicas),
-        out_shape=jax.ShapeDtypeStruct((cover * lanes // width, width), jnp.float32),
+    chunks = 2 if cover % 32 == 0 else 1
+    shape = (cover * lanes // width, width)
+    return pl.pallas_call(
+        functools.partial(final_kernel, replicas, chunks),
+        out_specs=pl.BlockSpec(memory_space=pltpu.HBM),
+        out_shape=pltpu.HBM(shape, jnp.float32),
+        scratch_shapes=[pltpu.VMEM(shape, jnp.float32), pltpu.SemaphoreType.DMA((chunks,))],
         compiler_params=pltpu.CompilerParams(vmem_limit_bytes=VMEM_LIMIT),
         name="final_sum",
     )(*blocks)

time: 39.9 us -> 40.3 us (1.010)
  no operation moved by 1% of the time
where the time goes in v13:
time: 40.3 us; the launch traced here: 40 us
  starting transfers between devices  20 us (50%)
  waiting for transfers between devices  11.5 us (29%)
  Pallas kernels  7.8 us (19%)
  between operations  0.76 us (2%)
    all_to_all x1, starting transfers between devices, on_device(): whole = lax.all_to_all(split[0], 'space', 0, 0)  6.33 us
    ppermute x3, starting transfers between devices, on_device(): lax.ppermute(gradient, 'space', [(i, (i + k) % bands) for i in range(band...  4.79 us
    ppermute x1, starting transfers between devices, on_device(): above = lax.ppermute(down, 'space', [(i, i + 1) for i in range(bands - 1)])  3.93 us
    ppermute x3, waiting for transfers between devices, on_device(): lax.ppermute(gradient, 'space', [(i, (i + k) % bands) for i in range(band...  3.7 us
    ppermute x3, starting transfers between devices, on_device(): came.append(lax.ppermute(blocks[k], 'dp', pairs))  3.55 us
    ppermute x1, waiting for transfers between devices, on_device(): below = lax.ppermute(up, 'space', [(i + 1, i) for i in range(bands - 1)])  3.06 us
    pallas_call x1, Pallas kernels, load(): pl.pallas_call(functools.partial(load_kernel, replicas, cover, chunks), i...  2.45 us
    ppermute x3, waiting for transfers between devices, on_device(): came.append(lax.ppermute(blocks[k], 'dp', pairs))  2.1 us
  transfers between devices with their start and end apart: 10, of which 9 were waited for; matrix products, arithmetic and copies ran while one was open for 0% of the time, Pallas kernels for 11%

profile of v13, /device:TPU:0, one launch (start us, length us, event | category | flops | bytes accessed | tf_op | source)
XLA Modules:
  0.0 40.0 jit_solution(11301810444607462740)
XLA Ops:
  0.6 2.5 %load.1 = (bf16[192,1024]{1,0:T(8,128)(2,1)S(1)}, bf16[9,1024,128]{2,1,0:T(8,128)(2,1)S(1)}, bf16[4,192,256]{2,1,0:T(8,128)(2,1)}) custom-call(bf16[192,1024]{1,0:T(8,128)(2,1)} %bitcast.13, bf16[9,1024,128]{2,1,0:T(8,128)(2,1)} %bitcast.11), custom_call_target="tpu_custom_call" | custom-call | bytes 3145728 | tf_op jit(solution)/shard_map/load/pallas_call | solution.py:93
  3.1 0.0 copy-start.2
  3.1 0.0 copy-start.3
  3.1 6.3 %all-to-all-start = ((bf16[4,192,256]{2,1,0:T(8,128)(2,1)}), bf16[4,192,256]{2,1,0:T(8,128)(2,1)S(1)}, u32[]{:S(2)}, u32[]{:S(2)}) async-start(bf16[4,192,256]{2,1,0:T(8,128)(2,1)} %get-tuple-element.17), calls=%async_computation | async-start | bytes 786432 | tf_op jit(solution)/shard_map/all_to_all | solution.py:450
  9.4 0.0 copy-start
  9.4 0.0 copy-start.1
  9.4 0.5 %halo.1 = (bf16[192,128]{1,0:T(8,128)(2,1)S(1)}, bf16[192,128]{1,0:T(8,128)(2,1)S(1)}) custom-call(bf16[192,1024]{1,0:T(8,128)(2,1)S(1)} %get-tuple-element.13.x_ref, bf16[9,1024,128]{2,1,0:T(8,128)(2,1)S(1)} %get-tuple-element.14.w_ref), custom_call_target="tpu_custom_call" | custom-call | flops 301989888 | bytes 1966080 | tf_op jit(solution)/shard_map/halo/pallas_call | solution.py:147
  9.9 3.9 %collective-permute-start = (bf16[192,128]{1,0:T(8,128)(2,1)S(1)}, bf16[192,128]{1,0:T(8,128)(2,1)S(1)}, u32[]{:S(2)}, u32[]{:S(2)}) collective-permute-start(bf16[192,128]{1,0:T(8,128)(2,1)S(1)} %get-tuple-element.16), channel_id=1, source_target_pairs={{0,1},{1,2},{2,3},{4,5},{5,6},{6,7},{8,9},{9,10},{10,11},{12,13},{... | collective-permute-start | bytes 147464 | tf_op jit(solution)/shard_map/ppermute | solution.py:452
  13.9 1.3 %collective-permute-start.1 = (bf16[192,128]{1,0:T(8,128)(2,1)S(1)}, bf16[192,128]{1,0:T(8,128)(2,1)S(1)}, u32[]{:S(2)}, u32[]{:S(2)}) collective-permute-start(bf16[192,128]{1,0:T(8,128)(2,1)S(1)} %get-tuple-element.15.after_ref), channel_id=1, source_target_pairs={{1,0},{2,1},{3,2},{5,4},{6,5},{7,6},{9,8},{10,9},{11,10},{13,12},{... | collective-permute-start | bytes 147464 | tf_op jit(solution)/shard_map/ppermute | solution.py:453
  15.2 0.0 copy-done.2
  15.2 0.0 copy-done.3
  15.2 0.4 middle_taps.1.middle_ref
  15.6 1.4 %collective-permute-done.above_ref = bf16[192,128]{1,0:T(8,128)(2,1)S(1)} collective-permute-done((bf16[192,128]{1,0:T(8,128)(2,1)S(1)}, bf16[192,128]{1,0:T(8,128)(2,1)S(1)}, u32[]{:S(2)}, u32[]{:S(2)}) %collective-permute-start) | collective-permute-done | bytes 49184 | tf_op jit(solution)/shard_map/ppermute | solution.py:452
  17.0 3.1 %collective-permute-done.1.below_ref = bf16[192,128]{1,0:T(8,128)(2,1)S(1)} collective-permute-done((bf16[192,128]{1,0:T(8,128)(2,1)S(1)}, bf16[192,128]{1,0:T(8,128)(2,1)S(1)}, u32[]{:S(2)}, u32[]{:S(2)}) %collective-permute-start.1) | collective-permute-done | bytes 49184 | tf_op jit(solution)/shard_map/ppermute | solution.py:453
  20.0 0.0 copy-done
  20.0 0.0 copy-done.1
  20.0 0.4 %pointwise.1.own_ref.refs_0_ = bf16[192,128]{1,0:T(8,128)(2,1)S(1)} custom-call(f32[192,128]{1,0:T(8,128)S(1)} %middle_taps.1.middle_ref, bf16[192,128]{1,0:T(8,128)(2,1)S(1)} %collective-permute-done.above_ref, bf16[192,128]{1,0:T(8,128)(2,1)S(1)} %collective-permute-done.1.below_ref, f32[1,128]{1,0:T(1,128)S(1)} %bitcast.10, bf16[3,128]{1,0:T(4,128)(2,1)S(1)} %bitcast.9, ...), custom_call_target="tpu_custom_call" | custom-call | flops 737280 | bytes 245760 | tf_op jit(solution)/shard_map/pointwise/pallas_call | solution.py:234
  20.5 2.8 %collective-permute-start.2 = (bf16[192,128]{1,0:T(8,128)(2,1)S(1)}, bf16[192,128]{1,0:T(8,128)(2,1)S(1)}, u32[]{:S(2)}, u32[]{:S(2)}) collective-permute-start(bf16[192,128]{1,0:T(8,128)(2,1)S(1)} %pointwise.1.own_ref.refs_0_), channel_id=1, source_target_pairs={{0,1},{1,2},{2,3},{3,0},{4,5},{5,6},{6,7},{7,4},{8,9},{9,10},{10,1... | collective-permute-start | bytes 147464 | tf_op jit(solution)/shard_map/ppermute | solution.py:466
  23.2 1.1 %collective-permute-start.3 = (bf16[192,128]{1,0:T(8,128)(2,1)S(1)}, bf16[192,128]{1,0:T(8,128)(2,1)S(1)}, u32[]{:S(2)}, u32[]{:S(2)}) collective-permute-start(bf16[192,128]{1,0:T(8,128)(2,1)S(1)} %pointwise.1.own_ref.refs_0_), channel_id=1, source_target_pairs={{0,3},{1,0},{2,1},{3,2},{4,7},{5,4},{6,5},{7,6},{8,11},{9,8},{10,9... | collective-permute-start | bytes 147464 | tf_op jit(solution)/shard_map/ppermute | solution.py:466
  24.4 0.9 %collective-permute-start.4 = (bf16[192,128]{1,0:T(8,128)(2,1)S(1)}, bf16[192,128]{1,0:T(8,128)(2,1)S(1)}, u32[]{:S(2)}, u32[]{:S(2)}) collective-permute-start(bf16[192,128]{1,0:T(8,128)(2,1)S(1)} %pointwise.1.own_ref.refs_0_), channel_id=1, source_target_pairs={{0,2},{1,3},{2,0},{3,1},{4,6},{5,7},{6,4},{7,5},{8,10},{9,11},{10,... | collective-permute-start | bytes 147464 | tf_op jit(solution)/shard_map/ppermute | solution.py:466
  25.3 1.2 %collective-permute-done.2.above_ref.refs_1_ = bf16[192,128]{1,0:T(8,128)(2,1)S(1)} collective-permute-done((bf16[192,128]{1,0:T(8,128)(2,1)S(1)}, bf16[192,128]{1,0:T(8,128)(2,1)S(1)}, u32[]{:S(2)}, u32[]{:S(2)}) %collective-permute-start.2) | collective-permute-done | bytes 49184 | tf_op jit(solution)/shard_map/ppermute | solution.py:466
  26.5 0.8 %collective-permute-done.3.below_ref.refs_2_ = bf16[192,128]{1,0:T(8,128)(2,1)S(1)} collective-permute-done((bf16[192,128]{1,0:T(8,128)(2,1)S(1)}, bf16[192,128]{1,0:T(8,128)(2,1)S(1)}, u32[]{:S(2)}, u32[]{:S(2)}) %collective-permute-start.3) | collective-permute-done | bytes 49184 | tf_op jit(solution)/shard_map/ppermute | solution.py:466
  27.3 0.0 all-to-all-done.x_ref
  27.3 0.9 %kernel_grad.3 = (f32[128,1152]{1,0:T(8,128)S(1)}, f32[128,1152]{1,0:T(8,128)S(1)}) custom-call(bf16[4,192,256]{2,1,0:T(8,128)(2,1)S(1)} %all-to-all-done.x_ref, bf16[192,128]{1,0:T(8,128)(2,1)S(1)} %pointwise.1.own_ref.refs_0_, bf16[192,128]{1,0:T(8,128)(2,1)S(1)} %collective-permute-done.2.above_ref.refs_1_, ...), custom_call_target="tpu_custom_call" | custom-call | flops 339738624 | bytes 393216 | tf_op jit(solution)/shard_map/kernel_grad/pallas_call | solution.py:297
  28.2 1.6 %collective-permute-done.4.refs_0_ = bf16[192,128]{1,0:T(8,128)(2,1)S(1)} collective-permute-done((bf16[192,128]{1,0:T(8,128)(2,1)S(1)}, bf16[192,128]{1,0:T(8,128)(2,1)S(1)}, u32[]{:S(2)}, u32[]{:S(2)}) %collective-permute-start.4) | collective-permute-done | bytes 49184 | tf_op jit(solution)/shard_map/ppermute | solution.py:466
  29.9 0.3 kernel_grad.5
  30.2 0.1 collective-permute-start.5
  30.3 0.4 kernel_grad.4.refs_0_
  30.7 1.2 %collective-permute-done.5.refs_1_ = bf16[128,1152]{1,0:T(8,128)(2,1)S(1)} collective-permute-done((bf16[128,1152]{1,0:T(8,128)(2,1)S(1)}, bf16[128,1152]{1,0:T(8,128)(2,1)S(1)}, u32[]{:S(2)}, u32[]{:S(2)}) %collective-permute-start.5) | collective-permute-done | bytes 294944 | tf_op jit(solution)/shard_map/ppermute | solution.py:480
  31.9 0.1 split_up.1
  31.9 2.5 %collective-permute-start.6 = (bf16[32,1152]{1,0:T(8,128)(2,1)S(1)}, bf16[32,1152]{1,0:T(8,128)(2,1)S(1)}, u32[]{:S(2)}, u32[]{:S(2)}) collective-permute-start(bf16[32,1152]{1,0:T(8,128)(2,1)S(1)} %get-tuple-element.21), channel_id=1, source_target_pairs={{0,24},{4,28},{8,16},{12,20},{16,8},{20,12},{24,0},{28,4},{1,25},{... | collective-permute-start | bytes 221192 | tf_op jit(solution)/shard_map/ppermute | solution.py:486
  34.5 0.5 %collective-permute-start.7 = (bf16[32,1152]{1,0:T(8,128)(2,1)S(1)}, bf16[32,1152]{1,0:T(8,128)(2,1)S(1)}, u32[]{:S(2)}, u32[]{:S(2)}) collective-permute-start(bf16[32,1152]{1,0:T(8,128)(2,1)S(1)} %get-tuple-element.22), channel_id=1, source_target_pairs={{0,16},{4,20},{8,24},{12,28},{16,0},{20,4},{24,8},{28,12},{1,17},{... | collective-permute-start | bytes 221192 | tf_op jit(solution)/shard_map/ppermute | solution.py:486
  35.0 0.5 %collective-permute-start.8 = (bf16[32,1152]{1,0:T(8,128)(2,1)S(1)}, bf16[32,1152]{1,0:T(8,128)(2,1)S(1)}, u32[]{:S(2)}, u32[]{:S(2)}) collective-permute-start(bf16[32,1152]{1,0:T(8,128)(2,1)S(1)} %get-tuple-element.23), channel_id=1, source_target_pairs={{0,8},{4,12},{8,0},{12,4},{16,24},{20,28},{24,16},{28,20},{1,9},{5... | collective-permute-start | bytes 221192 | tf_op jit(solution)/shard_map/ppermute | solution.py:486
  35.5 1.7 %feature_grad.1 = f32[192,1024]{1,0:T(8,128)} custom-call(bf16[192,128]{1,0:T(8,128)(2,1)S(1)} %pointwise.1.own_ref.refs_0_, bf16[192,128]{1,0:T(8,128)(2,1)S(1)} %collective-permute-done.2.above_ref.refs_1_, bf16[192,128]{1,0:T(8,128)(2,1)S(1)} %collective-permute-done.3.below_ref.refs_2_, bf16[9,1024,128]{2,1,0:T(8,128)(2,1)S(1)} %get-tuple-element.14.w_ref), custom_call_target="tpu_custom_call" | custom-call | flops 452984832 | bytes 3145728 | tf_op jit(solution)/shard_map/feature_grad/pallas_call | solution.py:411
  37.2 0.1 collective-permute-done.6.refs_1_
  37.3 1.5 %collective-permute-done.7.refs_2_ = bf16[32,1152]{1,0:T(8,128)(2,1)S(1)} collective-permute-done((bf16[32,1152]{1,0:T(8,128)(2,1)S(1)}, bf16[32,1152]{1,0:T(8,128)(2,1)S(1)}, u32[]{:S(2)}, u32[]{:S(2)}) %collective-permute-start.7) | collective-permute-done | bytes 73760 | tf_op jit(solution)/shard_map/ppermute | solution.py:486
  38.8 0.5 %collective-permute-done.8.refs_3_ = bf16[32,1152]{1,0:T(8,128)(2,1)S(1)} collective-permute-done((bf16[32,1152]{1,0:T(8,128)(2,1)S(1)}, bf16[32,1152]{1,0:T(8,128)(2,1)S(1)}, u32[]{:S(2)}, u32[]{:S(2)}) %collective-permute-start.8) | collective-permute-done | bytes 73760 | tf_op jit(solution)/shard_map/ppermute | solution.py:486
  39.3 0.7 %final_sum.1 = f32[288,128]{1,0:T(8,128)} custom-call(bf16[32,1152]{1,0:T(8,128)(2,1)S(1)} %get-tuple-element.20.refs_0_, bf16[32,1152]{1,0:T(8,128)(2,1)S(1)} %collective-permute-done.6.refs_1_, bf16[32,1152]{1,0:T(8,128)(2,1)S(1)} %collective-permute-done.7.refs_2_, bf16[32,1152]{1,0:T(8,128)(2,1)S(1)} %collective-permute-done.8.refs_3_), custom_call_target="tpu_custom_call" | custom-call | tf_op jit(solution)/shard_map/final_sum/pallas_call | solution.py:369
  (1 shorter events, 0.0 us)
Async XLA Ops:
  3.1 12.1 %copy-start.2 = (s32[1,6,32]{2,0,1:T(1,128)S(1)}, s32[1,6,32]{2,0,1:T(1,128)}, u32[]{:S(2)}) copy-start(s32[1,6,32]{2,0,1:T(1,128)} %param.8) | copy-start | bytes 2308
  3.1 12.1 %copy-start.3 = (s32[1,6,32]{2,0,1:T(1,128)S(1)}, s32[1,6,32]{2,0,1:T(1,128)}, u32[]{:S(2)}) copy-start(s32[1,6,32]{2,0,1:T(1,128)} %param.7) | copy-start | bytes 2308
  3.1 24.2 %all-to-all-start = ((bf16[4,192,256]{2,1,0:T(8,128)(2,1)}), bf16[4,192,256]{2,1,0:T(8,128)(2,1)S(1)}, u32[]{:S(2)}, u32[]{:S(2)}) async-start(bf16[4,192,256]{2,1,0:T(8,128)(2,1)} %get-tuple-element.17), calls=%async_computation | async-start | bytes 786432 | tf_op jit(solution)/shard_map/all_to_all | solution.py:450
  9.4 10.6 %copy-start = (bf16[128,3]{0,1:T(4,128)(2,1)S(1)}, bf16[128,3]{0,1:T(4,128)(2,1)}, u32[]{:S(2)}) copy-start(bf16[128,3]{0,1:T(4,128)(2,1)} %param.11) | copy-start | bytes 2308
  9.4 10.6 %copy-start.1 = (f32[128]{0:T(128)S(1)}, f32[128]{0:T(128)}, u32[]{:S(2)}) copy-start(f32[128]{0:T(128)} %param.10) | copy-start | bytes 1540
  9.9 7.0 %collective-permute-start = (bf16[192,128]{1,0:T(8,128)(2,1)S(1)}, bf16[192,128]{1,0:T(8,128)(2,1)S(1)}, u32[]{:S(2)}, u32[]{:S(2)}) collective-permute-start(bf16[192,128]{1,0:T(8,128)(2,1)S(1)} %get-tuple-element.16), channel_id=1, source_target_pairs={{0,1},{1,2},{2,3},{4,5},{5,6},{6,7},{8,9},{9,10},{10,11},{12,13},{... | collective-permute-start | bytes 147464 | tf_op jit(solution)/shard_map/ppermute | solution.py:452
  13.9 6.2 %collective-permute-start.1 = (bf16[192,128]{1,0:T(8,128)(2,1)S(1)}, bf16[192,128]{1,0:T(8,128)(2,1)S(1)}, u32[]{:S(2)}, u32[]{:S(2)}) collective-permute-start(bf16[192,128]{1,0:T(8,128)(2,1)S(1)} %get-tuple-element.15.after_ref), channel_id=1, source_target_pairs={{1,0},{2,1},{3,2},{5,4},{6,5},{7,6},{9,8},{10,9},{11,10},{13,12},{... | collective-permute-start | bytes 147464 | tf_op jit(solution)/shard_map/ppermute | solution.py:453
  20.5 6.0 %collective-permute-start.2 = (bf16[192,128]{1,0:T(8,128)(2,1)S(1)}, bf16[192,128]{1,0:T(8,128)(2,1)S(1)}, u32[]{:S(2)}, u32[]{:S(2)}) collective-permute-start(bf16[192,128]{1,0:T(8,128)(2,1)S(1)} %pointwise.1.own_ref.refs_0_), channel_id=1, source_target_pairs={{0,1},{1,2},{2,3},{3,0},{4,5},{5,6},{6,7},{7,4},{8,9},{9,10},{10,1... | collective-permute-start | bytes 147464 | tf_op jit(solution)/shard_map/ppermute | solution.py:466
  23.2 4.1 %collective-permute-start.3 = (bf16[192,128]{1,0:T(8,128)(2,1)S(1)}, bf16[192,128]{1,0:T(8,128)(2,1)S(1)}, u32[]{:S(2)}, u32[]{:S(2)}) collective-permute-start(bf16[192,128]{1,0:T(8,128)(2,1)S(1)} %pointwise.1.own_ref.refs_0_), channel_id=1, source_target_pairs={{0,3},{1,0},{2,1},{3,2},{4,7},{5,4},{6,5},{7,6},{8,11},{9,8},{10,9... | collective-permute-start | bytes 147464 | tf_op jit(solution)/shard_map/ppermute | solution.py:466
  24.4 5.5 %collective-permute-start.4 = (bf16[192,128]{1,0:T(8,128)(2,1)S(1)}, bf16[192,128]{1,0:T(8,128)(2,1)S(1)}, u32[]{:S(2)}, u32[]{:S(2)}) collective-permute-start(bf16[192,128]{1,0:T(8,128)(2,1)S(1)} %pointwise.1.own_ref.refs_0_), channel_id=1, source_target_pairs={{0,2},{1,3},{2,0},{3,1},{4,6},{5,7},{6,4},{7,5},{8,10},{9,11},{10,... | collective-permute-start | bytes 147464 | tf_op jit(solution)/shard_map/ppermute | solution.py:466
  30.2 1.6 %collective-permute-start.5 = (bf16[128,1152]{1,0:T(8,128)(2,1)S(1)}, bf16[128,1152]{1,0:T(8,128)(2,1)S(1)}, u32[]{:S(2)}, u32[]{:S(2)}) collective-permute-start(bf16[128,1152]{1,0:T(8,128)(2,1)S(1)} %kernel_grad.5), channel_id=1, source_target_pairs={{0,4},{4,0},{8,12},{12,8},{16,20},{20,16},{24,28},{28,24},{1,5},{5... | collective-permute-start | bytes 884744 | tf_op jit(solution)/shard_map/ppermute | solution.py:480
  31.9 5.4 %collective-permute-start.6 = (bf16[32,1152]{1,0:T(8,128)(2,1)S(1)}, bf16[32,1152]{1,0:T(8,128)(2,1)S(1)}, u32[]{:S(2)}, u32[]{:S(2)}) collective-permute-start(bf16[32,1152]{1,0:T(8,128)(2,1)S(1)} %get-tuple-element.21), channel_id=1, source_target_pairs={{0,24},{4,28},{8,16},{12,20},{16,8},{20,12},{24,0},{28,4},{1,25},{... | collective-permute-start | bytes 221192 | tf_op jit(solution)/shard_map/ppermute | solution.py:486
  34.5 4.4 %collective-permute-start.7 = (bf16[32,1152]{1,0:T(8,128)(2,1)S(1)}, bf16[32,1152]{1,0:T(8,128)(2,1)S(1)}, u32[]{:S(2)}, u32[]{:S(2)}) collective-permute-start(bf16[32,1152]{1,0:T(8,128)(2,1)S(1)} %get-tuple-element.22), channel_id=1, source_target_pairs={{0,16},{4,20},{8,24},{12,28},{16,0},{20,4},{24,8},{28,12},{1,17},{... | collective-permute-start | bytes 221192 | tf_op jit(solution)/shard_map/ppermute | solution.py:486
  35.0 4.4 %collective-permute-start.8 = (bf16[32,1152]{1,0:T(8,128)(2,1)S(1)}, bf16[32,1152]{1,0:T(8,128)(2,1)S(1)}, u32[]{:S(2)}, u32[]{:S(2)}) collective-permute-start(bf16[32,1152]{1,0:T(8,128)(2,1)S(1)} %get-tuple-element.23), channel_id=1, source_target_pairs={{0,8},{4,12},{8,0},{12,4},{16,24},{20,28},{24,16},{28,20},{1,9},{5... | collective-permute-start | bytes 221192 | tf_op jit(solution)/shard_map/ppermute | solution.py:486

commit v14 on v12

--- a/solution.py
+++ b/solution.py
@@ -49,8 +49,9 @@
     )
 
 
-def load_kernel(replicas, cover, x_hbm, w_hbm, x_ref, w_ref, *refs):
+def load_kernel(replicas, cover, tail, x_hbm, w_hbm, x_ref, w_ref, *refs):
     *outs, room, x_sem, w_sem, out_sems = refs
+    outs, tails = outs[:1], outs[1:]
     x_load = pltpu.make_async_copy(x_hbm, x_ref, x_sem)
     w_load = pltpu.make_async_copy(w_hbm, w_ref, w_sem)
     x_load.start()
@@ -68,28 +69,37 @@
                 ],
                 axis=1,
             )
-            copies.append(pltpu.make_async_copy(room.at[s], out.at[s], out_sems.at[s]))
+            head = pl.ds(0, out.shape[1])
+            copies.append(pltpu.make_async_copy(room.at[s, head], out.at[s], out_sems.at[s]))
             copies[-1].start()
+            for tail_ref in tails:
+                width = tail_ref.shape[2]
+                for p in range(room.shape[2] // width):
+                    block = room[s, out.shape[1] :, p * width : (p + 1) * width]
+                    tail_ref[s, p * tail : (p + 1) * tail] = block
     w_load.wait()
     for copy in copies:
         copy.wait()
 
 
-def load(flat, weight, bands, replicas, cover, blocks):
+def load(flat, weight, bands, replicas, cover, blocks, tail):
     pixels, channels = flat.shape
     hbm = pl.BlockSpec(memory_space=pltpu.HBM)
     vmem = pl.BlockSpec(memory_space=pltpu.VMEM)
     shape = (bands, pixels, replicas * cover)
+    width = weight.shape[2]
     count = 1 if blocks else 0
-    return pl.pallas_call(
-        functools.partial(load_kernel, replicas, cover),
+    tails = 1 if tail else 0
+    return pl.pallas_call(
+        functools.partial(load_kernel, replicas, cover, tail),
         in_specs=[hbm, hbm],
-        out_specs=[vmem, vmem] + [hbm] * count,
+        out_specs=[vmem, vmem] + [hbm] * count + [vmem] * tails,
         out_shape=[
             pltpu.VMEM(flat.shape, flat.dtype),
             pltpu.VMEM(weight.shape, weight.dtype),
         ]
-        + [pltpu.HBM(shape, flat.dtype)] * count,
+        + [pltpu.HBM((bands, pixels - tail, shape[2]), flat.dtype)] * count
+        + [pltpu.VMEM((bands, shape[2] // width * tail, width), flat.dtype)] * tails,
         scratch_shapes=[
             pltpu.VMEM(shape, flat.dtype),
             pltpu.SemaphoreType.DMA,
@@ -190,7 +200,7 @@
 
 
 def pointwise_kernel(
-    middle_ref, above_ref, below_ref, bias_ref, class_ref, label_ref, scale_ref, out_ref
+    extras, middle_ref, above_ref, below_ref, bias_ref, class_ref, label_ref, scale_ref, *refs
 ):
     pixels, width = middle_ref.shape
     edge = above_ref.shape[0]
@@ -217,14 +227,24 @@
         grad_logits[:, k : k + 1] * wide[k : k + 1] for k in range(classes.shape[0])
     )
     gradient = hidden_grad * sigmoid_z * (1.0 + preact * (1.0 - sigmoid_z))
-    out_ref[...] = gradient.astype(out_ref.dtype)
-
-
-def pointwise(middle, above, below, bias, classes, labels, scale):
+    gradient = gradient.astype(jnp.bfloat16)
+    tails, outs = refs[:extras], refs[extras:]
+    band = lax.axis_index("space")
+    bands = len(outs)
+    outs[0][...] = gradient
+    for k in range(1, bands):
+        outs[k][:pixels] = gradient
+        for tail_ref in tails:
+            outs[k][pixels:] = tail_ref[lax.rem(band + k, bands)]
+
+
+def pointwise(middle, above, below, bias, classes, labels, scale, bands, tails):
     pixels, width = middle.shape
-    return pl.pallas_call(
-        pointwise_kernel,
-        out_shape=jax.ShapeDtypeStruct((pixels, width), jnp.bfloat16),
+    rows = pixels + sum(t.shape[1] for t in tails)
+    shapes = [(pixels, width)] + [(rows, width)] * (bands - 1)
+    return pl.pallas_call(
+        functools.partial(pointwise_kernel, len(tails)),
+        out_shape=[pltpu.VMEM(shape, jnp.bfloat16) for shape in shapes],
         compiler_params=pltpu.CompilerParams(vmem_limit_bytes=VMEM_LIMIT),
         cost_estimate=pl.CostEstimate(
             flops=30 * pixels * width,
@@ -232,7 +252,7 @@
             transcendentals=pixels * width,
         ),
         name="pointwise",
-    )(middle, above, below, bias, classes, labels, scale)
+    )(middle, above, below, bias, classes, labels, scale, *tails)
 
 
 def shifted_taps(gradient, columns, reach):
@@ -243,20 +263,27 @@
     )
 
 
-def kernel_grad_kernel(columns, reach, parts, others, distances, before, x_ref, *refs):
-    count = len(distances)
-    g_refs, sums, outs = refs[:count], refs[count : count + before], refs[count + before : -1]
-    padded = refs[-1]
-    bands, pixels, lanes = x_ref.shape
-    width = g_refs[0].shape[1]
+def kernel_grad_kernel(columns, reach, parts, others, here, late, before, tail, x_ref, *refs):
+    bands, head, lanes = x_ref.shape
+    g_refs, refs = refs[:bands], refs[bands:]
+    tails, refs = refs[: 1 if tail else 0], refs[1 if tail else 0 :]
+    sums, outs, padded = refs[:before], refs[before:-1], refs[-1]
+    pixels, width = g_refs[0].shape
     total = bands * pixels
     edge = reach * columns
     extra = lanes // parts
     band = lax.axis_index("space")
-    none = jnp.zeros((edge, padded.shape[1]), padded.dtype)
+    none = jnp.zeros((edge, extra), padded.dtype)
     padded[:edge] = none
     padded[edge + total :] = none
-    shifted = [shifted_taps(g_ref[...], columns, reach) for g_ref in g_refs]
+    shifted = {k: shifted_taps(g_refs[k][:pixels], columns, reach) for k in here}
+    last = lax.rem(band + bands - late, bands)
+    near = {}
+    if tail and before:
+        for a, k in ((0, (late - 1) % bands), (2, (late + 1) % bands)):
+            rows = shifted_taps(g_refs[k][:pixels], columns, reach)[head:]
+            there = (last + 1 < bands) if a == 0 else (last > 0)
+            near[a] = jnp.where(there, rows, jnp.zeros_like(rows))
     for n, (other, out_ref) in enumerate(zip(others, outs)):
         part = lax.rem(lax.axis_index("dp") + other, parts)
         if extra % 128 == 0:
@@ -265,29 +292,50 @@
             features = x_ref[:, :, :extra]
             for k in range(1, parts):
                 features = jnp.where(part == k, x_ref[:, :, k * extra : (k + 1) * extra], features)
-        padded[edge : edge + total] = features.reshape(total, extra)
+        for s in range(bands):
+            padded[edge + s * pixels : edge + s * pixels + head] = features[s]
+        for tail_ref in tails:
+            for k in range(bands):
+                from_band = lax.rem(band + bands - k, bands)
+                rows = pl.multiple_of(part * tail, 16)
+                if k == late and not before:
+                    block = jnp.zeros((tail, extra), padded.dtype)
+                elif k:
+                    block = g_refs[k][pl.ds(pixels + rows, tail)]
+                else:
+                    block = tail_ref[band, pl.ds(rows, tail)]
+                start = pl.multiple_of(edge + from_band * pixels + head, 16)
+                padded[pl.ds(start, tail)] = block
         for a in range(3):
-            here = pl.ds(3 * a * width, 3 * width)
-            grad = sums[n][:, here] if before else None
-            for k, right in zip(distances, shifted):
+            lane = pl.ds(3 * a * width, 3 * width)
+            grad = sums[n][:, lane] if before else None
+            pairs = []
+            for k, right in shifted.items():
                 first = lax.rem(band + bands - k, bands) * pixels + a * edge
-                left = padded[pl.ds(pl.multiple_of(first, 16), pixels)]
+                pairs.append((padded[pl.ds(pl.multiple_of(first, 16), pixels)], right))
+            if a in near:
+                start = pl.multiple_of(edge + last * pixels + head, 16)
+                pairs.append((padded[pl.ds(start, tail)], near[a]))
+            for left, right in pairs:
                 term = lax.dot_general(
                     left, right, (((0,), (0,)), ((), ())), preferred_element_type=jnp.float32
                 )
                 grad = term if grad is None else grad + term
-            out_ref[:, here] = grad.astype(out_ref.dtype)
-
-
-def kernel_grad(features, gradients, sums, columns, reach, parts, others, dtype):
-    bands, pixels, lanes = features.shape
+            out_ref[:, lane] = grad.astype(out_ref.dtype)
+
+
+def kernel_grad(features, gradients, tails, sums, columns, reach, parts, others, late, dtype):
+    bands, head, lanes = features.shape
+    pixels, width = gradients[0].shape
     extra = lanes // parts
-    distances = tuple(gradients)
-    width = gradients[distances[0]].shape[1]
-    work = len(others) * len(distances) * pixels * extra * width
+    here = [late] if sums else [k for k in range(bands) if k != late or bands == 1]
+    work = len(others) * len(here) * pixels * extra * width
+    given = list(gradients)
+    if not sums and bands > 1:
+        given[late] = gradients[0]
     return pl.pallas_call(
         functools.partial(
-            kernel_grad_kernel, columns, reach, parts, others, distances, len(sums)
+            kernel_grad_kernel, columns, reach, parts, others, here, late, len(sums), pixels - head
         ),
         out_shape=[pltpu.VMEM((extra, 9 * width), dtype)] * len(others),
         scratch_shapes=[pltpu.VMEM((bands * pixels + 2 * reach * columns, extra), features.dtype)],
@@ -296,7 +344,7 @@
             flops=18 * work, bytes_accessed=2 * bands * pixels * lanes, transcendentals=0
         ),
         name="kernel_grad",
-    )(features, *gradients.values(), *sums)
+    )(features, *given, *tails, *sums)
 
 
 def partner(i, k, count):
@@ -358,7 +406,7 @@
     pixels, width = own_ref.shape
     edge = reach * columns
     own = own_ref[...]
-    above = above_ref[pixels - edge :]
+    above = above_ref[pixels - edge : pixels]
     below = below_ref[:edge]
     above = jnp.where(band > 0, above, jnp.zeros_like(above))
     below = jnp.where(band + 1 < bands, below, jnp.zeros_like(below))
@@ -419,7 +467,10 @@
     even = block_rows % taps == 0
     parts = 2 if replicas % 2 == 0 else 1
     count = replicas // parts
-    flat, weight, *split = load(flat, weight, bands, replicas, cover, even)
+    apart = even and bands > 1 and band_rows == reach and count * cover == width
+    tail = pixels // 6 // 16 * 16 if apart else 0
+    flat, weight, *split = load(flat, weight, bands, replicas, cover, even, tail)
+    tails = split[1:]
     if not even:
         order = jnp.array([c for line in picks for c in line], jnp.int32)
         blocks = jnp.take(flat, order, axis=1).reshape(pixels, bands, replicas * cover)
@@ -430,7 +481,7 @@
     below = lax.ppermute(up, "space", [(i + 1, i) for i in range(bands - 1)])
     middle = middle_taps(flat, weight, up, columns, reach)
 
-    gradient = pointwise(
+    gradient, *packed = pointwise(
         middle,
         above,
         below,
@@ -438,20 +489,21 @@
         class_weight.T,
         labels.reshape(band_rows, columns),
         pixel_weight.reshape(band_rows, columns),
+        bands,
+        tails,
     )
     gradients = [gradient] + [
-        lax.ppermute(gradient, "space", [(i, (i + k) % bands) for i in range(bands)])
+        lax.ppermute(packed[k - 1], "space", [(i, (i + k) % bands) for i in range(bands)])
         for k in range(1, bands)
     ]
     late = bands // 2
-    early = {k: g for k, g in enumerate(gradients) if k != late or bands == 1}
-    others = (0, 1)[:parts]
-    terms = kernel_grad(whole, early, [], columns, reach, parts, others, jnp.float32)
+    grads = functools.partial(kernel_grad, whole, gradients, tails)
+    terms = grads([], columns, reach, parts, (0, 1)[:parts], late, jnp.float32)
     if bands > 1:
-        last = {late: gradients[late]}
         own, *theirs = terms
-        terms = kernel_grad(whole, last, [own], columns, reach, parts, (0,), jnp.float32)
-        terms += kernel_grad(whole, last, theirs, columns, reach, parts, (1,), jnp.bfloat16) if theirs else []
+        terms = grads([own], columns, reach, parts, (0,), late, jnp.float32)
+        if theirs:
+            terms += grads(theirs, columns, reach, parts, (1,), late, jnp.bfloat16)
     if parts == 2:
         theirs = terms[1].astype(jnp.bfloat16)
         terms = [terms[0], lax.ppermute(theirs, "dp", [(i, i ^ 1) for i in range(replicas)])]

time: 39.9 us -> 40 us (level)
  starting transfers between devices: 20 us -> 19.1 us
  waiting for transfers between devices: 11.5 us -> 12.3 us
    ppermute x1, waiting for transfers between devices: 3.06 us -> 4.5 us  [on_device(): below = lax.ppermute(up, 'space', [(i + 1, i) for i in range(bands - 1)])]
    ppermute x1, waiting for transfers between devices: 1.4 us -> 0.34 us  [on_device(): above = lax.ppermute(down, 'space', [(i, i + 1) for i in range(bands - 1)])]
    ppermute x3, starting transfers between devices: 4.79 us -> 3.88 us  [on_device(): lax.ppermute(packed[k - 1], 'space', [(i, (i + k) % bands) for i in range...]
    ppermute x3, waiting for transfers between devices: 3.7 us -> 4.26 us  [on_device(): lax.ppermute(packed[k - 1], 'space', [(i, (i + k) % bands) for i in range...]
  transfers between devices with their start and end apart: 10 -> 10, of which waited for: 9 -> 8; matrix products, arithmetic and copies ran while one was open for 0% -> 0% of each run, Pallas kernels for 11% -> 11%
where the time goes in v14:
time: 40 us; the launch traced here: 39.7 us
  starting transfers between devices  19.1 us (48%)
  waiting for transfers between devices  12.3 us (31%)
  Pallas kernels  7.55 us (19%)
  between operations  0.76 us (2%)
    all_to_all x1, starting transfers between devices, on_device(): whole = lax.all_to_all(split[0], 'space', 0, 0)  6.33 us
    ppermute x1, waiting for transfers between devices, on_device(): below = lax.ppermute(up, 'space', [(i + 1, i) for i in range(bands - 1)])  4.5 us
    ppermute x3, waiting for transfers between devices, on_device(): lax.ppermute(packed[k - 1], 'space', [(i, (i + k) % bands) for i in range...  4.26 us
    ppermute x1, starting transfers between devices, on_device(): above = lax.ppermute(down, 'space', [(i, i + 1) for i in range(bands - 1)])  3.93 us
    ppermute x3, starting transfers between devices, on_device(): lax.ppermute(packed[k - 1], 'space', [(i, (i + k) % bands) for i in range...  3.88 us
    ppermute x3, starting transfers between devices, on_device(): came.append(lax.ppermute(blocks[k], 'dp', pairs))  3.55 us
    ppermute x3, waiting for transfers between devices, on_device(): came.append(lax.ppermute(blocks[k], 'dp', pairs))  2.09 us
    pallas_call x1, Pallas kernels, load(): pl.pallas_call(functools.partial(load_kernel, replicas, cover, tail), in_...  2.07 us
  transfers between devices with their start and end apart: 10, of which 8 were waited for; matrix products, arithmetic and copies ran while one was open for 0% of the time, Pallas kernels for 11%

profile of v14, /device:TPU:0, one launch (start us, length us, event | category | flops | bytes accessed | tf_op | source)
XLA Modules:
  0.0 39.7 jit_solution(8239803634053781938)
XLA Ops:
  0.6 2.1 %load.1 = (bf16[192,1024]{1,0:T(8,128)(2,1)S(1)}, bf16[9,1024,128]{2,1,0:T(8,128)(2,1)S(1)}, bf16[4,160,256]{2,1,0:T(8,128)(2,1)}, bf16[4,64,128]{2,1,0:T(8,128)(2,1)S(1)}) custom-call(bf16[192,1024]{1,0:T(8,128)(2,1)} %bitcast.13, bf16[9,1024,128]{2,1,0:T(8,128)(2,1)} %bitcast.11), custom_call_target="tpu_custom_call" | custom-call | bytes 3145728 | tf_op jit(solution)/shard_map/load/pallas_call | solution.py:93
  2.7 0.0 copy-start.2
  2.7 0.0 copy-start.3
  2.7 6.3 %all-to-all-start = ((bf16[4,160,256]{2,1,0:T(8,128)(2,1)}), bf16[4,160,256]{2,1,0:T(8,128)(2,1)S(1)}, u32[]{:S(2)}, u32[]{:S(2)}) async-start(bf16[4,160,256]{2,1,0:T(8,128)(2,1)} %get-tuple-element.26), calls=%async_computation | async-start | bytes 655360 | tf_op jit(solution)/shard_map/all_to_all | solution.py:478
  9.1 0.0 copy-start
  9.1 0.0 copy-start.1
  9.1 0.5 %halo.1 = (bf16[192,128]{1,0:T(8,128)(2,1)S(1)}, bf16[192,128]{1,0:T(8,128)(2,1)S(1)}) custom-call(bf16[192,1024]{1,0:T(8,128)(2,1)S(1)} %get-tuple-element.18.x_ref, bf16[9,1024,128]{2,1,0:T(8,128)(2,1)S(1)} %get-tuple-element.19.w_ref), custom_call_target="tpu_custom_call" | custom-call | flops 301989888 | bytes 1966080 | tf_op jit(solution)/shard_map/halo/pallas_call | solution.py:148
  9.6 3.9 %collective-permute-start = (bf16[192,128]{1,0:T(8,128)(2,1)S(1)}, bf16[192,128]{1,0:T(8,128)(2,1)S(1)}, u32[]{:S(2)}, u32[]{:S(2)}) collective-permute-start(bf16[192,128]{1,0:T(8,128)(2,1)S(1)} %get-tuple-element.21), channel_id=1, source_target_pairs={{0,1},{1,2},{2,3},{4,5},{5,6},{6,7},{8,9},{9,10},{10,11},{12,13},{... | collective-permute-start | bytes 147464 | tf_op jit(solution)/shard_map/ppermute | solution.py:480
  13.5 1.3 %collective-permute-start.1 = (bf16[192,128]{1,0:T(8,128)(2,1)S(1)}, bf16[192,128]{1,0:T(8,128)(2,1)S(1)}, u32[]{:S(2)}, u32[]{:S(2)}) collective-permute-start(bf16[192,128]{1,0:T(8,128)(2,1)S(1)} %get-tuple-element.20.after_ref), channel_id=1, source_target_pairs={{1,0},{2,1},{3,2},{5,4},{6,5},{7,6},{9,8},{10,9},{11,10},{13,12},{... | collective-permute-start | bytes 147464 | tf_op jit(solution)/shard_map/ppermute | solution.py:481
  14.8 0.0 copy-done.2
  14.8 0.0 copy-done.3
  14.8 0.4 middle_taps.1.middle_ref
  15.2 0.3 collective-permute-done.above_ref
  15.5 4.5 %collective-permute-done.1.below_ref = bf16[192,128]{1,0:T(8,128)(2,1)S(1)} collective-permute-done((bf16[192,128]{1,0:T(8,128)(2,1)S(1)}, bf16[192,128]{1,0:T(8,128)(2,1)S(1)}, u32[]{:S(2)}, u32[]{:S(2)}) %collective-permute-start.1) | collective-permute-done | bytes 49184 | tf_op jit(solution)/shard_map/ppermute | solution.py:481
  20.0 0.0 copy-done
  20.0 0.0 copy-done.1
  20.0 0.4 %pointwise.1 = (bf16[192,128]{1,0:T(8,128)(2,1)S(1)}, bf16[256,128]{1,0:T(8,128)(2,1)S(1)}, bf16[256,128]{1,0:T(8,128)(2,1)S(1)}, bf16[256,128]{1,0:T(8,128)(2,1)S(1)}) custom-call(f32[192,128]{1,0:T(8,128)S(1)} %middle_taps.1.middle_ref, bf16[192,128]{1,0:T(8,128)(2,1)S(1)} %collective-permute-done.above_ref, ...), custom_call_target="tpu_custom_call" | custom-call | flops 737280 | bytes 245760 | tf_op jit(solution)/shard_map/pointwise/pallas_call | solution.py:245
  20.5 1.0 %collective-permute-start.2 = (bf16[256,128]{1,0:T(8,128)(2,1)S(1)}, bf16[256,128]{1,0:T(8,128)(2,1)S(1)}, u32[]{:S(2)}, u32[]{:S(2)}) collective-permute-start(bf16[256,128]{1,0:T(8,128)(2,1)S(1)} %get-tuple-element.24), channel_id=1, source_target_pairs={{0,1},{1,2},{2,3},{3,0},{4,5},{5,6},{6,7},{7,4},{8,9},{9,10},{10,1... | collective-permute-start | bytes 196616 | tf_op jit(solution)/shard_map/ppermute | solution.py:496
  21.5 2.9 %collective-permute-start.3 = (bf16[256,128]{1,0:T(8,128)(2,1)S(1)}, bf16[256,128]{1,0:T(8,128)(2,1)S(1)}, u32[]{:S(2)}, u32[]{:S(2)}) collective-permute-start(bf16[256,128]{1,0:T(8,128)(2,1)S(1)} %get-tuple-element.25), channel_id=1, source_target_pairs={{0,3},{1,0},{2,1},{3,2},{4,7},{5,4},{6,5},{7,6},{8,11},{9,8},{10,9... | collective-permute-start | bytes 196616 | tf_op jit(solution)/shard_map/ppermute | solution.py:496
  24.4 0.0 collective-permute-start.4
  24.4 2.3 %collective-permute-done.2.above_ref.refs_1_ = bf16[256,128]{1,0:T(8,128)(2,1)S(1)} collective-permute-done((bf16[256,128]{1,0:T(8,128)(2,1)S(1)}, bf16[256,128]{1,0:T(8,128)(2,1)S(1)}, u32[]{:S(2)}, u32[]{:S(2)}) %collective-permute-start.2) | collective-permute-done | bytes 65568 | tf_op jit(solution)/shard_map/ppermute | solution.py:496
  26.6 0.0 collective-permute-done.3.below_ref.refs_3_
  26.6 0.0 all-to-all-done.x_ref
  26.6 0.9 %kernel_grad.3 = (f32[128,1152]{1,0:T(8,128)S(1)}, f32[128,1152]{1,0:T(8,128)S(1)}) custom-call(bf16[4,160,256]{2,1,0:T(8,128)(2,1)S(1)} %all-to-all-done.x_ref, bf16[192,128]{1,0:T(8,128)(2,1)S(1)} %get-tuple-element.23.own_ref.refs_0_.refs_2_, bf16[256,128]{1,0:T(8,128)(2,1)S(1)} %collective-permute-done.2.above_ref.refs_1_, ...), custom_call_target="tpu_custom_call" | custom-call | flops 339738624 | bytes 393216 | tf_op jit(solution)/shard_map/kernel_grad/pallas_call | solution.py:336
  27.5 2.0 %collective-permute-done.4.refs_2_ = bf16[256,128]{1,0:T(8,128)(2,1)S(1)} collective-permute-done((bf16[256,128]{1,0:T(8,128)(2,1)S(1)}, bf16[256,128]{1,0:T(8,128)(2,1)S(1)}, u32[]{:S(2)}, u32[]{:S(2)}) %collective-permute-start.4) | collective-permute-done | bytes 65568 | tf_op jit(solution)/shard_map/ppermute | solution.py:496
  29.5 0.4 %kernel_grad.5 = bf16[128,1152]{1,0:T(8,128)(2,1)S(1)} custom-call(bf16[4,160,256]{2,1,0:T(8,128)(2,1)S(1)} %all-to-all-done.x_ref, bf16[192,128]{1,0:T(8,128)(2,1)S(1)} %get-tuple-element.23.own_ref.refs_0_.refs_2_, bf16[256,128]{1,0:T(8,128)(2,1)S(1)} %collective-permute-done.2.above_ref.refs_1_, bf16[256,128]{1,0:T(8,128)(2,1)S(1)} %collective-permute-done.4.refs_2_, ...), custom_call_target="tpu_custom_call" | custom-call | flops 56623104 | bytes 393216 | tf_op jit(solution)/shard_map/kernel_grad/pallas_call | solution.py:336
  29.9 0.1 collective-permute-start.5
  30.0 0.4 %kernel_grad.4.refs_0_ = f32[128,1152]{1,0:T(8,128)S(1)} custom-call(bf16[4,160,256]{2,1,0:T(8,128)(2,1)S(1)} %all-to-all-done.x_ref, bf16[192,128]{1,0:T(8,128)(2,1)S(1)} %get-tuple-element.23.own_ref.refs_0_.refs_2_, bf16[256,128]{1,0:T(8,128)(2,1)S(1)} %collective-permute-done.2.above_ref.refs_1_, bf16[256,128]{1,0:T(8,128)(2,1)S(1)} %collective-permute-done.4.refs_2_, ...), custom_call_target="tpu_custom_call" | custom-call | flops 56623104 | bytes 393216 | tf_op jit(solution)/shard_map/kernel_grad/pallas_call | solution.py:336
  30.4 1.1 %collective-permute-done.5.refs_1_ = bf16[128,1152]{1,0:T(8,128)(2,1)S(1)} collective-permute-done((bf16[128,1152]{1,0:T(8,128)(2,1)S(1)}, bf16[128,1152]{1,0:T(8,128)(2,1)S(1)}, u32[]{:S(2)}, u32[]{:S(2)}) %collective-permute-start.5) | collective-permute-done | bytes 294944 | tf_op jit(solution)/shard_map/ppermute | solution.py:509
  31.6 0.1 split_up.1
  31.6 2.5 %collective-permute-start.6 = (bf16[32,1152]{1,0:T(8,128)(2,1)S(1)}, bf16[32,1152]{1,0:T(8,128)(2,1)S(1)}, u32[]{:S(2)}, u32[]{:S(2)}) collective-permute-start(bf16[32,1152]{1,0:T(8,128)(2,1)S(1)} %get-tuple-element.31), channel_id=1, source_target_pairs={{0,24},{4,28},{8,16},{12,20},{16,8},{20,12},{24,0},{28,4},{1,25},{... | collective-permute-start | bytes 221192 | tf_op jit(solution)/shard_map/ppermute | solution.py:515
  34.2 0.5 %collective-permute-start.7 = (bf16[32,1152]{1,0:T(8,128)(2,1)S(1)}, bf16[32,1152]{1,0:T(8,128)(2,1)S(1)}, u32[]{:S(2)}, u32[]{:S(2)}) collective-permute-start(bf16[32,1152]{1,0:T(8,128)(2,1)S(1)} %get-tuple-element.32), channel_id=1, source_target_pairs={{0,16},{4,20},{8,24},{12,28},{16,0},{20,4},{24,8},{28,12},{1,17},{... | collective-permute-start | bytes 221192 | tf_op jit(solution)/shard_map/ppermute | solution.py:515
  34.7 0.5 %collective-permute-start.8 = (bf16[32,1152]{1,0:T(8,128)(2,1)S(1)}, bf16[32,1152]{1,0:T(8,128)(2,1)S(1)}, u32[]{:S(2)}, u32[]{:S(2)}) collective-permute-start(bf16[32,1152]{1,0:T(8,128)(2,1)S(1)} %get-tuple-element.33), channel_id=1, source_target_pairs={{0,8},{4,12},{8,0},{12,4},{16,24},{20,28},{24,16},{28,20},{1,9},{5... | collective-permute-start | bytes 221192 | tf_op jit(solution)/shard_map/ppermute | solution.py:515
  35.2 1.7 %feature_grad.1 = f32[192,1024]{1,0:T(8,128)} custom-call(bf16[192,128]{1,0:T(8,128)(2,1)S(1)} %get-tuple-element.23.own_ref.refs_0_.refs_2_, bf16[256,128]{1,0:T(8,128)(2,1)S(1)} %collective-permute-done.2.above_ref.refs_1_, bf16[256,128]{1,0:T(8,128)(2,1)S(1)} %collective-permute-done.3.below_ref.refs_3_, bf16[9,1024,128]{2,1,0:T(8,128)(2,1)S(1)} %get-tuple-element.19.w_ref), custom_call_target="tpu_custom_call" | custom-call | flops 452984832 | bytes 3145728 | tf_op jit(solution)/shard_map/feature_grad/pallas_call | solution.py:436
  36.9 0.1 collective-permute-done.6.refs_1_
  37.0 1.5 %collective-permute-done.7.refs_2_ = bf16[32,1152]{1,0:T(8,128)(2,1)S(1)} collective-permute-done((bf16[32,1152]{1,0:T(8,128)(2,1)S(1)}, bf16[32,1152]{1,0:T(8,128)(2,1)S(1)}, u32[]{:S(2)}, u32[]{:S(2)}) %collective-permute-start.7) | collective-permute-done | bytes 73760 | tf_op jit(solution)/shard_map/ppermute | solution.py:515
  38.5 0.5 %collective-permute-done.8.refs_3_ = bf16[32,1152]{1,0:T(8,128)(2,1)S(1)} collective-permute-done((bf16[32,1152]{1,0:T(8,128)(2,1)S(1)}, bf16[32,1152]{1,0:T(8,128)(2,1)S(1)}, u32[]{:S(2)}, u32[]{:S(2)}) %collective-permute-start.8) | collective-permute-done | bytes 73760 | tf_op jit(solution)/shard_map/ppermute | solution.py:515
  39.0 0.7 %final_sum.1 = f32[288,128]{1,0:T(8,128)} custom-call(bf16[32,1152]{1,0:T(8,128)(2,1)S(1)} %get-tuple-element.30.refs_0_, bf16[32,1152]{1,0:T(8,128)(2,1)S(1)} %collective-permute-done.6.refs_1_, bf16[32,1152]{1,0:T(8,128)(2,1)S(1)} %collective-permute-done.7.refs_2_, bf16[32,1152]{1,0:T(8,128)(2,1)S(1)} %collective-permute-done.8.refs_3_), custom_call_target="tpu_custom_call" | custom-call | tf_op jit(solution)/shard_map/final_sum/pallas_call | solution.py:396
  (1 shorter events, 0.0 us)
Async XLA Ops:
  2.7 12.1 %copy-start.2 = (s32[1,6,32]{2,0,1:T(1,128)S(1)}, s32[1,6,32]{2,0,1:T(1,128)}, u32[]{:S(2)}) copy-start(s32[1,6,32]{2,0,1:T(1,128)} %param.8) | copy-start | bytes 2308
  2.7 12.1 %copy-start.3 = (s32[1,6,32]{2,0,1:T(1,128)S(1)}, s32[1,6,32]{2,0,1:T(1,128)}, u32[]{:S(2)}) copy-start(s32[1,6,32]{2,0,1:T(1,128)} %param.7) | copy-start | bytes 2308
  2.7 23.9 %all-to-all-start = ((bf16[4,160,256]{2,1,0:T(8,128)(2,1)}), bf16[4,160,256]{2,1,0:T(8,128)(2,1)S(1)}, u32[]{:S(2)}, u32[]{:S(2)}) async-start(bf16[4,160,256]{2,1,0:T(8,128)(2,1)} %get-tuple-element.26), calls=%async_computation | async-start | bytes 655360 | tf_op jit(solution)/shard_map/all_to_all | solution.py:478
  9.1 11.0 %copy-start = (bf16[128,3]{0,1:T(4,128)(2,1)S(1)}, bf16[128,3]{0,1:T(4,128)(2,1)}, u32[]{:S(2)}) copy-start(bf16[128,3]{0,1:T(4,128)(2,1)} %param.11) | copy-start | bytes 2308
  9.1 11.0 %copy-start.1 = (f32[128]{0:T(128)S(1)}, f32[128]{0:T(128)}, u32[]{:S(2)}) copy-start(f32[128]{0:T(128)} %param.10) | copy-start | bytes 1540
  9.6 6.0 %collective-permute-start = (bf16[192,128]{1,0:T(8,128)(2,1)S(1)}, bf16[192,128]{1,0:T(8,128)(2,1)S(1)}, u32[]{:S(2)}, u32[]{:S(2)}) collective-permute-start(bf16[192,128]{1,0:T(8,128)(2,1)S(1)} %get-tuple-element.21), channel_id=1, source_target_pairs={{0,1},{1,2},{2,3},{4,5},{5,6},{6,7},{8,9},{9,10},{10,11},{12,13},{... | collective-permute-start | bytes 147464 | tf_op jit(solution)/shard_map/ppermute | solution.py:480
  13.5 6.5 %collective-permute-start.1 = (bf16[192,128]{1,0:T(8,128)(2,1)S(1)}, bf16[192,128]{1,0:T(8,128)(2,1)S(1)}, u32[]{:S(2)}, u32[]{:S(2)}) collective-permute-start(bf16[192,128]{1,0:T(8,128)(2,1)S(1)} %get-tuple-element.20.after_ref), channel_id=1, source_target_pairs={{1,0},{2,1},{3,2},{5,4},{6,5},{7,6},{9,8},{10,9},{11,10},{13,12},{... | collective-permute-start | bytes 147464 | tf_op jit(solution)/shard_map/ppermute | solution.py:481
  20.5 6.2 %collective-permute-start.2 = (bf16[256,128]{1,0:T(8,128)(2,1)S(1)}, bf16[256,128]{1,0:T(8,128)(2,1)S(1)}, u32[]{:S(2)}, u32[]{:S(2)}) collective-permute-start(bf16[256,128]{1,0:T(8,128)(2,1)S(1)} %get-tuple-element.24), channel_id=1, source_target_pairs={{0,1},{1,2},{2,3},{3,0},{4,5},{5,6},{6,7},{7,4},{8,9},{9,10},{10,1... | collective-permute-start | bytes 196616 | tf_op jit(solution)/shard_map/ppermute | solution.py:496
  21.5 5.2 %collective-permute-start.3 = (bf16[256,128]{1,0:T(8,128)(2,1)S(1)}, bf16[256,128]{1,0:T(8,128)(2,1)S(1)}, u32[]{:S(2)}, u32[]{:S(2)}) collective-permute-start(bf16[256,128]{1,0:T(8,128)(2,1)S(1)} %get-tuple-element.25), channel_id=1, source_target_pairs={{0,3},{1,0},{2,1},{3,2},{4,7},{5,4},{6,5},{7,6},{8,11},{9,8},{10,9... | collective-permute-start | bytes 196616 | tf_op jit(solution)/shard_map/ppermute | solution.py:496
  24.4 5.2 %collective-permute-start.4 = (bf16[256,128]{1,0:T(8,128)(2,1)S(1)}, bf16[256,128]{1,0:T(8,128)(2,1)S(1)}, u32[]{:S(2)}, u32[]{:S(2)}) collective-permute-start(bf16[256,128]{1,0:T(8,128)(2,1)S(1)} %get-tuple-element.27), channel_id=1, source_target_pairs={{0,2},{1,3},{2,0},{3,1},{4,6},{5,7},{6,4},{7,5},{8,10},{9,11},{10,... | collective-permute-start | bytes 196616 | tf_op jit(solution)/shard_map/ppermute | solution.py:496
  29.9 1.6 %collective-permute-start.5 = (bf16[128,1152]{1,0:T(8,128)(2,1)S(1)}, bf16[128,1152]{1,0:T(8,128)(2,1)S(1)}, u32[]{:S(2)}, u32[]{:S(2)}) collective-permute-start(bf16[128,1152]{1,0:T(8,128)(2,1)S(1)} %kernel_grad.5), channel_id=1, source_target_pairs={{0,4},{4,0},{8,12},{12,8},{16,20},{20,16},{24,28},{28,24},{1,5},{5... | collective-permute-start | bytes 884744 | tf_op jit(solution)/shard_map/ppermute | solution.py:509
  31.6 5.4 %collective-permute-start.6 = (bf16[32,1152]{1,0:T(8,128)(2,1)S(1)}, bf16[32,1152]{1,0:T(8,128)(2,1)S(1)}, u32[]{:S(2)}, u32[]{:S(2)}) collective-permute-start(bf16[32,1152]{1,0:T(8,128)(2,1)S(1)} %get-tuple-element.31), channel_id=1, source_target_pairs={{0,24},{4,28},{8,16},{12,20},{16,8},{20,12},{24,0},{28,4},{1,25},{... | collective-permute-start | bytes 221192 | tf_op jit(solution)/shard_map/ppermute | solution.py:515
  34.2 4.4 %collective-permute-start.7 = (bf16[32,1152]{1,0:T(8,128)(2,1)S(1)}, bf16[32,1152]{1,0:T(8,128)(2,1)S(1)}, u32[]{:S(2)}, u32[]{:S(2)}) collective-permute-start(bf16[32,1152]{1,0:T(8,128)(2,1)S(1)} %get-tuple-element.32), channel_id=1, source_target_pairs={{0,16},{4,20},{8,24},{12,28},{16,0},{20,4},{24,8},{28,12},{1,17},{... | collective-permute-start | bytes 221192 | tf_op jit(solution)/shard_map/ppermute | solution.py:515
  34.7 4.4 %collective-permute-start.8 = (bf16[32,1152]{1,0:T(8,128)(2,1)S(1)}, bf16[32,1152]{1,0:T(8,128)(2,1)S(1)}, u32[]{:S(2)}, u32[]{:S(2)}) collective-permute-start(bf16[32,1152]{1,0:T(8,128)(2,1)S(1)} %get-tuple-element.33), channel_id=1, source_target_pairs={{0,8},{4,12},{8,0},{12,4},{16,24},{20,28},{24,16},{28,20},{1,9},{5... | collective-permute-start | bytes 221192 | tf_op jit(solution)/shard_map/ppermute | solution.py:515

commit v15 on v12

--- a/solution.py
+++ b/solution.py
@@ -109,24 +109,94 @@
     )
 
 
-def halo_kernel(columns, reach, x_ref, w_ref, down_ref, up_ref):
+def halo_sums(x_ref, w_ref, columns, reach):
     pixels, edge = x_ref.shape[0], reach * columns
     width = w_ref.shape[2]
     if pixels > edge:
         down = tap_row(x_ref[pixels - edge :], w_ref, 0, columns, reach)
         up = tap_row(x_ref[:edge], w_ref, 2, columns, reach)
-    else:
-        weight = jnp.concatenate([w_ref[t] for t in (0, 1, 2, 6, 7, 8)], axis=1)
-        product = jnp.dot(x_ref[...], weight, preferred_element_type=jnp.float32)
-        down, up = [
-            sum(
-                shift_columns(
-                    product[:, (3 * k + b) * width : (3 * k + b + 1) * width], (b - 1) * reach, columns
-                )
-                for b in range(3)
+        return down, up
+    weight = jnp.concatenate([w_ref[t] for t in (0, 1, 2, 6, 7, 8)], axis=1)
+    product = jnp.dot(x_ref[...], weight, preferred_element_type=jnp.float32)
+    return [
+        sum(
+            shift_columns(
+                product[:, (3 * k + b) * width : (3 * k + b + 1) * width], (b - 1) * reach, columns
             )
-            for k in range(2)
+            for b in range(3)
+        )
+        for k in range(2)
+    ]
+
+
+def lay_out_kernel(columns, reach, replicas, cover, x_hbm, w_hbm, x_ref, w_ref, *refs):
+    *blocks, room, x_sem, w_sems = refs
+    bands = len(blocks)
+    band = lax.axis_index("space")
+    lanes = room.shape[2]
+    x_load = pltpu.make_async_copy(x_hbm, x_ref, x_sem)
+    x_load.start()
+    w_loads = []
+    for n, (t, size) in enumerate(((0, 3), (6, 3), (3, 3))):
+        here = pl.ds(t, size)
+        w_loads.append(pltpu.make_async_copy(w_hbm.at[here], w_ref.at[here], w_sems.at[n]))
+        w_loads[-1].start()
+    x_load.wait()
+    x = x_ref[...]
+    for s in range(bands):
+        room[s] = jnp.concatenate(
+            [
+                x[:, (d * bands + s) * cover : (d * bands + s + 1) * cover]
+                for d in replica_order(replicas)
+            ],
+            axis=1,
+        )
+    for k, block in enumerate(blocks):
+        block[:, :lanes] = room[jnp.bitwise_xor(band, k)]
+    w_loads[0].wait()
+    w_loads[1].wait()
+    down, up = halo_sums(x_ref, w_ref, columns, reach)
+    blocks[1][:, lanes:] = jnp.where(lax.rem(band, 2) == 0, down, up).astype(x.dtype)
+    blocks[3][:, lanes:] = jnp.where(band < 2, down, up).astype(x.dtype)
+    w_loads[2].wait()
+
+
+def lay_out(flat, weight, columns, reach, bands, replicas, cover):
+    pixels, channels = flat.shape
+    width = weight.shape[2]
+    hbm = pl.BlockSpec(memory_space=pltpu.HBM)
+    vmem = pl.BlockSpec(memory_space=pltpu.VMEM)
+    lanes = replicas * cover
+    shapes = [(pixels, lanes + (width if k % 2 else 0)) for k in range(bands)]
+    return pl.pallas_call(
+        functools.partial(lay_out_kernel, columns, reach, replicas, cover),
+        in_specs=[hbm, hbm],
+        out_specs=[vmem] * (2 + bands),
+        out_shape=[
+            pltpu.VMEM(flat.shape, flat.dtype),
+            pltpu.VMEM(weight.shape, weight.dtype),
         ]
+        + [pltpu.VMEM(shape, flat.dtype) for shape in shapes],
+        scratch_shapes=[
+            pltpu.VMEM((bands, pixels, lanes), flat.dtype),
+            pltpu.SemaphoreType.DMA,
+            pltpu.SemaphoreType.DMA((3,)),
+        ],
+        compiler_params=pltpu.CompilerParams(vmem_limit_bytes=VMEM_LIMIT),
+        cost_estimate=pl.CostEstimate(
+            flops=12 * pixels * channels * width,
+            bytes_accessed=2 * weight.size + 4 * pixels * channels,
+            transcendentals=0,
+        ),
+        name="lay_out",
+    )(
+        pltpu.with_memory_space_constraint(flat, pltpu.HBM),
+        pltpu.with_memory_space_constraint(weight, pltpu.HBM),
+    )
+
+
+def halo_kernel(columns, reach, x_ref, w_ref, down_ref, up_ref):
+    down, up = halo_sums(x_ref, w_ref, columns, reach)
     down_ref[...] = down.astype(down_ref.dtype)
     up_ref[...] = up.astype(up_ref.dtype)
 
@@ -190,12 +260,15 @@
 
 
 def pointwise_kernel(
-    middle_ref, above_ref, below_ref, bias_ref, class_ref, label_ref, scale_ref, out_ref
+    paired, middle_ref, above_ref, below_ref, bias_ref, class_ref, label_ref, scale_ref, out_ref
 ):
     pixels, width = middle_ref.shape
     edge = above_ref.shape[0]
-    above = above_ref[...].astype(jnp.float32)
-    below = below_ref[...].astype(jnp.float32)
+    above = above_ref[:, above_ref.shape[1] - width :].astype(jnp.float32)
+    below = below_ref[:, below_ref.shape[1] - width :].astype(jnp.float32)
+    if paired:
+        band = lax.axis_index("space")
+        below = jnp.where((band == 1) | (band == 2), below, 0.0)
     if pixels > edge:
         none = jnp.zeros((pixels - edge, width), jnp.float32)
         above = jnp.concatenate([above, none], axis=0)
@@ -220,10 +293,10 @@
     out_ref[...] = gradient.astype(out_ref.dtype)
 
 
-def pointwise(middle, above, below, bias, classes, labels, scale):
+def pointwise(middle, above, below, bias, classes, labels, scale, paired):
     pixels, width = middle.shape
     return pl.pallas_call(
-        pointwise_kernel,
+        functools.partial(pointwise_kernel, paired),
         out_shape=jax.ShapeDtypeStruct((pixels, width), jnp.bfloat16),
         compiler_params=pltpu.CompilerParams(vmem_limit_bytes=VMEM_LIMIT),
         cost_estimate=pl.CostEstimate(
@@ -243,35 +316,51 @@
     )
 
 
-def kernel_grad_kernel(columns, reach, parts, others, distances, before, x_ref, *refs):
+def kernel_grad_kernel(columns, reach, parts, others, distances, before, given, lanes, *refs):
+    x_refs, refs = refs[:given], refs[given:]
     count = len(distances)
     g_refs, sums, outs = refs[:count], refs[count : count + before], refs[count + before : -1]
     padded = refs[-1]
-    bands, pixels, lanes = x_ref.shape
-    width = g_refs[0].shape[1]
-    total = bands * pixels
+    pixels, width = g_refs[0].shape
+    total = padded.shape[1] - 2 * reach * columns
+    bands = total // pixels
     edge = reach * columns
     extra = lanes // parts
     band = lax.axis_index("space")
-    none = jnp.zeros((edge, padded.shape[1]), padded.dtype)
-    padded[:edge] = none
-    padded[edge + total :] = none
+    slots = given > 1
     shifted = [shifted_taps(g_ref[...], columns, reach) for g_ref in g_refs]
     for n, (other, out_ref) in enumerate(zip(others, outs)):
         part = lax.rem(lax.axis_index("dp") + other, parts)
-        if extra % 128 == 0:
-            features = x_ref[:, :, pl.ds(pl.multiple_of(part * extra, 128), extra)]
+        for k, x_ref in enumerate(x_refs):
+            if extra % 128 == 0:
+                features = x_ref[..., pl.ds(pl.multiple_of(part * extra, 128), extra)]
+            else:
+                features = x_ref[..., :extra]
+                for j in range(1, parts):
+                    other_part = x_ref[..., j * extra : (j + 1) * extra]
+                    features = jnp.where(part == j, other_part, features)
+            if slots:
+                padded[n, k * pixels : (k + 1) * pixels] = features
+            else:
+                padded[n, edge : edge + total] = features.reshape(total, extra)
+        if slots:
+            padded[n, total : total + pixels] = jnp.zeros((pixels, extra), padded.dtype)
         else:
-            features = x_ref[:, :, :extra]
-            for k in range(1, parts):
-                features = jnp.where(part == k, x_ref[:, :, k * extra : (k + 1) * extra], features)
-        padded[edge : edge + total] = features.reshape(total, extra)
+            padded[n, :edge] = jnp.zeros((edge, extra), padded.dtype)
+            padded[n, edge + total :] = jnp.zeros((edge, extra), padded.dtype)
         for a in range(3):
             here = pl.ds(3 * a * width, 3 * width)
             grad = sums[n][:, here] if before else None
             for k, right in zip(distances, shifted):
-                first = lax.rem(band + bands - k, bands) * pixels + a * edge
-                left = padded[pl.ds(pl.multiple_of(first, 16), pixels)]
+                from_band = lax.rem(band + bands - k, bands)
+                if slots:
+                    row = from_band + (a - 1)
+                    inside = (row >= 0) & (row < bands)
+                    slot = jnp.bitwise_xor(band, jnp.clip(row, 0, bands - 1))
+                    first = jnp.where(inside, slot, bands) * pixels
+                else:
+                    first = from_band * pixels + a * edge
+                left = padded[n, pl.ds(pl.multiple_of(first, 16), pixels)]
                 term = lax.dot_general(
                     left, right, (((0,), (0,)), ((), ())), preferred_element_type=jnp.float32
                 )
@@ -279,24 +368,31 @@
             out_ref[:, here] = grad.astype(out_ref.dtype)
 
 
-def kernel_grad(features, gradients, sums, columns, reach, parts, others, dtype):
-    bands, pixels, lanes = features.shape
+def kernel_grad(features, gradients, sums, columns, reach, parts, others, dtype, bands, lanes):
+    distances = tuple(gradients)
+    pixels, width = gradients[distances[0]].shape
     extra = lanes // parts
-    distances = tuple(gradients)
-    width = gradients[distances[0]].shape[1]
     work = len(others) * len(distances) * pixels * extra * width
     return pl.pallas_call(
         functools.partial(
-            kernel_grad_kernel, columns, reach, parts, others, distances, len(sums)
+            kernel_grad_kernel,
+            columns,
+            reach,
+            parts,
+            others,
+            distances,
+            len(sums),
+            len(features),
+            lanes,
         ),
         out_shape=[pltpu.VMEM((extra, 9 * width), dtype)] * len(others),
-        scratch_shapes=[pltpu.VMEM((bands * pixels + 2 * reach * columns, extra), features.dtype)],
+        scratch_shapes=[pltpu.VMEM((len(others), bands * pixels + 2 * reach * columns, extra), jnp.bfloat16)],
         compiler_params=pltpu.CompilerParams(vmem_limit_bytes=VMEM_LIMIT),
         cost_estimate=pl.CostEstimate(
             flops=18 * work, bytes_accessed=2 * bands * pixels * lanes, transcendentals=0
         ),
         name="kernel_grad",
-    )(features, *gradients.values(), *sums)
+    )(*features, *gradients.values(), *sums)
 
 
 def partner(i, k, count):
@@ -419,16 +515,26 @@
     even = block_rows % taps == 0
     parts = 2 if replicas % 2 == 0 else 1
     count = replicas // parts
-    flat, weight, *split = load(flat, weight, bands, replicas, cover, even)
-    if not even:
-        order = jnp.array([c for line in picks for c in line], jnp.int32)
-        blocks = jnp.take(flat, order, axis=1).reshape(pixels, bands, replicas * cover)
-        split = [blocks.transpose(1, 0, 2)]
-    whole = lax.all_to_all(split[0], "space", 0, 0)
-    down, up = halo(flat, weight, columns, reach)
-    above = lax.ppermute(down, "space", [(i, i + 1) for i in range(bands - 1)])
-    below = lax.ppermute(up, "space", [(i + 1, i) for i in range(bands - 1)])
-    middle = middle_taps(flat, weight, up, columns, reach)
+    paired = bands == 4 and band_rows == reach and even
+    if paired:
+        flat, weight, own, *blocks = lay_out(flat, weight, columns, reach, bands, replicas, cover)
+        whole = [own] + [
+            lax.ppermute(block, "space", [(i, i ^ k) for i in range(bands)])
+            for k, block in enumerate(blocks, 1)
+        ]
+        above, below, after = whole[1], whole[3], blocks[0]
+    else:
+        flat, weight, *split = load(flat, weight, bands, replicas, cover, even)
+        if not even:
+            order = jnp.array([c for line in picks for c in line], jnp.int32)
+            split = jnp.take(flat, order, axis=1).reshape(pixels, bands, replicas * cover)
+            split = [split.transpose(1, 0, 2)]
+        whole = [lax.all_to_all(split[0], "space", 0, 0)]
+        down, up = halo(flat, weight, columns, reach)
+        above = lax.ppermute(down, "space", [(i, i + 1) for i in range(bands - 1)])
+        below = lax.ppermute(up, "space", [(i + 1, i) for i in range(bands - 1)])
+        after = up
+    middle = middle_taps(flat, weight, after, columns, reach)
 
     gradient = pointwise(
         middle,
@@ -438,6 +544,7 @@
         class_weight.T,
         labels.reshape(band_rows, columns),
         pixel_weight.reshape(band_rows, columns),
+        paired,
     )
     gradients = [gradient] + [
         lax.ppermute(gradient, "space", [(i, (i + k) % bands) for i in range(bands)])
@@ -446,12 +553,14 @@
     late = bands // 2
     early = {k: g for k, g in enumerate(gradients) if k != late or bands == 1}
     others = (0, 1)[:parts]
-    terms = kernel_grad(whole, early, [], columns, reach, parts, others, jnp.float32)
+    size = (bands, replicas * cover)
+    terms = kernel_grad(whole, early, [], columns, reach, parts, others, jnp.float32, *size)
     if bands > 1:
         last = {late: gradients[late]}
         own, *theirs = terms
-        terms = kernel_grad(whole, last, [own], columns, reach, parts, (0,), jnp.float32)
-        terms += kernel_grad(whole, last, theirs, columns, reach, parts, (1,), jnp.bfloat16) if theirs else []
+        terms = kernel_grad(whole, last, [own], columns, reach, parts, (0,), jnp.float32, *size)
+        if theirs:
+            terms += kernel_grad(whole, last, theirs, columns, reach, parts, (1,), jnp.bfloat16, *size)
     if parts == 2:
         theirs = terms[1].astype(jnp.bfloat16)
         terms = [terms[0], lax.ppermute(theirs, "dp", [(i, i ^ 1) for i in range(replicas)])]

time: 39.9 us -> 36.7 us (0.920)
  starting transfers between devices: 20 us -> 15.3 us
  waiting for transfers between devices: 11.5 us -> 13.2 us
    all_to_all x1 -> x0, starting transfers between devices: 6.33 us -> none  [on_device(): whole = lax.all_to_all(split[0], 'space', 0, 0)]
    ppermute x2 -> x3, waiting for transfers between devices: 4.46 us -> 7.37 us  [on_device(): lax.ppermute(block, 'space', [(i, i ^ k) for i in range(bands)])]
    ppermute x3, waiting for transfers between devices: 3.7 us -> 2.49 us  [on_device(): lax.ppermute(gradient, 'space', [(i, (i + k) % bands) for i in range(band...]
    ppermute x3, starting transfers between devices: 4.79 us -> 5.96 us  [on_device(): lax.ppermute(gradient, 'space', [(i, (i + k) % bands) for i in range(band...]
    ppermute x2 -> x3, starting transfers between devices: 5.22 us -> 5.69 us  [on_device(): lax.ppermute(block, 'space', [(i, i ^ k) for i in range(bands)])]
    pallas_call x3 -> x2, Pallas kernels: 2.98 us -> 2.84 us  [the longest x1 2.43 us: lay_out(): pl.pallas_call(functools.partial(lay_out_kernel, columns, reach, replicas...]
  transfers between devices with their start and end apart: 10 -> 10, of which waited for: 9 -> 9; matrix products, arithmetic and copies ran while one was open for 0% -> 0% of each run, Pallas kernels for 11% -> 10%
where the time goes in v15:
time: 36.7 us; the launch traced here: 36.5 us
  starting transfers between devices  15.3 us (42%)
  waiting for transfers between devices  13.2 us (36%)
  Pallas kernels  7.32 us (20%)
  between operations  0.73 us (2%)
    ppermute x3, waiting for transfers between devices, on_device(): lax.ppermute(block, 'space', [(i, i ^ k) for i in range(bands)])  7.37 us
    ppermute x3, starting transfers between devices, on_device(): lax.ppermute(gradient, 'space', [(i, (i + k) % bands) for i in range(band...  5.96 us
    ppermute x3, starting transfers between devices, on_device(): lax.ppermute(block, 'space', [(i, i ^ k) for i in range(bands)])  5.69 us
    ppermute x3, starting transfers between devices, on_device(): came.append(lax.ppermute(blocks[k], 'dp', pairs))  3.55 us
    ppermute x3, waiting for transfers between devices, on_device(): lax.ppermute(gradient, 'space', [(i, (i + k) % bands) for i in range(band...  2.49 us
    pallas_call x1, Pallas kernels, lay_out(): pl.pallas_call(functools.partial(lay_out_kernel, columns, reach, replicas...  2.43 us
    ppermute x3, waiting for transfers between devices, on_device(): came.append(lax.ppermute(blocks[k], 'dp', pairs))  2.1 us
    pallas_call x1, Pallas kernels, feature_grad(): pl.pallas_call(functools.partial(feature_grad_kernel, columns, reach, ban...  1.72 us
  transfers between devices with their start and end apart: 10, of which 9 were waited for; matrix products, arithmetic and copies ran while one was open for 0% of the time, Pallas kernels for 10%

profile of v15, /device:TPU:0, one launch (start us, length us, event | category | flops | bytes accessed | tf_op | source)
XLA Modules:
  0.0 36.5 jit_solution(6429398116565256252)
XLA Ops:
  0.6 0.0 copy-start.2
  0.6 0.0 copy-start.3
  0.7 0.0 copy-start
  0.7 0.0 copy-start.1
  0.7 2.4 %lay_out.1 = (bf16[192,1024]{1,0:T(8,128)(2,1)S(1)}, bf16[9,1024,128]{2,1,0:T(8,128)(2,1)S(1)}, bf16[192,256]{1,0:T(8,128)(2,1)S(1)}, bf16[192,384]{1,0:T(8,128)...) custom-call(bf16[192,1024]{1,0:T(8,128)(2,1)} %bitcast.13, bf16[9,1024,128]{2,1,0:T(8,128)(2,1)} %bitcast.11), custom_call_target="tpu_custom_call" | custom-call | flops 301989888 | bytes 3145728 | tf_op jit(solution)/shard_map/lay_out/pallas_call | solution.py:171
  3.1 3.1 %collective-permute-start = (bf16[192,384]{1,0:T(8,128)(2,1)S(1)}, bf16[192,384]{1,0:T(8,128)(2,1)S(1)}, u32[]{:S(2)}, u32[]{:S(2)}) collective-permute-start(bf16[192,384]{1,0:T(8,128)(2,1)S(1)} %get-tuple-element.16.after_ref), channel_id=1, source_target_pairs={{0,1},{1,0},{2,3},{3,2},{4,5},{5,4},{6,7},{7,6},{8,9},{9,8},{10,11... | collective-permute-start | bytes 442376 | tf_op jit(solution)/shard_map/ppermute | solution.py:522
  6.2 2.5 %collective-permute-start.1 = (bf16[192,384]{1,0:T(8,128)(2,1)S(1)}, bf16[192,384]{1,0:T(8,128)(2,1)S(1)}, u32[]{:S(2)}, u32[]{:S(2)}) collective-permute-start(bf16[192,384]{1,0:T(8,128)(2,1)S(1)} %get-tuple-element.17), channel_id=1, source_target_pairs={{0,3},{1,2},{2,1},{3,0},{4,7},{5,6},{6,5},{7,4},{8,11},{9,10},{10,... | collective-permute-start | bytes 442376 | tf_op jit(solution)/shard_map/ppermute | solution.py:522
  8.7 0.1 collective-permute-start.4
  8.8 0.0 copy-done.2
  8.8 0.0 copy-done.3
  8.8 0.4 middle_taps.1.middle_ref
  9.2 1.1 %collective-permute-done.above_ref.refs_1_ = bf16[192,384]{1,0:T(8,128)(2,1)S(1)} collective-permute-done((bf16[192,384]{1,0:T(8,128)(2,1)S(1)}, bf16[192,384]{1,0:T(8,128)(2,1)S(1)}, u32[]{:S(2)}, u32[]{:S(2)}) %collective-permute-start) | collective-permute-done | bytes 147488 | tf_op jit(solution)/shard_map/ppermute | solution.py:522
  10.3 6.3 %collective-permute-done.1.below_ref.refs_3_ = bf16[192,384]{1,0:T(8,128)(2,1)S(1)} collective-permute-done((bf16[192,384]{1,0:T(8,128)(2,1)S(1)}, bf16[192,384]{1,0:T(8,128)(2,1)S(1)}, u32[]{:S(2)}, u32[]{:S(2)}) %collective-permute-start.1) | collective-permute-done | bytes 147488 | tf_op jit(solution)/shard_map/ppermute | solution.py:522
  16.5 0.0 copy-done
  16.5 0.0 copy-done.1
  16.5 0.4 %pointwise.1.own_ref.refs_4_ = bf16[192,128]{1,0:T(8,128)(2,1)S(1)} custom-call(f32[192,128]{1,0:T(8,128)S(1)} %middle_taps.1.middle_ref, bf16[192,384]{1,0:T(8,128)(2,1)S(1)} %collective-permute-done.above_ref.refs_1_, bf16[192,384]{1,0:T(8,128)(2,1)S(1)} %collective-permute-done.1.below_ref.refs_3_, f32[1,128]{1,0:T(1,128)S(1)} %bitcast.10, ...), custom_call_target="tpu_custom_call" | custom-call | flops 737280 | bytes 245760 | tf_op jit(solution)/shard_map/pointwise/pallas_call | solution.py:298
  17.0 2.8 %collective-permute-start.2 = (bf16[192,128]{1,0:T(8,128)(2,1)S(1)}, bf16[192,128]{1,0:T(8,128)(2,1)S(1)}, u32[]{:S(2)}, u32[]{:S(2)}) collective-permute-start(bf16[192,128]{1,0:T(8,128)(2,1)S(1)} %pointwise.1.own_ref.refs_4_), channel_id=1, source_target_pairs={{0,1},{1,2},{2,3},{3,0},{4,5},{5,6},{6,7},{7,4},{8,9},{9,10},{10,1... | collective-permute-start | bytes 147464 | tf_op jit(solution)/shard_map/ppermute | solution.py:550
  19.7 1.1 %collective-permute-start.3 = (bf16[192,128]{1,0:T(8,128)(2,1)S(1)}, bf16[192,128]{1,0:T(8,128)(2,1)S(1)}, u32[]{:S(2)}, u32[]{:S(2)}) collective-permute-start(bf16[192,128]{1,0:T(8,128)(2,1)S(1)} %pointwise.1.own_ref.refs_4_), channel_id=1, source_target_pairs={{0,3},{1,0},{2,1},{3,2},{4,7},{5,4},{6,5},{7,6},{8,11},{9,8},{10,9... | collective-permute-start | bytes 147464 | tf_op jit(solution)/shard_map/ppermute | solution.py:550
  20.8 2.1 %collective-permute-start.5 = (bf16[192,128]{1,0:T(8,128)(2,1)S(1)}, bf16[192,128]{1,0:T(8,128)(2,1)S(1)}, u32[]{:S(2)}, u32[]{:S(2)}) collective-permute-start(bf16[192,128]{1,0:T(8,128)(2,1)S(1)} %pointwise.1.own_ref.refs_4_), channel_id=1, source_target_pairs={{0,2},{1,3},{2,0},{3,1},{4,6},{5,7},{6,4},{7,5},{8,10},{9,11},{10,... | collective-permute-start | bytes 147464 | tf_op jit(solution)/shard_map/ppermute | solution.py:550
  22.9 0.0 collective-permute-done.4.refs_2_
  22.9 0.2 collective-permute-done.2.above_ref.refs_5_
  23.2 0.6 %collective-permute-done.3.below_ref.refs_6_ = bf16[192,128]{1,0:T(8,128)(2,1)S(1)} collective-permute-done((bf16[192,128]{1,0:T(8,128)(2,1)S(1)}, bf16[192,128]{1,0:T(8,128)(2,1)S(1)}, u32[]{:S(2)}, u32[]{:S(2)}) %collective-permute-start.3) | collective-permute-done | bytes 49184 | tf_op jit(solution)/shard_map/ppermute | solution.py:550
  23.8 0.9 %kernel_grad.3 = (f32[128,1152]{1,0:T(8,128)S(1)}, f32[128,1152]{1,0:T(8,128)S(1)}) custom-call(bf16[192,256]{1,0:T(8,128)(2,1)S(1)} %get-tuple-element.18.refs_0_, bf16[192,384]{1,0:T(8,128)(2,1)S(1)} %collective-permute-done.above_ref.refs_1_, bf16[192,256]{1,0:T(8,128)(2,1)S(1)} %collective-permute-done.4.refs_2_, ...), custom_call_target="tpu_custom_call" | custom-call | flops 339738624 | bytes 393216 | tf_op jit(solution)/shard_map/kernel_grad/pallas_call | solution.py:376
  24.8 1.6 %collective-permute-done.5.refs_4_ = bf16[192,128]{1,0:T(8,128)(2,1)S(1)} collective-permute-done((bf16[192,128]{1,0:T(8,128)(2,1)S(1)}, bf16[192,128]{1,0:T(8,128)(2,1)S(1)}, u32[]{:S(2)}, u32[]{:S(2)}) %collective-permute-start.5) | collective-permute-done | bytes 49184 | tf_op jit(solution)/shard_map/ppermute | solution.py:550
  26.4 0.3 kernel_grad.5
  26.7 0.1 collective-permute-start.6
  26.8 0.4 kernel_grad.4.refs_0_
  27.2 1.2 %collective-permute-done.6.refs_1_ = bf16[128,1152]{1,0:T(8,128)(2,1)S(1)} collective-permute-done((bf16[128,1152]{1,0:T(8,128)(2,1)S(1)}, bf16[128,1152]{1,0:T(8,128)(2,1)S(1)}, u32[]{:S(2)}, u32[]{:S(2)}) %collective-permute-start.6) | collective-permute-done | bytes 294944 | tf_op jit(solution)/shard_map/ppermute | solution.py:566
  28.4 0.1 split_up.1
  28.4 2.5 %collective-permute-start.7 = (bf16[32,1152]{1,0:T(8,128)(2,1)S(1)}, bf16[32,1152]{1,0:T(8,128)(2,1)S(1)}, u32[]{:S(2)}, u32[]{:S(2)}) collective-permute-start(bf16[32,1152]{1,0:T(8,128)(2,1)S(1)} %get-tuple-element.23), channel_id=1, source_target_pairs={{0,24},{4,28},{8,16},{12,20},{16,8},{20,12},{24,0},{28,4},{1,25},{... | collective-permute-start | bytes 221192 | tf_op jit(solution)/shard_map/ppermute | solution.py:572
  31.0 0.5 %collective-permute-start.8 = (bf16[32,1152]{1,0:T(8,128)(2,1)S(1)}, bf16[32,1152]{1,0:T(8,128)(2,1)S(1)}, u32[]{:S(2)}, u32[]{:S(2)}) collective-permute-start(bf16[32,1152]{1,0:T(8,128)(2,1)S(1)} %get-tuple-element.24), channel_id=1, source_target_pairs={{0,16},{4,20},{8,24},{12,28},{16,0},{20,4},{24,8},{28,12},{1,17},{... | collective-permute-start | bytes 221192 | tf_op jit(solution)/shard_map/ppermute | solution.py:572
  31.5 0.5 %collective-permute-start.9 = (bf16[32,1152]{1,0:T(8,128)(2,1)S(1)}, bf16[32,1152]{1,0:T(8,128)(2,1)S(1)}, u32[]{:S(2)}, u32[]{:S(2)}) collective-permute-start(bf16[32,1152]{1,0:T(8,128)(2,1)S(1)} %get-tuple-element.25), channel_id=1, source_target_pairs={{0,8},{4,12},{8,0},{12,4},{16,24},{20,28},{24,16},{28,20},{1,9},{5... | collective-permute-start | bytes 221192 | tf_op jit(solution)/shard_map/ppermute | solution.py:572
  32.0 1.7 %feature_grad.1 = f32[192,1024]{1,0:T(8,128)} custom-call(bf16[192,128]{1,0:T(8,128)(2,1)S(1)} %pointwise.1.own_ref.refs_4_, bf16[192,128]{1,0:T(8,128)(2,1)S(1)} %collective-permute-done.2.above_ref.refs_5_, bf16[192,128]{1,0:T(8,128)(2,1)S(1)} %collective-permute-done.3.below_ref.refs_6_, bf16[9,1024,128]{2,1,0:T(8,128)(2,1)S(1)} %get-tuple-element.15.w_ref), custom_call_target="tpu_custom_call" | custom-call | flops 452984832 | bytes 3145728 | tf_op jit(solution)/shard_map/feature_grad/pallas_call | solution.py:484
  33.7 0.1 collective-permute-done.7.refs_1_
  33.8 1.5 %collective-permute-done.8.refs_2_ = bf16[32,1152]{1,0:T(8,128)(2,1)S(1)} collective-permute-done((bf16[32,1152]{1,0:T(8,128)(2,1)S(1)}, bf16[32,1152]{1,0:T(8,128)(2,1)S(1)}, u32[]{:S(2)}, u32[]{:S(2)}) %collective-permute-start.8) | collective-permute-done | bytes 73760 | tf_op jit(solution)/shard_map/ppermute | solution.py:572
  35.3 0.5 %collective-permute-done.9.refs_3_ = bf16[32,1152]{1,0:T(8,128)(2,1)S(1)} collective-permute-done((bf16[32,1152]{1,0:T(8,128)(2,1)S(1)}, bf16[32,1152]{1,0:T(8,128)(2,1)S(1)}, u32[]{:S(2)}, u32[]{:S(2)}) %collective-permute-start.9) | collective-permute-done | bytes 73760 | tf_op jit(solution)/shard_map/ppermute | solution.py:572
  35.8 0.7 %final_sum.1 = f32[288,128]{1,0:T(8,128)} custom-call(bf16[32,1152]{1,0:T(8,128)(2,1)S(1)} %get-tuple-element.22.refs_0_, bf16[32,1152]{1,0:T(8,128)(2,1)S(1)} %collective-permute-done.7.refs_1_, bf16[32,1152]{1,0:T(8,128)(2,1)S(1)} %collective-permute-done.8.refs_2_, bf16[32,1152]{1,0:T(8,128)(2,1)S(1)} %collective-permute-done.9.refs_3_), custom_call_target="tpu_custom_call" | custom-call | tf_op jit(solution)/shard_map/final_sum/pallas_call | solution.py:444
  (1 shorter events, 0.0 us)
Async XLA Ops:
  0.6 8.2 %copy-start.2 = (s32[1,6,32]{2,0,1:T(1,128)S(1)}, s32[1,6,32]{2,0,1:T(1,128)}, u32[]{:S(2)}) copy-start(s32[1,6,32]{2,0,1:T(1,128)} %param.8) | copy-start | bytes 2308
  0.6 8.2 %copy-start.3 = (s32[1,6,32]{2,0,1:T(1,128)S(1)}, s32[1,6,32]{2,0,1:T(1,128)}, u32[]{:S(2)}) copy-start(s32[1,6,32]{2,0,1:T(1,128)} %param.7) | copy-start | bytes 2308
  0.7 15.9 %copy-start = (bf16[128,3]{0,1:T(4,128)(2,1)S(1)}, bf16[128,3]{0,1:T(4,128)(2,1)}, u32[]{:S(2)}) copy-start(bf16[128,3]{0,1:T(4,128)(2,1)} %param.11) | copy-start | bytes 2308
  0.7 15.9 %copy-start.1 = (f32[128]{0:T(128)S(1)}, f32[128]{0:T(128)}, u32[]{:S(2)}) copy-start(f32[128]{0:T(128)} %param.10) | copy-start | bytes 1540
  3.1 7.1 %collective-permute-start = (bf16[192,384]{1,0:T(8,128)(2,1)S(1)}, bf16[192,384]{1,0:T(8,128)(2,1)S(1)}, u32[]{:S(2)}, u32[]{:S(2)}) collective-permute-start(bf16[192,384]{1,0:T(8,128)(2,1)S(1)} %get-tuple-element.16.after_ref), channel_id=1, source_target_pairs={{0,1},{1,0},{2,3},{3,2},{4,5},{5,4},{6,7},{7,6},{8,9},{9,8},{10,11... | collective-permute-start | bytes 442376 | tf_op jit(solution)/shard_map/ppermute | solution.py:522
  6.2 10.3 %collective-permute-start.1 = (bf16[192,384]{1,0:T(8,128)(2,1)S(1)}, bf16[192,384]{1,0:T(8,128)(2,1)S(1)}, u32[]{:S(2)}, u32[]{:S(2)}) collective-permute-start(bf16[192,384]{1,0:T(8,128)(2,1)S(1)} %get-tuple-element.17), channel_id=1, source_target_pairs={{0,3},{1,2},{2,1},{3,0},{4,7},{5,6},{6,5},{7,4},{8,11},{9,10},{10,... | collective-permute-start | bytes 442376 | tf_op jit(solution)/shard_map/ppermute | solution.py:522
  8.7 14.3 %collective-permute-start.4 = (bf16[192,256]{1,0:T(8,128)(2,1)S(1)}, bf16[192,256]{1,0:T(8,128)(2,1)S(1)}, u32[]{:S(2)}, u32[]{:S(2)}) collective-permute-start(bf16[192,256]{1,0:T(8,128)(2,1)S(1)} %get-tuple-element.19), channel_id=1, source_target_pairs={{0,2},{1,3},{2,0},{3,1},{4,6},{5,7},{6,4},{7,5},{8,10},{9,11},{10,... | collective-permute-start | bytes 294920 | tf_op jit(solution)/shard_map/ppermute | solution.py:522
  17.0 6.2 %collective-permute-start.2 = (bf16[192,128]{1,0:T(8,128)(2,1)S(1)}, bf16[192,128]{1,0:T(8,128)(2,1)S(1)}, u32[]{:S(2)}, u32[]{:S(2)}) collective-permute-start(bf16[192,128]{1,0:T(8,128)(2,1)S(1)} %pointwise.1.own_ref.refs_4_), channel_id=1, source_target_pairs={{0,1},{1,2},{2,3},{3,0},{4,5},{5,6},{6,7},{7,4},{8,9},{9,10},{10,1... | collective-permute-start | bytes 147464 | tf_op jit(solution)/shard_map/ppermute | solution.py:550
  19.7 4.1 %collective-permute-start.3 = (bf16[192,128]{1,0:T(8,128)(2,1)S(1)}, bf16[192,128]{1,0:T(8,128)(2,1)S(1)}, u32[]{:S(2)}, u32[]{:S(2)}) collective-permute-start(bf16[192,128]{1,0:T(8,128)(2,1)S(1)} %pointwise.1.own_ref.refs_4_), channel_id=1, source_target_pairs={{0,3},{1,0},{2,1},{3,2},{4,7},{5,4},{6,5},{7,6},{8,11},{9,8},{10,9... | collective-permute-start | bytes 147464 | tf_op jit(solution)/shard_map/ppermute | solution.py:550
  20.8 5.5 %collective-permute-start.5 = (bf16[192,128]{1,0:T(8,128)(2,1)S(1)}, bf16[192,128]{1,0:T(8,128)(2,1)S(1)}, u32[]{:S(2)}, u32[]{:S(2)}) collective-permute-start(bf16[192,128]{1,0:T(8,128)(2,1)S(1)} %pointwise.1.own_ref.refs_4_), channel_id=1, source_target_pairs={{0,2},{1,3},{2,0},{3,1},{4,6},{5,7},{6,4},{7,5},{8,10},{9,11},{10,... | collective-permute-start | bytes 147464 | tf_op jit(solution)/shard_map/ppermute | solution.py:550
  26.7 1.6 %collective-permute-start.6 = (bf16[128,1152]{1,0:T(8,128)(2,1)S(1)}, bf16[128,1152]{1,0:T(8,128)(2,1)S(1)}, u32[]{:S(2)}, u32[]{:S(2)}) collective-permute-start(bf16[128,1152]{1,0:T(8,128)(2,1)S(1)} %kernel_grad.5), channel_id=1, source_target_pairs={{0,4},{4,0},{8,12},{12,8},{16,20},{20,16},{24,28},{28,24},{1,5},{5... | collective-permute-start | bytes 884744 | tf_op jit(solution)/shard_map/ppermute | solution.py:566
  28.4 5.4 %collective-permute-start.7 = (bf16[32,1152]{1,0:T(8,128)(2,1)S(1)}, bf16[32,1152]{1,0:T(8,128)(2,1)S(1)}, u32[]{:S(2)}, u32[]{:S(2)}) collective-permute-start(bf16[32,1152]{1,0:T(8,128)(2,1)S(1)} %get-tuple-element.23), channel_id=1, source_target_pairs={{0,24},{4,28},{8,16},{12,20},{16,8},{20,12},{24,0},{28,4},{1,25},{... | collective-permute-start | bytes 221192 | tf_op jit(solution)/shard_map/ppermute | solution.py:572
  31.0 4.4 %collective-permute-start.8 = (bf16[32,1152]{1,0:T(8,128)(2,1)S(1)}, bf16[32,1152]{1,0:T(8,128)(2,1)S(1)}, u32[]{:S(2)}, u32[]{:S(2)}) collective-permute-start(bf16[32,1152]{1,0:T(8,128)(2,1)S(1)} %get-tuple-element.24), channel_id=1, source_target_pairs={{0,16},{4,20},{8,24},{12,28},{16,0},{20,4},{24,8},{28,12},{1,17},{... | collective-permute-start | bytes 221192 | tf_op jit(solution)/shard_map/ppermute | solution.py:572
  31.5 4.4 %collective-permute-start.9 = (bf16[32,1152]{1,0:T(8,128)(2,1)S(1)}, bf16[32,1152]{1,0:T(8,128)(2,1)S(1)}, u32[]{:S(2)}, u32[]{:S(2)}) collective-permute-start(bf16[32,1152]{1,0:T(8,128)(2,1)S(1)} %get-tuple-element.25), channel_id=1, source_target_pairs={{0,8},{4,12},{8,0},{12,4},{16,24},{20,28},{24,16},{28,20},{1,9},{5... | collective-permute-start | bytes 221192 | tf_op jit(solution)/shard_map/ppermute | solution.py:572

commit v16 on v15

--- a/solution.py
+++ b/solution.py
@@ -130,7 +130,7 @@
 
 
 def lay_out_kernel(columns, reach, replicas, cover, x_hbm, w_hbm, x_ref, w_ref, *refs):
-    *blocks, room, x_sem, w_sems = refs
+    *blocks, sums_ref, room, x_sem, w_sems = refs
     bands = len(blocks)
     band = lax.axis_index("space")
     lanes = room.shape[2]
@@ -156,8 +156,8 @@
     w_loads[0].wait()
     w_loads[1].wait()
     down, up = halo_sums(x_ref, w_ref, columns, reach)
+    sums_ref[...] = jnp.where(band < 2, down, up).astype(x.dtype)
     blocks[1][:, lanes:] = jnp.where(lax.rem(band, 2) == 0, down, up).astype(x.dtype)
-    blocks[3][:, lanes:] = jnp.where(band < 2, down, up).astype(x.dtype)
     w_loads[2].wait()
 
 
@@ -167,11 +167,11 @@
     hbm = pl.BlockSpec(memory_space=pltpu.HBM)
     vmem = pl.BlockSpec(memory_space=pltpu.VMEM)
     lanes = replicas * cover
-    shapes = [(pixels, lanes + (width if k % 2 else 0)) for k in range(bands)]
+    shapes = [(pixels, lanes + (width if k == 1 else 0)) for k in range(bands)] + [(pixels, width)]
     return pl.pallas_call(
         functools.partial(lay_out_kernel, columns, reach, replicas, cover),
         in_specs=[hbm, hbm],
-        out_specs=[vmem] * (2 + bands),
+        out_specs=[vmem] * (3 + bands),
         out_shape=[
             pltpu.VMEM(flat.shape, flat.dtype),
             pltpu.VMEM(weight.shape, weight.dtype),
@@ -260,15 +260,12 @@
 
 
 def pointwise_kernel(
-    paired, middle_ref, above_ref, below_ref, bias_ref, class_ref, label_ref, scale_ref, out_ref
+    middle_ref, above_ref, below_ref, bias_ref, class_ref, label_ref, scale_ref, out_ref
 ):
     pixels, width = middle_ref.shape
     edge = above_ref.shape[0]
     above = above_ref[:, above_ref.shape[1] - width :].astype(jnp.float32)
     below = below_ref[:, below_ref.shape[1] - width :].astype(jnp.float32)
-    if paired:
-        band = lax.axis_index("space")
-        below = jnp.where((band == 1) | (band == 2), below, 0.0)
     if pixels > edge:
         none = jnp.zeros((pixels - edge, width), jnp.float32)
         above = jnp.concatenate([above, none], axis=0)
@@ -293,10 +290,10 @@
     out_ref[...] = gradient.astype(out_ref.dtype)
 
 
-def pointwise(middle, above, below, bias, classes, labels, scale, paired):
+def pointwise(middle, above, below, bias, classes, labels, scale):
     pixels, width = middle.shape
     return pl.pallas_call(
-        functools.partial(pointwise_kernel, paired),
+        pointwise_kernel,
         out_shape=jax.ShapeDtypeStruct((pixels, width), jnp.bfloat16),
         compiler_params=pltpu.CompilerParams(vmem_limit_bytes=VMEM_LIMIT),
         cost_estimate=pl.CostEstimate(
@@ -517,12 +514,15 @@
     count = replicas // parts
     paired = bands == 4 and band_rows == reach and even
     if paired:
-        flat, weight, own, *blocks = lay_out(flat, weight, columns, reach, bands, replicas, cover)
+        flat, weight, own, *blocks, sums = lay_out(
+            flat, weight, columns, reach, bands, replicas, cover
+        )
+        below = lax.ppermute(sums, "space", [(1, 2), (2, 1)])
         whole = [own] + [
             lax.ppermute(block, "space", [(i, i ^ k) for i in range(bands)])
             for k, block in enumerate(blocks, 1)
         ]
-        above, below, after = whole[1], whole[3], blocks[0]
+        above, after = whole[1], sums
     else:
         flat, weight, *split = load(flat, weight, bands, replicas, cover, even)
         if not even:
@@ -544,7 +544,6 @@
         class_weight.T,
         labels.reshape(band_rows, columns),
         pixel_weight.reshape(band_rows, columns),
-        paired,
     )
     gradients = [gradient] + [
         lax.ppermute(gradient, "space", [(i, (i + k) % bands) for i in range(bands)])

time: 36.7 us -> 35.1 us (0.956)
  waiting for transfers between devices: 13.2 us -> 6.42 us
  starting transfers between devices: 15.3 us -> 20.4 us
    ppermute x3, waiting for transfers between devices: 7.37 us -> 0.46 us  [on_device(): lax.ppermute(block, 'space', [(i, i ^ k) for i in range(bands)])]
    ppermute x3, starting transfers between devices: 5.69 us -> 9.93 us  [on_device(): lax.ppermute(block, 'space', [(i, i ^ k) for i in range(bands)])]
    ppermute x0 -> x1, starting transfers between devices: none -> 0.65 us  [on_device(): below = lax.ppermute(sums, 'space', [(1, 2), (2, 1)])]
  transfers between devices with their start and end apart: 10 -> 11, of which waited for: 9 -> 7; matrix products, arithmetic and copies ran while one was open for 0% -> 0% of each run, Pallas kernels for 10% -> 11%
where the time goes in v16:
time: 35.1 us; the launch traced here: 34.9 us
  starting transfers between devices  20.4 us (58%)
  Pallas kernels  7.33 us (21%)
  waiting for transfers between devices  6.42 us (18%)
  between operations  0.77 us (2%)
    ppermute x3, starting transfers between devices, on_device(): lax.ppermute(block, 'space', [(i, i ^ k) for i in range(bands)])  9.93 us
    ppermute x3, starting transfers between devices, on_device(): lax.ppermute(gradient, 'space', [(i, (i + k) % bands) for i in range(band...  6.18 us
    ppermute x3, starting transfers between devices, on_device(): came.append(lax.ppermute(blocks[k], 'dp', pairs))  3.55 us
    ppermute x3, waiting for transfers between devices, on_device(): lax.ppermute(gradient, 'space', [(i, (i + k) % bands) for i in range(band...  2.66 us
    pallas_call x1, Pallas kernels, lay_out(): pl.pallas_call(functools.partial(lay_out_kernel, columns, reach, replicas...  2.43 us
    ppermute x3, waiting for transfers between devices, on_device(): came.append(lax.ppermute(blocks[k], 'dp', pairs))  2.08 us
    pallas_call x1, Pallas kernels, feature_grad(): pl.pallas_call(functools.partial(feature_grad_kernel, columns, reach, ban...  1.73 us
    pallas_call x3, Pallas kernels, kernel_grad(): pl.pallas_call(functools.partial(kernel_grad_kernel, columns, reach, part...  1.62 us
  transfers between devices with their start and end apart: 11, of which 7 were waited for; matrix products, arithmetic and copies ran while one was open for 0% of the time, Pallas kernels for 11%

profile of v16, /device:TPU:0, one launch (start us, length us, event | category | flops | bytes accessed | tf_op | source)
XLA Modules:
  0.0 34.9 jit_solution(17403699405273191671)
XLA Ops:
  0.6 0.0 copy-start.2
  0.6 0.0 copy-start.3
  0.7 0.0 copy-start
  0.7 0.0 copy-start.1
  0.7 2.4 %lay_out.1 = (bf16[192,1024]{1,0:T(8,128)(2,1)S(1)}, bf16[9,1024,128]{2,1,0:T(8,128)(2,1)S(1)}, bf16[192,256]{1,0:T(8,128)(2,1)S(1)}, bf16[192,384]{1,0:T(8,128)...) custom-call(bf16[192,1024]{1,0:T(8,128)(2,1)} %bitcast.13, ...), custom_call_target="tpu_custom_call" | custom-call | flops 301989888 | bytes 3145728 | tf_op jit(solution)/shard_map/lay_out/pallas_call | solution.py:171
  3.1 3.1 %collective-permute-start = (bf16[192,384]{1,0:T(8,128)(2,1)S(1)}, bf16[192,384]{1,0:T(8,128)(2,1)S(1)}, u32[]{:S(2)}, u32[]{:S(2)}) collective-permute-start(bf16[192,384]{1,0:T(8,128)(2,1)S(1)} %get-tuple-element.18), channel_id=1, source_target_pairs={{0,1},{1,0},{2,3},{3,2},{4,5},{5,4},{6,7},{7,6},{8,9},{9,8},{10,11... | collective-permute-start | bytes 442376 | tf_op jit(solution)/shard_map/ppermute | solution.py:522
  6.2 0.7 %collective-permute-start.1 = (bf16[192,128]{1,0:T(8,128)(2,1)S(1)}, bf16[192,128]{1,0:T(8,128)(2,1)S(1)}, u32[]{:S(2)}, u32[]{:S(2)}) collective-permute-start(bf16[192,128]{1,0:T(8,128)(2,1)S(1)} %get-tuple-element.17.after_ref), channel_id=1, source_target_pairs={{1,2},{2,1},{5,6},{6,5},{9,10},{10,9},{13,14},{14,13},{17,18},{18,... | collective-permute-start | bytes 147464 | tf_op jit(solution)/shard_map/ppermute | solution.py:520
  6.9 3.9 %collective-permute-start.4 = (bf16[192,256]{1,0:T(8,128)(2,1)S(1)}, bf16[192,256]{1,0:T(8,128)(2,1)S(1)}, u32[]{:S(2)}, u32[]{:S(2)}) collective-permute-start(bf16[192,256]{1,0:T(8,128)(2,1)S(1)} %get-tuple-element.20), channel_id=1, source_target_pairs={{0,2},{1,3},{2,0},{3,1},{4,6},{5,7},{6,4},{7,5},{8,10},{9,11},{10,... | collective-permute-start | bytes 294920 | tf_op jit(solution)/shard_map/ppermute | solution.py:522
  10.8 2.9 %collective-permute-start.5 = (bf16[192,256]{1,0:T(8,128)(2,1)S(1)}, bf16[192,256]{1,0:T(8,128)(2,1)S(1)}, u32[]{:S(2)}, u32[]{:S(2)}) collective-permute-start(bf16[192,256]{1,0:T(8,128)(2,1)S(1)} %get-tuple-element.21), channel_id=1, source_target_pairs={{0,3},{1,2},{2,1},{3,0},{4,7},{5,6},{6,5},{7,4},{8,11},{9,10},{10,... | collective-permute-start | bytes 294920 | tf_op jit(solution)/shard_map/ppermute | solution.py:522
  13.7 0.0 copy-done.2
  13.7 0.0 copy-done.3
  13.7 0.4 %middle_taps.1.middle_ref = f32[192,128]{1,0:T(8,128)S(1)} custom-call(bf16[192,1024]{1,0:T(8,128)(2,1)S(1)} %get-tuple-element.15.x_ref, bf16[9,1024,128]{2,1,0:T(8,128)(2,1)S(1)} %get-tuple-element.16.w_ref, bf16[192,128]{1,0:T(8,128)(2,1)S(1)} %get-tuple-element.17.after_ref), custom_call_target="tpu_custom_call" | custom-call | flops 150994944 | bytes 1179648 | tf_op jit(solution)/shard_map/middle_taps/pallas_call | solution.py:234
  14.1 0.0 collective-permute-done.1.below_ref
  14.1 0.0 collective-permute-done.above_ref.refs_1_
  14.1 0.0 copy-done
  14.1 0.0 copy-done.1
  14.1 0.4 %pointwise.1.own_ref.refs_4_ = bf16[192,128]{1,0:T(8,128)(2,1)S(1)} custom-call(f32[192,128]{1,0:T(8,128)S(1)} %middle_taps.1.middle_ref, bf16[192,384]{1,0:T(8,128)(2,1)S(1)} %collective-permute-done.above_ref.refs_1_, bf16[192,128]{1,0:T(8,128)(2,1)S(1)} %collective-permute-done.1.below_ref, f32[1,128]{1,0:T(1,128)S(1)} %bitcast.10, ...), custom_call_target="tpu_custom_call" | custom-call | flops 737280 | bytes 245760 | tf_op jit(solution)/shard_map/pointwise/pallas_call | solution.py:295
  14.6 2.2 %collective-permute-start.2 = (bf16[192,128]{1,0:T(8,128)(2,1)S(1)}, bf16[192,128]{1,0:T(8,128)(2,1)S(1)}, u32[]{:S(2)}, u32[]{:S(2)}) collective-permute-start(bf16[192,128]{1,0:T(8,128)(2,1)S(1)} %pointwise.1.own_ref.refs_4_), channel_id=1, source_target_pairs={{0,1},{1,2},{2,3},{3,0},{4,5},{5,6},{6,7},{7,4},{8,9},{9,10},{10,1... | collective-permute-start | bytes 147464 | tf_op jit(solution)/shard_map/ppermute | solution.py:549
  16.8 1.7 %collective-permute-start.3 = (bf16[192,128]{1,0:T(8,128)(2,1)S(1)}, bf16[192,128]{1,0:T(8,128)(2,1)S(1)}, u32[]{:S(2)}, u32[]{:S(2)}) collective-permute-start(bf16[192,128]{1,0:T(8,128)(2,1)S(1)} %pointwise.1.own_ref.refs_4_), channel_id=1, source_target_pairs={{0,3},{1,0},{2,1},{3,2},{4,7},{5,4},{6,5},{7,6},{8,11},{9,8},{10,9... | collective-permute-start | bytes 147464 | tf_op jit(solution)/shard_map/ppermute | solution.py:549
  18.4 2.3 %collective-permute-start.6 = (bf16[192,128]{1,0:T(8,128)(2,1)S(1)}, bf16[192,128]{1,0:T(8,128)(2,1)S(1)}, u32[]{:S(2)}, u32[]{:S(2)}) collective-permute-start(bf16[192,128]{1,0:T(8,128)(2,1)S(1)} %pointwise.1.own_ref.refs_4_), channel_id=1, source_target_pairs={{0,2},{1,3},{2,0},{3,1},{4,6},{5,7},{6,4},{7,5},{8,10},{9,11},{10,... | collective-permute-start | bytes 147464 | tf_op jit(solution)/shard_map/ppermute | solution.py:549
  20.7 0.5 %collective-permute-done.4.refs_2_ = bf16[192,256]{1,0:T(8,128)(2,1)S(1)} collective-permute-done((bf16[192,256]{1,0:T(8,128)(2,1)S(1)}, bf16[192,256]{1,0:T(8,128)(2,1)S(1)}, u32[]{:S(2)}, u32[]{:S(2)}) %collective-permute-start.4) | collective-permute-done | bytes 98336 | tf_op jit(solution)/shard_map/ppermute | solution.py:522
  21.2 0.0 collective-permute-done.5.refs_3_
  21.2 0.0 collective-permute-done.2.above_ref.refs_5_
  21.2 0.3 collective-permute-done.3.below_ref.refs_6_
  21.5 0.9 %kernel_grad.3 = (f32[128,1152]{1,0:T(8,128)S(1)}, f32[128,1152]{1,0:T(8,128)S(1)}) custom-call(bf16[192,256]{1,0:T(8,128)(2,1)S(1)} %get-tuple-element.19.refs_0_, bf16[192,384]{1,0:T(8,128)(2,1)S(1)} %collective-permute-done.above_ref.refs_1_, bf16[192,256]{1,0:T(8,128)(2,1)S(1)} %collective-permute-done.4.refs_2_, ...), custom_call_target="tpu_custom_call" | custom-call | flops 339738624 | bytes 393216 | tf_op jit(solution)/shard_map/kernel_grad/pallas_call | solution.py:373
  22.4 2.3 %collective-permute-done.6.refs_4_ = bf16[192,128]{1,0:T(8,128)(2,1)S(1)} collective-permute-done((bf16[192,128]{1,0:T(8,128)(2,1)S(1)}, bf16[192,128]{1,0:T(8,128)(2,1)S(1)}, u32[]{:S(2)}, u32[]{:S(2)}) %collective-permute-start.6) | collective-permute-done | bytes 49184 | tf_op jit(solution)/shard_map/ppermute | solution.py:549
  24.8 0.4 %kernel_grad.5 = bf16[128,1152]{1,0:T(8,128)(2,1)S(1)} custom-call(bf16[192,256]{1,0:T(8,128)(2,1)S(1)} %get-tuple-element.19.refs_0_, bf16[192,384]{1,0:T(8,128)(2,1)S(1)} %collective-permute-done.above_ref.refs_1_, bf16[192,256]{1,0:T(8,128)(2,1)S(1)} %collective-permute-done.4.refs_2_, bf16[192,256]{1,0:T(8,128)(2,1)S(1)} %collective-permute-done.5.refs_3_, ...), custom_call_target="tpu_custom_call" | custom-call | flops 56623104 | bytes 393216 | tf_op jit(solution)/shard_map/kernel_grad/pallas_call | solution.py:373
  25.1 0.1 collective-permute-start.7
  25.2 0.3 kernel_grad.4.refs_0_
  25.6 1.2 %collective-permute-done.7.refs_1_ = bf16[128,1152]{1,0:T(8,128)(2,1)S(1)} collective-permute-done((bf16[128,1152]{1,0:T(8,128)(2,1)S(1)}, bf16[128,1152]{1,0:T(8,128)(2,1)S(1)}, u32[]{:S(2)}, u32[]{:S(2)}) %collective-permute-start.7) | collective-permute-done | bytes 294944 | tf_op jit(solution)/shard_map/ppermute | solution.py:565
  26.8 0.1 split_up.1
  26.9 2.5 %collective-permute-start.8 = (bf16[32,1152]{1,0:T(8,128)(2,1)S(1)}, bf16[32,1152]{1,0:T(8,128)(2,1)S(1)}, u32[]{:S(2)}, u32[]{:S(2)}) collective-permute-start(bf16[32,1152]{1,0:T(8,128)(2,1)S(1)} %get-tuple-element.25), channel_id=1, source_target_pairs={{0,24},{4,28},{8,16},{12,20},{16,8},{20,12},{24,0},{28,4},{1,25},{... | collective-permute-start | bytes 221192 | tf_op jit(solution)/shard_map/ppermute | solution.py:571
  29.4 0.5 %collective-permute-start.9 = (bf16[32,1152]{1,0:T(8,128)(2,1)S(1)}, bf16[32,1152]{1,0:T(8,128)(2,1)S(1)}, u32[]{:S(2)}, u32[]{:S(2)}) collective-permute-start(bf16[32,1152]{1,0:T(8,128)(2,1)S(1)} %get-tuple-element.26), channel_id=1, source_target_pairs={{0,16},{4,20},{8,24},{12,28},{16,0},{20,4},{24,8},{28,12},{1,17},{... | collective-permute-start | bytes 221192 | tf_op jit(solution)/shard_map/ppermute | solution.py:571
  29.9 0.5 %collective-permute-start.10 = (bf16[32,1152]{1,0:T(8,128)(2,1)S(1)}, bf16[32,1152]{1,0:T(8,128)(2,1)S(1)}, u32[]{:S(2)}, u32[]{:S(2)}) collective-permute-start(bf16[32,1152]{1,0:T(8,128)(2,1)S(1)} %get-tuple-element.27), channel_id=1, source_target_pairs={{0,8},{4,12},{8,0},{12,4},{16,24},{20,28},{24,16},{28,20},{1,9},{5... | collective-permute-start | bytes 221192 | tf_op jit(solution)/shard_map/ppermute | solution.py:571
  30.4 1.7 %feature_grad.1 = f32[192,1024]{1,0:T(8,128)} custom-call(bf16[192,128]{1,0:T(8,128)(2,1)S(1)} %pointwise.1.own_ref.refs_4_, bf16[192,128]{1,0:T(8,128)(2,1)S(1)} %collective-permute-done.2.above_ref.refs_5_, bf16[192,128]{1,0:T(8,128)(2,1)S(1)} %collective-permute-done.3.below_ref.refs_6_, bf16[9,1024,128]{2,1,0:T(8,128)(2,1)S(1)} %get-tuple-element.16.w_ref), custom_call_target="tpu_custom_call" | custom-call | flops 452984832 | bytes 3145728 | tf_op jit(solution)/shard_map/feature_grad/pallas_call | solution.py:481
  32.1 0.1 collective-permute-done.8.refs_1_
  32.2 1.5 %collective-permute-done.9.refs_2_ = bf16[32,1152]{1,0:T(8,128)(2,1)S(1)} collective-permute-done((bf16[32,1152]{1,0:T(8,128)(2,1)S(1)}, bf16[32,1152]{1,0:T(8,128)(2,1)S(1)}, u32[]{:S(2)}, u32[]{:S(2)}) %collective-permute-start.9) | collective-permute-done | bytes 73760 | tf_op jit(solution)/shard_map/ppermute | solution.py:571
  33.8 0.5 %collective-permute-done.10.refs_3_ = bf16[32,1152]{1,0:T(8,128)(2,1)S(1)} collective-permute-done((bf16[32,1152]{1,0:T(8,128)(2,1)S(1)}, bf16[32,1152]{1,0:T(8,128)(2,1)S(1)}, u32[]{:S(2)}, u32[]{:S(2)}) %collective-permute-start.10) | collective-permute-done | bytes 73760 | tf_op jit(solution)/shard_map/ppermute | solution.py:571
  34.2 0.7 %final_sum.1 = f32[288,128]{1,0:T(8,128)} custom-call(bf16[32,1152]{1,0:T(8,128)(2,1)S(1)} %get-tuple-element.24.refs_0_, bf16[32,1152]{1,0:T(8,128)(2,1)S(1)} %collective-permute-done.8.refs_1_, bf16[32,1152]{1,0:T(8,128)(2,1)S(1)} %collective-permute-done.9.refs_2_, bf16[32,1152]{1,0:T(8,128)(2,1)S(1)} %collective-permute-done.10.refs_3_), custom_call_target="tpu_custom_call" | custom-call | tf_op jit(solution)/shard_map/final_sum/pallas_call | solution.py:441
  (1 shorter events, 0.0 us)
Async XLA Ops:
  0.6 13.1 %copy-start.2 = (s32[1,6,32]{2,0,1:T(1,128)S(1)}, s32[1,6,32]{2,0,1:T(1,128)}, u32[]{:S(2)}) copy-start(s32[1,6,32]{2,0,1:T(1,128)} %param.8) | copy-start | bytes 2308
  0.6 13.1 %copy-start.3 = (s32[1,6,32]{2,0,1:T(1,128)S(1)}, s32[1,6,32]{2,0,1:T(1,128)}, u32[]{:S(2)}) copy-start(s32[1,6,32]{2,0,1:T(1,128)} %param.7) | copy-start | bytes 2308
  0.7 13.4 %copy-start = (bf16[128,3]{0,1:T(4,128)(2,1)S(1)}, bf16[128,3]{0,1:T(4,128)(2,1)}, u32[]{:S(2)}) copy-start(bf16[128,3]{0,1:T(4,128)(2,1)} %param.11) | copy-start | bytes 2308
  0.7 13.4 %copy-start.1 = (f32[128]{0:T(128)S(1)}, f32[128]{0:T(128)}, u32[]{:S(2)}) copy-start(f32[128]{0:T(128)} %param.10) | copy-start | bytes 1540
  3.1 11.0 %collective-permute-start = (bf16[192,384]{1,0:T(8,128)(2,1)S(1)}, bf16[192,384]{1,0:T(8,128)(2,1)S(1)}, u32[]{:S(2)}, u32[]{:S(2)}) collective-permute-start(bf16[192,384]{1,0:T(8,128)(2,1)S(1)} %get-tuple-element.18), channel_id=1, source_target_pairs={{0,1},{1,0},{2,3},{3,2},{4,5},{5,4},{6,7},{7,6},{8,9},{9,8},{10,11... | collective-permute-start | bytes 442376 | tf_op jit(solution)/shard_map/ppermute | solution.py:522
  6.2 7.9 %collective-permute-start.1 = (bf16[192,128]{1,0:T(8,128)(2,1)S(1)}, bf16[192,128]{1,0:T(8,128)(2,1)S(1)}, u32[]{:S(2)}, u32[]{:S(2)}) collective-permute-start(bf16[192,128]{1,0:T(8,128)(2,1)S(1)} %get-tuple-element.17.after_ref), channel_id=1, source_target_pairs={{1,2},{2,1},{5,6},{6,5},{9,10},{10,9},{13,14},{14,13},{17,18},{18,... | collective-permute-start | bytes 147464 | tf_op jit(solution)/shard_map/ppermute | solution.py:520
  6.9 14.3 %collective-permute-start.4 = (bf16[192,256]{1,0:T(8,128)(2,1)S(1)}, bf16[192,256]{1,0:T(8,128)(2,1)S(1)}, u32[]{:S(2)}, u32[]{:S(2)}) collective-permute-start(bf16[192,256]{1,0:T(8,128)(2,1)S(1)} %get-tuple-element.20), channel_id=1, source_target_pairs={{0,2},{1,3},{2,0},{3,1},{4,6},{5,7},{6,4},{7,5},{8,10},{9,11},{10,... | collective-permute-start | bytes 294920 | tf_op jit(solution)/shard_map/ppermute | solution.py:522
  10.8 10.4 %collective-permute-start.5 = (bf16[192,256]{1,0:T(8,128)(2,1)S(1)}, bf16[192,256]{1,0:T(8,128)(2,1)S(1)}, u32[]{:S(2)}, u32[]{:S(2)}) collective-permute-start(bf16[192,256]{1,0:T(8,128)(2,1)S(1)} %get-tuple-element.21), channel_id=1, source_target_pairs={{0,3},{1,2},{2,1},{3,0},{4,7},{5,6},{6,5},{7,4},{8,11},{9,10},{10,... | collective-permute-start | bytes 294920 | tf_op jit(solution)/shard_map/ppermute | solution.py:522
  14.6 6.6 %collective-permute-start.2 = (bf16[192,128]{1,0:T(8,128)(2,1)S(1)}, bf16[192,128]{1,0:T(8,128)(2,1)S(1)}, u32[]{:S(2)}, u32[]{:S(2)}) collective-permute-start(bf16[192,128]{1,0:T(8,128)(2,1)S(1)} %pointwise.1.own_ref.refs_4_), channel_id=1, source_target_pairs={{0,1},{1,2},{2,3},{3,0},{4,5},{5,6},{6,7},{7,4},{8,9},{9,10},{10,1... | collective-permute-start | bytes 147464 | tf_op jit(solution)/shard_map/ppermute | solution.py:549
  16.8 4.8 %collective-permute-start.3 = (bf16[192,128]{1,0:T(8,128)(2,1)S(1)}, bf16[192,128]{1,0:T(8,128)(2,1)S(1)}, u32[]{:S(2)}, u32[]{:S(2)}) collective-permute-start(bf16[192,128]{1,0:T(8,128)(2,1)S(1)} %pointwise.1.own_ref.refs_4_), channel_id=1, source_target_pairs={{0,3},{1,0},{2,1},{3,2},{4,7},{5,4},{6,5},{7,6},{8,11},{9,8},{10,9... | collective-permute-start | bytes 147464 | tf_op jit(solution)/shard_map/ppermute | solution.py:549
  18.4 6.3 %collective-permute-start.6 = (bf16[192,128]{1,0:T(8,128)(2,1)S(1)}, bf16[192,128]{1,0:T(8,128)(2,1)S(1)}, u32[]{:S(2)}, u32[]{:S(2)}) collective-permute-start(bf16[192,128]{1,0:T(8,128)(2,1)S(1)} %pointwise.1.own_ref.refs_4_), channel_id=1, source_target_pairs={{0,2},{1,3},{2,0},{3,1},{4,6},{5,7},{6,4},{7,5},{8,10},{9,11},{10,... | collective-permute-start | bytes 147464 | tf_op jit(solution)/shard_map/ppermute | solution.py:549
  25.1 1.6 %collective-permute-start.7 = (bf16[128,1152]{1,0:T(8,128)(2,1)S(1)}, bf16[128,1152]{1,0:T(8,128)(2,1)S(1)}, u32[]{:S(2)}, u32[]{:S(2)}) collective-permute-start(bf16[128,1152]{1,0:T(8,128)(2,1)S(1)} %kernel_grad.5), channel_id=1, source_target_pairs={{0,4},{4,0},{8,12},{12,8},{16,20},{20,16},{24,28},{28,24},{1,5},{5... | collective-permute-start | bytes 884744 | tf_op jit(solution)/shard_map/ppermute | solution.py:565
  26.9 5.4 %collective-permute-start.8 = (bf16[32,1152]{1,0:T(8,128)(2,1)S(1)}, bf16[32,1152]{1,0:T(8,128)(2,1)S(1)}, u32[]{:S(2)}, u32[]{:S(2)}) collective-permute-start(bf16[32,1152]{1,0:T(8,128)(2,1)S(1)} %get-tuple-element.25), channel_id=1, source_target_pairs={{0,24},{4,28},{8,16},{12,20},{16,8},{20,12},{24,0},{28,4},{1,25},{... | collective-permute-start | bytes 221192 | tf_op jit(solution)/shard_map/ppermute | solution.py:571
  29.4 4.4 %collective-permute-start.9 = (bf16[32,1152]{1,0:T(8,128)(2,1)S(1)}, bf16[32,1152]{1,0:T(8,128)(2,1)S(1)}, u32[]{:S(2)}, u32[]{:S(2)}) collective-permute-start(bf16[32,1152]{1,0:T(8,128)(2,1)S(1)} %get-tuple-element.26), channel_id=1, source_target_pairs={{0,16},{4,20},{8,24},{12,28},{16,0},{20,4},{24,8},{28,12},{1,17},{... | collective-permute-start | bytes 221192 | tf_op jit(solution)/shard_map/ppermute | solution.py:571
  29.9 4.4 %collective-permute-start.10 = (bf16[32,1152]{1,0:T(8,128)(2,1)S(1)}, bf16[32,1152]{1,0:T(8,128)(2,1)S(1)}, u32[]{:S(2)}, u32[]{:S(2)}) collective-permute-start(bf16[32,1152]{1,0:T(8,128)(2,1)S(1)} %get-tuple-element.27), channel_id=1, source_target_pairs={{0,8},{4,12},{8,0},{12,4},{16,24},{20,28},{24,16},{28,20},{1,9},{5... | collective-permute-start | bytes 221192 | tf_op jit(solution)/shard_map/ppermute | solution.py:571

commit v17 on v16

--- a/solution.py
+++ b/solution.py
@@ -259,9 +259,8 @@
     )
 
 
-def pointwise_kernel(
-    middle_ref, above_ref, below_ref, bias_ref, class_ref, label_ref, scale_ref, out_ref
-):
+def pointwise_kernel(*refs):
+    middle_ref, above_ref, below_ref, bias_ref, class_ref, label_ref, scale_ref, out_ref = refs[-8:]
     pixels, width = middle_ref.shape
     edge = above_ref.shape[0]
     above = above_ref[:, above_ref.shape[1] - width :].astype(jnp.float32)
@@ -290,7 +289,7 @@
     out_ref[...] = gradient.astype(out_ref.dtype)
 
 
-def pointwise(middle, above, below, bias, classes, labels, scale):
+def pointwise(middle, above, below, bias, classes, labels, scale, after):
     pixels, width = middle.shape
     return pl.pallas_call(
         pointwise_kernel,
@@ -302,7 +301,7 @@
             transcendentals=pixels * width,
         ),
         name="pointwise",
-    )(middle, above, below, bias, classes, labels, scale)
+    )(*after, middle, above, below, bias, classes, labels, scale)
 
 
 def shifted_taps(gradient, columns, reach):
@@ -544,6 +543,7 @@
         class_weight.T,
         labels.reshape(band_rows, columns),
         pixel_weight.reshape(band_rows, columns),
+        whole[2:3],
     )
     gradients = [gradient] + [
         lax.ppermute(gradient, "space", [(i, (i + k) % bands) for i in range(bands)])

time: 35.1 us -> 33.4 us (0.952)
  starting transfers between devices: 20.4 us -> 15.3 us
  waiting for transfers between devices: 6.42 us -> 9.83 us
    ppermute x3, starting transfers between devices: 9.93 us -> 5.75 us  [on_device(): lax.ppermute(block, 'space', [(i, i ^ k) for i in range(bands)])]
    ppermute x3, waiting for transfers between devices: 0.46 us -> 3.72 us  [on_device(): lax.ppermute(block, 'space', [(i, i ^ k) for i in range(bands)])]
    ppermute x3, starting transfers between devices: 6.18 us -> 5.28 us  [on_device(): lax.ppermute(gradient, 'space', [(i, (i + k) % bands) for i in range(band...]
  transfers between devices with their start and end apart: 11 -> 11, of which waited for: 7 -> 8; matrix products, arithmetic and copies ran while one was open for 0% -> 0% of each run, Pallas kernels for 11% -> 11%
where the time goes in v17:
time: 33.4 us; the launch traced here: 33.3 us
  starting transfers between devices  15.3 us (46%)
  waiting for transfers between devices  9.83 us (29%)
  Pallas kernels  7.33 us (22%)
  between operations  0.78 us (2%)
    ppermute x3, starting transfers between devices, on_device(): lax.ppermute(block, 'space', [(i, i ^ k) for i in range(bands)])  5.75 us
    ppermute x3, starting transfers between devices, on_device(): lax.ppermute(gradient, 'space', [(i, (i + k) % bands) for i in range(band...  5.28 us
    ppermute x3, waiting for transfers between devices, on_device(): lax.ppermute(block, 'space', [(i, i ^ k) for i in range(bands)])  3.72 us
    ppermute x3, starting transfers between devices, on_device(): came.append(lax.ppermute(blocks[k], 'dp', pairs))  3.55 us
    ppermute x3, waiting for transfers between devices, on_device(): lax.ppermute(gradient, 'space', [(i, (i + k) % bands) for i in range(band...  2.73 us
    pallas_call x1, Pallas kernels, lay_out(): pl.pallas_call(functools.partial(lay_out_kernel, columns, reach, replicas...  2.43 us
    ppermute x3, waiting for transfers between devices, on_device(): came.append(lax.ppermute(blocks[k], 'dp', pairs))  2.16 us
    pallas_call x1, Pallas kernels, feature_grad(): pl.pallas_call(functools.partial(feature_grad_kernel, columns, reach, ban...  1.72 us
  transfers between devices with their start and end apart: 11, of which 8 were waited for; matrix products, arithmetic and copies ran while one was open for 0% of the time, Pallas kernels for 11%

profile of v17, /device:TPU:0, one launch (start us, length us, event | category | flops | bytes accessed | tf_op | source)
XLA Modules:
  0.0 33.3 jit_solution(6726571989081764278)
XLA Ops:
  0.6 0.0 copy-start.2
  0.6 0.0 copy-start.3
  0.7 0.0 copy-start
  0.7 0.0 copy-start.1
  0.7 2.4 %lay_out.1 = (bf16[192,1024]{1,0:T(8,128)(2,1)S(1)}, bf16[9,1024,128]{2,1,0:T(8,128)(2,1)S(1)}, bf16[192,256]{1,0:T(8,128)(2,1)S(1)}, bf16[192,384]{1,0:T(8,128)...) custom-call(bf16[192,1024]{1,0:T(8,128)(2,1)} %bitcast.13, ...), custom_call_target="tpu_custom_call" | custom-call | flops 301989888 | bytes 3145728 | tf_op jit(solution)/shard_map/lay_out/pallas_call | solution.py:171
  3.1 4.1 %collective-permute-start = (bf16[192,256]{1,0:T(8,128)(2,1)S(1)}, bf16[192,256]{1,0:T(8,128)(2,1)S(1)}, u32[]{:S(2)}, u32[]{:S(2)}) collective-permute-start(bf16[192,256]{1,0:T(8,128)(2,1)S(1)} %get-tuple-element.15), channel_id=1, source_target_pairs={{0,2},{1,3},{2,0},{3,1},{4,6},{5,7},{6,4},{7,5},{8,10},{9,11},{10,... | collective-permute-start | bytes 294920 | tf_op jit(solution)/shard_map/ppermute | solution.py:521
  7.2 1.6 %collective-permute-start.1 = (bf16[192,384]{1,0:T(8,128)(2,1)S(1)}, bf16[192,384]{1,0:T(8,128)(2,1)S(1)}, u32[]{:S(2)}, u32[]{:S(2)}) collective-permute-start(bf16[192,384]{1,0:T(8,128)(2,1)S(1)} %get-tuple-element.19), channel_id=1, source_target_pairs={{0,1},{1,0},{2,3},{3,2},{4,5},{5,4},{6,7},{7,6},{8,9},{9,8},{10,11... | collective-permute-start | bytes 442376 | tf_op jit(solution)/shard_map/ppermute | solution.py:521
  8.8 0.7 %collective-permute-start.2 = (bf16[192,128]{1,0:T(8,128)(2,1)S(1)}, bf16[192,128]{1,0:T(8,128)(2,1)S(1)}, u32[]{:S(2)}, u32[]{:S(2)}) collective-permute-start(bf16[192,128]{1,0:T(8,128)(2,1)S(1)} %get-tuple-element.18.after_ref), channel_id=1, source_target_pairs={{1,2},{2,1},{5,6},{6,5},{9,10},{10,9},{13,14},{14,13},{17,18},{18,... | collective-permute-start | bytes 147464 | tf_op jit(solution)/shard_map/ppermute | solution.py:519
  9.4 0.1 collective-permute-start.5
  9.5 0.0 copy-done.2
  9.5 0.0 copy-done.3
  9.6 0.4 %middle_taps.1.refs_1_ = f32[192,128]{1,0:T(8,128)S(1)} custom-call(bf16[192,1024]{1,0:T(8,128)(2,1)S(1)} %get-tuple-element.16.x_ref, bf16[9,1024,128]{2,1,0:T(8,128)(2,1)S(1)} %get-tuple-element.17.w_ref, bf16[192,128]{1,0:T(8,128)(2,1)S(1)} %get-tuple-element.18.after_ref), custom_call_target="tpu_custom_call" | custom-call | flops 150994944 | bytes 1179648 | tf_op jit(solution)/shard_map/middle_taps/pallas_call | solution.py:234
  9.9 0.0 collective-permute-done.2.refs_3_
  9.9 2.1 %collective-permute-done.refs_0_.refs_2_ = bf16[192,256]{1,0:T(8,128)(2,1)S(1)} collective-permute-done((bf16[192,256]{1,0:T(8,128)(2,1)S(1)}, bf16[192,256]{1,0:T(8,128)(2,1)S(1)}, u32[]{:S(2)}, u32[]{:S(2)}) %collective-permute-start) | collective-permute-done | bytes 98336 | tf_op jit(solution)/shard_map/ppermute | solution.py:521
  12.0 1.7 %collective-permute-done.1.refs_2_.refs_1_ = bf16[192,384]{1,0:T(8,128)(2,1)S(1)} collective-permute-done((bf16[192,384]{1,0:T(8,128)(2,1)S(1)}, bf16[192,384]{1,0:T(8,128)(2,1)S(1)}, u32[]{:S(2)}, u32[]{:S(2)}) %collective-permute-start.1) | collective-permute-done | bytes 147488 | tf_op jit(solution)/shard_map/ppermute | solution.py:521
  13.7 0.0 copy-done
  13.7 0.0 copy-done.1
  13.7 0.4 %pointwise.1.own_ref.refs_4_ = bf16[192,128]{1,0:T(8,128)(2,1)S(1)} custom-call(bf16[192,256]{1,0:T(8,128)(2,1)S(1)} %collective-permute-done.refs_0_.refs_2_, f32[192,128]{1,0:T(8,128)S(1)} %middle_taps.1.refs_1_, bf16[192,384]{1,0:T(8,128)(2,1)S(1)} %collective-permute-done.1.refs_2_.refs_1_, bf16[192,128]{1,0:T(8,128)(2,1)S(1)} %collective-permute-done.2.refs_3_, ...), custom_call_target="tpu_custom_call" | custom-call | flops 737280 | bytes 245760 | tf_op jit(solution)/shard_map/pointwise/pallas_call | solution.py:294
  14.1 3.6 %collective-permute-start.3 = (bf16[192,128]{1,0:T(8,128)(2,1)S(1)}, bf16[192,128]{1,0:T(8,128)(2,1)S(1)}, u32[]{:S(2)}, u32[]{:S(2)}) collective-permute-start(bf16[192,128]{1,0:T(8,128)(2,1)S(1)} %pointwise.1.own_ref.refs_4_), channel_id=1, source_target_pairs={{0,1},{1,2},{2,3},{3,0},{4,5},{5,6},{6,7},{7,4},{8,9},{9,10},{10,1... | collective-permute-start | bytes 147464 | tf_op jit(solution)/shard_map/ppermute | solution.py:549
  17.7 0.3 collective-permute-start.4
  18.0 1.4 %collective-permute-start.6 = (bf16[192,128]{1,0:T(8,128)(2,1)S(1)}, bf16[192,128]{1,0:T(8,128)(2,1)S(1)}, u32[]{:S(2)}, u32[]{:S(2)}) collective-permute-start(bf16[192,128]{1,0:T(8,128)(2,1)S(1)} %pointwise.1.own_ref.refs_4_), channel_id=1, source_target_pairs={{0,2},{1,3},{2,0},{3,1},{4,6},{5,7},{6,4},{7,5},{8,10},{9,11},{10,... | collective-permute-start | bytes 147464 | tf_op jit(solution)/shard_map/ppermute | solution.py:549
  19.4 0.0 collective-permute-done.5.refs_3_
  19.4 1.0 %collective-permute-done.3.above_ref.refs_5_ = bf16[192,128]{1,0:T(8,128)(2,1)S(1)} collective-permute-done((bf16[192,128]{1,0:T(8,128)(2,1)S(1)}, bf16[192,128]{1,0:T(8,128)(2,1)S(1)}, u32[]{:S(2)}, u32[]{:S(2)}) %collective-permute-start.3) | collective-permute-done | bytes 49184 | tf_op jit(solution)/shard_map/ppermute | solution.py:549
  20.4 1.7 %collective-permute-done.4.below_ref.refs_6_ = bf16[192,128]{1,0:T(8,128)(2,1)S(1)} collective-permute-done((bf16[192,128]{1,0:T(8,128)(2,1)S(1)}, bf16[192,128]{1,0:T(8,128)(2,1)S(1)}, u32[]{:S(2)}, u32[]{:S(2)}) %collective-permute-start.4) | collective-permute-done | bytes 49184 | tf_op jit(solution)/shard_map/ppermute | solution.py:549
  22.1 0.9 %kernel_grad.3 = (f32[128,1152]{1,0:T(8,128)S(1)}, f32[128,1152]{1,0:T(8,128)S(1)}) custom-call(bf16[192,256]{1,0:T(8,128)(2,1)S(1)} %get-tuple-element.20.refs_0_, bf16[192,384]{1,0:T(8,128)(2,1)S(1)} %collective-permute-done.1.refs_2_.refs_1_, bf16[192,256]{1,0:T(8,128)(2,1)S(1)} %collective-permute-done.refs_0_.refs_2_, ...), custom_call_target="tpu_custom_call" | custom-call | flops 339738624 | bytes 393216 | tf_op jit(solution)/shard_map/kernel_grad/pallas_call | solution.py:372
  23.0 0.0 collective-permute-done.6.refs_4_
  23.0 0.4 %kernel_grad.5 = bf16[128,1152]{1,0:T(8,128)(2,1)S(1)} custom-call(bf16[192,256]{1,0:T(8,128)(2,1)S(1)} %get-tuple-element.20.refs_0_, bf16[192,384]{1,0:T(8,128)(2,1)S(1)} %collective-permute-done.1.refs_2_.refs_1_, bf16[192,256]{1,0:T(8,128)(2,1)S(1)} %collective-permute-done.refs_0_.refs_2_, bf16[192,256]{1,0:T(8,128)(2,1)S(1)} %collective-permute-done.5.refs_3_, ...), custom_call_target="tpu_custom_call" | custom-call | flops 56623104 | bytes 393216 | tf_op jit(solution)/shard_map/kernel_grad/pallas_call | solution.py:372
  23.4 0.1 collective-permute-start.7
  23.5 0.3 %kernel_grad.4.refs_0_ = f32[128,1152]{1,0:T(8,128)S(1)} custom-call(bf16[192,256]{1,0:T(8,128)(2,1)S(1)} %get-tuple-element.20.refs_0_, bf16[192,384]{1,0:T(8,128)(2,1)S(1)} %collective-permute-done.1.refs_2_.refs_1_, bf16[192,256]{1,0:T(8,128)(2,1)S(1)} %collective-permute-done.refs_0_.refs_2_, bf16[192,256]{1,0:T(8,128)(2,1)S(1)} %collective-permute-done.5.refs_3_, ...), custom_call_target="tpu_custom_call" | custom-call | flops 56623104 | bytes 393216 | tf_op jit(solution)/shard_map/kernel_grad/pallas_call | solution.py:372
  23.8 1.2 %collective-permute-done.7.refs_1_ = bf16[128,1152]{1,0:T(8,128)(2,1)S(1)} collective-permute-done((bf16[128,1152]{1,0:T(8,128)(2,1)S(1)}, bf16[128,1152]{1,0:T(8,128)(2,1)S(1)}, u32[]{:S(2)}, u32[]{:S(2)}) %collective-permute-start.7) | collective-permute-done | bytes 294944 | tf_op jit(solution)/shard_map/ppermute | solution.py:565
  25.1 0.1 split_up.1
  25.1 2.6 %collective-permute-start.8 = (bf16[32,1152]{1,0:T(8,128)(2,1)S(1)}, bf16[32,1152]{1,0:T(8,128)(2,1)S(1)}, u32[]{:S(2)}, u32[]{:S(2)}) collective-permute-start(bf16[32,1152]{1,0:T(8,128)(2,1)S(1)} %get-tuple-element.25), channel_id=1, source_target_pairs={{0,24},{4,28},{8,16},{12,20},{16,8},{20,12},{24,0},{28,4},{1,25},{... | collective-permute-start | bytes 221192 | tf_op jit(solution)/shard_map/ppermute | solution.py:571
  27.7 0.5 %collective-permute-start.9 = (bf16[32,1152]{1,0:T(8,128)(2,1)S(1)}, bf16[32,1152]{1,0:T(8,128)(2,1)S(1)}, u32[]{:S(2)}, u32[]{:S(2)}) collective-permute-start(bf16[32,1152]{1,0:T(8,128)(2,1)S(1)} %get-tuple-element.26), channel_id=1, source_target_pairs={{0,16},{4,20},{8,24},{12,28},{16,0},{20,4},{24,8},{28,12},{1,17},{... | collective-permute-start | bytes 221192 | tf_op jit(solution)/shard_map/ppermute | solution.py:571
  28.2 0.5 %collective-permute-start.10 = (bf16[32,1152]{1,0:T(8,128)(2,1)S(1)}, bf16[32,1152]{1,0:T(8,128)(2,1)S(1)}, u32[]{:S(2)}, u32[]{:S(2)}) collective-permute-start(bf16[32,1152]{1,0:T(8,128)(2,1)S(1)} %get-tuple-element.27), channel_id=1, source_target_pairs={{0,8},{4,12},{8,0},{12,4},{16,24},{20,28},{24,16},{28,20},{1,9},{5... | collective-permute-start | bytes 221192 | tf_op jit(solution)/shard_map/ppermute | solution.py:571
  28.7 1.7 %feature_grad.1 = f32[192,1024]{1,0:T(8,128)} custom-call(bf16[192,128]{1,0:T(8,128)(2,1)S(1)} %pointwise.1.own_ref.refs_4_, bf16[192,128]{1,0:T(8,128)(2,1)S(1)} %collective-permute-done.3.above_ref.refs_5_, bf16[192,128]{1,0:T(8,128)(2,1)S(1)} %collective-permute-done.4.below_ref.refs_6_, bf16[9,1024,128]{2,1,0:T(8,128)(2,1)S(1)} %get-tuple-element.17.w_ref), custom_call_target="tpu_custom_call" | custom-call | flops 452984832 | bytes 3145728 | tf_op jit(solution)/shard_map/feature_grad/pallas_call | solution.py:480
  30.4 0.1 collective-permute-done.8.refs_1_
  30.5 1.6 %collective-permute-done.9.refs_2_ = bf16[32,1152]{1,0:T(8,128)(2,1)S(1)} collective-permute-done((bf16[32,1152]{1,0:T(8,128)(2,1)S(1)}, bf16[32,1152]{1,0:T(8,128)(2,1)S(1)}, u32[]{:S(2)}, u32[]{:S(2)}) %collective-permute-start.9) | collective-permute-done | bytes 73760 | tf_op jit(solution)/shard_map/ppermute | solution.py:571
  32.1 0.5 %collective-permute-done.10.refs_3_ = bf16[32,1152]{1,0:T(8,128)(2,1)S(1)} collective-permute-done((bf16[32,1152]{1,0:T(8,128)(2,1)S(1)}, bf16[32,1152]{1,0:T(8,128)(2,1)S(1)}, u32[]{:S(2)}, u32[]{:S(2)}) %collective-permute-start.10) | collective-permute-done | bytes 73760 | tf_op jit(solution)/shard_map/ppermute | solution.py:571
  32.6 0.7 %final_sum.1 = f32[288,128]{1,0:T(8,128)} custom-call(bf16[32,1152]{1,0:T(8,128)(2,1)S(1)} %get-tuple-element.24.refs_0_, bf16[32,1152]{1,0:T(8,128)(2,1)S(1)} %collective-permute-done.8.refs_1_, bf16[32,1152]{1,0:T(8,128)(2,1)S(1)} %collective-permute-done.9.refs_2_, bf16[32,1152]{1,0:T(8,128)(2,1)S(1)} %collective-permute-done.10.refs_3_), custom_call_target="tpu_custom_call" | custom-call | tf_op jit(solution)/shard_map/final_sum/pallas_call | solution.py:440
  (1 shorter events, 0.0 us)
Async XLA Ops:
  0.6 8.9 %copy-start.2 = (s32[1,6,32]{2,0,1:T(1,128)S(1)}, s32[1,6,32]{2,0,1:T(1,128)}, u32[]{:S(2)}) copy-start(s32[1,6,32]{2,0,1:T(1,128)} %param.8) | copy-start | bytes 2308
  0.6 8.9 %copy-start.3 = (s32[1,6,32]{2,0,1:T(1,128)S(1)}, s32[1,6,32]{2,0,1:T(1,128)}, u32[]{:S(2)}) copy-start(s32[1,6,32]{2,0,1:T(1,128)} %param.7) | copy-start | bytes 2308
  0.7 13.0 %copy-start = (bf16[128,3]{0,1:T(4,128)(2,1)S(1)}, bf16[128,3]{0,1:T(4,128)(2,1)}, u32[]{:S(2)}) copy-start(bf16[128,3]{0,1:T(4,128)(2,1)} %param.11) | copy-start | bytes 2308
  0.7 13.0 %copy-start.1 = (f32[128]{0:T(128)S(1)}, f32[128]{0:T(128)}, u32[]{:S(2)}) copy-start(f32[128]{0:T(128)} %param.10) | copy-start | bytes 1540
  3.1 8.9 %collective-permute-start = (bf16[192,256]{1,0:T(8,128)(2,1)S(1)}, bf16[192,256]{1,0:T(8,128)(2,1)S(1)}, u32[]{:S(2)}, u32[]{:S(2)}) collective-permute-start(bf16[192,256]{1,0:T(8,128)(2,1)S(1)} %get-tuple-element.15), channel_id=1, source_target_pairs={{0,2},{1,3},{2,0},{3,1},{4,6},{5,7},{6,4},{7,5},{8,10},{9,11},{10,... | collective-permute-start | bytes 294920 | tf_op jit(solution)/shard_map/ppermute | solution.py:521
  7.2 6.4 %collective-permute-start.1 = (bf16[192,384]{1,0:T(8,128)(2,1)S(1)}, bf16[192,384]{1,0:T(8,128)(2,1)S(1)}, u32[]{:S(2)}, u32[]{:S(2)}) collective-permute-start(bf16[192,384]{1,0:T(8,128)(2,1)S(1)} %get-tuple-element.19), channel_id=1, source_target_pairs={{0,1},{1,0},{2,3},{3,2},{4,5},{5,4},{6,7},{7,6},{8,9},{9,8},{10,11... | collective-permute-start | bytes 442376 | tf_op jit(solution)/shard_map/ppermute | solution.py:521
  8.8 1.1 %collective-permute-start.2 = (bf16[192,128]{1,0:T(8,128)(2,1)S(1)}, bf16[192,128]{1,0:T(8,128)(2,1)S(1)}, u32[]{:S(2)}, u32[]{:S(2)}) collective-permute-start(bf16[192,128]{1,0:T(8,128)(2,1)S(1)} %get-tuple-element.18.after_ref), channel_id=1, source_target_pairs={{1,2},{2,1},{5,6},{6,5},{9,10},{10,9},{13,14},{14,13},{17,18},{18,... | collective-permute-start | bytes 147464 | tf_op jit(solution)/shard_map/ppermute | solution.py:519
  9.4 9.9 %collective-permute-start.5 = (bf16[192,256]{1,0:T(8,128)(2,1)S(1)}, bf16[192,256]{1,0:T(8,128)(2,1)S(1)}, u32[]{:S(2)}, u32[]{:S(2)}) collective-permute-start(bf16[192,256]{1,0:T(8,128)(2,1)S(1)} %get-tuple-element.21), channel_id=1, source_target_pairs={{0,3},{1,2},{2,1},{3,0},{4,7},{5,6},{6,5},{7,4},{8,11},{9,10},{10,... | collective-permute-start | bytes 294920 | tf_op jit(solution)/shard_map/ppermute | solution.py:521
  14.1 6.3 %collective-permute-start.3 = (bf16[192,128]{1,0:T(8,128)(2,1)S(1)}, bf16[192,128]{1,0:T(8,128)(2,1)S(1)}, u32[]{:S(2)}, u32[]{:S(2)}) collective-permute-start(bf16[192,128]{1,0:T(8,128)(2,1)S(1)} %pointwise.1.own_ref.refs_4_), channel_id=1, source_target_pairs={{0,1},{1,2},{2,3},{3,0},{4,5},{5,6},{6,7},{7,4},{8,9},{9,10},{10,1... | collective-permute-start | bytes 147464 | tf_op jit(solution)/shard_map/ppermute | solution.py:549
  17.7 4.4 %collective-permute-start.4 = (bf16[192,128]{1,0:T(8,128)(2,1)S(1)}, bf16[192,128]{1,0:T(8,128)(2,1)S(1)}, u32[]{:S(2)}, u32[]{:S(2)}) collective-permute-start(bf16[192,128]{1,0:T(8,128)(2,1)S(1)} %pointwise.1.own_ref.refs_4_), channel_id=1, source_target_pairs={{0,3},{1,0},{2,1},{3,2},{4,7},{5,4},{6,5},{7,6},{8,11},{9,8},{10,9... | collective-permute-start | bytes 147464 | tf_op jit(solution)/shard_map/ppermute | solution.py:549
  18.0 5.1 %collective-permute-start.6 = (bf16[192,128]{1,0:T(8,128)(2,1)S(1)}, bf16[192,128]{1,0:T(8,128)(2,1)S(1)}, u32[]{:S(2)}, u32[]{:S(2)}) collective-permute-start(bf16[192,128]{1,0:T(8,128)(2,1)S(1)} %pointwise.1.own_ref.refs_4_), channel_id=1, source_target_pairs={{0,2},{1,3},{2,0},{3,1},{4,6},{5,7},{6,4},{7,5},{8,10},{9,11},{10,... | collective-permute-start | bytes 147464 | tf_op jit(solution)/shard_map/ppermute | solution.py:549
  23.4 1.6 %collective-permute-start.7 = (bf16[128,1152]{1,0:T(8,128)(2,1)S(1)}, bf16[128,1152]{1,0:T(8,128)(2,1)S(1)}, u32[]{:S(2)}, u32[]{:S(2)}) collective-permute-start(bf16[128,1152]{1,0:T(8,128)(2,1)S(1)} %kernel_grad.5), channel_id=1, source_target_pairs={{0,4},{4,0},{8,12},{12,8},{16,20},{20,16},{24,28},{28,24},{1,5},{5... | collective-permute-start | bytes 884744 | tf_op jit(solution)/shard_map/ppermute | solution.py:565
  25.1 5.3 %collective-permute-start.8 = (bf16[32,1152]{1,0:T(8,128)(2,1)S(1)}, bf16[32,1152]{1,0:T(8,128)(2,1)S(1)}, u32[]{:S(2)}, u32[]{:S(2)}) collective-permute-start(bf16[32,1152]{1,0:T(8,128)(2,1)S(1)} %get-tuple-element.25), channel_id=1, source_target_pairs={{0,24},{4,28},{8,16},{12,20},{16,8},{20,12},{24,0},{28,4},{1,25},{... | collective-permute-start | bytes 221192 | tf_op jit(solution)/shard_map/ppermute | solution.py:571
  27.7 4.4 %collective-permute-start.9 = (bf16[32,1152]{1,0:T(8,128)(2,1)S(1)}, bf16[32,1152]{1,0:T(8,128)(2,1)S(1)}, u32[]{:S(2)}, u32[]{:S(2)}) collective-permute-start(bf16[32,1152]{1,0:T(8,128)(2,1)S(1)} %get-tuple-element.26), channel_id=1, source_target_pairs={{0,16},{4,20},{8,24},{12,28},{16,0},{20,4},{24,8},{28,12},{1,17},{... | collective-permute-start | bytes 221192 | tf_op jit(solution)/shard_map/ppermute | solution.py:571
  28.2 4.4 %collective-permute-start.10 = (bf16[32,1152]{1,0:T(8,128)(2,1)S(1)}, bf16[32,1152]{1,0:T(8,128)(2,1)S(1)}, u32[]{:S(2)}, u32[]{:S(2)}) collective-permute-start(bf16[32,1152]{1,0:T(8,128)(2,1)S(1)} %get-tuple-element.27), channel_id=1, source_target_pairs={{0,8},{4,12},{8,0},{12,4},{16,24},{20,28},{24,16},{28,20},{1,9},{5... | collective-permute-start | bytes 221192 | tf_op jit(solution)/shard_map/ppermute | solution.py:571

commit v18 on v17

--- a/solution.py
+++ b/solution.py
@@ -260,7 +260,7 @@
 
 
 def pointwise_kernel(*refs):
-    middle_ref, above_ref, below_ref, bias_ref, class_ref, label_ref, scale_ref, out_ref = refs[-8:]
+    middle_ref, below_ref, above_ref, bias_ref, class_ref, label_ref, scale_ref, out_ref = refs[-8:]
     pixels, width = middle_ref.shape
     edge = above_ref.shape[0]
     above = above_ref[:, above_ref.shape[1] - width :].astype(jnp.float32)
@@ -301,7 +301,7 @@
             transcendentals=pixels * width,
         ),
         name="pointwise",
-    )(*after, middle, above, below, bias, classes, labels, scale)
+    )(*after, middle, below, above, bias, classes, labels, scale)
 
 
 def shifted_taps(gradient, columns, reach):

time: 33.4 us -> 36.9 us (1.10)
  starting transfers between devices: 15.3 us -> 20.1 us
  waiting for transfers between devices: 9.83 us -> 8.46 us
    ppermute x3, starting transfers between devices: 5.75 us -> 9.93 us  [on_device(): lax.ppermute(block, 'space', [(i, i ^ k) for i in range(bands)])]
    ppermute x3, waiting for transfers between devices: 3.72 us -> 1.52 us  [on_device(): lax.ppermute(block, 'space', [(i, i ^ k) for i in range(bands)])]
    ppermute x3, waiting for transfers between devices: 2.73 us -> 3.64 us  [on_device(): lax.ppermute(gradient, 'space', [(i, (i + k) % bands) for i in range(band...]
    ppermute x3, starting transfers between devices: 5.28 us -> 5.92 us  [on_device(): lax.ppermute(gradient, 'space', [(i, (i + k) % bands) for i in range(band...]
  transfers between devices with their start and end apart: 11 -> 11, of which waited for: 8 -> 7; matrix products, arithmetic and copies ran while one was open for 0% -> 0% of each run, Pallas kernels for 11% -> 10%
where the time goes in v18:
time: 36.9 us; the launch traced here: 36.7 us
  starting transfers between devices  20.1 us (54%)
  waiting for transfers between devices  8.46 us (23%)
  Pallas kernels  7.33 us (20%)
  between operations  0.76 us (2%)
    ppermute x3, starting transfers between devices, on_device(): lax.ppermute(block, 'space', [(i, i ^ k) for i in range(bands)])  9.93 us
    ppermute x3, starting transfers between devices, on_device(): lax.ppermute(gradient, 'space', [(i, (i + k) % bands) for i in range(band...  5.92 us
    ppermute x3, waiting for transfers between devices, on_device(): lax.ppermute(gradient, 'space', [(i, (i + k) % bands) for i in range(band...  3.64 us
    ppermute x3, starting transfers between devices, on_device(): came.append(lax.ppermute(blocks[k], 'dp', pairs))  3.55 us
    pallas_call x1, Pallas kernels, lay_out(): pl.pallas_call(functools.partial(lay_out_kernel, columns, reach, replicas...  2.43 us
    ppermute x3, waiting for transfers between devices, on_device(): came.append(lax.ppermute(blocks[k], 'dp', pairs))  2.08 us
    pallas_call x1, Pallas kernels, feature_grad(): pl.pallas_call(functools.partial(feature_grad_kernel, columns, reach, ban...  1.73 us
    pallas_call x3, Pallas kernels, kernel_grad(): pl.pallas_call(functools.partial(kernel_grad_kernel, columns, reach, part...  1.62 us
  transfers between devices with their start and end apart: 11, of which 7 were waited for; matrix products, arithmetic and copies ran while one was open for 0% of the time, Pallas kernels for 10%

profile of v18, /device:TPU:0, one launch (start us, length us, event | category | flops | bytes accessed | tf_op | source)
XLA Modules:
  0.0 36.7 jit_solution(14221026102635157417)
XLA Ops:
  0.6 0.0 copy-start.2
  0.6 0.0 copy-start.3
  0.7 0.0 copy-start
  0.7 0.0 copy-start.1
  0.7 2.4 %lay_out.1 = (bf16[192,1024]{1,0:T(8,128)(2,1)S(1)}, bf16[9,1024,128]{2,1,0:T(8,128)(2,1)S(1)}, bf16[192,256]{1,0:T(8,128)(2,1)S(1)}, bf16[192,384]{1,0:T(8,128)...) custom-call(bf16[192,1024]{1,0:T(8,128)(2,1)} %bitcast.13, ...), custom_call_target="tpu_custom_call" | custom-call | flops 301989888 | bytes 3145728 | tf_op jit(solution)/shard_map/lay_out/pallas_call | solution.py:171
  3.1 4.1 %collective-permute-start = (bf16[192,256]{1,0:T(8,128)(2,1)S(1)}, bf16[192,256]{1,0:T(8,128)(2,1)S(1)}, u32[]{:S(2)}, u32[]{:S(2)}) collective-permute-start(bf16[192,256]{1,0:T(8,128)(2,1)S(1)} %get-tuple-element.15), channel_id=1, source_target_pairs={{0,2},{1,3},{2,0},{3,1},{4,6},{5,7},{6,4},{7,5},{8,10},{9,11},{10,... | collective-permute-start | bytes 294920 | tf_op jit(solution)/shard_map/ppermute | solution.py:521
  7.2 0.7 %collective-permute-start.1 = (bf16[192,128]{1,0:T(8,128)(2,1)S(1)}, bf16[192,128]{1,0:T(8,128)(2,1)S(1)}, u32[]{:S(2)}, u32[]{:S(2)}) collective-permute-start(bf16[192,128]{1,0:T(8,128)(2,1)S(1)} %get-tuple-element.18.after_ref), channel_id=1, source_target_pairs={{1,2},{2,1},{5,6},{6,5},{9,10},{10,9},{13,14},{14,13},{17,18},{18,... | collective-permute-start | bytes 147464 | tf_op jit(solution)/shard_map/ppermute | solution.py:519
  7.9 2.9 %collective-permute-start.2 = (bf16[192,384]{1,0:T(8,128)(2,1)S(1)}, bf16[192,384]{1,0:T(8,128)(2,1)S(1)}, u32[]{:S(2)}, u32[]{:S(2)}) collective-permute-start(bf16[192,384]{1,0:T(8,128)(2,1)S(1)} %get-tuple-element.19), channel_id=1, source_target_pairs={{0,1},{1,0},{2,3},{3,2},{4,5},{5,4},{6,7},{7,6},{8,9},{9,8},{10,11... | collective-permute-start | bytes 442376 | tf_op jit(solution)/shard_map/ppermute | solution.py:521
  10.8 2.9 %collective-permute-start.5 = (bf16[192,256]{1,0:T(8,128)(2,1)S(1)}, bf16[192,256]{1,0:T(8,128)(2,1)S(1)}, u32[]{:S(2)}, u32[]{:S(2)}) collective-permute-start(bf16[192,256]{1,0:T(8,128)(2,1)S(1)} %get-tuple-element.21), channel_id=1, source_target_pairs={{0,3},{1,2},{2,1},{3,0},{4,7},{5,6},{6,5},{7,4},{8,11},{9,10},{10,... | collective-permute-start | bytes 294920 | tf_op jit(solution)/shard_map/ppermute | solution.py:521
  13.7 0.0 copy-done.2
  13.7 0.0 copy-done.3
  13.7 0.4 middle_taps.1.refs_1_
  14.1 0.0 collective-permute-done.1.refs_2_
  14.1 0.0 collective-permute-done.refs_0_.refs_2_
  14.1 1.5 %collective-permute-done.2.refs_3_.refs_1_ = bf16[192,384]{1,0:T(8,128)(2,1)S(1)} collective-permute-done((bf16[192,384]{1,0:T(8,128)(2,1)S(1)}, bf16[192,384]{1,0:T(8,128)(2,1)S(1)}, u32[]{:S(2)}, u32[]{:S(2)}) %collective-permute-start.2) | collective-permute-done | bytes 147488 | tf_op jit(solution)/shard_map/ppermute | solution.py:521
  15.6 0.0 copy-done
  15.6 0.0 copy-done.1
  15.6 0.4 %pointwise.1.own_ref.refs_4_ = bf16[192,128]{1,0:T(8,128)(2,1)S(1)} custom-call(bf16[192,256]{1,0:T(8,128)(2,1)S(1)} %collective-permute-done.refs_0_.refs_2_, f32[192,128]{1,0:T(8,128)S(1)} %middle_taps.1.refs_1_, bf16[192,128]{1,0:T(8,128)(2,1)S(1)} %collective-permute-done.1.refs_2_, bf16[192,384]{1,0:T(8,128)(2,1)S(1)} %collective-permute-done.2.refs_3_.refs_1_, ...), custom_call_target="tpu_custom_call" | custom-call | flops 737280 | bytes 245760 | tf_op jit(solution)/shard_map/pointwise/pallas_call | solution.py:294
  16.0 1.3 %collective-permute-start.3 = (bf16[192,128]{1,0:T(8,128)(2,1)S(1)}, bf16[192,128]{1,0:T(8,128)(2,1)S(1)}, u32[]{:S(2)}, u32[]{:S(2)}) collective-permute-start(bf16[192,128]{1,0:T(8,128)(2,1)S(1)} %pointwise.1.own_ref.refs_4_), channel_id=1, source_target_pairs={{0,1},{1,2},{2,3},{3,0},{4,5},{5,6},{6,7},{7,4},{8,9},{9,10},{10,1... | collective-permute-start | bytes 147464 | tf_op jit(solution)/shard_map/ppermute | solution.py:549
  17.4 4.1 %collective-permute-start.4 = (bf16[192,128]{1,0:T(8,128)(2,1)S(1)}, bf16[192,128]{1,0:T(8,128)(2,1)S(1)}, u32[]{:S(2)}, u32[]{:S(2)}) collective-permute-start(bf16[192,128]{1,0:T(8,128)(2,1)S(1)} %pointwise.1.own_ref.refs_4_), channel_id=1, source_target_pairs={{0,3},{1,0},{2,1},{3,2},{4,7},{5,4},{6,5},{7,6},{8,11},{9,8},{10,9... | collective-permute-start | bytes 147464 | tf_op jit(solution)/shard_map/ppermute | solution.py:549
  21.5 0.5 %collective-permute-start.6 = (bf16[192,128]{1,0:T(8,128)(2,1)S(1)}, bf16[192,128]{1,0:T(8,128)(2,1)S(1)}, u32[]{:S(2)}, u32[]{:S(2)}) collective-permute-start(bf16[192,128]{1,0:T(8,128)(2,1)S(1)} %pointwise.1.own_ref.refs_4_), channel_id=1, source_target_pairs={{0,2},{1,3},{2,0},{3,1},{4,6},{5,7},{6,4},{7,5},{8,10},{9,11},{10,... | collective-permute-start | bytes 147464 | tf_op jit(solution)/shard_map/ppermute | solution.py:549
  22.0 0.0 collective-permute-done.5.refs_3_
  22.0 1.6 %collective-permute-done.3.above_ref.refs_5_ = bf16[192,128]{1,0:T(8,128)(2,1)S(1)} collective-permute-done((bf16[192,128]{1,0:T(8,128)(2,1)S(1)}, bf16[192,128]{1,0:T(8,128)(2,1)S(1)}, u32[]{:S(2)}, u32[]{:S(2)}) %collective-permute-start.3) | collective-permute-done | bytes 49184 | tf_op jit(solution)/shard_map/ppermute | solution.py:549
  23.5 0.0 collective-permute-done.4.below_ref.refs_6_
  23.5 0.9 %kernel_grad.3 = (f32[128,1152]{1,0:T(8,128)S(1)}, f32[128,1152]{1,0:T(8,128)S(1)}) custom-call(bf16[192,256]{1,0:T(8,128)(2,1)S(1)} %get-tuple-element.20.refs_0_, bf16[192,384]{1,0:T(8,128)(2,1)S(1)} %collective-permute-done.2.refs_3_.refs_1_, bf16[192,256]{1,0:T(8,128)(2,1)S(1)} %collective-permute-done.refs_0_.refs_2_, ...), custom_call_target="tpu_custom_call" | custom-call | flops 339738624 | bytes 393216 | tf_op jit(solution)/shard_map/kernel_grad/pallas_call | solution.py:372
  24.5 2.1 %collective-permute-done.6.refs_4_ = bf16[192,128]{1,0:T(8,128)(2,1)S(1)} collective-permute-done((bf16[192,128]{1,0:T(8,128)(2,1)S(1)}, bf16[192,128]{1,0:T(8,128)(2,1)S(1)}, u32[]{:S(2)}, u32[]{:S(2)}) %collective-permute-start.6) | collective-permute-done | bytes 49184 | tf_op jit(solution)/shard_map/ppermute | solution.py:549
  26.5 0.4 kernel_grad.5
  26.9 0.1 collective-permute-start.7
  27.0 0.3 kernel_grad.4.refs_0_
  27.3 1.2 %collective-permute-done.7.refs_1_ = bf16[128,1152]{1,0:T(8,128)(2,1)S(1)} collective-permute-done((bf16[128,1152]{1,0:T(8,128)(2,1)S(1)}, bf16[128,1152]{1,0:T(8,128)(2,1)S(1)}, u32[]{:S(2)}, u32[]{:S(2)}) %collective-permute-start.7) | collective-permute-done | bytes 294944 | tf_op jit(solution)/shard_map/ppermute | solution.py:565
  28.6 0.1 split_up.1
  28.6 2.5 %collective-permute-start.8 = (bf16[32,1152]{1,0:T(8,128)(2,1)S(1)}, bf16[32,1152]{1,0:T(8,128)(2,1)S(1)}, u32[]{:S(2)}, u32[]{:S(2)}) collective-permute-start(bf16[32,1152]{1,0:T(8,128)(2,1)S(1)} %get-tuple-element.25), channel_id=1, source_target_pairs={{0,24},{4,28},{8,16},{12,20},{16,8},{20,12},{24,0},{28,4},{1,25},{... | collective-permute-start | bytes 221192 | tf_op jit(solution)/shard_map/ppermute | solution.py:571
  31.1 0.5 %collective-permute-start.9 = (bf16[32,1152]{1,0:T(8,128)(2,1)S(1)}, bf16[32,1152]{1,0:T(8,128)(2,1)S(1)}, u32[]{:S(2)}, u32[]{:S(2)}) collective-permute-start(bf16[32,1152]{1,0:T(8,128)(2,1)S(1)} %get-tuple-element.26), channel_id=1, source_target_pairs={{0,16},{4,20},{8,24},{12,28},{16,0},{20,4},{24,8},{28,12},{1,17},{... | collective-permute-start | bytes 221192 | tf_op jit(solution)/shard_map/ppermute | solution.py:571
  31.6 0.5 %collective-permute-start.10 = (bf16[32,1152]{1,0:T(8,128)(2,1)S(1)}, bf16[32,1152]{1,0:T(8,128)(2,1)S(1)}, u32[]{:S(2)}, u32[]{:S(2)}) collective-permute-start(bf16[32,1152]{1,0:T(8,128)(2,1)S(1)} %get-tuple-element.27), channel_id=1, source_target_pairs={{0,8},{4,12},{8,0},{12,4},{16,24},{20,28},{24,16},{28,20},{1,9},{5... | collective-permute-start | bytes 221192 | tf_op jit(solution)/shard_map/ppermute | solution.py:571
  32.2 1.7 %feature_grad.1 = f32[192,1024]{1,0:T(8,128)} custom-call(bf16[192,128]{1,0:T(8,128)(2,1)S(1)} %pointwise.1.own_ref.refs_4_, bf16[192,128]{1,0:T(8,128)(2,1)S(1)} %collective-permute-done.3.above_ref.refs_5_, bf16[192,128]{1,0:T(8,128)(2,1)S(1)} %collective-permute-done.4.below_ref.refs_6_, bf16[9,1024,128]{2,1,0:T(8,128)(2,1)S(1)} %get-tuple-element.17.w_ref), custom_call_target="tpu_custom_call" | custom-call | flops 452984832 | bytes 3145728 | tf_op jit(solution)/shard_map/feature_grad/pallas_call | solution.py:480
  33.9 0.1 collective-permute-done.8.refs_1_
  34.0 1.5 %collective-permute-done.9.refs_2_ = bf16[32,1152]{1,0:T(8,128)(2,1)S(1)} collective-permute-done((bf16[32,1152]{1,0:T(8,128)(2,1)S(1)}, bf16[32,1152]{1,0:T(8,128)(2,1)S(1)}, u32[]{:S(2)}, u32[]{:S(2)}) %collective-permute-start.9) | collective-permute-done | bytes 73760 | tf_op jit(solution)/shard_map/ppermute | solution.py:571
  35.5 0.5 %collective-permute-done.10.refs_3_ = bf16[32,1152]{1,0:T(8,128)(2,1)S(1)} collective-permute-done((bf16[32,1152]{1,0:T(8,128)(2,1)S(1)}, bf16[32,1152]{1,0:T(8,128)(2,1)S(1)}, u32[]{:S(2)}, u32[]{:S(2)}) %collective-permute-start.10) | collective-permute-done | bytes 73760 | tf_op jit(solution)/shard_map/ppermute | solution.py:571
  36.0 0.7 %final_sum.1 = f32[288,128]{1,0:T(8,128)} custom-call(bf16[32,1152]{1,0:T(8,128)(2,1)S(1)} %get-tuple-element.24.refs_0_, bf16[32,1152]{1,0:T(8,128)(2,1)S(1)} %collective-permute-done.8.refs_1_, bf16[32,1152]{1,0:T(8,128)(2,1)S(1)} %collective-permute-done.9.refs_2_, bf16[32,1152]{1,0:T(8,128)(2,1)S(1)} %collective-permute-done.10.refs_3_), custom_call_target="tpu_custom_call" | custom-call | tf_op jit(solution)/shard_map/final_sum/pallas_call | solution.py:440
  (1 shorter events, 0.0 us)
Async XLA Ops:
  0.6 13.1 %copy-start.2 = (s32[1,6,32]{2,0,1:T(1,128)S(1)}, s32[1,6,32]{2,0,1:T(1,128)}, u32[]{:S(2)}) copy-start(s32[1,6,32]{2,0,1:T(1,128)} %param.8) | copy-start | bytes 2308
  0.6 13.1 %copy-start.3 = (s32[1,6,32]{2,0,1:T(1,128)S(1)}, s32[1,6,32]{2,0,1:T(1,128)}, u32[]{:S(2)}) copy-start(s32[1,6,32]{2,0,1:T(1,128)} %param.7) | copy-start | bytes 2308
  0.7 15.0 %copy-start = (bf16[128,3]{0,1:T(4,128)(2,1)S(1)}, bf16[128,3]{0,1:T(4,128)(2,1)}, u32[]{:S(2)}) copy-start(bf16[128,3]{0,1:T(4,128)(2,1)} %param.11) | copy-start | bytes 2308
  0.7 15.0 %copy-start.1 = (f32[128]{0:T(128)S(1)}, f32[128]{0:T(128)}, u32[]{:S(2)}) copy-start(f32[128]{0:T(128)} %param.10) | copy-start | bytes 1540
  3.1 11.0 %collective-permute-start = (bf16[192,256]{1,0:T(8,128)(2,1)S(1)}, bf16[192,256]{1,0:T(8,128)(2,1)S(1)}, u32[]{:S(2)}, u32[]{:S(2)}) collective-permute-start(bf16[192,256]{1,0:T(8,128)(2,1)S(1)} %get-tuple-element.15), channel_id=1, source_target_pairs={{0,2},{1,3},{2,0},{3,1},{4,6},{5,7},{6,4},{7,5},{8,10},{9,11},{10,... | collective-permute-start | bytes 294920 | tf_op jit(solution)/shard_map/ppermute | solution.py:521
  7.2 6.9 %collective-permute-start.1 = (bf16[192,128]{1,0:T(8,128)(2,1)S(1)}, bf16[192,128]{1,0:T(8,128)(2,1)S(1)}, u32[]{:S(2)}, u32[]{:S(2)}) collective-permute-start(bf16[192,128]{1,0:T(8,128)(2,1)S(1)} %get-tuple-element.18.after_ref), channel_id=1, source_target_pairs={{1,2},{2,1},{5,6},{6,5},{9,10},{10,9},{13,14},{14,13},{17,18},{18,... | collective-permute-start | bytes 147464 | tf_op jit(solution)/shard_map/ppermute | solution.py:519
  7.9 7.7 %collective-permute-start.2 = (bf16[192,384]{1,0:T(8,128)(2,1)S(1)}, bf16[192,384]{1,0:T(8,128)(2,1)S(1)}, u32[]{:S(2)}, u32[]{:S(2)}) collective-permute-start(bf16[192,384]{1,0:T(8,128)(2,1)S(1)} %get-tuple-element.19), channel_id=1, source_target_pairs={{0,1},{1,0},{2,3},{3,2},{4,5},{5,4},{6,7},{7,6},{8,9},{9,8},{10,11... | collective-permute-start | bytes 442376 | tf_op jit(solution)/shard_map/ppermute | solution.py:521
  10.8 11.2 %collective-permute-start.5 = (bf16[192,256]{1,0:T(8,128)(2,1)S(1)}, bf16[192,256]{1,0:T(8,128)(2,1)S(1)}, u32[]{:S(2)}, u32[]{:S(2)}) collective-permute-start(bf16[192,256]{1,0:T(8,128)(2,1)S(1)} %get-tuple-element.21), channel_id=1, source_target_pairs={{0,3},{1,2},{2,1},{3,0},{4,7},{5,6},{6,5},{7,4},{8,11},{9,10},{10,... | collective-permute-start | bytes 294920 | tf_op jit(solution)/shard_map/ppermute | solution.py:521
  16.0 7.5 %collective-permute-start.3 = (bf16[192,128]{1,0:T(8,128)(2,1)S(1)}, bf16[192,128]{1,0:T(8,128)(2,1)S(1)}, u32[]{:S(2)}, u32[]{:S(2)}) collective-permute-start(bf16[192,128]{1,0:T(8,128)(2,1)S(1)} %pointwise.1.own_ref.refs_4_), channel_id=1, source_target_pairs={{0,1},{1,2},{2,3},{3,0},{4,5},{5,6},{6,7},{7,4},{8,9},{9,10},{10,1... | collective-permute-start | bytes 147464 | tf_op jit(solution)/shard_map/ppermute | solution.py:549
  17.4 6.1 %collective-permute-start.4 = (bf16[192,128]{1,0:T(8,128)(2,1)S(1)}, bf16[192,128]{1,0:T(8,128)(2,1)S(1)}, u32[]{:S(2)}, u32[]{:S(2)}) collective-permute-start(bf16[192,128]{1,0:T(8,128)(2,1)S(1)} %pointwise.1.own_ref.refs_4_), channel_id=1, source_target_pairs={{0,3},{1,0},{2,1},{3,2},{4,7},{5,4},{6,5},{7,6},{8,11},{9,8},{10,9... | collective-permute-start | bytes 147464 | tf_op jit(solution)/shard_map/ppermute | solution.py:549
  21.5 5.1 %collective-permute-start.6 = (bf16[192,128]{1,0:T(8,128)(2,1)S(1)}, bf16[192,128]{1,0:T(8,128)(2,1)S(1)}, u32[]{:S(2)}, u32[]{:S(2)}) collective-permute-start(bf16[192,128]{1,0:T(8,128)(2,1)S(1)} %pointwise.1.own_ref.refs_4_), channel_id=1, source_target_pairs={{0,2},{1,3},{2,0},{3,1},{4,6},{5,7},{6,4},{7,5},{8,10},{9,11},{10,... | collective-permute-start | bytes 147464 | tf_op jit(solution)/shard_map/ppermute | solution.py:549
  26.9 1.6 %collective-permute-start.7 = (bf16[128,1152]{1,0:T(8,128)(2,1)S(1)}, bf16[128,1152]{1,0:T(8,128)(2,1)S(1)}, u32[]{:S(2)}, u32[]{:S(2)}) collective-permute-start(bf16[128,1152]{1,0:T(8,128)(2,1)S(1)} %kernel_grad.5), channel_id=1, source_target_pairs={{0,4},{4,0},{8,12},{12,8},{16,20},{20,16},{24,28},{28,24},{1,5},{5... | collective-permute-start | bytes 884744 | tf_op jit(solution)/shard_map/ppermute | solution.py:565
  28.6 5.4 %collective-permute-start.8 = (bf16[32,1152]{1,0:T(8,128)(2,1)S(1)}, bf16[32,1152]{1,0:T(8,128)(2,1)S(1)}, u32[]{:S(2)}, u32[]{:S(2)}) collective-permute-start(bf16[32,1152]{1,0:T(8,128)(2,1)S(1)} %get-tuple-element.25), channel_id=1, source_target_pairs={{0,24},{4,28},{8,16},{12,20},{16,8},{20,12},{24,0},{28,4},{1,25},{... | collective-permute-start | bytes 221192 | tf_op jit(solution)/shard_map/ppermute | solution.py:571
  31.1 4.4 %collective-permute-start.9 = (bf16[32,1152]{1,0:T(8,128)(2,1)S(1)}, bf16[32,1152]{1,0:T(8,128)(2,1)S(1)}, u32[]{:S(2)}, u32[]{:S(2)}) collective-permute-start(bf16[32,1152]{1,0:T(8,128)(2,1)S(1)} %get-tuple-element.26), channel_id=1, source_target_pairs={{0,16},{4,20},{8,24},{12,28},{16,0},{20,4},{24,8},{28,12},{1,17},{... | collective-permute-start | bytes 221192 | tf_op jit(solution)/shard_map/ppermute | solution.py:571
  31.6 4.4 %collective-permute-start.10 = (bf16[32,1152]{1,0:T(8,128)(2,1)S(1)}, bf16[32,1152]{1,0:T(8,128)(2,1)S(1)}, u32[]{:S(2)}, u32[]{:S(2)}) collective-permute-start(bf16[32,1152]{1,0:T(8,128)(2,1)S(1)} %get-tuple-element.27), channel_id=1, source_target_pairs={{0,8},{4,12},{8,0},{12,4},{16,24},{20,28},{24,16},{28,20},{1,9},{5... | collective-permute-start | bytes 221192 | tf_op jit(solution)/shard_map/ppermute | solution.py:571

commit v19 on v17

--- a/solution.py
+++ b/solution.py
@@ -549,13 +549,13 @@
         lax.ppermute(gradient, "space", [(i, (i + k) % bands) for i in range(bands)])
         for k in range(1, bands)
     ]
-    late = bands // 2
-    early = {k: g for k, g in enumerate(gradients) if k != late or bands == 1}
+    late = range(bands // 2, min(bands // 2 + 2, bands))
+    early = {k: g for k, g in enumerate(gradients) if k not in late or bands == 1}
     others = (0, 1)[:parts]
     size = (bands, replicas * cover)
     terms = kernel_grad(whole, early, [], columns, reach, parts, others, jnp.float32, *size)
     if bands > 1:
-        last = {late: gradients[late]}
+        last = {k: gradients[k] for k in late}
         own, *theirs = terms
         terms = kernel_grad(whole, last, [own], columns, reach, parts, (0,), jnp.float32, *size)
         if theirs:

time: 33.4 us -> 33.6 us (level)
  no operation moved by 1% of the time
where the time goes in v19:
time: 33.6 us; the launch traced here: 33.4 us
  starting transfers between devices  15.3 us (46%)
  waiting for transfers between devices  9.98 us (30%)
  Pallas kernels  7.31 us (22%)
  between operations  0.78 us (2%)
    ppermute x3, starting transfers between devices, on_device(): lax.ppermute(block, 'space', [(i, i ^ k) for i in range(bands)])  5.75 us
    ppermute x3, starting transfers between devices, on_device(): lax.ppermute(gradient, 'space', [(i, (i + k) % bands) for i in range(band...  5.28 us
    ppermute x3, waiting for transfers between devices, on_device(): lax.ppermute(block, 'space', [(i, i ^ k) for i in range(bands)])  3.72 us
    ppermute x3, starting transfers between devices, on_device(): came.append(lax.ppermute(blocks[k], 'dp', pairs))  3.55 us
    ppermute x3, waiting for transfers between devices, on_device(): lax.ppermute(gradient, 'space', [(i, (i + k) % bands) for i in range(band...  2.9 us
    pallas_call x1, Pallas kernels, lay_out(): pl.pallas_call(functools.partial(lay_out_kernel, columns, reach, replicas...  2.43 us
    ppermute x3, waiting for transfers between devices, on_device(): came.append(lax.ppermute(blocks[k], 'dp', pairs))  2.26 us
    pallas_call x1, Pallas kernels, feature_grad(): pl.pallas_call(functools.partial(feature_grad_kernel, columns, reach, ban...  1.72 us
  transfers between devices with their start and end apart: 11, of which 8 were waited for; matrix products, arithmetic and copies ran while one was open for 0% of the time, Pallas kernels for 11%

profile of v19, /device:TPU:0, one launch (start us, length us, event | category | flops | bytes accessed | tf_op | source)
XLA Modules:
  0.0 33.4 jit_solution(10710860724905522519)
XLA Ops:
  0.6 0.0 copy-start.2
  0.6 0.0 copy-start.3
  0.7 0.0 copy-start
  0.7 0.0 copy-start.1
  0.7 2.4 %lay_out.1 = (bf16[192,1024]{1,0:T(8,128)(2,1)S(1)}, bf16[9,1024,128]{2,1,0:T(8,128)(2,1)S(1)}, bf16[192,256]{1,0:T(8,128)(2,1)S(1)}, bf16[192,384]{1,0:T(8,128)...) custom-call(bf16[192,1024]{1,0:T(8,128)(2,1)} %bitcast.13, ...), custom_call_target="tpu_custom_call" | custom-call | flops 301989888 | bytes 3145728 | tf_op jit(solution)/shard_map/lay_out/pallas_call | solution.py:171
  3.1 4.1 %collective-permute-start = (bf16[192,256]{1,0:T(8,128)(2,1)S(1)}, bf16[192,256]{1,0:T(8,128)(2,1)S(1)}, u32[]{:S(2)}, u32[]{:S(2)}) collective-permute-start(bf16[192,256]{1,0:T(8,128)(2,1)S(1)} %get-tuple-element.15), channel_id=1, source_target_pairs={{0,2},{1,3},{2,0},{3,1},{4,6},{5,7},{6,4},{7,5},{8,10},{9,11},{10,... | collective-permute-start | bytes 294920 | tf_op jit(solution)/shard_map/ppermute | solution.py:521
  7.2 1.6 %collective-permute-start.1 = (bf16[192,384]{1,0:T(8,128)(2,1)S(1)}, bf16[192,384]{1,0:T(8,128)(2,1)S(1)}, u32[]{:S(2)}, u32[]{:S(2)}) collective-permute-start(bf16[192,384]{1,0:T(8,128)(2,1)S(1)} %get-tuple-element.19), channel_id=1, source_target_pairs={{0,1},{1,0},{2,3},{3,2},{4,5},{5,4},{6,7},{7,6},{8,9},{9,8},{10,11... | collective-permute-start | bytes 442376 | tf_op jit(solution)/shard_map/ppermute | solution.py:521
  8.8 0.7 %collective-permute-start.2 = (bf16[192,128]{1,0:T(8,128)(2,1)S(1)}, bf16[192,128]{1,0:T(8,128)(2,1)S(1)}, u32[]{:S(2)}, u32[]{:S(2)}) collective-permute-start(bf16[192,128]{1,0:T(8,128)(2,1)S(1)} %get-tuple-element.18.after_ref), channel_id=1, source_target_pairs={{1,2},{2,1},{5,6},{6,5},{9,10},{10,9},{13,14},{14,13},{17,18},{18,... | collective-permute-start | bytes 147464 | tf_op jit(solution)/shard_map/ppermute | solution.py:519
  9.4 0.1 collective-permute-start.5
  9.5 0.0 copy-done.2
  9.5 0.0 copy-done.3
  9.6 0.4 %middle_taps.1.refs_1_ = f32[192,128]{1,0:T(8,128)S(1)} custom-call(bf16[192,1024]{1,0:T(8,128)(2,1)S(1)} %get-tuple-element.16.x_ref, bf16[9,1024,128]{2,1,0:T(8,128)(2,1)S(1)} %get-tuple-element.17.w_ref, bf16[192,128]{1,0:T(8,128)(2,1)S(1)} %get-tuple-element.18.after_ref), custom_call_target="tpu_custom_call" | custom-call | flops 150994944 | bytes 1179648 | tf_op jit(solution)/shard_map/middle_taps/pallas_call | solution.py:234
  9.9 0.0 collective-permute-done.2.refs_3_
  9.9 2.1 %collective-permute-done.refs_0_.refs_2_ = bf16[192,256]{1,0:T(8,128)(2,1)S(1)} collective-permute-done((bf16[192,256]{1,0:T(8,128)(2,1)S(1)}, bf16[192,256]{1,0:T(8,128)(2,1)S(1)}, u32[]{:S(2)}, u32[]{:S(2)}) %collective-permute-start) | collective-permute-done | bytes 98336 | tf_op jit(solution)/shard_map/ppermute | solution.py:521
  12.0 1.7 %collective-permute-done.1.refs_2_.refs_1_ = bf16[192,384]{1,0:T(8,128)(2,1)S(1)} collective-permute-done((bf16[192,384]{1,0:T(8,128)(2,1)S(1)}, bf16[192,384]{1,0:T(8,128)(2,1)S(1)}, u32[]{:S(2)}, u32[]{:S(2)}) %collective-permute-start.1) | collective-permute-done | bytes 147488 | tf_op jit(solution)/shard_map/ppermute | solution.py:521
  13.7 0.0 copy-done
  13.7 0.0 copy-done.1
  13.7 0.4 %pointwise.1.own_ref.refs_4_ = bf16[192,128]{1,0:T(8,128)(2,1)S(1)} custom-call(bf16[192,256]{1,0:T(8,128)(2,1)S(1)} %collective-permute-done.refs_0_.refs_2_, f32[192,128]{1,0:T(8,128)S(1)} %middle_taps.1.refs_1_, bf16[192,384]{1,0:T(8,128)(2,1)S(1)} %collective-permute-done.1.refs_2_.refs_1_, bf16[192,128]{1,0:T(8,128)(2,1)S(1)} %collective-permute-done.2.refs_3_, ...), custom_call_target="tpu_custom_call" | custom-call | flops 737280 | bytes 245760 | tf_op jit(solution)/shard_map/pointwise/pallas_call | solution.py:294
  14.1 3.6 %collective-permute-start.3 = (bf16[192,128]{1,0:T(8,128)(2,1)S(1)}, bf16[192,128]{1,0:T(8,128)(2,1)S(1)}, u32[]{:S(2)}, u32[]{:S(2)}) collective-permute-start(bf16[192,128]{1,0:T(8,128)(2,1)S(1)} %pointwise.1.own_ref.refs_4_), channel_id=1, source_target_pairs={{0,1},{1,2},{2,3},{3,0},{4,5},{5,6},{6,7},{7,4},{8,9},{9,10},{10,1... | collective-permute-start | bytes 147464 | tf_op jit(solution)/shard_map/ppermute | solution.py:549
  17.7 0.3 collective-permute-start.4
  18.0 1.4 %collective-permute-start.6 = (bf16[192,128]{1,0:T(8,128)(2,1)S(1)}, bf16[192,128]{1,0:T(8,128)(2,1)S(1)}, u32[]{:S(2)}, u32[]{:S(2)}) collective-permute-start(bf16[192,128]{1,0:T(8,128)(2,1)S(1)} %pointwise.1.own_ref.refs_4_), channel_id=1, source_target_pairs={{0,2},{1,3},{2,0},{3,1},{4,6},{5,7},{6,4},{7,5},{8,10},{9,11},{10,... | collective-permute-start | bytes 147464 | tf_op jit(solution)/shard_map/ppermute | solution.py:549
  19.4 0.0 collective-permute-done.5.refs_3_
  19.4 1.0 %collective-permute-done.3.above_ref.refs_5_ = bf16[192,128]{1,0:T(8,128)(2,1)S(1)} collective-permute-done((bf16[192,128]{1,0:T(8,128)(2,1)S(1)}, bf16[192,128]{1,0:T(8,128)(2,1)S(1)}, u32[]{:S(2)}, u32[]{:S(2)}) %collective-permute-start.3) | collective-permute-done | bytes 49184 | tf_op jit(solution)/shard_map/ppermute | solution.py:549
  20.4 0.7 %kernel_grad.3 = (f32[128,1152]{1,0:T(8,128)S(1)}, f32[128,1152]{1,0:T(8,128)S(1)}) custom-call(bf16[192,256]{1,0:T(8,128)(2,1)S(1)} %get-tuple-element.20.refs_0_, bf16[192,384]{1,0:T(8,128)(2,1)S(1)} %collective-permute-done.1.refs_2_.refs_1_, bf16[192,256]{1,0:T(8,128)(2,1)S(1)} %collective-permute-done.refs_0_.refs_2_, ...), custom_call_target="tpu_custom_call" | custom-call | flops 226492416 | bytes 393216 | tf_op jit(solution)/shard_map/kernel_grad/pallas_call | solution.py:372
  21.1 1.0 %collective-permute-done.4.below_ref.refs_5_ = bf16[192,128]{1,0:T(8,128)(2,1)S(1)} collective-permute-done((bf16[192,128]{1,0:T(8,128)(2,1)S(1)}, bf16[192,128]{1,0:T(8,128)(2,1)S(1)}, u32[]{:S(2)}, u32[]{:S(2)}) %collective-permute-start.4) | collective-permute-done | bytes 49184 | tf_op jit(solution)/shard_map/ppermute | solution.py:549
  22.1 0.9 %collective-permute-done.6.refs_4_ = bf16[192,128]{1,0:T(8,128)(2,1)S(1)} collective-permute-done((bf16[192,128]{1,0:T(8,128)(2,1)S(1)}, bf16[192,128]{1,0:T(8,128)(2,1)S(1)}, u32[]{:S(2)}, u32[]{:S(2)}) %collective-permute-start.6) | collective-permute-done | bytes 49184 | tf_op jit(solution)/shard_map/ppermute | solution.py:549
  23.0 0.5 %kernel_grad.5 = bf16[128,1152]{1,0:T(8,128)(2,1)S(1)} custom-call(bf16[192,256]{1,0:T(8,128)(2,1)S(1)} %get-tuple-element.20.refs_0_, bf16[192,384]{1,0:T(8,128)(2,1)S(1)} %collective-permute-done.1.refs_2_.refs_1_, bf16[192,256]{1,0:T(8,128)(2,1)S(1)} %collective-permute-done.refs_0_.refs_2_, bf16[192,256]{1,0:T(8,128)(2,1)S(1)} %collective-permute-done.5.refs_3_, ...), custom_call_target="tpu_custom_call" | custom-call | flops 113246208 | bytes 393216 | tf_op jit(solution)/shard_map/kernel_grad/pallas_call | solution.py:372
  23.4 0.1 collective-permute-start.7
  23.5 0.5 %kernel_grad.4.refs_0_ = f32[128,1152]{1,0:T(8,128)S(1)} custom-call(bf16[192,256]{1,0:T(8,128)(2,1)S(1)} %get-tuple-element.20.refs_0_, bf16[192,384]{1,0:T(8,128)(2,1)S(1)} %collective-permute-done.1.refs_2_.refs_1_, bf16[192,256]{1,0:T(8,128)(2,1)S(1)} %collective-permute-done.refs_0_.refs_2_, bf16[192,256]{1,0:T(8,128)(2,1)S(1)} %collective-permute-done.5.refs_3_, ...), custom_call_target="tpu_custom_call" | custom-call | flops 113246208 | bytes 393216 | tf_op jit(solution)/shard_map/kernel_grad/pallas_call | solution.py:372
  24.0 1.1 %collective-permute-done.7.refs_1_ = bf16[128,1152]{1,0:T(8,128)(2,1)S(1)} collective-permute-done((bf16[128,1152]{1,0:T(8,128)(2,1)S(1)}, bf16[128,1152]{1,0:T(8,128)(2,1)S(1)}, u32[]{:S(2)}, u32[]{:S(2)}) %collective-permute-start.7) | collective-permute-done | bytes 294944 | tf_op jit(solution)/shard_map/ppermute | solution.py:565
  25.1 0.1 split_up.1
  25.1 2.7 %collective-permute-start.8 = (bf16[32,1152]{1,0:T(8,128)(2,1)S(1)}, bf16[32,1152]{1,0:T(8,128)(2,1)S(1)}, u32[]{:S(2)}, u32[]{:S(2)}) collective-permute-start(bf16[32,1152]{1,0:T(8,128)(2,1)S(1)} %get-tuple-element.25), channel_id=1, source_target_pairs={{0,24},{4,28},{8,16},{12,20},{16,8},{20,12},{24,0},{28,4},{1,25},{... | collective-permute-start | bytes 221192 | tf_op jit(solution)/shard_map/ppermute | solution.py:571
  27.8 0.5 %collective-permute-start.9 = (bf16[32,1152]{1,0:T(8,128)(2,1)S(1)}, bf16[32,1152]{1,0:T(8,128)(2,1)S(1)}, u32[]{:S(2)}, u32[]{:S(2)}) collective-permute-start(bf16[32,1152]{1,0:T(8,128)(2,1)S(1)} %get-tuple-element.26), channel_id=1, source_target_pairs={{0,16},{4,20},{8,24},{12,28},{16,0},{20,4},{24,8},{28,12},{1,17},{... | collective-permute-start | bytes 221192 | tf_op jit(solution)/shard_map/ppermute | solution.py:571
  28.3 0.4 %collective-permute-start.10 = (bf16[32,1152]{1,0:T(8,128)(2,1)S(1)}, bf16[32,1152]{1,0:T(8,128)(2,1)S(1)}, u32[]{:S(2)}, u32[]{:S(2)}) collective-permute-start(bf16[32,1152]{1,0:T(8,128)(2,1)S(1)} %get-tuple-element.27), channel_id=1, source_target_pairs={{0,8},{4,12},{8,0},{12,4},{16,24},{20,28},{24,16},{28,20},{1,9},{5... | collective-permute-start | bytes 221192 | tf_op jit(solution)/shard_map/ppermute | solution.py:571
  28.7 1.7 %feature_grad.1 = f32[192,1024]{1,0:T(8,128)} custom-call(bf16[192,128]{1,0:T(8,128)(2,1)S(1)} %pointwise.1.own_ref.refs_4_, bf16[192,128]{1,0:T(8,128)(2,1)S(1)} %collective-permute-done.3.above_ref.refs_5_, bf16[192,128]{1,0:T(8,128)(2,1)S(1)} %collective-permute-done.4.below_ref.refs_5_, bf16[9,1024,128]{2,1,0:T(8,128)(2,1)S(1)} %get-tuple-element.17.w_ref), custom_call_target="tpu_custom_call" | custom-call | flops 452984832 | bytes 3145728 | tf_op jit(solution)/shard_map/feature_grad/pallas_call | solution.py:480
  30.4 0.1 collective-permute-done.8.refs_1_
  30.5 1.7 %collective-permute-done.9.refs_2_ = bf16[32,1152]{1,0:T(8,128)(2,1)S(1)} collective-permute-done((bf16[32,1152]{1,0:T(8,128)(2,1)S(1)}, bf16[32,1152]{1,0:T(8,128)(2,1)S(1)}, u32[]{:S(2)}, u32[]{:S(2)}) %collective-permute-start.9) | collective-permute-done | bytes 73760 | tf_op jit(solution)/shard_map/ppermute | solution.py:571
  32.2 0.5 %collective-permute-done.10.refs_3_ = bf16[32,1152]{1,0:T(8,128)(2,1)S(1)} collective-permute-done((bf16[32,1152]{1,0:T(8,128)(2,1)S(1)}, bf16[32,1152]{1,0:T(8,128)(2,1)S(1)}, u32[]{:S(2)}, u32[]{:S(2)}) %collective-permute-start.10) | collective-permute-done | bytes 73760 | tf_op jit(solution)/shard_map/ppermute | solution.py:571
  32.7 0.7 %final_sum.1 = f32[288,128]{1,0:T(8,128)} custom-call(bf16[32,1152]{1,0:T(8,128)(2,1)S(1)} %get-tuple-element.24.refs_0_, bf16[32,1152]{1,0:T(8,128)(2,1)S(1)} %collective-permute-done.8.refs_1_, bf16[32,1152]{1,0:T(8,128)(2,1)S(1)} %collective-permute-done.9.refs_2_, bf16[32,1152]{1,0:T(8,128)(2,1)S(1)} %collective-permute-done.10.refs_3_), custom_call_target="tpu_custom_call" | custom-call | tf_op jit(solution)/shard_map/final_sum/pallas_call | solution.py:440
  (1 shorter events, 0.0 us)
Async XLA Ops:
  0.6 8.9 %copy-start.2 = (s32[1,6,32]{2,0,1:T(1,128)S(1)}, s32[1,6,32]{2,0,1:T(1,128)}, u32[]{:S(2)}) copy-start(s32[1,6,32]{2,0,1:T(1,128)} %param.8) | copy-start | bytes 2308
  0.6 8.9 %copy-start.3 = (s32[1,6,32]{2,0,1:T(1,128)S(1)}, s32[1,6,32]{2,0,1:T(1,128)}, u32[]{:S(2)}) copy-start(s32[1,6,32]{2,0,1:T(1,128)} %param.7) | copy-start | bytes 2308
  0.7 13.0 %copy-start = (bf16[128,3]{0,1:T(4,128)(2,1)S(1)}, bf16[128,3]{0,1:T(4,128)(2,1)}, u32[]{:S(2)}) copy-start(bf16[128,3]{0,1:T(4,128)(2,1)} %param.11) | copy-start | bytes 2308
  0.7 13.0 %copy-start.1 = (f32[128]{0:T(128)S(1)}, f32[128]{0:T(128)}, u32[]{:S(2)}) copy-start(f32[128]{0:T(128)} %param.10) | copy-start | bytes 1540
  3.1 8.9 %collective-permute-start = (bf16[192,256]{1,0:T(8,128)(2,1)S(1)}, bf16[192,256]{1,0:T(8,128)(2,1)S(1)}, u32[]{:S(2)}, u32[]{:S(2)}) collective-permute-start(bf16[192,256]{1,0:T(8,128)(2,1)S(1)} %get-tuple-element.15), channel_id=1, source_target_pairs={{0,2},{1,3},{2,0},{3,1},{4,6},{5,7},{6,4},{7,5},{8,10},{9,11},{10,... | collective-permute-start | bytes 294920 | tf_op jit(solution)/shard_map/ppermute | solution.py:521
  7.2 6.4 %collective-permute-start.1 = (bf16[192,384]{1,0:T(8,128)(2,1)S(1)}, bf16[192,384]{1,0:T(8,128)(2,1)S(1)}, u32[]{:S(2)}, u32[]{:S(2)}) collective-permute-start(bf16[192,384]{1,0:T(8,128)(2,1)S(1)} %get-tuple-element.19), channel_id=1, source_target_pairs={{0,1},{1,0},{2,3},{3,2},{4,5},{5,4},{6,7},{7,6},{8,9},{9,8},{10,11... | collective-permute-start | bytes 442376 | tf_op jit(solution)/shard_map/ppermute | solution.py:521
  8.8 1.1 %collective-permute-start.2 = (bf16[192,128]{1,0:T(8,128)(2,1)S(1)}, bf16[192,128]{1,0:T(8,128)(2,1)S(1)}, u32[]{:S(2)}, u32[]{:S(2)}) collective-permute-start(bf16[192,128]{1,0:T(8,128)(2,1)S(1)} %get-tuple-element.18.after_ref), channel_id=1, source_target_pairs={{1,2},{2,1},{5,6},{6,5},{9,10},{10,9},{13,14},{14,13},{17,18},{18,... | collective-permute-start | bytes 147464 | tf_op jit(solution)/shard_map/ppermute | solution.py:519
  9.4 9.9 %collective-permute-start.5 = (bf16[192,256]{1,0:T(8,128)(2,1)S(1)}, bf16[192,256]{1,0:T(8,128)(2,1)S(1)}, u32[]{:S(2)}, u32[]{:S(2)}) collective-permute-start(bf16[192,256]{1,0:T(8,128)(2,1)S(1)} %get-tuple-element.21), channel_id=1, source_target_pairs={{0,3},{1,2},{2,1},{3,0},{4,7},{5,6},{6,5},{7,4},{8,11},{9,10},{10,... | collective-permute-start | bytes 294920 | tf_op jit(solution)/shard_map/ppermute | solution.py:521
  14.1 6.3 %collective-permute-start.3 = (bf16[192,128]{1,0:T(8,128)(2,1)S(1)}, bf16[192,128]{1,0:T(8,128)(2,1)S(1)}, u32[]{:S(2)}, u32[]{:S(2)}) collective-permute-start(bf16[192,128]{1,0:T(8,128)(2,1)S(1)} %pointwise.1.own_ref.refs_4_), channel_id=1, source_target_pairs={{0,1},{1,2},{2,3},{3,0},{4,5},{5,6},{6,7},{7,4},{8,9},{9,10},{10,1... | collective-permute-start | bytes 147464 | tf_op jit(solution)/shard_map/ppermute | solution.py:549
  17.7 4.4 %collective-permute-start.4 = (bf16[192,128]{1,0:T(8,128)(2,1)S(1)}, bf16[192,128]{1,0:T(8,128)(2,1)S(1)}, u32[]{:S(2)}, u32[]{:S(2)}) collective-permute-start(bf16[192,128]{1,0:T(8,128)(2,1)S(1)} %pointwise.1.own_ref.refs_4_), channel_id=1, source_target_pairs={{0,3},{1,0},{2,1},{3,2},{4,7},{5,4},{6,5},{7,6},{8,11},{9,8},{10,9... | collective-permute-start | bytes 147464 | tf_op jit(solution)/shard_map/ppermute | solution.py:549
  18.0 5.0 %collective-permute-start.6 = (bf16[192,128]{1,0:T(8,128)(2,1)S(1)}, bf16[192,128]{1,0:T(8,128)(2,1)S(1)}, u32[]{:S(2)}, u32[]{:S(2)}) collective-permute-start(bf16[192,128]{1,0:T(8,128)(2,1)S(1)} %pointwise.1.own_ref.refs_4_), channel_id=1, source_target_pairs={{0,2},{1,3},{2,0},{3,1},{4,6},{5,7},{6,4},{7,5},{8,10},{9,11},{10,... | collective-permute-start | bytes 147464 | tf_op jit(solution)/shard_map/ppermute | solution.py:549
  23.4 1.6 %collective-permute-start.7 = (bf16[128,1152]{1,0:T(8,128)(2,1)S(1)}, bf16[128,1152]{1,0:T(8,128)(2,1)S(1)}, u32[]{:S(2)}, u32[]{:S(2)}) collective-permute-start(bf16[128,1152]{1,0:T(8,128)(2,1)S(1)} %kernel_grad.5), channel_id=1, source_target_pairs={{0,4},{4,0},{8,12},{12,8},{16,20},{20,16},{24,28},{28,24},{1,5},{5... | collective-permute-start | bytes 884744 | tf_op jit(solution)/shard_map/ppermute | solution.py:565
  25.1 5.3 %collective-permute-start.8 = (bf16[32,1152]{1,0:T(8,128)(2,1)S(1)}, bf16[32,1152]{1,0:T(8,128)(2,1)S(1)}, u32[]{:S(2)}, u32[]{:S(2)}) collective-permute-start(bf16[32,1152]{1,0:T(8,128)(2,1)S(1)} %get-tuple-element.25), channel_id=1, source_target_pairs={{0,24},{4,28},{8,16},{12,20},{16,8},{20,12},{24,0},{28,4},{1,25},{... | collective-permute-start | bytes 221192 | tf_op jit(solution)/shard_map/ppermute | solution.py:571
  27.8 4.4 %collective-permute-start.9 = (bf16[32,1152]{1,0:T(8,128)(2,1)S(1)}, bf16[32,1152]{1,0:T(8,128)(2,1)S(1)}, u32[]{:S(2)}, u32[]{:S(2)}) collective-permute-start(bf16[32,1152]{1,0:T(8,128)(2,1)S(1)} %get-tuple-element.26), channel_id=1, source_target_pairs={{0,16},{4,20},{8,24},{12,28},{16,0},{20,4},{24,8},{28,12},{1,17},{... | collective-permute-start | bytes 221192 | tf_op jit(solution)/shard_map/ppermute | solution.py:571
  28.3 4.4 %collective-permute-start.10 = (bf16[32,1152]{1,0:T(8,128)(2,1)S(1)}, bf16[32,1152]{1,0:T(8,128)(2,1)S(1)}, u32[]{:S(2)}, u32[]{:S(2)}) collective-permute-start(bf16[32,1152]{1,0:T(8,128)(2,1)S(1)} %get-tuple-element.27), channel_id=1, source_target_pairs={{0,8},{4,12},{8,0},{12,4},{16,24},{20,28},{24,16},{28,20},{1,9},{5... | collective-permute-start | bytes 221192 | tf_op jit(solution)/shard_map/ppermute | solution.py:571
